TPU v7x, 32 devices: a whole 2x2x4 slice. The times are simulated.
32 devices in a mesh: groups: 2 (over y), tm: 4 (over z), mp: 4 (over x, core).
Axes of the slice: x: 2, y: 2, z: 4, core: 2. Of those that a mesh axis runs over, the one named last changes fastest.
Arguments:
- waveform: float32 [1310720], P(('groups', 'tm', 'mp')), parts along dimension 0, may hold values from -0.8 to 0.8
- segment_start: int32 [2048], P(('groups', 'tm')), parts along dimension 0, may hold values from 0 to 1023, as said below
- segment_end: int32 [2048], P(('groups', 'tm')), parts along dimension 0, may hold values from 1 to 1024, as said below
- w_subsample: bfloat16 [512, 1536], replicated, may hold values from -0.25 to 0.25
- w_attention: bfloat16 [3, 1536, 1536], P(None, None, 'mp')
- w_output: bfloat16 [1536, 1536], P('mp'), may hold values from -0.15625 to 0.15625
- gain_convolution: float32 [1536], replicated, may hold values from 0.1 to 1.9
- w_depthwise: bfloat16 [31, 1536], replicated, may hold values from -1 to 1
Outputs:
- encoded: bfloat16 [2048, 1536], P(('groups', 'tm', 'mp')), parts along dimension 0
There are 2 independent parts, one for each index of `groups`. A program takes and returns all parts, laid end to end along the dimension named above; an argument that names none is the same for every part. Nothing has to cross between parts.
Inputs may be any that keep to these rules, and one draw needn't show every extreme that they name: Segments are contiguous runs of frames that tile the slab: segment_start[i] <= i < segment_end[i], and all frames of a run share both values; every run has 150 to 750 frames except the first and the last, which may be shorter; one run of exactly 750 frames lies in every draw. `segment_end`: the end of the run holding each frame, as described for segment_start.
All inputs are finite; a program needn't handle non-finite values.
Results may differ from a plain program's by a relative error of at most 0.015.
Values may be sent and summed in bfloat16 or wider, within the bound.
No kernel may reach another device: no remote copies, remote signals or barrier semaphores. Data moves between devices by JAX's collectives and lax.ppermute only.
A program may use at most 64 MiB of HBM per device.

v0:
```python
import math

import jax
import jax.numpy as jnp
from jax import lax
from jax.sharding import PartitionSpec as P

HD = 64
NMEL = 128
NFFT = 400
HOP = 160
BINS = 256
SUB = 4
KERNEL = 31
SEG_MAX = 750


def shifted(block, axis, distance):
    devices = range(lax.axis_size(axis))
    route = [(i - distance, i) for i in devices if i - distance in devices]
    return lax.ppermute(block, axis, route)


def with_halo(cells, sides, width):
    for axis, dim in sides:
        count = lax.axis_size(axis)
        ends = count - 1
        head = lax.slice_in_dim(cells, 0, width, axis=dim)
        tail = lax.slice_in_dim(cells, cells.shape[dim] - width, cells.shape[dim], axis=dim)
        cells = jnp.concatenate(
            [
                lax.ppermute(tail, axis, [(i, (i + 1) % count) for i in range(ends)]),
                cells,
                lax.ppermute(head, axis, [((i + 1) % count, i) for i in range(ends)]),
            ],
            axis=dim,
        )
    return cells


def fourier_table():
    sample_index = jnp.arange(NFFT, dtype=jnp.int32)[:, None]
    bin_index = jnp.arange(BINS, dtype=jnp.int32)[None, :]
    phase_int = sample_index * bin_index % NFFT
    angle_rad = phase_int.astype(jnp.float32) * (2.0 * math.pi / NFFT)
    window_row = 0.5 - 0.5 * jnp.cos(jnp.arange(NFFT, dtype=jnp.float32) * (2.0 * math.pi / NFFT))
    kept_bins = bin_index <= NFFT // 2
    cosine_part = jnp.where(kept_bins, jnp.cos(angle_rad), 0.0) * window_row[:, None]
    sine_part = jnp.where(kept_bins, -jnp.sin(angle_rad), 0.0) * window_row[:, None]
    return jnp.concatenate([cosine_part, sine_part], axis=1)


def mel_bank():
    mel_top = 2595.0 * math.log10(1.0 + 8000.0 / 700.0)
    mel_points = jnp.arange(NMEL + 2, dtype=jnp.float32) * (mel_top / (NMEL + 1))
    hertz_points = 700.0 * (jnp.power(10.0, mel_points / 2595.0) - 1.0)
    edges = hertz_points * (NFFT / 16000.0)
    centers = edges[1:-1]
    widths = jnp.maximum(edges[2:] - edges[1:-1], 1.0)
    bin_value = jnp.arange(BINS, dtype=jnp.float32)[:, None]
    triangle = jnp.maximum(0.0, 1.0 - jnp.abs(bin_value - centers[None, :]) / widths[None, :])
    return jnp.where(bin_value <= NFFT // 2, triangle, 0.0)


def frame_rows(padded, frame_count):
    blocks_needed = -(-NFFT // HOP)
    blocks = padded.reshape(frame_count + blocks_needed - 1, HOP)
    pieces = [blocks[offset : offset + frame_count] for offset in range(blocks_needed)]
    return jnp.concatenate(pieces, axis=1)[:, :NFFT]


def log_mel(frames):
    spectrum = jnp.dot(
        frames, fourier_table(), precision=lax.Precision.HIGHEST, preferred_element_type=jnp.float32
    )
    spectral_power = jnp.square(spectrum[:, :BINS]) + jnp.square(spectrum[:, BINS:])
    energy = jnp.dot(
        spectral_power,
        mel_bank(),
        precision=lax.Precision.HIGHEST,
        preferred_element_type=jnp.float32,
    )
    return jnp.log(energy + 1e-06)


def normalize(values):
    values = values.astype(jnp.float32)
    center = jnp.mean(values, axis=-1, keepdims=True)
    spread = jnp.mean(jnp.square(values - center), axis=-1, keepdims=True)
    return (values - center) * lax.rsqrt(spread + 1e-05)


def layer_norm(values, gain_row):
    return normalize(values) * gain_row


def fold_keys(state, pair_block, positions, queries, starts, finish):
    running_max, denominator, numerator = state
    row_count = pair_block.shape[0]
    heads_local = queries.shape[1]
    local_width = heads_local * HD
    key_block = pair_block[:, :local_width].reshape(row_count, heads_local, HD)
    value_block = pair_block[:, local_width:].reshape(row_count, heads_local, HD)
    scores = jnp.einsum("qhd,khd->qhk", queries, key_block, preferred_element_type=jnp.float32) * (
        1.0 / math.sqrt(HD)
    )
    allowed = (positions[None, :] >= starts[:, None]) & (positions[None, :] < finish[:, None])
    scores = jnp.where(allowed[:, None, :], scores, -1e30)
    new_max = jnp.maximum(running_max, jnp.max(scores, axis=-1))
    weights = jnp.exp(scores - new_max[..., None])
    factor = jnp.exp(running_max - new_max)
    denominator = denominator * factor + jnp.sum(weights, axis=-1)
    numerator = numerator * factor[..., None] + jnp.einsum(
        "qhk,khd->qhd",
        weights.astype(jnp.bfloat16),
        value_block,
        preferred_element_type=jnp.float32,
    )
    return (new_max, denominator, numerator)


def shards(
    waveform,
    segment_start,
    segment_end,
    w_subsample,
    w_attention,
    w_output,
    gain_convolution,
    w_depthwise,
):
    frames_local = waveform.shape[0] // (SUB * HOP)
    frames_shard = segment_start.shape[0]
    local_width = w_attention.shape[2]
    heads_local = local_width // HD
    time_index = lax.axis_index("tm")
    model_index = lax.axis_index("mp")
    blocks_needed = -(-NFFT // HOP)
    next_samples = shifted(waveform[: NFFT - HOP], ("tm", "mp"), -1)
    tail_zeros = jnp.zeros((blocks_needed * HOP - NFFT,), waveform.dtype)
    padded = jnp.concatenate([waveform, next_samples, tail_zeros])
    stacked = (
        log_mel(frame_rows(padded, frames_local * SUB))
        .reshape(frames_local, SUB * NMEL)
        .astype(jnp.bfloat16)
    )
    all_stacked = lax.all_gather(stacked, "mp", axis=0, tiled=True)
    all_features = jnp.dot(all_stacked, w_subsample, preferred_element_type=jnp.float32).astype(
        jnp.bfloat16
    )
    features = lax.dynamic_slice_in_dim(all_features, model_index * frames_local, frames_local, 0)
    portion = normalize(all_features).astype(jnp.bfloat16)
    mapped = jnp.einsum("rd,kdc->rkc", portion, w_attention, preferred_element_type=jnp.float32)
    projected = mapped.astype(jnp.bfloat16).reshape(portion.shape[0], 3 * local_width)
    queries = projected[:, :local_width].reshape(frames_shard, heads_local, HD)
    pair_rows = projected[:, local_width:]
    own_positions = time_index * frames_shard + jnp.arange(frames_shard, dtype=jnp.int32)
    state = (
        jnp.full((frames_shard, heads_local), -1e30, jnp.float32),
        jnp.zeros((frames_shard, heads_local), jnp.float32),
        jnp.zeros((frames_shard, heads_local, HD), jnp.float32),
    )
    state = fold_keys(state, pair_rows, own_positions, queries, segment_start, segment_end)
    reach_shards = min((SEG_MAX - 2) // frames_shard + 1, lax.axis_size("tm") - 1)
    for distance in range(1, reach_shards + 1):
        for leftward in (True, False):
            shift_by = distance if leftward else -distance
            arrived = shifted(pair_rows, "tm", shift_by)
            positions = (time_index - shift_by) * frames_shard + jnp.arange(
                frames_shard, dtype=jnp.int32
            )
            state = fold_keys(state, arrived, positions, queries, segment_start, segment_end)
    running_max, denominator, numerator = state
    attended = (
        (numerator / denominator[..., None]).reshape(frames_shard, local_width).astype(jnp.bfloat16)
    )
    branch = lax.psum_scatter(
        jnp.dot(attended, w_output, preferred_element_type=jnp.float32).astype(jnp.bfloat16),
        "mp",
        scatter_dimension=0,
        tiled=True,
    ).astype(jnp.float32)
    mixed_rows = (features.astype(jnp.float32) + branch).astype(jnp.bfloat16)
    conv_input = layer_norm(mixed_rows, gain_convolution).astype(jnp.bfloat16)
    half_kernel = KERNEL // 2
    haloed = with_halo(conv_input, ((("tm", "mp"), 0),), half_kernel)
    convolved = jnp.zeros((frames_local, conv_input.shape[1]), jnp.float32)
    for tap_index in range(KERNEL):
        convolved = convolved + haloed[tap_index : tap_index + frames_local].astype(
            jnp.float32
        ) * w_depthwise[tap_index].astype(jnp.float32)
    return (mixed_rows.astype(jnp.float32) + jax.nn.silu(convolved)).astype(jnp.bfloat16)


def solution(mesh):
    placed = (
        P(("groups", "tm", "mp")),
        P(("groups", "tm")),
        P(("groups", "tm")),
        P(),
        P(None, None, "mp"),
        P("mp", None),
        P(),
        P(),
    )
    return jax.shard_map(
        shards,
        mesh=mesh,
        in_specs=placed,
        out_specs=P(("groups", "tm", "mp"), None),
        check_vma=False,
    )
```

profile of v0, /device:TPU:3, one launch (start us, length us, event | category | flops | bytes accessed | tf_op | source)
XLA Modules:
  0.0 143.1 jit_solution(2434125317610870211)
XLA Ops:
  6.5 0.8 slice.318
  7.4 2.7 %collective-permute-start = (f32[240]{0:T(256)S(1)}, f32[240]{0:T(256)S(1)}, u32[]{:S(2)}, u32[]{:S(2)}) collective-permute-start(f32[240]{0:T(256)S(1)} %slice.318), channel_id=1, source_target_pairs={{1,0},{2,1},{3,2},{4,3},{5,4},{6,5},{7,6},{8,7},{9,8},{10,9},{11,1... | collective-permute-start | bytes 2888 | tf_op jit(solution)/shard_map/ppermute | solution.py:21
  10.1 0.5 iota_compare_fusion.1
  10.7 0.7 fusion.125
  11.3 3.2 %select_multiply_fusion.1 = (f32[400,256]{1,0:T(8,128)}, f32[400,256]{1,0:T(8,128)}) fusion(f32[400]{0:T(512)S(1)} %multiply_subtract_fusion, pred[256]{0:T(512)(128)(4,1)} %iota_compare_fusion.1), kind=kLoop, calls=%fused_computation.116 | loop fusion | flops 1433600 | bytes 821056 | tf_op jit(solution)/shard_map/mul | solution.py:48
  14.6 1.9 %compare_and_fusion.6 = (pred[256,256]{0,1:T(8,128)(4,1)}, pred[256,256]{0,1:T(8,128)(4,1)}, pred[256,256]{0,1:T(8,128)(4,1)}, pred[256,256]{0,1:T(8,128)(4,1)},...) fusion(s32[256]{0:T(256)} %param.10, s32[256]{0:T(256)} %param.9, ...), kind=kLoop, calls=%fused_computation.135 | loop fusion | flops 1376256 | bytes 467968 | tf_op jit(solution)/shard_map/and | solution.py:107
  16.4 1.8 %slice.317 = f32[256,160]{1,0:T(8,128)} reshape(f32[40960]{0:T(1024)} %param.8) | data formatting | bytes 327680 | tf_op jit(solution)/shard_map/slice | solution.py:68
  18.2 1.7 %concatenate.48 = f32[41280]{0:T(1024)} concatenate(f32[40960]{0:T(1024)} %param.8, f32[240]{0:T(256)S(1)} %collective-permute-done, f32[80]{0:T(128)S(1)} %broadcast_in_dim.82), dimensions={0} | concatenate | bytes 330240 | tf_op jit(solution)/shard_map/concatenate | solution.py:141
  19.8 1.7 %slice.407 = f32[40960]{0:T(1024)} slice(f32[41280]{0:T(1024)} %concatenate.48), slice={[320:41280]} | slice | bytes 327680 | tf_op jit(solution)/shard_map/slice | solution.py:68
  21.6 1.8 %slice.322 = f32[256,160]{1,0:T(8,128)} reshape(f32[40960]{0:T(1024)} %slice.407) | data formatting | bytes 327680 | tf_op jit(solution)/shard_map/slice | solution.py:68
  23.3 1.7 %pad_maximum_fusion.6 = f32[40960]{0:T(1024)} fusion(f32[240]{0:T(256)S(1)} %collective-permute-done, f32[40960]{0:T(1024)} %param.8), kind=kLoop, calls=%fused_computation.190 | loop fusion | flops 40960 | bytes 328640 | tf_op jit(solution)/shard_map/concatenate | solution.py:141
  25.0 1.8 %slice.320 = f32[256,160]{1,0:T(8,128)} reshape(f32[40960]{0:T(1024)} %pad_maximum_fusion.6) | data formatting | bytes 327680 | tf_op jit(solution)/shard_map/slice | solution.py:68
  26.8 2.5 %fusion.35 = f32[256,512]{1,0:T(8,128)S(1)} fusion(f32[400,256]{1,0:T(8,128)} %get-tuple-element.71, f32[400,256]{1,0:T(8,128)} %get-tuple-element.70, f32[256,160]{1,0:T(8,128)} %slice.322, f32[256,160]{1,0:T(8,128)} %slice.320, f32[256,160]{1,0:T(8,128)} %slice.317), kind=kOutput, calls=%fused_computation.90 | convolution fusion | flops 629555200 | bytes 1835008 | tf_op jit(solution)/shard_map/dot_general | solution.py:73
  29.3 1.1 fusion.34
  30.4 1.5 %convert_element_type.229 = bf16[64,512]{1,0:T(8,128)(2,1)} reshape(bf16[256,128]{1,0:T(8,128)(2,1)} %fusion.34) | data formatting | bytes 131072 | tf_op jit(solution)/shard_map/convert_element_type | solution.py:145
  31.9 6.1 %all_gather.3 = bf16[256,512]{1,0:T(8,128)(2,1)S(1)} all-gather(bf16[64,512]{1,0:T(8,128)(2,1)} %convert_element_type.229), channel_id=1, replica_groups=mesh['groups'=2,'tm'=4,'mp'=4] {'mp'}, dimensions={0}, use_global_device_ids=true | all-gather | bytes 327680 | tf_op jit(solution)/shard_map/all_gather | solution.py:147
  37.9 2.1 %convert_reduce_fusion = (f32[256]{0:T(256)S(1)}, bf16[256,1536]{1,0:T(8,128)(2,1)S(1)}) fusion(bf16[256,512]{1,0:T(8,128)(2,1)S(1)} %all_gather.3, bf16[512,1536]{1,0:T(8,128)(2,1)} %param.11), kind=kOutput, calls=%fused_computation.3 | convolution fusion | flops 403832576 | bytes 2622464 | tf_op jit(solution)/shard_map/dot_general | solution.py:148
  40.4 0.5 copy-done.1
  40.9 2.1 %convolution_convert_fusion.2 = bf16[256,3,384]{2,0,1:T(8,128)(2,1)} fusion(bf16[3,1536,384]{2,1,0:T(8,128)(2,1)S(1)} %copy-done, bf16[256,1536]{1,0:T(8,128)(2,1)S(1)} %get-tuple-element.82, f32[256]{0:T(256)S(1)} %add_rsqrt_fusion, f32[256]{0:T(256)S(1)} %broadcast_multiply_fusion), kind=kOutput, calls=%fused_computation.36 | convolution fusion | flops 907837440 | bytes 4917248 | tf_op jit(solution)/shard_map/rd,kdc->rkc/dot_general | solution.py:153
  42.9 2.1 %copy.16 = bf16[256,3,384]{0,2,1:T(8,128)(2,1)} copy(bf16[256,3,384]{2,0,1:T(8,128)(2,1)} %convolution_convert_fusion.2) | data formatting | bytes 1179648 | tf_op jit(solution)/shard_map/convert_element_type | solution.py:154
  45.1 1.1 slice.413
  46.2 4.2 %collective-permute-start.3 = (bf16[256,768]{0,1:T(8,128)(2,1)S(1)}, bf16[256,768]{0,1:T(8,128)(2,1)S(1)}, u32[]{:S(2)}, u32[]{:S(2)}) collective-permute-start(bf16[256,768]{0,1:T(8,128)(2,1)S(1)} %slice.413), channel_id=1, source_target_pairs={{0,8},{4,12},{1,9},{5,13},{2,10},{6,14},{3,11},{7,15},{16,24},{20,... | collective-permute-start | bytes 1179656 | tf_op jit(solution)/shard_map/ppermute | solution.py:21
  50.4 1.2 fusion.117
  51.6 1.4 collective-permute-start.2
  53.0 4.0 %collective-permute-start.1 = (bf16[256,768]{0,1:T(8,128)(2,1)S(1)}, bf16[256,768]{0,1:T(8,128)(2,1)S(1)}, u32[]{:S(2)}, u32[]{:S(2)}) collective-permute-start(bf16[256,768]{0,1:T(8,128)(2,1)S(1)} %slice.413), channel_id=1, source_target_pairs={{0,4},{4,8},{8,12},{1,5},{5,9},{9,13},{2,6},{6,10},{10,14},{3,7},{... | collective-permute-start | bytes 1179656 | tf_op jit(solution)/shard_map/ppermute | solution.py:21
  57.0 1.3 collective-permute-start.4
  58.3 5.9 %collective-permute-start.5 = (bf16[256,768]{0,1:T(8,128)(2,1)S(1)}, bf16[256,768]{0,1:T(8,128)(2,1)S(1)}, u32[]{:S(2)}, u32[]{:S(2)}) collective-permute-start(bf16[256,768]{0,1:T(8,128)(2,1)S(1)} %slice.413), channel_id=1, source_target_pairs={{0,12},{1,13},{2,14},{3,15},{16,28},{17,29},{18,30},{19,31}} | collective-permute-start | bytes 1179656 | tf_op jit(solution)/shard_map/ppermute | solution.py:21
  64.2 0.4 fusion.132
  64.7 1.5 %collective-permute-start.6 = (bf16[256,768]{0,1:T(8,128)(2,1)S(1)}, bf16[256,768]{0,1:T(8,128)(2,1)S(1)}, u32[]{:S(2)}, u32[]{:S(2)}) collective-permute-start(bf16[256,768]{0,1:T(8,128)(2,1)S(1)} %slice.413), channel_id=1, source_target_pairs={{12,0},{13,1},{14,2},{15,3},{28,16},{29,17},{30,18},{31,19}} | collective-permute-start | bytes 1179656 | tf_op jit(solution)/shard_map/ppermute | solution.py:21
  66.3 0.4 fusion.129
  67.1 0.4 fusion.130
  67.6 0.4 fusion.131
  68.1 22.1 %collective-permute-done.4 = bf16[256,768]{0,1:T(8,128)(2,1)S(1)} collective-permute-done((bf16[256,768]{0,1:T(8,128)(2,1)S(1)}, bf16[256,768]{0,1:T(8,128)(2,1)S(1)}, u32[]{:S(2)}, u32[]{:S(2)}) %collective-permute-start.4) | collective-permute-done | bytes 393248 | tf_op jit(solution)/shard_map/ppermute | solution.py:21
  90.2 0.4 fusion.128
  91.0 0.4 fusion.127
  91.5 0.4 fusion.126
  95.9 0.4 fusion.32
  96.3 0.8 copy-done.2
  97.2 1.5 %convolution_convert_fusion = bf16[256,1536]{1,0:T(8,128)(2,1)} fusion(bf16[256,384]{0,1:T(8,128)(2,1)S(1)} %bitcast.113, bf16[384,1536]{1,0:T(8,128)(2,1)S(1)} %copy-done.2), kind=kOutput, calls=%fused_computation | convolution fusion | flops 302383104 | bytes 2162688 | tf_op jit(solution)/shard_map/dot_general | solution.py:178
  98.7 2.3 %convert_reduce_fusion.32 = (f32[1536]{0:T(1024)S(1)}, f32[1536]{0:T(1024)S(1)}, f32[1536]{0:T(1024)}, f32[1536]{0:T(1024)}, f32[1536]{0:T(1024)}, /*index=5*/f3...) fusion(bf16[31,1536]{1,0:T(8,128)(2,1)} %param.15), kind=kLoop, calls=%fused_computation.241 | loop fusion | flops 29184 | bytes 175104 | tf_op jit(solution)/shard_map/mul | solution.py:189
  101.0 18.9 %reduce-scatter.2.cloned.1.call-done = bf16[64,1536]{1,0:T(8,128)(2,1)} async-done(((bf16[256,1536]{1,0:T(8,128)(2,1)}), bf16[64,1536]{1,0:T(8,128)(2,1)}) %reduce-scatter.2.cloned.1.call-update) | async-done | bytes 196624 | tf_op jit(solution)/shard_map/reduce_scatter | solution.py:177
  120.0 1.3 convert_reduce_fusion.1
  121.6 0.8 fusion.67
  122.4 4.7 %collective-permute-start.7 = (bf16[15,1536]{1,0:T(8,128)(2,1)S(1)}, bf16[15,1536]{1,0:T(8,128)(2,1)S(1)}, u32[]{:S(2)}, u32[]{:S(2)}) collective-permute-start(bf16[15,1536]{1,0:T(8,128)(2,1)S(1)} %get-tuple-element.66), channel_id=1, source_target_pairs={{0,1},{1,2},{2,3},{3,4},{4,5},{5,6},{6,7},{7,8},{8,9},{9,10},{10,1... | collective-permute-start | bytes 138248 | tf_op jit(solution)/shard_map/ppermute | solution.py:32
  127.1 1.9 %collective-permute-start.8 = (bf16[15,1536]{1,0:T(8,128)(2,1)S(1)}, bf16[15,1536]{1,0:T(8,128)(2,1)S(1)}, u32[]{:S(2)}, u32[]{:S(2)}) collective-permute-start(bf16[15,1536]{1,0:T(8,128)(2,1)S(1)} %get-tuple-element.67), channel_id=1, source_target_pairs={{1,0},{2,1},{3,2},{4,3},{5,4},{6,5},{7,6},{8,7},{9,8},{10,9},{11,1... | collective-permute-start | bytes 138248 | tf_op jit(solution)/shard_map/ppermute | solution.py:34
  129.0 1.3 convert_reduce_fusion.31
  130.3 3.1 %collective-permute-done.8 = bf16[15,1536]{1,0:T(8,128)(2,1)S(1)} collective-permute-done((bf16[15,1536]{1,0:T(8,128)(2,1)S(1)}, bf16[15,1536]{1,0:T(8,128)(2,1)S(1)}, u32[]{:S(2)}, u32[]{:S(2)}) %collective-permute-start.8) | collective-permute-done | bytes 46112 | tf_op jit(solution)/shard_map/ppermute | solution.py:34
  133.5 2.7 %fusion.68 = bf16[64,1536]{1,0:T(8,128)(2,1)} fusion(bf16[64,1536]{1,0:T(8,128)(2,1)S(1)} %get-tuple-element.37, bf16[64,1536]{1,0:T(8,128)(2,1)S(1)} %fusion.67, bf16[15,1536]{1,0:T(8,128)(2,1)S(1)} %collective-permute-done.8, bf16[15,1536]{1,0:T(8,128)(2,1)S(1)} %collective-permute-done.7, f32[1536]{0:T(1024)S(1)} %get-tuple-element.34, ...), kind=kLoop, calls=%fused_computation.124 | loop fusion | flops 18579456 | bytes 872448 | tf_op jit(solution)/shard_map/convert_element_type | solution.py:192
  (101 shorter events, 5.5 us)
Async XLA Ops:
  6.5 34.4 %copy-start = (bf16[3,1536,384]{2,1,0:T(8,128)(2,1)S(1)}, bf16[3,1536,384]{2,1,0:T(8,128)(2,1)}, u32[]{:S(2)}) copy-start(bf16[3,1536,384]{2,1,0:T(8,128)(2,1)} %param.12) | copy-start | bytes 10616836
  6.5 113.4 %reduce-scatter.2.cloned.1.call-start = ((), (), s32[]{:S(2)}) async-start(), calls=%async_computation.1 | async-start | bytes 983040 | tf_op jit(solution)/shard_map/reduce_scatter | solution.py:177
  7.4 10.8 %collective-permute-start = (f32[240]{0:T(256)S(1)}, f32[240]{0:T(256)S(1)}, u32[]{:S(2)}, u32[]{:S(2)}) collective-permute-start(f32[240]{0:T(256)S(1)} %slice.318), channel_id=1, source_target_pairs={{1,0},{2,1},{3,2},{4,3},{5,4},{6,5},{7,6},{8,7},{9,8},{10,9},{11,1... | collective-permute-start | bytes 2888 | tf_op jit(solution)/shard_map/ppermute | solution.py:21
  21.5 7.7 %copy-start.27 = (f32[128]{0:T(128)S(1)}, f32[128]{0:T(128)}, u32[]{:S(2)}) copy-start(f32[128]{0:T(128)} %get-tuple-element.79) | copy-start | bytes 1540
  21.5 7.7 %copy-start.28 = (f32[128]{0:T(128)S(1)}, f32[128]{0:T(128)}, u32[]{:S(2)}) copy-start(f32[128]{0:T(128)} %get-tuple-element.80) | copy-start | bytes 1540
  40.0 0.9 copy-start.1
  45.1 19.1 %copy-start.9 = (pred[256,256]{0,1:T(8,128)(4,1)S(1)}, pred[256,256]{0,1:T(8,128)(4,1)}, u32[]{:S(2)}) copy-start(pred[256,256]{0,1:T(8,128)(4,1)} %get-tuple-element.72) | copy-start | bytes 196612
  46.2 18.6 %collective-permute-start.3 = (bf16[256,768]{0,1:T(8,128)(2,1)S(1)}, bf16[256,768]{0,1:T(8,128)(2,1)S(1)}, u32[]{:S(2)}, u32[]{:S(2)}) collective-permute-start(bf16[256,768]{0,1:T(8,128)(2,1)S(1)} %slice.413), channel_id=1, source_target_pairs={{0,8},{4,12},{1,9},{5,13},{2,10},{6,14},{3,11},{7,15},{16,24},{20,... | collective-permute-start | bytes 1179656 | tf_op jit(solution)/shard_map/ppermute | solution.py:21
  51.6 14.7 %copy-start.8 = (pred[256,256]{0,1:T(8,128)(4,1)S(1)}, pred[256,256]{0,1:T(8,128)(4,1)}, u32[]{:S(2)}) copy-start(pred[256,256]{0,1:T(8,128)(4,1)} %get-tuple-element.75) | copy-start | bytes 196612
  51.6 15.1 %collective-permute-start.2 = (bf16[256,768]{0,1:T(8,128)(2,1)S(1)}, bf16[256,768]{0,1:T(8,128)(2,1)S(1)}, u32[]{:S(2)}, u32[]{:S(2)}) collective-permute-start(bf16[256,768]{0,1:T(8,128)(2,1)S(1)} %slice.413), channel_id=1, source_target_pairs={{4,0},{8,4},{12,8},{5,1},{9,5},{13,9},{6,2},{10,6},{14,10},{7,3},{... | collective-permute-start | bytes 1179656 | tf_op jit(solution)/shard_map/ppermute | solution.py:21
  53.0 14.5 %collective-permute-start.1 = (bf16[256,768]{0,1:T(8,128)(2,1)S(1)}, bf16[256,768]{0,1:T(8,128)(2,1)S(1)}, u32[]{:S(2)}, u32[]{:S(2)}) collective-permute-start(bf16[256,768]{0,1:T(8,128)(2,1)S(1)} %slice.413), channel_id=1, source_target_pairs={{0,4},{4,8},{8,12},{1,5},{5,9},{9,13},{2,6},{6,10},{10,14},{3,7},{... | collective-permute-start | bytes 1179656 | tf_op jit(solution)/shard_map/ppermute | solution.py:21
  57.0 33.1 %collective-permute-start.4 = (bf16[256,768]{0,1:T(8,128)(2,1)S(1)}, bf16[256,768]{0,1:T(8,128)(2,1)S(1)}, u32[]{:S(2)}, u32[]{:S(2)}) collective-permute-start(bf16[256,768]{0,1:T(8,128)(2,1)S(1)} %slice.413), channel_id=1, source_target_pairs={{8,0},{12,4},{9,1},{13,5},{10,2},{14,6},{11,3},{15,7},{24,16},{28,... | collective-permute-start | bytes 1179656 | tf_op jit(solution)/shard_map/ppermute | solution.py:21
  58.3 32.3 %collective-permute-start.5 = (bf16[256,768]{0,1:T(8,128)(2,1)S(1)}, bf16[256,768]{0,1:T(8,128)(2,1)S(1)}, u32[]{:S(2)}, u32[]{:S(2)}) collective-permute-start(bf16[256,768]{0,1:T(8,128)(2,1)S(1)} %slice.413), channel_id=1, source_target_pairs={{0,12},{1,13},{2,14},{3,15},{16,28},{17,29},{18,30},{19,31}} | collective-permute-start | bytes 1179656 | tf_op jit(solution)/shard_map/ppermute | solution.py:21
  64.7 26.7 %collective-permute-start.6 = (bf16[256,768]{0,1:T(8,128)(2,1)S(1)}, bf16[256,768]{0,1:T(8,128)(2,1)S(1)}, u32[]{:S(2)}, u32[]{:S(2)}) collective-permute-start(bf16[256,768]{0,1:T(8,128)(2,1)S(1)} %slice.413), channel_id=1, source_target_pairs={{12,0},{13,1},{14,2},{15,3},{28,16},{29,17},{30,18},{31,19}} | collective-permute-start | bytes 1179656 | tf_op jit(solution)/shard_map/ppermute | solution.py:21
  66.2 0.8 copy-start.7
  66.8 0.8 copy-start.6
  67.6 22.6 %copy-start.5 = (pred[256,256]{0,1:T(8,128)(4,1)S(1)}, pred[256,256]{0,1:T(8,128)(4,1)}, u32[]{:S(2)}) copy-start(pred[256,256]{0,1:T(8,128)(4,1)} %get-tuple-element.76) | copy-start | bytes 196612
  90.1 0.8 copy-start.4
  90.7 0.8 copy-start.3
  95.9 1.3 copy-start.2
  119.9 13.5 %copy-start.10 = (f32[1536]{0:T(1024)S(1)}, f32[1536]{0:T(1024)}, u32[]{:S(2)}) copy-start(f32[1536]{0:T(1024)} %get-tuple-element.7) | copy-start | bytes 18436
  119.9 13.5 %copy-start.11 = (f32[1536]{0:T(1024)S(1)}, f32[1536]{0:T(1024)}, u32[]{:S(2)}) copy-start(f32[1536]{0:T(1024)} %get-tuple-element.8) | copy-start | bytes 18436
  119.9 13.5 %copy-start.12 = (f32[1536]{0:T(1024)S(1)}, f32[1536]{0:T(1024)}, u32[]{:S(2)}) copy-start(f32[1536]{0:T(1024)} %get-tuple-element.9) | copy-start | bytes 18436
  119.9 13.5 %copy-start.13 = (f32[1536]{0:T(1024)S(1)}, f32[1536]{0:T(1024)}, u32[]{:S(2)}) copy-start(f32[1536]{0:T(1024)} %get-tuple-element.10) | copy-start | bytes 18436
  119.9 13.5 %copy-start.14 = (f32[1536]{0:T(1024)S(1)}, f32[1536]{0:T(1024)}, u32[]{:S(2)}) copy-start(f32[1536]{0:T(1024)} %get-tuple-element.11) | copy-start | bytes 18436
  119.9 13.5 %copy-start.15 = (f32[1536]{0:T(1024)S(1)}, f32[1536]{0:T(1024)}, u32[]{:S(2)}) copy-start(f32[1536]{0:T(1024)} %get-tuple-element.12) | copy-start | bytes 18436
  119.9 13.5 %copy-start.16 = (f32[1536]{0:T(1024)S(1)}, f32[1536]{0:T(1024)}, u32[]{:S(2)}) copy-start(f32[1536]{0:T(1024)} %get-tuple-element.13) | copy-start | bytes 18436
  119.9 13.5 %copy-start.17 = (f32[1536]{0:T(1024)S(1)}, f32[1536]{0:T(1024)}, u32[]{:S(2)}) copy-start(f32[1536]{0:T(1024)} %get-tuple-element.14) | copy-start | bytes 18436
  119.9 13.5 %copy-start.18 = (f32[1536]{0:T(1024)S(1)}, f32[1536]{0:T(1024)}, u32[]{:S(2)}) copy-start(f32[1536]{0:T(1024)} %get-tuple-element.15) | copy-start | bytes 18436
  120.0 13.5 %copy-start.19 = (f32[1536]{0:T(1024)S(1)}, f32[1536]{0:T(1024)}, u32[]{:S(2)}) copy-start(f32[1536]{0:T(1024)} %get-tuple-element.16) | copy-start | bytes 18436
  120.0 13.5 %copy-start.20 = (f32[1536]{0:T(1024)S(1)}, f32[1536]{0:T(1024)}, u32[]{:S(2)}) copy-start(f32[1536]{0:T(1024)} %get-tuple-element.17) | copy-start | bytes 18436
  120.0 13.5 %copy-start.21 = (f32[1536]{0:T(1024)S(1)}, f32[1536]{0:T(1024)}, u32[]{:S(2)}) copy-start(f32[1536]{0:T(1024)} %get-tuple-element.18) | copy-start | bytes 18436
  120.0 13.5 %copy-start.22 = (f32[1536]{0:T(1024)S(1)}, f32[1536]{0:T(1024)}, u32[]{:S(2)}) copy-start(f32[1536]{0:T(1024)} %get-tuple-element.19) | copy-start | bytes 18436
  120.0 13.5 %copy-start.23 = (f32[1536]{0:T(1024)S(1)}, f32[1536]{0:T(1024)}, u32[]{:S(2)}) copy-start(f32[1536]{0:T(1024)} %get-tuple-element.20) | copy-start | bytes 18436
  120.0 13.5 %copy-start.24 = (f32[1536]{0:T(1024)S(1)}, f32[1536]{0:T(1024)}, u32[]{:S(2)}) copy-start(f32[1536]{0:T(1024)} %get-tuple-element.21) | copy-start | bytes 18436
  120.0 13.5 %copy-start.25 = (f32[1536]{0:T(1024)S(1)}, f32[1536]{0:T(1024)}, u32[]{:S(2)}) copy-start(f32[1536]{0:T(1024)} %get-tuple-element.22) | copy-start | bytes 18436
  120.0 13.5 %copy-start.26 = (f32[1536]{0:T(1024)S(1)}, f32[1536]{0:T(1024)}, u32[]{:S(2)}) copy-start(f32[1536]{0:T(1024)} %get-tuple-element.23) | copy-start | bytes 18436
  122.4 7.9 %collective-permute-start.7 = (bf16[15,1536]{1,0:T(8,128)(2,1)S(1)}, bf16[15,1536]{1,0:T(8,128)(2,1)S(1)}, u32[]{:S(2)}, u32[]{:S(2)}) collective-permute-start(bf16[15,1536]{1,0:T(8,128)(2,1)S(1)} %get-tuple-element.66), channel_id=1, source_target_pairs={{0,1},{1,2},{2,3},{3,4},{4,5},{5,6},{6,7},{7,8},{8,9},{9,10},{10,1... | collective-permute-start | bytes 138248 | tf_op jit(solution)/shard_map/ppermute | solution.py:32
  127.1 6.3 %collective-permute-start.8 = (bf16[15,1536]{1,0:T(8,128)(2,1)S(1)}, bf16[15,1536]{1,0:T(8,128)(2,1)S(1)}, u32[]{:S(2)}, u32[]{:S(2)}) collective-permute-start(bf16[15,1536]{1,0:T(8,128)(2,1)S(1)} %get-tuple-element.67), channel_id=1, source_target_pairs={{1,0},{2,1},{3,2},{4,3},{5,4},{6,5},{7,6},{8,7},{9,8},{10,9},{11,1... | collective-permute-start | bytes 138248 | tf_op jit(solution)/shard_map/ppermute | solution.py:34
Sparse Core Ops, SparseCore 0:
  98.8 21.0 reduce-scatter.1
where the time goes:
time: 144 us; the launch traced here: 143 us
  waiting for transfers between devices  44.1 us (31%)
  starting transfers between devices  27.6 us (19%)
  other arithmetic  18.7 us (13%)
  local copies, waits for them, and re-layouts  17.6 us (12%)
  matrix products  15 us (10%)
  between operations  14.1 us (10%)
  blocking collectives  6.06 us (4%)
    ppermute x7, waiting for transfers between devices, shifted(): return lax.ppermute(block, axis, route)  22.1 us
    ppermute x7, starting transfers between devices, shifted(): return lax.ppermute(block, axis, route)  21.1 us
    reduce_scatter x1, waiting for transfers between devices, shards(): lax.psum_scatter(jnp.dot(attended, w_output, preferred_element_type=jnp.f...  18.9 us
    slice x4, local copies, waits for them, and re-layouts, frame_rows(): blocks[offset:offset + frame_count]  6.98 us
    all_gather x1, blocking collectives, shards(): all_stacked = lax.all_gather(stacked, 'mp', axis=0, tiled=True)  6.06 us
    ppermute x1, starting transfers between devices, with_halo(): lax.ppermute(tail, axis, [(i, (i + 1) % count) for i in range(ends)])  4.65 us
    mul x2, other arithmetic, shards(): haloed[tap_index:tap_index + frames_local].astype(jnp.float32)  3.57 us
    mul x1, other arithmetic, fourier_table(): jnp.where(kept_bins, jnp.cos(angle_rad), 0.0) * window_row[:, None]  3.21 us
  transfers between devices with their start and end apart: 10, of which 3 were waited for; matrix products, arithmetic and copies ran while one was open for 11% of the time, Pallas kernels for 0%

commit v1 on v0

v1 whole, which is shorter than its diff:
```python
import math

import jax
import jax.numpy as jnp
import numpy as np
from jax import lax
from jax.experimental import pallas as pl
from jax.experimental.pallas import tpu as pltpu
from jax.sharding import PartitionSpec as P

HD = 64
NMEL = 128
NFFT = 400
HOP = 160
BINS = 256
SUB = 4
KERNEL = 31
SEG_MAX = 750
LANES = 128
HALO = 16
FRAME_ROWS = SUB * HOP // LANES
WIDE = -(-NFFT // LANES) * LANES
VMEM_BYTES = 40 * 1024 * 1024


def split_high_low(table):
    high = table.astype(jnp.bfloat16)
    low = (table - high.astype(np.float32)).astype(jnp.bfloat16)
    return high, low


def fourier_table():
    sample_index = np.arange(NFFT)[:, None]
    bin_index = np.arange(BINS)[None, :]
    angle = (sample_index * bin_index % NFFT) * (2.0 * math.pi / NFFT)
    window = 0.5 - 0.5 * np.cos(np.arange(NFFT) * (2.0 * math.pi / NFFT))
    kept = bin_index <= NFFT // 2
    cosine = np.where(kept, np.cos(angle), 0.0) * window[:, None]
    sine = np.where(kept, -np.sin(angle), 0.0) * window[:, None]
    table = np.concatenate([cosine, sine], axis=1).astype(np.float32)
    return np.pad(table, ((0, WIDE - NFFT), (0, 0)))


def mel_bank():
    mel_top = 2595.0 * math.log10(1.0 + 8000.0 / 700.0)
    mel_points = np.arange(NMEL + 2) * (mel_top / (NMEL + 1))
    edges = 700.0 * (np.power(10.0, mel_points / 2595.0) - 1.0) * (NFFT / 16000.0)
    widths = np.maximum(edges[2:] - edges[1:-1], 1.0)
    bin_value = np.arange(BINS)[:, None]
    triangle = np.maximum(0.0, 1.0 - np.abs(bin_value - edges[None, 1:-1]) / widths[None, :])
    return np.where(bin_value <= NFFT // 2, triangle, 0.0).astype(np.float32)


def dot32(left, right):
    return jnp.dot(left, right, preferred_element_type=jnp.float32)


def dot_split(values, high_ref, low_ref):
    high = values.astype(jnp.bfloat16)
    low = (values - high.astype(jnp.float32)).astype(jnp.bfloat16)
    return dot32(high, high_ref[...]) + (dot32(low, high_ref[...]) + dot32(high, low_ref[...]))


def normalize(values):
    center = jnp.mean(values, axis=-1, keepdims=True)
    shifted = values - center
    spread = jnp.mean(jnp.square(shifted), axis=-1, keepdims=True)
    return shifted * lax.rsqrt(spread + 1e-05)


def call(kernel, out_shape, operands, scratch=(), scalars=0, flops=0):
    specs = [pl.BlockSpec(memory_space=pltpu.SMEM)] * scalars
    specs += [pl.BlockSpec(memory_space=pltpu.VMEM)] * (len(operands) - scalars)
    return pl.pallas_call(
        kernel,
        out_shape=out_shape,
        in_specs=specs,
        out_specs=jax.tree.map(lambda _: pl.BlockSpec(memory_space=pltpu.VMEM), out_shape),
        scratch_shapes=list(scratch),
        compiler_params=pltpu.CompilerParams(vmem_limit_bytes=VMEM_BYTES),
        cost_estimate=pl.CostEstimate(flops=flops, bytes_accessed=1000000, transcendentals=0),
    )(*operands)


def log_mel_rows(samples, next_samples, frames_local):
    table_high, table_low = split_high_low(fourier_table())
    bank_high, bank_low = split_high_low(mel_bank())
    rows = frames_local * FRAME_ROWS
    extra = next_samples.shape[0]

    def kernel(wave, following, th, tl, bh, bl, out, held):
        held[0:rows, :] = wave[...]
        held[rows : rows + extra, :] = following[...]
        lines = [
            held[pl.ds(j, frames_local, stride=FRAME_ROWS), :] for j in range(FRAME_ROWS + extra)
        ]
        windows = []
        for sub in range(SUB):
            line, lane = divmod(sub * HOP, LANES)
            taken = jnp.concatenate(lines[line : line + WIDE // LANES], axis=1)
            windows.append(pltpu.roll(taken, WIDE - lane, axis=1) if lane else taken)
        spectrum = dot_split(jnp.concatenate(windows, axis=0), th, tl)
        power = jnp.square(spectrum[:, :BINS]) + jnp.square(spectrum[:, BINS:])
        mel = jnp.log(dot_split(power, bh, bl) + 1e-06)
        for sub in range(SUB):
            out[:, sub * NMEL : (sub + 1) * NMEL] = mel[
                sub * frames_local : (sub + 1) * frames_local
            ].astype(jnp.bfloat16)

    return call(
        kernel,
        jax.ShapeDtypeStruct((frames_local, SUB * NMEL), jnp.bfloat16),
        (samples, next_samples, table_high, table_low, bank_high, bank_low),
        scratch=[pltpu.VMEM((rows + 8, LANES), jnp.float32)],
        flops=6 * frames_local * SUB * WIDE * 2 * BINS,
    )


def project_rows(stacks, w_subsample, w_attention):
    counts = [stack.shape[0] for stack in stacks]
    rows, width = sum(counts), w_attention.shape[2]
    model = w_subsample.shape[1]

    def kernel(*refs):
        stack_refs, (w_sub, w_att), outs = refs[: len(counts)], refs[len(counts) : -3], refs[-3:]
        begin = 0
        for stack_ref, count in zip(stack_refs, counts):
            features = dot32(stack_ref[...], w_sub[...]).astype(jnp.bfloat16)
            normed = normalize(features.astype(jnp.float32)).astype(jnp.bfloat16)
            for part in range(3):
                outs[part][begin : begin + count, :] = dot32(normed, w_att[part]).astype(
                    jnp.bfloat16
                )
            begin += count

    shape = jax.ShapeDtypeStruct((rows, width), jnp.bfloat16)
    return call(
        kernel,
        (shape, shape, shape),
        (*stacks, w_subsample, w_attention),
        flops=2 * rows * model * (w_subsample.shape[0] + 3 * width),
    )


def attend(indices, bounds, key_positions, queries, keys, values, frames_local, parts):
    counts = [q.shape[0] for q in queries]
    rows, width = sum(counts), queries[0].shape[1]
    groups = len(counts)
    frames_shard = frames_local * parts
    extended = frames_shard + 2 * HALO
    window = frames_local + 2 * HALO

    def kernel(*refs):
        index_ref, bound_ref, position_ref = refs[:3]
        q_refs, k_refs, v_refs = (
            refs[3 + groups * part : 3 + groups * (part + 1)] for part in range(3)
        )
        outs = refs[3 + 3 * groups : 3 + 3 * groups + parts]
        q_all, q_rows, result, bias = refs[3 + 3 * groups + parts :]
        begin = 0
        for q_ref, count in zip(q_refs, counts):
            q_all[begin : begin + count, :] = q_ref[...]
            begin += count

        def source(slot, offset, count):
            start = pl.multiple_of(index_ref[slot] * frames_local + offset, HALO)
            return q_all[pl.ds(start, count), :]

        q_rows[0:HALO, :] = source(0, frames_local - HALO, HALO)
        for part in range(parts):
            begin = HALO + part * frames_local
            q_rows[begin : begin + frames_local, :] = source(1 + part, 0, frames_local)
        q_rows[HALO + frames_shard : extended, :] = source(1 + parts, 0, HALO)
        first, last = (
            jnp.transpose(
                jnp.broadcast_to(bound_ref[line : line + 1, :].astype(jnp.float32), (LANES, extended))
            )
            for line in range(2)
        )
        for begin in range(0, rows, LANES):
            at = position_ref[0:1, begin : begin + LANES].astype(jnp.float32)
            allowed = (at >= first) & (at < last)
            bias[:, begin : begin + LANES] = jnp.where(allowed, 0.0, -1e30)
        for lane in range(0, width, LANES):
            span = min(LANES, width - lane)
            q_pair = q_rows[:, lane : lane + span]
            k_pairs = [k_ref[:, lane : lane + span] for k_ref in k_refs]
            v_pairs = [v_ref[:, lane : lane + span] for v_ref in v_refs]
            head_of = lax.broadcasted_iota(jnp.int32, (extended, span), 1) // HD
            merged = jnp.zeros((extended, span), jnp.float32)
            for head in range(span // HD):
                mine = head_of == head
                q_head = jnp.where(mine, q_pair, jnp.zeros_like(q_pair)) * jnp.bfloat16(
                    1.0 / math.sqrt(HD)
                )
                scores = jnp.concatenate(
                    [
                        lax.dot_general(
                            q_head,
                            k_pair,
                            (((1,), (1,)), ((), ())),
                            preferred_element_type=jnp.float32,
                        )
                        for k_pair in k_pairs
                    ],
                    axis=1,
                )
                scores = scores + bias[...]
                weights = jnp.exp(scores - jnp.max(scores, axis=1, keepdims=True))
                total = jnp.sum(weights, axis=1, keepdims=True)
                rounded = weights.astype(jnp.bfloat16)
                numerator = jnp.zeros((extended, span), jnp.float32)
                begin = 0
                for v_pair, count in zip(v_pairs, counts):
                    numerator += dot32(rounded[:, begin : begin + count], v_pair)
                    begin += count
                merged = jnp.where(mine, numerator / total, merged)
            result[:, lane : lane + span] = merged.astype(jnp.bfloat16)
        for part in range(parts):
            start = pl.multiple_of(index_ref[2 + parts + part] * frames_local, HALO)
            outs[part][...] = result[pl.ds(start, window), :]

    return call(
        kernel,
        [jax.ShapeDtypeStruct((window, width), jnp.bfloat16)] * parts,
        (indices, bounds, key_positions, *queries, *keys, *values),
        scratch=[
            pltpu.VMEM((rows, width), jnp.bfloat16),
            pltpu.VMEM((extended, width), jnp.bfloat16),
            pltpu.VMEM((extended, width), jnp.bfloat16),
            pltpu.VMEM((extended, rows), jnp.float32),
        ],
        scalars=1,
        flops=4 * extended * rows * width * 4,
    )


def window_features(indices, stacks, w_subsample, frames_local):
    counts = [stack.shape[0] for stack in stacks]
    depth, model = w_subsample.shape
    window = frames_local + 2 * HALO

    def kernel(index_ref, *refs):
        stack_refs, w_sub, out, held, taken = refs[:-4], refs[-4], refs[-3], refs[-2], refs[-1]
        begin = 0
        for stack_ref, count in zip(stack_refs, counts):
            held[begin : begin + count, :] = stack_ref[...]
            begin += count

        def source(slot, offset, count):
            start = pl.multiple_of(index_ref[slot] * frames_local + offset, HALO)
            return held[pl.ds(start, count), :]

        taken[0:HALO, :] = source(0, frames_local - HALO, HALO)
        taken[HALO : HALO + frames_local, :] = source(1, 0, frames_local)
        taken[HALO + frames_local : window, :] = source(2, 0, HALO)
        out[...] = dot32(taken[...], w_sub[...]).astype(jnp.bfloat16)

    return call(
        kernel,
        jax.ShapeDtypeStruct((window, model), jnp.bfloat16),
        (indices, *stacks, w_subsample),
        scratch=[
            pltpu.VMEM((sum(counts), depth), jnp.bfloat16),
            pltpu.VMEM((window, depth), jnp.bfloat16),
        ],
        scalars=1,
        flops=2 * window * depth * model,
    )


def finish_rows(inside, features, attended, w_rows, gain, taps, frames_local):
    parts = len(attended)
    model = features.shape[1]
    window = frames_local + 2 * HALO
    chunk = 2 * LANES
    offset = HALO - KERNEL // 2

    def kernel(inside_ref, *refs):
        feature_ref, a_refs, w_refs = refs[0], refs[1 : 1 + parts], refs[1 + parts : 1 + 2 * parts]
        gain_ref, tap_ref, out, held, mixed_rows = refs[1 + 2 * parts :]
        branch = jnp.zeros((window, model), jnp.float32)
        for a_ref, w_ref in zip(a_refs, w_refs):
            branch += dot32(a_ref[...], w_ref[...]).astype(jnp.bfloat16).astype(jnp.float32)
        mixed = (feature_ref[...].astype(jnp.float32) + branch).astype(jnp.bfloat16)
        mixed = mixed.astype(jnp.float32)
        mixed_rows[...] = mixed[HALO : HALO + frames_local]
        conv_in = (normalize(mixed) * gain_ref[...]).astype(jnp.bfloat16).astype(jnp.float32)
        held[HALO : HALO + frames_local, :] = conv_in[HALO : HALO + frames_local]
        before = inside_ref[0] > 0
        held[0:HALO, :] = jnp.where(before, conv_in[0:HALO], 0.0)
        after = inside_ref[1] > 0
        held[HALO + frames_local : window, :] = jnp.where(after, conv_in[HALO + frames_local :], 0.0)
        for lane in range(0, model, chunk):
            here = slice(lane, lane + chunk)
            total = jnp.zeros((frames_local, chunk), jnp.float32)
            tap_rows = tap_ref[:, here].astype(jnp.float32)
            for phase in range(8):
                taken = [tap for tap in range(KERNEL) if (tap + offset) % 8 == phase]
                reach = (taken[-1] + offset) // 8 * 8 + frames_local
                moved = held[pl.ds(phase, reach), here]
                for tap in taken:
                    begin = (tap + offset) // 8 * 8
                    total += moved[begin : begin + frames_local] * tap_rows[tap : tap + 1]
            silu = total / (1.0 + jnp.exp(-total))
            out[:, here] = (mixed_rows[:, here] + silu).astype(jnp.bfloat16)

    return call(
        kernel,
        jax.ShapeDtypeStruct((frames_local, model), jnp.bfloat16),
        (inside, features, *attended, *w_rows, gain, taps),
        scratch=[
            pltpu.VMEM((window, model), jnp.float32),
            pltpu.VMEM((frames_local, model), jnp.float32),
        ],
        scalars=1,
        flops=2 * window * model * model,
    )


def exchange(block, axis, bit):
    return lax.ppermute(block, axis, [(i, i ^ bit) for i in range(lax.axis_size(axis))])


def shifted(block, axis, distance):
    count = lax.axis_size(axis)
    route = [(i - distance, i) for i in range(count) if 0 <= i - distance < count]
    return lax.ppermute(block, axis, route)


def shards(
    waveform,
    segment_start,
    segment_end,
    w_subsample,
    w_attention,
    w_output,
    gain_convolution,
    w_depthwise,
):
    frames_local = waveform.shape[0] // (SUB * HOP)
    frames_shard = segment_start.shape[0]
    parts, shards_total = lax.axis_size("mp"), lax.axis_size("tm")
    time_index = lax.axis_index("tm")
    model_index = lax.axis_index("mp")
    bits = [1 << b for b in reversed(range((parts - 1).bit_length()))]

    ahead = -(-(NFFT - HOP) // LANES) * LANES
    next_samples = shifted(waveform[:ahead], ("tm", "mp"), -1)
    own_bounds = jnp.stack([segment_start, segment_end])
    bounds = jnp.concatenate(
        [
            shifted(own_bounds[:, frames_shard - HALO :], "tm", 1),
            own_bounds,
            shifted(own_bounds[:, :HALO], "tm", -1),
        ],
        axis=1,
    )
    stacked = log_mel_rows(
        waveform.reshape(-1, LANES), next_samples.reshape(-1, LANES), frames_local
    )

    reach = min((SEG_MAX + HALO - 2) // frames_shard + 1, shards_total - 1)
    whole = reach == shards_total - 1 and shards_total & (shards_total - 1) == 0
    column, places = [stacked], [(time_index, model_index)]
    if whole:
        for bit in range(1, shards_total):
            column.append(exchange(stacked, "tm", bit))
            places.append((time_index ^ bit, model_index))
    else:
        for distance in range(1, reach + 1):
            for step in (distance, -distance):
                column.append(shifted(stacked, "tm", step))
                places.append((time_index - step, model_index))
    column = jnp.concatenate(column)

    gathered = [column]
    for bit in bits:
        gathered += [exchange(block, "mp", bit) for block in gathered]
        places += [(tm, mp ^ bit) for tm, mp in places]

    w_rows = [w_output]
    for bit in bits:
        w_rows += [exchange(block, "mp", bit) for block in w_rows]

    half = len(gathered) // 2
    projected = [project_rows([block], w_subsample, w_attention) for block in gathered[:half]]
    projected.append(project_rows(gathered[half:], w_subsample, w_attention))
    queries, keys, values = zip(*projected)

    key_positions = jnp.concatenate(
        [
            tm * frames_shard + mp * frames_local + jnp.arange(frames_local, dtype=jnp.int32)
            for tm, mp in places
        ]
    )[None, :]

    def place(tm, mp):
        found = 0
        for slot, (slot_tm, slot_mp) in enumerate(places):
            found += jnp.where((slot_tm == tm) & (slot_mp == mp), slot, 0)
        return found

    indices = [place(time_index - 1, parts - 1)]
    indices += [place(time_index, mp) for mp in range(parts)]
    indices += [place(time_index + 1, 0)]
    indices += [model_index ^ bit for bit in range(parts)]
    indices = jnp.stack(indices).astype(jnp.int32)
    attended = attend(indices, bounds, key_positions, queries, keys, values, frames_local, parts)
    arrived = [attended[0]] + [exchange(attended[bit], "mp", bit) for bit in range(1, parts)]
    w_order = [0]
    for bit in bits:
        w_order += [other ^ bit for other in w_order]
    w_rows = [w_rows[w_order.index(bit)] for bit in range(parts)]

    block = time_index * parts + model_index
    around = [block - 1, block, block + 1]
    around = jnp.stack([place(b // parts, b % parts) for b in around]).astype(jnp.int32)
    features = window_features(around, gathered, w_subsample, frames_local)
    inside = jnp.stack([block > 0, block < shards_total * parts - 1]).astype(jnp.int32)
    return finish_rows(
        inside, features, arrived, w_rows, gain_convolution[None, :], w_depthwise, frames_local
    )


def solution(mesh):
    placed = (
        P(("groups", "tm", "mp")),
        P(("groups", "tm")),
        P(("groups", "tm")),
        P(),
        P(None, None, "mp"),
        P("mp", None),
        P(),
        P(),
    )
    return jax.shard_map(
        shards,
        mesh=mesh,
        in_specs=placed,
        out_specs=P(("groups", "tm", "mp"), None),
        check_vma=False,
    )
```

time: 144 us -> 79.6 us (0.55)
  the two profiles are of different devices: /device:TPU:3 before, /device:TPU:0 now
where the time goes in v1:
time: 79.6 us; the launch traced here: 78 us
  starting transfers between devices  36.1 us (45%)
  Pallas kernels  20.1 us (25%)
  waiting for transfers between devices  11.4 us (14%)
  local copies, waits for them, and re-layouts  7.58 us (10%)
  between operations  1.85 us (2%)
  other arithmetic  1.07 us (1%)
    ppermute x12, starting transfers between devices, exchange(): lax.ppermute(block, axis, [(i, i ^ bit) for i in range(lax.axis_size(axis...  31.8 us
    pallas_call x7, Pallas kernels, call(): pl.pallas_call(kernel, out_shape=out_shape, in_specs=specs, out_specs=jax...  20.1 us
    ppermute x12, waiting for transfers between devices, exchange(): lax.ppermute(block, axis, [(i, i ^ bit) for i in range(lax.axis_size(axis...  10.5 us
    unnamed x26, local copies, waits for them, and re-layouts  6.71 us
    ppermute x3, starting transfers between devices, shifted(): return lax.ppermute(block, axis, route)  4.24 us
  transfers between devices with their start and end apart: 15, of which 5 were waited for; matrix products, arithmetic and copies ran while one was open for 2% of the time, Pallas kernels for 19%

profile of v1, /device:TPU:0, one launch (start us, length us, event | category | flops | bytes accessed | tf_op | source)
XLA Modules:
  0.0 78.0 jit_solution(6964274933753588958)
XLA Ops:
  0.0 2.9 %collective-permute-start.13 = (bf16[384,1536]{1,0:T(8,128)(2,1)}, bf16[384,1536]{1,0:T(8,128)(2,1)S(1)}, u32[]{:S(2)}, u32[]{:S(2)}) collective-permute-start(bf16[384,1536]{1,0:T(8,128)(2,1)} %refs_5_.1), channel_id=1, source_target_pairs={{0,2},{1,3},{2,0},{3,1},{4,6},{5,7},{6,4},{7,5},{8,10},{9,11},{10,... | collective-permute-start | bytes 3538952 | tf_op jit(solution)/shard_map/ppermute | solution.py:322
  2.9 0.0 collective-permute-start.12
  2.9 0.7 slice.9
  3.6 1.3 %collective-permute-start = (f32[256]{0:T(256)S(1)}, f32[256]{0:T(256)S(1)}, u32[]{:S(2)}, u32[]{:S(2)}) collective-permute-start(f32[256]{0:T(256)S(1)} %slice.9), channel_id=1, source_target_pairs={{1,0},{2,1},{3,2},{4,3},{5,4},{6,5},{7,6},{8,7},{9,8},{10,9},{11,1... | collective-permute-start | bytes 3080 | tf_op jit(solution)/shard_map/ppermute | solution.py:328
  5.0 0.8 %fusion = (s32[2,16]{1,0:T(2,128)S(1)}, s32[2,16]{1,0:T(2,128)S(1)}) fusion(s32[1,256]{1,0:T(1,128)} %bitcast.23, s32[1,256]{1,0:T(1,128)} %bitcast.25), kind=kLoop, calls=%fused_computation.5 | loop fusion | flops 64 | bytes 2304 | tf_op jit(solution)/shard_map/stack | solution.py:350
  5.8 0.9 %collective-permute-done = f32[256]{0:T(256)S(1)} collective-permute-done((f32[256]{0:T(256)S(1)}, f32[256]{0:T(256)S(1)}, u32[]{:S(2)}, u32[]{:S(2)}) %collective-permute-start) | collective-permute-done | bytes 1056 | tf_op jit(solution)/shard_map/ppermute | solution.py:328
  6.7 0.9 %copy-done.5 = f32[40960]{0:T(1024)S(1)} copy-done((f32[40960]{0:T(1024)S(1)}, f32[40960]{0:T(1024)}, u32[]{:S(2)}) %copy-start.5) | copy-done | bytes 163864
  7.6 1.0 %copy-done.6 = bf16[512,512]{1,0:T(8,128)(2,1)S(1)} copy-done((bf16[512,512]{1,0:T(8,128)(2,1)S(1)}, bf16[512,512]{1,0:T(8,128)(2,1)}, u32[]{:S(2)}) %copy-start.6) | copy-done | bytes 524312
  8.6 1.0 %copy-done.7 = bf16[512,512]{1,0:T(8,128)(2,1)S(1)} copy-done((bf16[512,512]{1,0:T(8,128)(2,1)S(1)}, bf16[512,512]{1,0:T(8,128)(2,1)}, u32[]{:S(2)}) %copy-start.7) | copy-done | bytes 524312
  9.7 0.8 %copy-done.8 = bf16[256,128]{1,0:T(8,128)(2,1)S(1)} copy-done((bf16[256,128]{1,0:T(8,128)(2,1)S(1)}, bf16[256,128]{1,0:T(8,128)(2,1)}, u32[]{:S(2)}) %copy-start.8) | copy-done | bytes 65560
  10.5 0.8 %copy-done.9 = bf16[256,128]{1,0:T(8,128)(2,1)S(1)} copy-done((bf16[256,128]{1,0:T(8,128)(2,1)S(1)}, bf16[256,128]{1,0:T(8,128)(2,1)}, u32[]{:S(2)}) %copy-start.9) | copy-done | bytes 65560
  11.3 0.9 %shard_map.118 = bf16[64,512]{1,0:T(8,128)(2,1)S(1)} custom-call(f32[320,128]{1,0:T(8,128)S(1)} %bitcast.21, f32[2,128]{1,0:T(2,128)S(1)} %bitcast.22, bf16[512,512]{1,0:T(8,128)(2,1)S(1)} %copy-done.7, bf16[512,512]{1,0:T(8,128)(2,1)S(1)} %copy-done.6, bf16[256,128]{1,0:T(8,128)(2,1)S(1)} %copy-done.9, bf16[256,128]{1,0:T(8,128)(2,1)S(1)} %copy-done.8), custom_call_target="tpu_custom_call" | custom-call | flops 402653184 | bytes 1000000 | tf_op jit(solution)/shard_map/pallas_call | solution.py:74
  12.2 0.0 copy-start
  12.2 4.3 %collective-permute-start.3 = (bf16[64,512]{1,0:T(8,128)(2,1)S(1)}, bf16[64,512]{1,0:T(8,128)(2,1)S(1)}, u32[]{:S(2)}, u32[]{:S(2)}) collective-permute-start(bf16[64,512]{1,0:T(8,128)(2,1)S(1)} %shard_map.118), channel_id=1, source_target_pairs={{0,12},{4,8},{8,4},{12,0},{1,13},{5,9},{9,5},{13,1},{2,14},{6,10},... | collective-permute-start | bytes 196616 | tf_op jit(solution)/shard_map/ppermute | solution.py:322
  16.6 0.0 collective-permute-start.2
  16.6 0.6 collective-permute-start.1
  17.2 1.6 %collective-permute-done.3 = bf16[64,512]{1,0:T(8,128)(2,1)S(1)} collective-permute-done((bf16[64,512]{1,0:T(8,128)(2,1)S(1)}, bf16[64,512]{1,0:T(8,128)(2,1)S(1)}, u32[]{:S(2)}, u32[]{:S(2)}) %collective-permute-start.3) | collective-permute-done | bytes 65568 | tf_op jit(solution)/shard_map/ppermute | solution.py:322
  18.8 1.7 %collective-permute-start.7 = (s32[2,16]{1,0:T(2,128)S(1)}, s32[2,16]{1,0:T(2,128)S(1)}, u32[]{:S(2)}, u32[]{:S(2)}) collective-permute-start(s32[2,16]{1,0:T(2,128)S(1)} %get-tuple-element.31), channel_id=1, source_target_pairs={{0,4},{4,8},{8,12},{1,5},{5,9},{9,13},{2,6},{6,10},{10,14},{3,7},{... | collective-permute-start | bytes 392 | tf_op jit(solution)/shard_map/ppermute | solution.py:328
  20.5 1.2 %collective-permute-done.2 = bf16[64,512]{1,0:T(8,128)(2,1)S(1)} collective-permute-done((bf16[64,512]{1,0:T(8,128)(2,1)S(1)}, bf16[64,512]{1,0:T(8,128)(2,1)S(1)}, u32[]{:S(2)}, u32[]{:S(2)}) %collective-permute-start.2) | collective-permute-done | bytes 65568 | tf_op jit(solution)/shard_map/ppermute | solution.py:322
  21.8 1.3 %collective-permute-start.8 = (s32[2,16]{1,0:T(2,128)S(1)}, s32[2,16]{1,0:T(2,128)S(1)}, u32[]{:S(2)}, u32[]{:S(2)}) collective-permute-start(s32[2,16]{1,0:T(2,128)S(1)} %get-tuple-element.32), channel_id=1, source_target_pairs={{4,0},{8,4},{12,8},{5,1},{9,5},{13,9},{6,2},{10,6},{14,10},{7,3},{... | collective-permute-start | bytes 392 | tf_op jit(solution)/shard_map/ppermute | solution.py:328
  23.1 0.0 collective-permute-done.1
  23.1 21.7 %collective-permute-start.4 = (bf16[256,512]{1,0:T(8,128)(2,1)S(1)}, bf16[256,512]{1,0:T(8,128)(2,1)S(1)}, u32[]{:S(2)}, u32[]{:S(2)}) collective-permute-start(bf16[256,512]{1,0:T(8,128)(2,1)S(1)} %pad_maximum_fusion.refs_0_), channel_id=1, source_target_pairs={{0,2},{1,3},{2,0},{3,1},{4,6},{5,7},{6,4},{7,5},{8,10},{9,11},{10,... | collective-permute-start | bytes 786440 | tf_op jit(solution)/shard_map/ppermute | solution.py:322
  44.8 0.0 collective-permute-done.13.refs_7_
  44.8 0.0 collective-permute-start.14
  44.8 0.1 add_convert_fusion.inside_ref
  46.5 0.1 stack.80.refs_0_
  46.6 0.1 concatenate.11
  46.7 0.0 collective-permute-done.7
  46.7 0.1 collective-permute-start.5
  46.8 5.1 %collective-permute-done.4.refs_1_.refs_0_ = bf16[256,512]{1,0:T(8,128)(2,1)S(1)} collective-permute-done((bf16[256,512]{1,0:T(8,128)(2,1)S(1)}, bf16[256,512]{1,0:T(8,128)(2,1)S(1)}, u32[]{:S(2)}, u32[]{:S(2)}) %collective-permute-start.4) | collective-permute-done | bytes 262176 | tf_op jit(solution)/shard_map/ppermute | solution.py:322
  51.9 0.1 collective-permute-start.6
  52.0 0.0 collective-permute-done.8
  52.0 0.1 pad_add_fusion.refs_1_
  52.1 2.0 %copy-done.1 = bf16[3,1536,384]{2,1,0:T(8,128)(2,1)S(1)} copy-done((bf16[3,1536,384]{2,1,0:T(8,128)(2,1)S(1)}, bf16[3,1536,384]{2,1,0:T(8,128)(2,1)}, u32[]{:S(2)}) %copy-start.1) | copy-done | bytes 3538968
  54.1 2.3 %shard_map.120 = (bf16[256,384]{1,0:T(8,128)(2,1)S(1)}, bf16[256,384]{1,0:T(8,128)(2,1)S(1)}, bf16[256,384]{1,0:T(8,128)(2,1)S(1)}) custom-call(bf16[256,512]{1,0:T(8,128)(2,1)S(1)} %pad_maximum_fusion.refs_0_, bf16[512,1536]{1,0:T(8,128)(2,1)S(1)} %copy-done, bf16[3,1536,384]{2,1,0:T(8,128)(2,1)S(1)} %copy-done.1), custom_call_target="tpu_custom_call" | custom-call | flops 1308622848 | bytes 1000000 | tf_op jit(solution)/shard_map/pallas_call | solution.py:74
  56.4 0.0 copy-start.2
  56.4 2.3 %shard_map.121 = (bf16[256,384]{1,0:T(8,128)(2,1)S(1)}, bf16[256,384]{1,0:T(8,128)(2,1)S(1)}, bf16[256,384]{1,0:T(8,128)(2,1)S(1)}) custom-call(bf16[256,512]{1,0:T(8,128)(2,1)S(1)} %collective-permute-done.4.refs_1_.refs_0_, bf16[512,1536]{1,0:T(8,128)(2,1)S(1)} %copy-done, bf16[3,1536,384]{2,1,0:T(8,128)(2,1)S(1)} %copy-done.1), custom_call_target="tpu_custom_call" | custom-call | flops 1308622848 | bytes 1000000 | tf_op jit(solution)/shard_map/pallas_call | solution.py:74
  58.7 0.0 collective-permute-done.5.refs_2_.refs_0_
  58.7 0.0 collective-permute-done.6.refs_3_.refs_1_
  58.7 4.4 %shard_map.122 = (bf16[512,384]{1,0:T(8,128)(2,1)S(1)}, bf16[512,384]{1,0:T(8,128)(2,1)S(1)}, bf16[512,384]{1,0:T(8,128)(2,1)S(1)}) custom-call(bf16[256,512]{1,0:T(8,128)(2,1)S(1)} %collective-permute-done.5.refs_2_.refs_0_, bf16[256,512]{1,0:T(8,128)(2,1)S(1)} %collective-permute-done.6.refs_3_.refs_1_, bf16[512,1536]{1,0:T(8,128)(2,1)S(1)} %copy-done, ...), custom_call_target="tpu_custom_call" | custom-call | flops 2617245696 | bytes 1000000 | tf_op jit(solution)/shard_map/pallas_call | solution.py:74
  63.1 4.0 %shard_map.123 = (bf16[96,384]{1,0:T(8,128)(2,1)S(1)}, bf16[96,384]{1,0:T(8,128)(2,1)S(1)}, bf16[96,384]{1,0:T(8,128)(2,1)S(1)}, bf16[96,384]{1,0:T(8,128)(2,1)S(1)}) custom-call(s32[10]{0:T(128)S(1)} %stack.80.refs_0_, s32[2,288]{1,0:T(2,128)S(1)} %pad_add_fusion.refs_1_, s32[1,1024]{1,0:T(1,128)S(1)} %bitcast.20, ...), custom_call_target="tpu_custom_call" | custom-call | flops 1811939328 | bytes 1000000 | tf_op jit(solution)/shard_map/pallas_call | solution.py:74
  67.0 0.4 collective-permute-start.9
  67.5 0.5 collective-permute-start.10
  67.9 1.0 %collective-permute-start.11 = (bf16[96,384]{1,0:T(8,128)(2,1)S(1)}, bf16[96,384]{1,0:T(8,128)(2,1)S(1)}, u32[]{:S(2)}, u32[]{:S(2)}) collective-permute-start(bf16[96,384]{1,0:T(8,128)(2,1)S(1)} %get-tuple-element.30), channel_id=1, source_target_pairs={{0,3},{1,2},{2,1},{3,0},{4,7},{5,6},{6,5},{7,4},{8,11},{9,10},{10,... | collective-permute-start | bytes 221192 | tf_op jit(solution)/shard_map/ppermute | solution.py:322
  69.0 0.1 pad_add_fusion.2.index_ref
  69.0 1.0 %shard_map.119.refs_0_ = bf16[96,1536]{1,0:T(8,128)(2,1)S(1)} custom-call(s32[3]{0:T(128)S(1)} %pad_add_fusion.2.index_ref, bf16[256,512]{1,0:T(8,128)(2,1)S(1)} %pad_maximum_fusion.refs_0_, bf16[256,512]{1,0:T(8,128)(2,1)S(1)} %collective-permute-done.4.refs_1_.refs_0_, bf16[256,512]{1,0:T(8,128)(2,1)S(1)} %collective-permute-done.5.refs_2_.refs_0_, ...), custom_call_target="tpu_custom_call" | custom-call | flops 150994944 | bytes 1000000 | tf_op jit(solution)/shard_map/pallas_call | solution.py:74
  70.0 2.5 %collective-permute-done.10.refs_3_ = bf16[96,384]{1,0:T(8,128)(2,1)S(1)} collective-permute-done((bf16[96,384]{1,0:T(8,128)(2,1)S(1)}, bf16[96,384]{1,0:T(8,128)(2,1)S(1)}, u32[]{:S(2)}, u32[]{:S(2)}) %collective-permute-start.10) | collective-permute-done | bytes 73760 | tf_op jit(solution)/shard_map/ppermute | solution.py:322
  72.6 5.4 %shard_map.124 = bf16[64,1536]{1,0:T(8,128)(2,1)} custom-call(s32[2]{0:T(128)S(1)} %add_convert_fusion.inside_ref, bf16[96,1536]{1,0:T(8,128)(2,1)S(1)} %shard_map.119.refs_0_, bf16[96,384]{1,0:T(8,128)(2,1)S(1)} %get-tuple-element.27.refs_1_, bf16[96,384]{1,0:T(8,128)(2,1)S(1)} %collective-permute-done.9.refs_2_, ...), custom_call_target="tpu_custom_call" | custom-call | flops 452984832 | bytes 1000000 | tf_op jit(solution)/shard_map/pallas_call | solution.py:74
  (32 shorter events, 0.1 us)
Async XLA Ops:
  0.0 44.8 %collective-permute-start.13 = (bf16[384,1536]{1,0:T(8,128)(2,1)}, bf16[384,1536]{1,0:T(8,128)(2,1)S(1)}, u32[]{:S(2)}, u32[]{:S(2)}) collective-permute-start(bf16[384,1536]{1,0:T(8,128)(2,1)} %refs_5_.1), channel_id=1, source_target_pairs={{0,2},{1,3},{2,0},{3,1},{4,6},{5,7},{6,4},{7,5},{8,10},{9,11},{10,... | collective-permute-start | bytes 3538952 | tf_op jit(solution)/shard_map/ppermute | solution.py:322
  2.9 69.6 %collective-permute-start.12 = (bf16[384,1536]{1,0:T(8,128)(2,1)}, bf16[384,1536]{1,0:T(8,128)(2,1)}, u32[]{:S(2)}, u32[]{:S(2)}) collective-permute-start(bf16[384,1536]{1,0:T(8,128)(2,1)} %refs_5_.1), channel_id=1, source_target_pairs={{0,1},{1,0},{2,3},{3,2},{4,5},{5,4},{6,7},{7,6},{8,9},{9,8},{10,11... | collective-permute-start | bytes 3538952 | tf_op jit(solution)/shard_map/ppermute | solution.py:322
  3.6 3.0 %collective-permute-start = (f32[256]{0:T(256)S(1)}, f32[256]{0:T(256)S(1)}, u32[]{:S(2)}, u32[]{:S(2)}) collective-permute-start(f32[256]{0:T(256)S(1)} %slice.9), channel_id=1, source_target_pairs={{1,0},{2,1},{3,2},{4,3},{5,4},{6,5},{7,6},{8,7},{9,8},{10,9},{11,1... | collective-permute-start | bytes 3080 | tf_op jit(solution)/shard_map/ppermute | solution.py:328
  6.7 0.9 %copy-start.5 = (f32[40960]{0:T(1024)S(1)}, f32[40960]{0:T(1024)}, u32[]{:S(2)}) copy-start(f32[40960]{0:T(1024)} %param.12) | copy-start | bytes 491524
  7.6 1.0 %copy-start.6 = (bf16[512,512]{1,0:T(8,128)(2,1)S(1)}, bf16[512,512]{1,0:T(8,128)(2,1)}, u32[]{:S(2)}) copy-start(bf16[512,512]{1,0:T(8,128)(2,1)} %constant.96.clone.tl) | copy-start | bytes 1572868
  8.6 1.0 %copy-start.7 = (bf16[512,512]{1,0:T(8,128)(2,1)S(1)}, bf16[512,512]{1,0:T(8,128)(2,1)}, u32[]{:S(2)}) copy-start(bf16[512,512]{1,0:T(8,128)(2,1)} %constant.95.clone.th) | copy-start | bytes 1572868
  9.7 0.8 %copy-start.8 = (bf16[256,128]{1,0:T(8,128)(2,1)S(1)}, bf16[256,128]{1,0:T(8,128)(2,1)}, u32[]{:S(2)}) copy-start(bf16[256,128]{1,0:T(8,128)(2,1)} %constant.98.clone.bl) | copy-start | bytes 196612
  10.5 0.8 %copy-start.9 = (bf16[256,128]{1,0:T(8,128)(2,1)S(1)}, bf16[256,128]{1,0:T(8,128)(2,1)}, u32[]{:S(2)}) copy-start(bf16[256,128]{1,0:T(8,128)(2,1)} %constant.97.clone.bh) | copy-start | bytes 196612
  11.3 34.7 %copy-start.10 = (f32[1536]{0:T(1024)S(1)}, f32[1536]{0:T(1024)}, u32[]{:S(2)}) copy-start(f32[1536]{0:T(1024)} %param.18) | copy-start | bytes 18436
  11.3 40.7 %copy-start.11 = (s32[256]{0:T(256)S(1)}, s32[256]{0:T(256)}, u32[]{:S(2)}) copy-start(s32[256]{0:T(256)} %param.13) | copy-start | bytes 3076
  11.3 40.7 %copy-start.12 = (s32[256]{0:T(256)S(1)}, s32[256]{0:T(256)}, u32[]{:S(2)}) copy-start(s32[256]{0:T(256)} %param.14) | copy-start | bytes 3076
  12.2 39.9 %copy-start = (bf16[512,1536]{1,0:T(8,128)(2,1)S(1)}, bf16[512,1536]{1,0:T(8,128)(2,1)}, u32[]{:S(2)}) copy-start(bf16[512,1536]{1,0:T(8,128)(2,1)} %refs_2_.5) | copy-start | bytes 4718596
  12.2 6.6 %collective-permute-start.3 = (bf16[64,512]{1,0:T(8,128)(2,1)S(1)}, bf16[64,512]{1,0:T(8,128)(2,1)S(1)}, u32[]{:S(2)}, u32[]{:S(2)}) collective-permute-start(bf16[64,512]{1,0:T(8,128)(2,1)S(1)} %shard_map.118), channel_id=1, source_target_pairs={{0,12},{4,8},{8,4},{12,0},{1,13},{5,9},{9,5},{13,1},{2,14},{6,10},... | collective-permute-start | bytes 196616 | tf_op jit(solution)/shard_map/ppermute | solution.py:322
  16.6 5.2 %collective-permute-start.2 = (bf16[64,512]{1,0:T(8,128)(2,1)S(1)}, bf16[64,512]{1,0:T(8,128)(2,1)S(1)}, u32[]{:S(2)}, u32[]{:S(2)}) collective-permute-start(bf16[64,512]{1,0:T(8,128)(2,1)S(1)} %shard_map.118), channel_id=1, source_target_pairs={{0,8},{4,12},{8,0},{12,4},{1,9},{5,13},{9,1},{13,5},{2,10},{6,14},... | collective-permute-start | bytes 196616 | tf_op jit(solution)/shard_map/ppermute | solution.py:322
  16.6 6.5 %collective-permute-start.1 = (bf16[64,512]{1,0:T(8,128)(2,1)S(1)}, bf16[64,512]{1,0:T(8,128)(2,1)S(1)}, u32[]{:S(2)}, u32[]{:S(2)}) collective-permute-start(bf16[64,512]{1,0:T(8,128)(2,1)S(1)} %shard_map.118), channel_id=1, source_target_pairs={{0,4},{4,0},{8,12},{12,8},{1,5},{5,1},{9,13},{13,9},{2,6},{6,2},{1... | collective-permute-start | bytes 196616 | tf_op jit(solution)/shard_map/ppermute | solution.py:322
  18.8 27.9 %collective-permute-start.7 = (s32[2,16]{1,0:T(2,128)S(1)}, s32[2,16]{1,0:T(2,128)S(1)}, u32[]{:S(2)}, u32[]{:S(2)}) collective-permute-start(s32[2,16]{1,0:T(2,128)S(1)} %get-tuple-element.31), channel_id=1, source_target_pairs={{0,4},{4,8},{8,12},{1,5},{5,9},{9,13},{2,6},{6,10},{10,14},{3,7},{... | collective-permute-start | bytes 392 | tf_op jit(solution)/shard_map/ppermute | solution.py:328
  21.8 30.3 %collective-permute-start.8 = (s32[2,16]{1,0:T(2,128)S(1)}, s32[2,16]{1,0:T(2,128)S(1)}, u32[]{:S(2)}, u32[]{:S(2)}) collective-permute-start(s32[2,16]{1,0:T(2,128)S(1)} %get-tuple-element.32), channel_id=1, source_target_pairs={{4,0},{8,4},{12,8},{5,1},{9,5},{13,9},{6,2},{10,6},{14,10},{7,3},{... | collective-permute-start | bytes 392 | tf_op jit(solution)/shard_map/ppermute | solution.py:328
  23.1 28.8 %collective-permute-start.4 = (bf16[256,512]{1,0:T(8,128)(2,1)S(1)}, bf16[256,512]{1,0:T(8,128)(2,1)S(1)}, u32[]{:S(2)}, u32[]{:S(2)}) collective-permute-start(bf16[256,512]{1,0:T(8,128)(2,1)S(1)} %pad_maximum_fusion.refs_0_), channel_id=1, source_target_pairs={{0,2},{1,3},{2,0},{3,1},{4,6},{5,7},{6,4},{7,5},{8,10},{9,11},{10,... | collective-permute-start | bytes 786440 | tf_op jit(solution)/shard_map/ppermute | solution.py:322
  44.8 27.7 %collective-permute-start.14 = (bf16[384,1536]{1,0:T(8,128)(2,1)S(1)}, bf16[384,1536]{1,0:T(8,128)(2,1)}, u32[]{:S(2)}, u32[]{:S(2)}) collective-permute-start(bf16[384,1536]{1,0:T(8,128)(2,1)S(1)} %collective-permute-done.13.refs_7_), channel_id=1, source_target_pairs={{0,1},{1,0},{2,3},{3,2},{4,5},{5,4},{6,7},{7,6},{8,9},{9,8},{10,11... | collective-permute-start | bytes 3538952 | tf_op jit(solution)/shard_map/ppermute | solution.py:322
  46.7 12.0 %collective-permute-start.5 = (bf16[256,512]{1,0:T(8,128)(2,1)S(1)}, bf16[256,512]{1,0:T(8,128)(2,1)S(1)}, u32[]{:S(2)}, u32[]{:S(2)}) collective-permute-start(bf16[256,512]{1,0:T(8,128)(2,1)S(1)} %pad_maximum_fusion.refs_0_), channel_id=1, source_target_pairs={{0,1},{1,0},{2,3},{3,2},{4,5},{5,4},{6,7},{7,6},{8,9},{9,8},{10,11... | collective-permute-start | bytes 786440 | tf_op jit(solution)/shard_map/ppermute | solution.py:322
  51.9 6.8 %collective-permute-start.6 = (bf16[256,512]{1,0:T(8,128)(2,1)S(1)}, bf16[256,512]{1,0:T(8,128)(2,1)S(1)}, u32[]{:S(2)}, u32[]{:S(2)}) collective-permute-start(bf16[256,512]{1,0:T(8,128)(2,1)S(1)} %collective-permute-done.4.refs_1_.refs_0_), channel_id=1, source_target_pairs={{0,1},{1,0},{2,3},{3,2},{4,5},{5,4},{6,7},{7,6},{8,9},{9,8},{10,11... | collective-permute-start | bytes 786440 | tf_op jit(solution)/shard_map/ppermute | solution.py:322
  52.1 2.0 %copy-start.1 = (bf16[3,1536,384]{2,1,0:T(8,128)(2,1)S(1)}, bf16[3,1536,384]{2,1,0:T(8,128)(2,1)}, u32[]{:S(2)}) copy-start(bf16[3,1536,384]{2,1,0:T(8,128)(2,1)} %refs_3_.1) | copy-start | bytes 10616836
  56.4 2.3 %copy-start.2 = (bf16[3,1536,384]{2,1,0:T(8,128)(2,1)S(1)}, bf16[3,1536,384]{2,1,0:T(8,128)(2,1)}, u32[]{:S(2)}) copy-start(bf16[3,1536,384]{2,1,0:T(8,128)(2,1)} %refs_3_.1) | copy-start | bytes 10616836
  67.0 3.0 %collective-permute-start.9 = (bf16[96,384]{1,0:T(8,128)(2,1)S(1)}, bf16[96,384]{1,0:T(8,128)(2,1)S(1)}, u32[]{:S(2)}, u32[]{:S(2)}) collective-permute-start(bf16[96,384]{1,0:T(8,128)(2,1)S(1)} %get-tuple-element.28), channel_id=1, source_target_pairs={{0,1},{1,0},{2,3},{3,2},{4,5},{5,4},{6,7},{7,6},{8,9},{9,8},{10,11... | collective-permute-start | bytes 221192 | tf_op jit(solution)/shard_map/ppermute | solution.py:322
  67.5 5.1 %collective-permute-start.10 = (bf16[96,384]{1,0:T(8,128)(2,1)S(1)}, bf16[96,384]{1,0:T(8,128)(2,1)S(1)}, u32[]{:S(2)}, u32[]{:S(2)}) collective-permute-start(bf16[96,384]{1,0:T(8,128)(2,1)S(1)} %get-tuple-element.29), channel_id=1, source_target_pairs={{0,2},{1,3},{2,0},{3,1},{4,6},{5,7},{6,4},{7,5},{8,10},{9,11},{10,... | collective-permute-start | bytes 221192 | tf_op jit(solution)/shard_map/ppermute | solution.py:322
  67.9 4.6 %collective-permute-start.11 = (bf16[96,384]{1,0:T(8,128)(2,1)S(1)}, bf16[96,384]{1,0:T(8,128)(2,1)S(1)}, u32[]{:S(2)}, u32[]{:S(2)}) collective-permute-start(bf16[96,384]{1,0:T(8,128)(2,1)S(1)} %get-tuple-element.30), channel_id=1, source_target_pairs={{0,3},{1,2},{2,1},{3,0},{4,7},{5,6},{6,5},{7,4},{8,11},{9,10},{10,... | collective-permute-start | bytes 221192 | tf_op jit(solution)/shard_map/ppermute | solution.py:322
  69.0 3.6 %copy-start.3 = (bf16[384,1536]{1,0:T(8,128)(2,1)S(1)}, bf16[384,1536]{1,0:T(8,128)(2,1)}, u32[]{:S(2)}) copy-start(bf16[384,1536]{1,0:T(8,128)(2,1)} %refs_5_.1) | copy-start | bytes 3538948
  69.0 3.6 %copy-start.4 = (bf16[31,1536]{1,0:T(8,128)(2,1)S(1)}, bf16[31,1536]{1,0:T(8,128)(2,1)}, u32[]{:S(2)}) copy-start(bf16[31,1536]{1,0:T(8,128)(2,1)} %refs_10_.1) | copy-start | bytes 285700

commit v2 on v1

v2 whole, which is shorter than its diff:
```python
import itertools
import math

import jax
import jax.numpy as jnp
import numpy as np
from jax import lax
from jax.experimental import pallas as pl
from jax.experimental.pallas import tpu as pltpu
from jax.sharding import PartitionSpec as P

HD = 64
NMEL = 128
NFFT = 400
HOP = 160
BINS = 256
SUB = 4
KERNEL = 31
SEG_MAX = 750
LANES = 128
HALO = 16
EXTRA = 8
TAIL_LINES = 3
HEAD_LINES = 2
DIGIT = 128
VMEM_MOST = 54
FRAME_ROWS = SUB * HOP // LANES
WIDE = -(-NFFT // LANES) * LANES


def split_high_low(table):
    high = table.astype(jnp.bfloat16)
    low = (table - high.astype(np.float32)).astype(jnp.bfloat16)
    return high, low


def fourier_table():
    sample_index = np.arange(NFFT)[:, None]
    bin_index = np.arange(BINS)[None, :]
    angle = (sample_index * bin_index % NFFT) * (2.0 * math.pi / NFFT)
    window = 0.5 - 0.5 * np.cos(np.arange(NFFT) * (2.0 * math.pi / NFFT))
    kept = bin_index <= NFFT // 2
    cosine = np.where(kept, np.cos(angle), 0.0) * window[:, None]
    sine = np.where(kept, -np.sin(angle), 0.0) * window[:, None]
    table = np.concatenate([cosine, sine], axis=1).astype(np.float32)
    return np.pad(table, ((0, WIDE - NFFT), (0, 0)))


def mel_bank():
    mel_top = 2595.0 * math.log10(1.0 + 8000.0 / 700.0)
    mel_points = np.arange(NMEL + 2) * (mel_top / (NMEL + 1))
    edges = 700.0 * (np.power(10.0, mel_points / 2595.0) - 1.0) * (NFFT / 16000.0)
    widths = np.maximum(edges[2:] - edges[1:-1], 1.0)
    bin_value = np.arange(BINS)[:, None]
    triangle = np.maximum(0.0, 1.0 - np.abs(bin_value - edges[None, 1:-1]) / widths[None, :])
    return np.where(bin_value <= NFFT // 2, triangle, 0.0).astype(np.float32)


def dot32(left, right):
    return jnp.dot(left, right, preferred_element_type=jnp.float32)


def dot_split(values, high_ref, low_ref):
    high = values.astype(jnp.bfloat16)
    low = (values - high.astype(jnp.float32)).astype(jnp.bfloat16)
    return dot32(high, high_ref[...]) + (dot32(low, high_ref[...]) + dot32(high, low_ref[...]))


def normalize(values):
    center = jnp.mean(values, axis=-1, keepdims=True)
    shifted = values - center
    spread = jnp.mean(jnp.square(shifted), axis=-1, keepdims=True)
    return shifted * lax.rsqrt(spread + 1e-05)


def call(kernel, out_shape, operands, scratch=(), flops=0, remote=0, vmem=16):
    specs = [pl.BlockSpec(memory_space=pltpu.VMEM)] * (len(operands) - remote)
    specs += [pl.BlockSpec(memory_space=pltpu.HBM)] * remote
    return pl.pallas_call(
        kernel,
        out_shape=out_shape,
        in_specs=specs,
        out_specs=jax.tree.map(lambda _: pl.BlockSpec(memory_space=pltpu.VMEM), out_shape),
        scratch_shapes=list(scratch),
        compiler_params=pltpu.CompilerParams(vmem_limit_bytes=vmem * 1024 * 1024),
        cost_estimate=pl.CostEstimate(flops=flops, bytes_accessed=1000000, transcendentals=0),
    )(*operands)


def spread_axes():
    return [axis for axis in ("groups", "tm") if lax.axis_size(axis) % 2 == 0]


def piece_number():
    number = 0
    for place_value, axis in enumerate(spread_axes()):
        number += lax.rem(lax.axis_index(axis), 2) << place_value
    return number


def fetch(after, arrays):
    count = len(arrays)

    def kernel(_, *refs):
        sources, outs, sems = refs[:count], refs[count:-1], refs[-1]
        copies = [
            pltpu.make_async_copy(source, target, sems.at[slot])
            for slot, (source, target) in enumerate(zip(sources, outs))
        ]
        for copy in copies:
            copy.start()
        for copy in copies:
            copy.wait()

    return call(
        kernel,
        [jax.ShapeDtypeStruct(array.shape, array.dtype) for array in arrays],
        (after, *arrays),
        scratch=[pltpu.SemaphoreType.DMA((count,))],
        remote=count,
    )


def padded_row(row):
    return jnp.concatenate([row, jnp.zeros((1, SUB * NMEL - row.shape[1]), row.dtype)], axis=1)


def log_mel(windows, th, tl, bh, bl):
    spectrum = dot_split(windows, th, tl)
    power = jnp.square(spectrum[:, :BINS]) + jnp.square(spectrum[:, BINS:])
    return jnp.log(dot_split(power, bh, bl) + 1e-06)


def log_mel_rows(starts, ends, samples, w_output, tables, frames_local):
    rows = frames_local * FRAME_ROWS
    frames_shard = starts.shape[1]
    pieces = 1 << len(spread_axes())
    piece_rows = w_output.shape[0] // pieces

    def kernel(start_ref, end_ref, wave, weight, *refs):
        sources, (out, out_piece), (held, th, tl, bh, bl, sems) = refs[:4], refs[4:6], refs[6:]
        copies = [pltpu.make_async_copy(wave, held.at[pl.ds(0, rows)], sems.at[0])]
        for slot, (source, target) in enumerate(zip(sources, (th, tl, bh, bl))):
            copies.append(pltpu.make_async_copy(source, target, sems.at[1 + slot]))
        begin = pl.multiple_of(piece_number() * piece_rows, HALO)
        copies.append(
            pltpu.make_async_copy(weight.at[pl.ds(begin, piece_rows)], out_piece, sems.at[5])
        )
        for copy in copies:
            copy.start()
        held[rows : rows + 8, :] = jnp.zeros((8, LANES), jnp.float32)
        copies[0].wait()
        lines = [held[pl.ds(j, frames_local, stride=FRAME_ROWS), :] for j in range(FRAME_ROWS + 2)]
        windows = []
        for sub in range(SUB):
            line, lane = divmod(sub * HOP, LANES)
            taken = jnp.concatenate(lines[line : line + WIDE // LANES], axis=1)
            windows.append(pltpu.roll(taken, WIDE - lane, axis=1) if lane else taken)
        extras = []
        for taken in (range(rows - TAIL_LINES, rows), range(HEAD_LINES)):
            line = jnp.concatenate([held[row : row + 1, :] for row in taken], axis=1)
            high = line.astype(jnp.bfloat16).astype(jnp.float32)
            extras += [padded_row(high), padded_row(line - high)]
        for ref in (start_ref, end_ref):
            edge = jnp.concatenate([ref[:, :HALO], ref[:, frames_shard - HALO :]], axis=1)
            high = edge // DIGIT
            low = edge - high * DIGIT
            extras += [padded_row(digit.astype(jnp.float32)) for digit in (high, low)]
        out[0, frames_local:, :] = jnp.concatenate(extras, axis=0).astype(jnp.bfloat16)
        for copy in copies[1:]:
            copy.wait()
        mel = log_mel(jnp.concatenate(windows, axis=0), th, tl, bh, bl)
        for sub in range(SUB):
            out[0, 0:frames_local, sub * NMEL : (sub + 1) * NMEL] = mel[
                sub * frames_local : (sub + 1) * frames_local
            ].astype(jnp.bfloat16)

    return call(
        kernel,
        (
            jax.ShapeDtypeStruct((1, frames_local + EXTRA, SUB * NMEL), jnp.bfloat16),
            jax.ShapeDtypeStruct((piece_rows, w_output.shape[1]), w_output.dtype),
        ),
        (starts, ends, samples, w_output, *tables),
        scratch=[pltpu.VMEM((rows + 8, LANES), jnp.float32)]
        + [pltpu.VMEM(table.shape, jnp.bfloat16) for table in tables]
        + [pltpu.SemaphoreType.DMA((6,))],
        remote=6,
        vmem=VMEM_MOST,
        flops=6 * frames_local * SUB * WIDE * 2 * BINS,
    )


def boundary_rows(places, starts, ends, stacks, tables, frames_local):
    counts = [stack.shape[0] for stack in stacks]
    slots = len(places)
    rows = -(-slots // HALO) * HALO
    frames_shard = starts.shape[1]
    parts = lax.axis_size("mp")
    final = lax.axis_size("tm") * parts - 1

    def kernel(start_ref, end_ref, *refs):
        stack_refs, refs = refs[: len(counts)], refs[len(counts) :]
        (th, tl, bh, bl), (out, bounds, tails, heads, nexts, edges) = refs[:4], refs[4:]
        time_index, model_index = lax.axis_index("tm"), lax.axis_index("mp")
        tails[...] = jnp.zeros_like(tails)
        nexts[...] = jnp.zeros_like(nexts)
        slot = 0
        for stack_ref, count in zip(stack_refs, counts):
            for block in range(count):
                kept = stack_ref[block, frames_local:, :].astype(jnp.float32)
                here = slice(slot, slot + 1)
                tails[here, :] = (kept[0:1] + kept[1:2])[:, : TAIL_LINES * LANES]
                heads[here, :] = (kept[2:3] + kept[3:4])[:, : HEAD_LINES * LANES]
                for line in range(2):
                    edge = kept[4 + 2 * line : 5 + 2 * line] * DIGIT + kept[5 + 2 * line : 6 + 2 * line]
                    edges[line, here, :] = edge[:, :LANES]
                slot += 1
        for slot, (slot_tm, slot_mp) in enumerate(places):
            following = slot_tm(time_index) * parts + (model_index ^ slot_mp) + 1
            found = slot_of(places, following // parts, lax.rem(following, parts))
            taken = heads[pl.ds(found, 1), :]
            nexts[slot : slot + 1, :] = jnp.where(following > final, 0.0, taken)
        line = jnp.concatenate([tails[...], nexts[...]], axis=1)
        windows = []
        for sub in range(SUB - 2, SUB):
            skip, lane = divmod(sub * HOP - (FRAME_ROWS - TAIL_LINES) * LANES, LANES)
            windows.append(
                pltpu.roll(line[:, skip * LANES : skip * LANES + WIDE], WIDE - lane, axis=1)
            )
        mel = log_mel(jnp.concatenate(windows, axis=0), th, tl, bh, bl).astype(jnp.bfloat16)
        for number in range(2):
            lane = number * NMEL
            out[:, lane : lane + NMEL] = mel[number * rows : (number + 1) * rows]
        left = slot_of(places, time_index - 1, model_index)
        right = slot_of(places, time_index + 1, model_index)
        for number, ref in enumerate((start_ref, end_ref)):
            bounds[number : number + 1, :] = jnp.concatenate(
                [
                    edges[number, pl.ds(left, 1), :][:, HALO : 2 * HALO],
                    ref[...].astype(jnp.float32),
                    edges[number, pl.ds(right, 1), :][:, 0:HALO],
                ],
                axis=1,
            )

    return call(
        kernel,
        (
            jax.ShapeDtypeStruct((rows, 2 * NMEL), jnp.bfloat16),
            jax.ShapeDtypeStruct((2, frames_shard + 2 * HALO), jnp.float32),
        ),
        (starts, ends, *stacks, *tables),
        scratch=[
            pltpu.VMEM((rows, TAIL_LINES * LANES), jnp.float32),
            pltpu.VMEM((rows, HEAD_LINES * LANES), jnp.float32),
            pltpu.VMEM((rows, HEAD_LINES * LANES), jnp.float32),
            pltpu.VMEM((2, rows, LANES), jnp.float32),
        ],
        flops=12 * rows * WIDE * 2 * BINS,
    )


def last_rows(stack_refs, counts, frames_local, fixed, rows):
    lasts = []
    for stack_ref, count in zip(stack_refs, counts):
        for block in range(count):
            kept = stack_ref[block, frames_local - HALO : frames_local, 0 : 2 * NMEL]
            lasts.append(kept.astype(jnp.float32)[HALO - 1 : HALO])
    if len(lasts) < rows:
        lasts.append(jnp.zeros((rows - len(lasts), 2 * NMEL), jnp.float32))
    return jnp.concatenate([jnp.concatenate(lasts, axis=0).astype(jnp.bfloat16), fixed], axis=1)


def patch(held, fixed, slots, frames_local):
    fixed = fixed.astype(jnp.float32)
    for slot in range(slots):
        here = slice((slot + 1) * frames_local - HALO, (slot + 1) * frames_local)
        kept = held[here, :].astype(jnp.float32)
        last = lax.broadcasted_iota(jnp.int32, kept.shape, 0) == HALO - 1
        held[here, :] = jnp.where(last, fixed[slot : slot + 1, :], kept).astype(held.dtype)


def assemble(parts):
    counts = [part.shape[0] for part in parts]

    def kernel(*refs):
        begin = 0
        for ref, count in zip(refs, counts):
            refs[-1][begin : begin + count] = ref[...]
            begin += count

    shape = jax.ShapeDtypeStruct((sum(counts), *parts[0].shape[1:]), parts[0].dtype)
    return call(kernel, shape, parts)


def project_rows(stack, w_subsample, w_attention, frames_local, every=(), fixed=None):
    count = stack.shape[0]
    rows, width = count * frames_local, w_attention.shape[2]
    model = w_subsample.shape[1]
    counts = [block.shape[0] for block in every]
    sizes = [rows] if fixed is None else [rows, fixed.shape[0]]

    def kernel(stack_ref, w_sub, w_att, *refs):
        stack_rows = [stack_ref[block, 0:frames_local, :] for block in range(count)]
        if fixed is not None:
            every_refs, fixed_ref, refs = refs[: len(every)], refs[len(every)], refs[len(every) + 1 :]
            stack_rows.append(
                last_rows(every_refs, counts, frames_local, fixed_ref[...], sizes[1])
            )
        features = dot32(jnp.concatenate(stack_rows, axis=0), w_sub[...]).astype(jnp.bfloat16)
        normed = normalize(features.astype(jnp.float32)).astype(jnp.bfloat16)
        for part in range(3):
            projected = dot32(normed, w_att[part]).astype(jnp.bfloat16)
            begin = 0
            for number, size in enumerate(sizes):
                refs[3 * number + part][...] = projected[begin : begin + size]
                begin += size

    return call(
        kernel,
        [jax.ShapeDtypeStruct((size, width), jnp.bfloat16) for size in sizes for _ in range(3)],
        (stack, w_subsample, w_attention) + (() if fixed is None else (*every, fixed)),
        flops=2 * sum(sizes) * model * (w_subsample.shape[0] + 3 * width),
    )


def slot_of(places, tm, mp):
    found = jnp.int32(0)
    for slot, (slot_tm, slot_mp) in enumerate(places):
        here = (slot_tm(lax.axis_index("tm")) == tm) & (lax.axis_index("mp") ^ slot_mp == mp)
        found = jnp.where(here, slot, found)
    return found


def attend(places, bounds, queries, keys, values, fixed, frames_local):
    counts = [q.shape[0] for q in queries]
    rows, width = sum(counts), queries[0].shape[1]
    groups = len(counts)
    parts = lax.axis_size("mp")
    frames_shard = frames_local * parts
    extended = frames_shard + 2 * HALO
    window = frames_local + 2 * HALO

    def kernel(*refs):
        bound_ref, refs = refs[0], refs[1:]
        sources, refs = refs[: 3 * groups], refs[3 * groups :]
        fixed_refs, refs = refs[:3], refs[3:]
        outs, (q_all, k_all, v_all, q_rows, result, bias) = refs[:parts], refs[parts:]
        for part, held in enumerate((q_all, k_all, v_all)):
            begin = 0
            for source, count in zip(sources[groups * part : groups * (part + 1)], counts):
                held[begin : begin + count, :] = source[...]
                begin += count
            patch(held, fixed_refs[part][...], len(places), frames_local)
        time_index, model_index = lax.axis_index("tm"), lax.axis_index("mp")

        def source(tm, mp, offset, count):
            start = pl.multiple_of(slot_of(places, tm, mp) * frames_local + offset, HALO)
            return q_all[pl.ds(start, count), :]

        q_rows[0:HALO, :] = source(time_index - 1, parts - 1, frames_local - HALO, HALO)
        for part in range(parts):
            begin = HALO + part * frames_local
            q_rows[begin : begin + frames_local, :] = source(time_index, part, 0, frames_local)
        q_rows[HALO + frames_shard : extended, :] = source(time_index + 1, 0, 0, HALO)
        first, last = (
            jnp.transpose(
                jnp.broadcast_to(bound_ref[line : line + 1, :], (LANES, extended))
            )
            for line in range(2)
        )
        lanes = lax.broadcasted_iota(jnp.int32, (1, LANES), 1)
        for begin in range(0, rows, LANES):
            at = jnp.zeros((1, LANES), jnp.int32)
            for slot in range(begin // frames_local, -(-(begin + LANES) // frames_local)):
                if slot < len(places):
                    slot_tm, slot_mp = places[slot]
                    base = slot_tm(time_index) * frames_shard
                    base += (model_index ^ slot_mp) * frames_local - slot * frames_local + begin
                    at = jnp.where(lanes >= slot * frames_local - begin, lanes + base, at)
            at = at.astype(jnp.float32)
            allowed = (at >= first) & (at < last)
            bias[:, begin : begin + LANES] = jnp.where(allowed, 0.0, -1e30)
        for lane in range(0, width, LANES):
            span = min(LANES, width - lane)
            q_pair = q_rows[:, lane : lane + span]
            k_pair = k_all[:, lane : lane + span]
            v_pair = v_all[:, lane : lane + span]
            head_of = lax.broadcasted_iota(jnp.int32, (extended, span), 1) // HD
            merged = jnp.zeros((extended, span), jnp.float32)
            for head in range(span // HD):
                mine = head_of == head
                q_head = jnp.where(mine, q_pair, jnp.zeros_like(q_pair)) * jnp.bfloat16(
                    1.0 / math.sqrt(HD)
                )
                scores = lax.dot_general(
                    q_head, k_pair, (((1,), (1,)), ((), ())), preferred_element_type=jnp.float32
                )
                scores = scores + bias[...]
                weights = jnp.exp(scores - jnp.max(scores, axis=1, keepdims=True))
                total = jnp.sum(weights, axis=1, keepdims=True)
                rounded = weights.astype(jnp.bfloat16)
                numerator = dot32(rounded, v_pair)
                merged = jnp.where(mine, numerator / total, merged)
            result[:, lane : lane + span] = merged.astype(jnp.bfloat16)
        for part in range(parts):
            start = pl.multiple_of((model_index ^ part) * frames_local, HALO)
            outs[part][...] = result[pl.ds(start, window), :]

    return call(
        kernel,
        [jax.ShapeDtypeStruct((window, width), jnp.bfloat16)] * parts,
        (bounds, *queries, *keys, *values, *fixed),
        scratch=[
            pltpu.VMEM((rows, width), jnp.bfloat16),
            pltpu.VMEM((rows, width), jnp.bfloat16),
            pltpu.VMEM((rows, width), jnp.bfloat16),
            pltpu.VMEM((extended, width), jnp.bfloat16),
            pltpu.VMEM((extended, width), jnp.bfloat16),
            pltpu.VMEM((extended, rows), jnp.float32),
        ],
        flops=4 * extended * rows * width * 4,
        vmem=16 + extended * rows * 20 // 1024 // 1024,
    )


def window_features(after, places, stacks, fixed, pieces, w_subsample, frames_local):
    counts = [stack.shape[0] for stack in stacks]
    depth, model = w_subsample.shape
    window = frames_local + 2 * HALO
    piece_slots = len(pieces[0])
    piece_rows = pieces[0][0].shape[0]
    flat = [piece for shard in pieces for piece in shard]
    slots = len(places)

    def kernel(_, *refs):
        stack_refs, refs = refs[: len(counts)], refs[len(counts) :]
        piece_refs, refs = refs[: len(flat)], refs[len(flat) :]
        fixed_ref, w_sub, out, *whole, held, taken = refs
        for number, piece_ref in enumerate(piece_refs):
            shard, slot = divmod(number, piece_slots)
            start = pl.multiple_of((piece_number() ^ slot) * piece_rows, HALO)
            whole[shard][pl.ds(start, piece_rows), :] = piece_ref[...]
        begin = 0
        for stack_ref, count in zip(stack_refs, counts):
            for block in range(count):
                held[begin : begin + frames_local, :] = stack_ref[block, 0:frames_local, :]
                begin += frames_local
        rows = last_rows(stack_refs, counts, frames_local, fixed_ref[...], fixed.shape[0])
        patch(held, rows, slots, frames_local)
        parts = lax.axis_size("mp")
        block = lax.axis_index("tm") * parts + lax.axis_index("mp") + parts

        def source(number, offset, count):
            slot = slot_of(places, number // parts - 1, lax.rem(number, parts))
            start = pl.multiple_of(slot * frames_local + offset, HALO)
            return held[pl.ds(start, count), :]

        taken[0:HALO, :] = source(block - 1, frames_local - HALO, HALO)
        taken[HALO : HALO + frames_local, :] = source(block, 0, frames_local)
        taken[HALO + frames_local : window, :] = source(block + 1, 0, HALO)
        out[...] = dot32(taken[...], w_sub[...]).astype(jnp.bfloat16)

    return call(
        kernel,
        [jax.ShapeDtypeStruct((window, model), jnp.bfloat16)]
        + [jax.ShapeDtypeStruct((piece_slots * piece_rows, model), jnp.bfloat16)] * len(pieces),
        (after, *stacks, *flat, fixed, w_subsample),
        scratch=[
            pltpu.VMEM((slots * frames_local, depth), jnp.bfloat16),
            pltpu.VMEM((window, depth), jnp.bfloat16),
        ],
        flops=2 * window * depth * model,
    )


def finish_rows(features, attended, w_rows, gain, taps, frames_local):
    parts = len(attended)
    model = features.shape[1]
    window = frames_local + 2 * HALO
    chunk = 2 * LANES
    offset = HALO - KERNEL // 2

    def kernel(*refs):
        feature_ref, a_refs, w_refs = refs[0], refs[1 : 1 + parts], refs[1 + parts : 1 + 2 * parts]
        gain_ref, tap_ref, out, held, mixed_rows = refs[1 + 2 * parts :]
        branch = jnp.zeros((window, model), jnp.float32)
        for a_ref, w_ref in zip(a_refs, w_refs):
            branch += dot32(a_ref[...], w_ref[...]).astype(jnp.bfloat16).astype(jnp.float32)
        mixed = (feature_ref[...].astype(jnp.float32) + branch).astype(jnp.bfloat16)
        mixed = mixed.astype(jnp.float32)
        mixed_rows[...] = mixed[HALO : HALO + frames_local]
        conv_in = (normalize(mixed) * gain_ref[...]).astype(jnp.bfloat16).astype(jnp.float32)
        held[HALO : HALO + frames_local, :] = conv_in[HALO : HALO + frames_local]
        block = lax.axis_index("tm") * parts + lax.axis_index("mp")
        before = block > 0
        held[0:HALO, :] = jnp.where(before, conv_in[0:HALO], 0.0)
        after = block < lax.axis_size("tm") * parts - 1
        held[HALO + frames_local : window, :] = jnp.where(after, conv_in[HALO + frames_local :], 0.0)
        for lane in range(0, model, chunk):
            here = slice(lane, lane + chunk)
            total = jnp.zeros((frames_local, chunk), jnp.float32)
            tap_rows = tap_ref[:, here].astype(jnp.float32)
            for phase in range(8):
                taken = [tap for tap in range(KERNEL) if (tap + offset) % 8 == phase]
                reach = (taken[-1] + offset) // 8 * 8 + frames_local
                moved = held[pl.ds(phase, reach), here]
                for tap in taken:
                    begin = (tap + offset) // 8 * 8
                    total += moved[begin : begin + frames_local] * tap_rows[tap : tap + 1]
            silu = total / (1.0 + jnp.exp(-total))
            out[:, here] = (mixed_rows[:, here] + silu).astype(jnp.bfloat16)

    return call(
        kernel,
        jax.ShapeDtypeStruct((frames_local, model), jnp.bfloat16),
        (features, *attended, *w_rows, gain, taps),
        scratch=[
            pltpu.VMEM((window, model), jnp.float32),
            pltpu.VMEM((frames_local, model), jnp.float32),
        ],
        flops=2 * window * model * model,
    )


def exchange(block, axis, bit):
    return lax.ppermute(block, axis, [(i, i ^ bit) for i in range(lax.axis_size(axis))])


def spread_piece(piece):
    axes = spread_axes()
    sizes = [lax.axis_size(axis) for axis in axes]
    pieces = [piece]
    for slot in range(1, 1 << len(axes)):
        route = []
        for source in itertools.product(*(range(size) for size in sizes)):
            target = [place ^ (slot >> number & 1) for number, place in enumerate(source)]
            route.append(tuple(np.ravel_multi_index(at, sizes).item() for at in (source, target)))
        pieces.append(lax.ppermute(piece, tuple(axes), route))
    return pieces


def shifted(block, axis, distance):
    count = lax.axis_size(axis)
    route = [(i - distance, i) for i in range(count) if 0 <= i - distance < count]
    return lax.ppermute(block, axis, route)


def shards(
    waveform,
    segment_start,
    segment_end,
    w_subsample,
    w_attention,
    w_output,
    gain_convolution,
    w_depthwise,
):
    frames_local = waveform.shape[0] // (SUB * HOP)
    frames_shard = segment_start.shape[0]
    parts, shards_total = lax.axis_size("mp"), lax.axis_size("tm")
    bits = [1 << b for b in reversed(range((parts - 1).bit_length()))]

    samples = waveform.reshape(-1, LANES)
    starts, ends = segment_start[None, :], segment_end[None, :]
    tables = (*split_high_low(fourier_table()), *split_high_low(mel_bank()))
    stacked, own_piece = log_mel_rows(starts, ends, samples, w_output, tables, frames_local)
    w_subsample, w_attention, *tables = fetch(stacked, (w_subsample, w_attention, *tables))

    received = [own_piece]
    for bit in bits[:-1]:
        received += [exchange(piece, "mp", bit) for piece in received]
    received = [spread_piece(piece) for piece in received[1:]]
    w_near = exchange(w_output, "mp", bits[-1])

    reach = min((SEG_MAX + HALO - 2) // frames_shard + 1, shards_total - 1)
    whole = reach == shards_total - 1 and shards_total & (shards_total - 1) == 0
    if whole:
        moves = [lambda tm, bit=bit: tm ^ bit for bit in range(1, shards_total)]
        column = [exchange(stacked, "tm", bit) for bit in range(1, shards_total)]
    else:
        steps = [sign * d for d in range(1, reach + 1) for sign in (1, -1)]
        moves = [lambda tm, step=step: tm - step for step in steps]
        column = [shifted(stacked, "tm", step) for step in steps]
    early = [(stacked, [(lambda tm: tm, 0)])]
    late = [(assemble(column), [(move, 0) for move in moves])]

    def across(blocks, bit):
        return [
            (exchange(block, "mp", bit), [(move, mp ^ bit) for move, mp in held])
            for block, held in blocks
        ]

    for bit in bits[:-1]:
        early, late = early + across(early, bit), late + across(late, bit)
    ready = early + late[:1]
    joined = (assemble([block for block, _ in ready]), sum([held for _, held in ready], []))
    groups = [joined] + across([joined], bits[-1]) + late[1:] + across(late[1:], bits[-1])
    stacks, held = zip(*groups)
    places = sum(held, [])
    projected = [
        project_rows(block, w_subsample, w_attention, frames_local) for block in stacks[:-1]
    ]
    fixed, bounds = boundary_rows(places, starts, ends, stacks, tables, frames_local)
    *outs, fixed_query, fixed_key, fixed_value = project_rows(
        stacks[-1], w_subsample, w_attention, frames_local, stacks, fixed
    )
    queries, keys, values = zip(*projected, outs)
    fixed_rows = (fixed_query, fixed_key, fixed_value)

    attended = attend(places, bounds, queries, keys, values, fixed_rows, frames_local)
    arrived = [attended[0]] + [exchange(attended[bit], "mp", bit) for bit in range(1, parts)]
    features, *far = window_features(
        attended[0], places, stacks, fixed, received, w_subsample, frames_local
    )
    w_rows = [w_output, *far, w_near, *(exchange(rows, "mp", bits[-1]) for rows in far)]
    w_order = [0]
    for bit in bits:
        w_order += [other ^ bit for other in w_order]
    w_rows = [w_rows[w_order.index(bit)] for bit in range(parts)]
    return finish_rows(
        features, arrived, w_rows, gain_convolution[None, :], w_depthwise, frames_local
    )


def solution(mesh):
    placed = (
        P(("groups", "tm", "mp")),
        P(("groups", "tm")),
        P(("groups", "tm")),
        P(),
        P(None, None, "mp"),
        P("mp", None),
        P(),
        P(),
    )
    return jax.shard_map(
        shards,
        mesh=mesh,
        in_specs=placed,
        out_specs=P(("groups", "tm", "mp"), None),
        check_vma=False,
    )
```

time: 79.6 us -> 53 us (0.67); the launches traced: 78 us -> 52.6 us
  starting transfers between devices: 36.1 us -> 15.1 us
  local copies, waits for them, and re-layouts: 7.58 us -> 4.33 us
  Pallas kernels: 20.1 us -> 22.5 us
  between operations: 1.85 us -> 0.22 us
  other arithmetic: 1.07 us -> 0 us
  waiting for transfers between devices: 11.4 us -> 10.4 us
    ppermute x12 -> x13, starting transfers between devices: 31.8 us -> 11.5 us  [exchange(): lax.ppermute(block, axis, [(i, i ^ bit) for i in range(lax.axis_size(axis...]
    pallas_call x7 -> x12, Pallas kernels: 20.1 us -> 22.5 us  [call(): pl.pallas_call(kernel, out_shape=out_shape, in_specs=specs, out_specs=jax...]
    unnamed x26 -> x24, local copies, waits for them, and re-layouts: 6.71 us -> 4.32 us
    ppermute x12 -> x13, waiting for transfers between devices: 10.5 us -> 8.12 us  [exchange(): lax.ppermute(block, axis, [(i, i ^ bit) for i in range(lax.axis_size(axis...]
    ppermute x3, waiting for transfers between devices: 0.87 us -> 2.27 us  [spread_piece(): pieces.append(lax.ppermute(piece, tuple(axes), route))]
    another operation x2 -> x0, other arithmetic: 0.86 us -> none  [the longest x1 0.78 us: shards(): own_bounds = jnp.stack([segment_start, segment_end])]
  transfers between devices with their start and end apart: 15 -> 16, of which waited for: 5 -> 6; matrix products, arithmetic and copies ran while one was open for 2% -> 0% of each run, Pallas kernels for 19% -> 28%
where the time goes in v2:
time: 53 us; the launch traced here: 52.6 us
  Pallas kernels  22.5 us (42%)
  starting transfers between devices  15.1 us (28%)
  waiting for transfers between devices  10.4 us (20%)
  local copies, waits for them, and re-layouts  4.33 us (8%)
    pallas_call x12, Pallas kernels, call(): pl.pallas_call(kernel, out_shape=out_shape, in_specs=specs, out_specs=jax...  22.5 us
    ppermute x13, starting transfers between devices, exchange(): lax.ppermute(block, axis, [(i, i ^ bit) for i in range(lax.axis_size(axis...  11.5 us
    ppermute x13, waiting for transfers between devices, exchange(): lax.ppermute(block, axis, [(i, i ^ bit) for i in range(lax.axis_size(axis...  8.12 us
    unnamed x24, local copies, waits for them, and re-layouts  4.32 us
    ppermute x3, starting transfers between devices, spread_piece(): pieces.append(lax.ppermute(piece, tuple(axes), route))  3.62 us
    ppermute x3, waiting for transfers between devices, spread_piece(): pieces.append(lax.ppermute(piece, tuple(axes), route))  2.27 us
  transfers between devices with their start and end apart: 16, of which 6 were waited for; matrix products, arithmetic and copies ran while one was open for 0% of the time, Pallas kernels for 28%

profile of v2, /device:TPU:0, one launch (start us, length us, event | category | flops | bytes accessed | tf_op | source)
XLA Modules:
  0.0 52.6 jit_solution(12005937529613375615)
XLA Ops:
  0.0 3.8 %shard_map.118 = (bf16[1,72,512]{2,1,0:T(8,128)(2,1)}, bf16[96,1536]{1,0:T(8,128)(2,1)}) custom-call(s32[1,256]{1,0:T(1,128)} %bitcast.3, s32[1,256]{1,0:T(1,128)} %bitcast.5, f32[320,128]{1,0:T(8,128)} %bitcast.7, bf16[384,1536]{1,0:T(8,128)(2,1)} %refs_5_.2, bf16[512,512]{1,0:T(8,128)(2,1)} %constant.8.clone.refs_0_.refs_2_, ...), custom_call_target="tpu_custom_call" | custom-call | flops 402653184 | bytes 1000000 | tf_op jit(solution)/shard_map/pallas_call | solution.py:79
  3.8 3.1 %collective-permute-start.1 = (bf16[1,72,512]{2,1,0:T(8,128)(2,1)}, bf16[1,72,512]{2,1,0:T(8,128)(2,1)S(1)}, u32[]{:S(2)}, u32[]{:S(2)}) collective-permute-start(bf16[1,72,512]{2,1,0:T(8,128)(2,1)} %get-tuple-element.36.refs_0_._), channel_id=1, source_target_pairs={{0,4},{4,0},{8,12},{12,8},{1,5},{5,1},{9,13},{13,9},{2,6},{6,2},{1... | collective-permute-start | bytes 221192 | tf_op jit(solution)/shard_map/ppermute | solution.py:528
  6.9 2.6 %collective-permute-start.2 = (bf16[1,72,512]{2,1,0:T(8,128)(2,1)}, bf16[1,72,512]{2,1,0:T(8,128)(2,1)S(1)}, u32[]{:S(2)}, u32[]{:S(2)}) collective-permute-start(bf16[1,72,512]{2,1,0:T(8,128)(2,1)} %get-tuple-element.36.refs_0_._), channel_id=1, source_target_pairs={{0,8},{4,12},{8,0},{12,4},{1,9},{5,13},{9,1},{13,5},{2,10},{6,14},... | collective-permute-start | bytes 221192 | tf_op jit(solution)/shard_map/ppermute | solution.py:528
  9.5 0.0 collective-permute-start.3
  9.5 1.7 %collective-permute-start = (bf16[1,72,512]{2,1,0:T(8,128)(2,1)}, bf16[1,72,512]{2,1,0:T(8,128)(2,1)S(1)}, u32[]{:S(2)}, u32[]{:S(2)}) collective-permute-start(bf16[1,72,512]{2,1,0:T(8,128)(2,1)} %get-tuple-element.36.refs_0_._), channel_id=1, source_target_pairs={{0,2},{1,3},{2,0},{3,1},{4,6},{5,7},{6,4},{7,5},{8,10},{9,11},{10,... | collective-permute-start | bytes 221192 | tf_op jit(solution)/shard_map/ppermute | solution.py:528
  11.2 0.3 collective-permute-start.7
  11.5 0.0 collective-permute-done.1.refs_0_
  11.5 3.4 %collective-permute-done.2.refs_1_ = bf16[1,72,512]{2,1,0:T(8,128)(2,1)S(1)} collective-permute-done((bf16[1,72,512]{2,1,0:T(8,128)(2,1)}, bf16[1,72,512]{2,1,0:T(8,128)(2,1)S(1)}, u32[]{:S(2)}, u32[]{:S(2)}) %collective-permute-start.2) | collective-permute-done | bytes 73760 | tf_op jit(solution)/shard_map/ppermute | solution.py:528
  14.9 1.0 %collective-permute-done.3.refs_2_ = bf16[1,72,512]{2,1,0:T(8,128)(2,1)S(1)} collective-permute-done((bf16[1,72,512]{2,1,0:T(8,128)(2,1)}, bf16[1,72,512]{2,1,0:T(8,128)(2,1)S(1)}, u32[]{:S(2)}, u32[]{:S(2)}) %collective-permute-start.3) | collective-permute-done | bytes 73760 | tf_op jit(solution)/shard_map/ppermute | solution.py:528
  16.0 0.0 collective-permute-done.refs_1_
  16.0 0.0 copy-start.5
  16.0 0.9 %copy-done.5 = bf16[1,72,512]{2,1,0:T(8,128)(2,1)S(1)} copy-done((bf16[1,72,512]{2,1,0:T(8,128)(2,1)S(1)}, bf16[1,72,512]{2,1,0:T(8,128)(2,1)}, u32[]{:S(2)}) %copy-start.5) | copy-done | bytes 73752
  16.9 0.1 collective-permute-start.4
  17.0 1.6 %collective-permute-start.5 = (bf16[3,72,512]{2,1,0:T(8,128)(2,1)S(1)}, bf16[3,72,512]{2,1,0:T(8,128)(2,1)S(1)}, u32[]{:S(2)}, u32[]{:S(2)}) collective-permute-start(bf16[3,72,512]{2,1,0:T(8,128)(2,1)S(1)} %shard_map.119.refs_2_), channel_id=1, source_target_pairs={{0,2},{1,3},{2,0},{3,1},{4,6},{5,7},{6,4},{7,5},{8,10},{9,11},{10,... | collective-permute-start | bytes 663560 | tf_op jit(solution)/shard_map/ppermute | solution.py:528
  18.6 0.2 collective-permute-start.14
  18.7 0.0 copy-start.1
  18.7 2.0 %copy-done.1 = bf16[3,1536,384]{2,1,0:T(8,128)(2,1)S(1)} copy-done((bf16[3,1536,384]{2,1,0:T(8,128)(2,1)S(1)}, bf16[3,1536,384]{2,1,0:T(8,128)(2,1)}, u32[]{:S(2)}) %copy-start.1) | copy-done | bytes 3538968
  20.7 1.4 %copy-done.4 = bf16[512,1536]{1,0:T(8,128)(2,1)S(1)} copy-done((bf16[512,1536]{1,0:T(8,128)(2,1)S(1)}, bf16[512,1536]{1,0:T(8,128)(2,1)}, u32[]{:S(2)}) %copy-start.4) | copy-done | bytes 1572888
  22.1 0.8 %shard_map.121 = (bf16[512,1536]{1,0:T(8,128)(2,1)S(1)}, bf16[3,1536,384]{2,1,0:T(8,128)(2,1)S(1)}, bf16[512,512]{1,0:T(8,128)(2,1)S(1)}, bf16[512,512]{1,0:T(8,...) custom-call(bf16[1,72,512]{2,1,0:T(8,128)(2,1)S(1)} %copy-done.5, ...), custom_call_target="tpu_custom_call" | custom-call | bytes 1000000 | tf_op jit(solution)/shard_map/pallas_call | solution.py:79
  23.0 2.7 %shard_map.123 = (bf16[320,384]{1,0:T(8,128)(2,1)S(1)}, bf16[320,384]{1,0:T(8,128)(2,1)S(1)}, bf16[320,384]{1,0:T(8,128)(2,1)S(1)}) custom-call(bf16[5,72,512]{2,1,0:T(8,128)(2,1)S(1)} %shard_map.120.refs_0_.stack_ref, bf16[512,1536]{1,0:T(8,128)(2,1)S(1)} %get-tuple-element.42.w_sub.refs_9_, bf16[3,1536,384]{2,1,0:T(8,128)(2,1)S(1)} %get-tuple-element.43.w_att), custom_call_target="tpu_custom_call" | custom-call | flops 1635778560 | bytes 1000000 | tf_op jit(solution)/shard_map/pallas_call | solution.py:79
  25.7 0.0 collective-permute-done.7.refs_4_
  25.7 2.1 %collective-permute-start.10 = (bf16[96,1536]{1,0:T(8,128)(2,1)S(1)}, bf16[96,1536]{1,0:T(8,128)(2,1)S(1)}, u32[]{:S(2)}, u32[]{:S(2)}) collective-permute-start(bf16[96,1536]{1,0:T(8,128)(2,1)S(1)} %collective-permute-done.7.refs_4_), channel_id=1, source_target_pairs={{0,20},{4,16},{8,28},{12,24},{16,4},{20,0},{24,12},{28,8},{1,21},{... | collective-permute-start | bytes 884744 | tf_op jit(solution)/shard_map/ppermute | solution.py:540
  27.8 0.5 collective-permute-start.8
  28.3 0.0 collective-permute-done.5.refs_2_.stack_ref
  28.3 0.0 collective-permute-start.6
  28.3 1.8 %shard_map.125 = (bf16[192,384]{1,0:T(8,128)(2,1)S(1)}, bf16[192,384]{1,0:T(8,128)(2,1)S(1)}, bf16[192,384]{1,0:T(8,128)(2,1)S(1)}) custom-call(bf16[3,72,512]{2,1,0:T(8,128)(2,1)S(1)} %collective-permute-done.5.refs_2_.stack_ref, bf16[512,1536]{1,0:T(8,128)(2,1)S(1)} %get-tuple-element.42.w_sub.refs_9_, bf16[3,1536,384]{2,1,0:T(8,128)(2,1)S(1)} %get-tuple-element.43.w_att), custom_call_target="tpu_custom_call" | custom-call | flops 981467136 | bytes 1000000 | tf_op jit(solution)/shard_map/pallas_call | solution.py:79
  30.1 0.0 copy-start.9
  30.2 0.0 copy-start.10
  30.2 1.0 %collective-permute-start.9 = (bf16[96,1536]{1,0:T(8,128)(2,1)S(1)}, bf16[96,1536]{1,0:T(8,128)(2,1)S(1)}, u32[]{:S(2)}, u32[]{:S(2)}) collective-permute-start(bf16[96,1536]{1,0:T(8,128)(2,1)S(1)} %collective-permute-done.7.refs_4_), channel_id=1, source_target_pairs={{0,4},{4,0},{8,12},{12,8},{16,20},{20,16},{24,28},{28,24},{1,5},{5... | collective-permute-start | bytes 884744 | tf_op jit(solution)/shard_map/ppermute | solution.py:540
  31.2 2.7 %shard_map.124 = (bf16[320,384]{1,0:T(8,128)(2,1)S(1)}, bf16[320,384]{1,0:T(8,128)(2,1)S(1)}, bf16[320,384]{1,0:T(8,128)(2,1)S(1)}) custom-call(bf16[5,72,512]{2,1,0:T(8,128)(2,1)S(1)} %collective-permute-done.4.refs_1_.stack_ref, bf16[512,1536]{1,0:T(8,128)(2,1)S(1)} %get-tuple-element.42.w_sub.refs_9_, bf16[3,1536,384]{2,1,0:T(8,128)(2,1)S(1)} %get-tuple-element.43.w_att), custom_call_target="tpu_custom_call" | custom-call | flops 1635778560 | bytes 1000000 | tf_op jit(solution)/shard_map/pallas_call | solution.py:79
  33.9 0.0 collective-permute-done.6.refs_3_.stack_ref
  33.9 0.8 %shard_map.122 = (bf16[16,256]{1,0:T(8,128)(2,1)S(1)}, f32[2,288]{1,0:T(2,128)S(1)}) custom-call(s32[1,256]{1,0:T(1,128)S(1)} %bitcast.4, s32[1,256]{1,0:T(1,128)S(1)} %bitcast.6, bf16[5,72,512]{2,1,0:T(8,128)(2,1)S(1)} %shard_map.120.refs_0_.stack_ref, bf16[5,72,512]{2,1,0:T(8,128)(2,1)S(1)} %collective-permute-done.4.refs_1_.stack_ref, ...), custom_call_target="tpu_custom_call" | custom-call | flops 50331648 | bytes 1000000 | tf_op jit(solution)/shard_map/pallas_call | solution.py:79
  34.8 1.9 %shard_map.126 = (bf16[192,384]{1,0:T(8,128)(2,1)S(1)}, bf16[192,384]{1,0:T(8,128)(2,1)S(1)}, bf16[192,384]{1,0:T(8,128)(2,1)S(1)}, bf16[16,384]{1,0:T(8,128)(2,...) custom-call(bf16[3,72,512]{2,1,0:T(8,128)(2,1)S(1)} %collective-permute-done.6.refs_3_.stack_ref, ...), custom_call_target="tpu_custom_call" | custom-call | flops 1063256064 | bytes 1000000 | tf_op jit(solution)/shard_map/pallas_call | solution.py:79
  36.7 3.3 %shard_map.127 = (bf16[96,384]{1,0:T(8,128)(2,1)S(1)}, bf16[96,384]{1,0:T(8,128)(2,1)S(1)}, bf16[96,384]{1,0:T(8,128)(2,1)S(1)}, bf16[96,384]{1,0:T(8,128)(2,1)S(1)}) custom-call(f32[2,288]{1,0:T(2,128)S(1)} %get-tuple-element.41.refs_0_, bf16[320,384]{1,0:T(8,128)(2,1)S(1)} %get-tuple-element.44.refs_1_, bf16[320,384]{1,0:T(8,128)(2,1)S(1)} %get-tuple-element.45.refs_2_, ...), custom_call_target="tpu_custom_call" | custom-call | flops 1811939328 | bytes 1000000 | tf_op jit(solution)/shard_map/pallas_call | solution.py:79
  40.1 0.0 collective-permute-done.10.refs_7_
  40.1 2.2 %collective-permute-done.8.refs_5_ = bf16[96,1536]{1,0:T(8,128)(2,1)S(1)} collective-permute-done((bf16[96,1536]{1,0:T(8,128)(2,1)S(1)}, bf16[96,1536]{1,0:T(8,128)(2,1)S(1)}, u32[]{:S(2)}, u32[]{:S(2)}) %collective-permute-start.8) | collective-permute-done | bytes 294944 | tf_op jit(solution)/shard_map/ppermute | solution.py:540
  42.2 0.1 collective-permute-done.9.refs_6_
  42.3 0.6 %shard_map.128 = (bf16[96,1536]{1,0:T(8,128)(2,1)S(1)}, bf16[384,1536]{1,0:T(8,128)(2,1)S(1)}) custom-call(bf16[96,384]{1,0:T(8,128)(2,1)S(1)} %get-tuple-element.60._.refs_1_, bf16[5,72,512]{2,1,0:T(8,128)(2,1)S(1)} %shard_map.120.refs_0_.stack_ref, bf16[5,72,512]{2,1,0:T(8,128)(2,1)S(1)} %collective-permute-done.4.refs_1_.stack_ref, ...), custom_call_target="tpu_custom_call" | custom-call | flops 150994944 | bytes 1000000 | tf_op jit(solution)/shard_map/pallas_call | solution.py:79
  42.9 0.1 collective-permute-start.15
  43.0 0.5 collective-permute-start.11
  43.5 0.5 %collective-permute-start.12 = (bf16[96,384]{1,0:T(8,128)(2,1)S(1)}, bf16[96,384]{1,0:T(8,128)(2,1)S(1)}, u32[]{:S(2)}, u32[]{:S(2)}) collective-permute-start(bf16[96,384]{1,0:T(8,128)(2,1)S(1)} %get-tuple-element.64), channel_id=1, source_target_pairs={{0,2},{1,3},{2,0},{3,1},{4,6},{5,7},{6,4},{7,5},{8,10},{9,11},{10,... | collective-permute-start | bytes 221192 | tf_op jit(solution)/shard_map/ppermute | solution.py:528
  44.0 0.9 %collective-permute-start.13 = (bf16[96,384]{1,0:T(8,128)(2,1)S(1)}, bf16[96,384]{1,0:T(8,128)(2,1)S(1)}, u32[]{:S(2)}, u32[]{:S(2)}) collective-permute-start(bf16[96,384]{1,0:T(8,128)(2,1)S(1)} %get-tuple-element.65), channel_id=1, source_target_pairs={{0,3},{1,2},{2,1},{3,0},{4,7},{5,6},{6,5},{7,4},{8,11},{9,10},{10,... | collective-permute-start | bytes 221192 | tf_op jit(solution)/shard_map/ppermute | solution.py:528
  44.9 1.0 %collective-permute-done.11.refs_2_ = bf16[96,384]{1,0:T(8,128)(2,1)S(1)} collective-permute-done((bf16[96,384]{1,0:T(8,128)(2,1)S(1)}, bf16[96,384]{1,0:T(8,128)(2,1)S(1)}, u32[]{:S(2)}, u32[]{:S(2)}) %collective-permute-start.11) | collective-permute-done | bytes 73760 | tf_op jit(solution)/shard_map/ppermute | solution.py:528
  46.0 2.7 %collective-permute-done.12.refs_3_ = bf16[96,384]{1,0:T(8,128)(2,1)S(1)} collective-permute-done((bf16[96,384]{1,0:T(8,128)(2,1)S(1)}, bf16[96,384]{1,0:T(8,128)(2,1)S(1)}, u32[]{:S(2)}, u32[]{:S(2)}) %collective-permute-start.12) | collective-permute-done | bytes 73760 | tf_op jit(solution)/shard_map/ppermute | solution.py:528
  48.6 0.0 collective-permute-done.13.refs_4_
  48.6 0.0 collective-permute-done.14.refs_6_
  48.6 0.0 collective-permute-done.15.refs_8_
  48.6 4.0 %shard_map.129 = bf16[64,1536]{1,0:T(8,128)(2,1)} custom-call(bf16[96,1536]{1,0:T(8,128)(2,1)S(1)} %get-tuple-element.62.refs_0_, bf16[96,384]{1,0:T(8,128)(2,1)S(1)} %get-tuple-element.60._.refs_1_, bf16[96,384]{1,0:T(8,128)(2,1)S(1)} %collective-permute-done.11.refs_2_, bf16[96,384]{1,0:T(8,128)(2,1)S(1)} %collective-permute-done.12.refs_3_, ...), custom_call_target="tpu_custom_call" | custom-call | flops 452984832 | bytes 1000000 | tf_op jit(solution)/shard_map/pallas_call | solution.py:79
  (21 shorter events, 0.1 us)
Async XLA Ops:
  0.0 18.5 %copy-start = (bf16[384,1536]{1,0:T(8,128)(2,1)S(1)}, bf16[384,1536]{1,0:T(8,128)(2,1)}, u32[]{:S(2)}) copy-start(bf16[384,1536]{1,0:T(8,128)(2,1)} %refs_5_.2) | copy-start | bytes 3538948
  0.0 18.7 %copy-start.2 = (bf16[512,512]{1,0:T(8,128)(2,1)S(1)}, bf16[512,512]{1,0:T(8,128)(2,1)}, u32[]{:S(2)}) copy-start(bf16[512,512]{1,0:T(8,128)(2,1)} %constant.8.clone.refs_0_.refs_2_) | copy-start | bytes 1572868
  0.0 18.7 %copy-start.3 = (bf16[512,512]{1,0:T(8,128)(2,1)S(1)}, bf16[512,512]{1,0:T(8,128)(2,1)}, u32[]{:S(2)}) copy-start(bf16[512,512]{1,0:T(8,128)(2,1)} %constant.9.clone.refs_1_.refs_3_) | copy-start | bytes 1572868
  0.0 18.7 %copy-start.6 = (bf16[256,128]{1,0:T(8,128)(2,1)S(1)}, bf16[256,128]{1,0:T(8,128)(2,1)}, u32[]{:S(2)}) copy-start(bf16[256,128]{1,0:T(8,128)(2,1)} %constant.10.clone.refs_2_.refs_4_) | copy-start | bytes 196612
  0.0 18.7 %copy-start.7 = (bf16[256,128]{1,0:T(8,128)(2,1)S(1)}, bf16[256,128]{1,0:T(8,128)(2,1)}, u32[]{:S(2)}) copy-start(bf16[256,128]{1,0:T(8,128)(2,1)} %constant.11.clone.refs_3_.refs_5_) | copy-start | bytes 196612
  3.8 7.7 %collective-permute-start.1 = (bf16[1,72,512]{2,1,0:T(8,128)(2,1)}, bf16[1,72,512]{2,1,0:T(8,128)(2,1)S(1)}, u32[]{:S(2)}, u32[]{:S(2)}) collective-permute-start(bf16[1,72,512]{2,1,0:T(8,128)(2,1)} %get-tuple-element.36.refs_0_._), channel_id=1, source_target_pairs={{0,4},{4,0},{8,12},{12,8},{1,5},{5,1},{9,13},{13,9},{2,6},{6,2},{1... | collective-permute-start | bytes 221192 | tf_op jit(solution)/shard_map/ppermute | solution.py:528
  6.9 8.0 %collective-permute-start.2 = (bf16[1,72,512]{2,1,0:T(8,128)(2,1)}, bf16[1,72,512]{2,1,0:T(8,128)(2,1)S(1)}, u32[]{:S(2)}, u32[]{:S(2)}) collective-permute-start(bf16[1,72,512]{2,1,0:T(8,128)(2,1)} %get-tuple-element.36.refs_0_._), channel_id=1, source_target_pairs={{0,8},{4,12},{8,0},{12,4},{1,9},{5,13},{9,1},{13,5},{2,10},{6,14},... | collective-permute-start | bytes 221192 | tf_op jit(solution)/shard_map/ppermute | solution.py:528
  9.5 6.5 %collective-permute-start.3 = (bf16[1,72,512]{2,1,0:T(8,128)(2,1)}, bf16[1,72,512]{2,1,0:T(8,128)(2,1)S(1)}, u32[]{:S(2)}, u32[]{:S(2)}) collective-permute-start(bf16[1,72,512]{2,1,0:T(8,128)(2,1)} %get-tuple-element.36.refs_0_._), channel_id=1, source_target_pairs={{0,12},{4,8},{8,4},{12,0},{1,13},{5,9},{9,5},{13,1},{2,14},{6,10},... | collective-permute-start | bytes 221192 | tf_op jit(solution)/shard_map/ppermute | solution.py:528
  9.5 6.5 %collective-permute-start = (bf16[1,72,512]{2,1,0:T(8,128)(2,1)}, bf16[1,72,512]{2,1,0:T(8,128)(2,1)S(1)}, u32[]{:S(2)}, u32[]{:S(2)}) collective-permute-start(bf16[1,72,512]{2,1,0:T(8,128)(2,1)} %get-tuple-element.36.refs_0_._), channel_id=1, source_target_pairs={{0,2},{1,3},{2,0},{3,1},{4,6},{5,7},{6,4},{7,5},{8,10},{9,11},{10,... | collective-permute-start | bytes 221192 | tf_op jit(solution)/shard_map/ppermute | solution.py:528
  11.2 14.5 %collective-permute-start.7 = (bf16[96,1536]{1,0:T(8,128)(2,1)}, bf16[96,1536]{1,0:T(8,128)(2,1)S(1)}, u32[]{:S(2)}, u32[]{:S(2)}) collective-permute-start(bf16[96,1536]{1,0:T(8,128)(2,1)} %get-tuple-element.61), channel_id=1, source_target_pairs={{0,2},{1,3},{2,0},{3,1},{4,6},{5,7},{6,4},{7,5},{8,10},{9,11},{10,... | collective-permute-start | bytes 884744 | tf_op jit(solution)/shard_map/ppermute | solution.py:528
  16.0 0.9 %copy-start.5 = (bf16[1,72,512]{2,1,0:T(8,128)(2,1)S(1)}, bf16[1,72,512]{2,1,0:T(8,128)(2,1)}, u32[]{:S(2)}) copy-start(bf16[1,72,512]{2,1,0:T(8,128)(2,1)} %get-tuple-element.36.refs_0_._) | copy-start | bytes 221188
  16.9 13.3 %collective-permute-start.4 = (bf16[5,72,512]{2,1,0:T(8,128)(2,1)S(1)}, bf16[5,72,512]{2,1,0:T(8,128)(2,1)S(1)}, u32[]{:S(2)}, u32[]{:S(2)}) collective-permute-start(bf16[5,72,512]{2,1,0:T(8,128)(2,1)S(1)} %shard_map.120.refs_0_.stack_ref), channel_id=1, source_target_pairs={{0,1},{1,0},{2,3},{3,2},{4,5},{5,4},{6,7},{7,6},{8,9},{9,8},{10,11... | collective-permute-start | bytes 1105928 | tf_op jit(solution)/shard_map/ppermute | solution.py:528
  17.0 11.3 %collective-permute-start.5 = (bf16[3,72,512]{2,1,0:T(8,128)(2,1)S(1)}, bf16[3,72,512]{2,1,0:T(8,128)(2,1)S(1)}, u32[]{:S(2)}, u32[]{:S(2)}) collective-permute-start(bf16[3,72,512]{2,1,0:T(8,128)(2,1)S(1)} %shard_map.119.refs_2_), channel_id=1, source_target_pairs={{0,2},{1,3},{2,0},{3,1},{4,6},{5,7},{6,4},{7,5},{8,10},{9,11},{10,... | collective-permute-start | bytes 663560 | tf_op jit(solution)/shard_map/ppermute | solution.py:528
  18.6 30.1 %collective-permute-start.14 = (bf16[384,1536]{1,0:T(8,128)(2,1)S(1)}, bf16[384,1536]{1,0:T(8,128)(2,1)S(1)}, u32[]{:S(2)}, u32[]{:S(2)}) collective-permute-start(bf16[384,1536]{1,0:T(8,128)(2,1)S(1)} %copy-done), channel_id=1, source_target_pairs={{0,1},{1,0},{2,3},{3,2},{4,5},{5,4},{6,7},{7,6},{8,9},{9,8},{10,11... | collective-permute-start | bytes 3538952 | tf_op jit(solution)/shard_map/ppermute | solution.py:528
  18.7 2.0 %copy-start.1 = (bf16[3,1536,384]{2,1,0:T(8,128)(2,1)S(1)}, bf16[3,1536,384]{2,1,0:T(8,128)(2,1)}, u32[]{:S(2)}) copy-start(bf16[3,1536,384]{2,1,0:T(8,128)(2,1)} %refs_1_.2) | copy-start | bytes 10616836
  20.7 1.4 %copy-start.4 = (bf16[512,1536]{1,0:T(8,128)(2,1)S(1)}, bf16[512,1536]{1,0:T(8,128)(2,1)}, u32[]{:S(2)}) copy-start(bf16[512,1536]{1,0:T(8,128)(2,1)} %refs_0_.2) | copy-start | bytes 4718596
  25.7 14.4 %collective-permute-start.10 = (bf16[96,1536]{1,0:T(8,128)(2,1)S(1)}, bf16[96,1536]{1,0:T(8,128)(2,1)S(1)}, u32[]{:S(2)}, u32[]{:S(2)}) collective-permute-start(bf16[96,1536]{1,0:T(8,128)(2,1)S(1)} %collective-permute-done.7.refs_4_), channel_id=1, source_target_pairs={{0,20},{4,16},{8,28},{12,24},{16,4},{20,0},{24,12},{28,8},{1,21},{... | collective-permute-start | bytes 884744 | tf_op jit(solution)/shard_map/ppermute | solution.py:540
  27.8 14.4 %collective-permute-start.8 = (bf16[96,1536]{1,0:T(8,128)(2,1)S(1)}, bf16[96,1536]{1,0:T(8,128)(2,1)S(1)}, u32[]{:S(2)}, u32[]{:S(2)}) collective-permute-start(bf16[96,1536]{1,0:T(8,128)(2,1)S(1)} %collective-permute-done.7.refs_4_), channel_id=1, source_target_pairs={{0,16},{4,20},{8,24},{12,28},{16,0},{20,4},{24,8},{28,12},{1,17},{... | collective-permute-start | bytes 884744 | tf_op jit(solution)/shard_map/ppermute | solution.py:540
  28.3 5.6 %collective-permute-start.6 = (bf16[3,72,512]{2,1,0:T(8,128)(2,1)S(1)}, bf16[3,72,512]{2,1,0:T(8,128)(2,1)S(1)}, u32[]{:S(2)}, u32[]{:S(2)}) collective-permute-start(bf16[3,72,512]{2,1,0:T(8,128)(2,1)S(1)} %collective-permute-done.5.refs_2_.stack_ref), channel_id=1, source_target_pairs={{0,1},{1,0},{2,3},{3,2},{4,5},{5,4},{6,7},{7,6},{8,9},{9,8},{10,11... | collective-permute-start | bytes 663560 | tf_op jit(solution)/shard_map/ppermute | solution.py:528
  30.1 3.8 %copy-start.9 = (s32[256]{0:T(256)S(1)}, s32[256]{0:T(256)}, u32[]{:S(2)}) copy-start(s32[256]{0:T(256)} %param.13) | copy-start | bytes 3076
  30.2 3.8 %copy-start.10 = (s32[256]{0:T(256)S(1)}, s32[256]{0:T(256)}, u32[]{:S(2)}) copy-start(s32[256]{0:T(256)} %param.14) | copy-start | bytes 3076
  30.2 12.1 %collective-permute-start.9 = (bf16[96,1536]{1,0:T(8,128)(2,1)S(1)}, bf16[96,1536]{1,0:T(8,128)(2,1)S(1)}, u32[]{:S(2)}, u32[]{:S(2)}) collective-permute-start(bf16[96,1536]{1,0:T(8,128)(2,1)S(1)} %collective-permute-done.7.refs_4_), channel_id=1, source_target_pairs={{0,4},{4,0},{8,12},{12,8},{16,20},{20,16},{24,28},{28,24},{1,5},{5... | collective-permute-start | bytes 884744 | tf_op jit(solution)/shard_map/ppermute | solution.py:540
  42.3 2.6 %copy-start.11 = (f32[1536]{0:T(1024)S(1)}, f32[1536]{0:T(1024)}, u32[]{:S(2)}) copy-start(f32[1536]{0:T(1024)} %param.18) | copy-start | bytes 18436
  42.3 6.3 %copy-start.8 = (bf16[31,1536]{1,0:T(8,128)(2,1)S(1)}, bf16[31,1536]{1,0:T(8,128)(2,1)}, u32[]{:S(2)}) copy-start(bf16[31,1536]{1,0:T(8,128)(2,1)} %refs_10_.1) | copy-start | bytes 285700
  42.9 5.7 %collective-permute-start.15 = (bf16[384,1536]{1,0:T(8,128)(2,1)S(1)}, bf16[384,1536]{1,0:T(8,128)(2,1)S(1)}, u32[]{:S(2)}, u32[]{:S(2)}) collective-permute-start(bf16[384,1536]{1,0:T(8,128)(2,1)S(1)} %get-tuple-element.66.refs_7_), channel_id=1, source_target_pairs={{0,1},{1,0},{2,3},{3,2},{4,5},{5,4},{6,7},{7,6},{8,9},{9,8},{10,11... | collective-permute-start | bytes 3538952 | tf_op jit(solution)/shard_map/ppermute | solution.py:528
  43.0 2.9 %collective-permute-start.11 = (bf16[96,384]{1,0:T(8,128)(2,1)S(1)}, bf16[96,384]{1,0:T(8,128)(2,1)S(1)}, u32[]{:S(2)}, u32[]{:S(2)}) collective-permute-start(bf16[96,384]{1,0:T(8,128)(2,1)S(1)} %get-tuple-element.63), channel_id=1, source_target_pairs={{0,1},{1,0},{2,3},{3,2},{4,5},{5,4},{6,7},{7,6},{8,9},{9,8},{10,11... | collective-permute-start | bytes 221192 | tf_op jit(solution)/shard_map/ppermute | solution.py:528
  43.5 5.1 %collective-permute-start.12 = (bf16[96,384]{1,0:T(8,128)(2,1)S(1)}, bf16[96,384]{1,0:T(8,128)(2,1)S(1)}, u32[]{:S(2)}, u32[]{:S(2)}) collective-permute-start(bf16[96,384]{1,0:T(8,128)(2,1)S(1)} %get-tuple-element.64), channel_id=1, source_target_pairs={{0,2},{1,3},{2,0},{3,1},{4,6},{5,7},{6,4},{7,5},{8,10},{9,11},{10,... | collective-permute-start | bytes 221192 | tf_op jit(solution)/shard_map/ppermute | solution.py:528
  44.0 4.6 %collective-permute-start.13 = (bf16[96,384]{1,0:T(8,128)(2,1)S(1)}, bf16[96,384]{1,0:T(8,128)(2,1)S(1)}, u32[]{:S(2)}, u32[]{:S(2)}) collective-permute-start(bf16[96,384]{1,0:T(8,128)(2,1)S(1)} %get-tuple-element.65), channel_id=1, source_target_pairs={{0,3},{1,2},{2,1},{3,0},{4,7},{5,6},{6,5},{7,4},{8,11},{9,10},{10,... | collective-permute-start | bytes 221192 | tf_op jit(solution)/shard_map/ppermute | solution.py:528

commit v3 on v2

v3 whole, which is shorter than its diff:
```python
import math

import jax
import jax.numpy as jnp
import ml_dtypes
import numpy as np
from jax import lax
from jax.experimental import pallas as pl
from jax.experimental.pallas import tpu as pltpu
from jax.sharding import PartitionSpec as P

HD = 64
NMEL = 128
NFFT = 400
HOP = 160
BINS = 256
SUB = 4
KERNEL = 31
SEG_MAX = 750
LANES = 128
HALO = 16
EXTRA = 8
FLOPS_PER_MICRO = 1000000000
TAIL_LINES = 3
HEAD_LINES = 2
DIGIT = 128
FRAME_ROWS = SUB * HOP // LANES
WIDE = -(-NFFT // LANES) * LANES


def split_high_low(table):
    high = table.astype(ml_dtypes.bfloat16)
    low = (table - high.astype(np.float32)).astype(ml_dtypes.bfloat16)
    return high, low


def fourier_table():
    sample_index = np.arange(NFFT)[:, None]
    bin_index = np.arange(BINS)[None, :]
    angle = (sample_index * bin_index % NFFT) * (2.0 * math.pi / NFFT)
    window = 0.5 - 0.5 * np.cos(np.arange(NFFT) * (2.0 * math.pi / NFFT))
    kept = bin_index <= NFFT // 2
    cosine = np.where(kept, np.cos(angle), 0.0) * window[:, None]
    sine = np.where(kept, -np.sin(angle), 0.0) * window[:, None]
    table = np.concatenate([cosine, sine], axis=1).astype(np.float32)
    return np.pad(table, ((0, WIDE - NFFT), (0, 0)))


def mel_bank():
    mel_top = 2595.0 * math.log10(1.0 + 8000.0 / 700.0)
    mel_points = np.arange(NMEL + 2) * (mel_top / (NMEL + 1))
    edges = 700.0 * (np.power(10.0, mel_points / 2595.0) - 1.0) * (NFFT / 16000.0)
    widths = np.maximum(edges[2:] - edges[1:-1], 1.0)
    bin_value = np.arange(BINS)[:, None]
    triangle = np.maximum(0.0, 1.0 - np.abs(bin_value - edges[None, 1:-1]) / widths[None, :])
    return np.where(bin_value <= NFFT // 2, triangle, 0.0).astype(np.float32)


def front_tables():
    high, low = split_high_low(fourier_table())
    bank = np.concatenate(split_high_low(mel_bank()), axis=0)
    return np.concatenate([high, low, bank], axis=1)


def dot32(left, right):
    return jnp.dot(left, right, preferred_element_type=jnp.float32)


def dot_split(values, table_high, table_low):
    high = values.astype(jnp.bfloat16)
    low = (values - high.astype(jnp.float32)).astype(jnp.bfloat16)
    return dot32(high, table_high) + (dot32(low, table_high) + dot32(high, table_low))


def normalize(values):
    center = jnp.mean(values, axis=-1, keepdims=True)
    shifted = values - center
    spread = jnp.mean(jnp.square(shifted), axis=-1, keepdims=True)
    return shifted * lax.rsqrt(spread + 1e-05)


def call(kernel, out_shape, operands, scratch=(), micros=1.0, remote=0, vmem=16):
    specs = [pl.BlockSpec(memory_space=pltpu.VMEM)] * (len(operands) - remote)
    specs += [pl.BlockSpec(memory_space=pltpu.HBM)] * remote
    return pl.pallas_call(
        kernel,
        out_shape=out_shape,
        in_specs=specs,
        out_specs=jax.tree.map(lambda _: pl.BlockSpec(memory_space=pltpu.VMEM), out_shape),
        scratch_shapes=list(scratch),
        compiler_params=pltpu.CompilerParams(vmem_limit_bytes=vmem * 1024 * 1024),
        cost_estimate=pl.CostEstimate(
            flops=int(micros * FLOPS_PER_MICRO), bytes_accessed=1000000, transcendentals=0
        ),
    )(*operands)


def fetch(after, arrays):
    count = len(arrays)

    def kernel(_, *refs):
        sources, outs, sems = refs[:count], refs[count:-1], refs[-1]
        copies = [
            pltpu.make_async_copy(source, target, sems.at[slot])
            for slot, (source, target) in enumerate(zip(sources, outs))
        ]
        for copy in copies:
            copy.start()
        for copy in copies:
            copy.wait()

    return call(
        kernel,
        [jax.ShapeDtypeStruct(array.shape, array.dtype) for array in arrays],
        (after, *arrays),
        scratch=[pltpu.SemaphoreType.DMA((count,))],
        remote=count,
    )


def padded_row(row):
    return jnp.concatenate([row, jnp.zeros((1, SUB * NMEL - row.shape[1]), row.dtype)], axis=1)


def log_mel(windows, tables):
    wide, bank = 2 * BINS, slice(4 * BINS, 4 * BINS + NMEL)
    spectrum = dot_split(windows, tables[:, 0:wide], tables[:, wide : 2 * wide])
    power = jnp.square(spectrum[:, :BINS]) + jnp.square(spectrum[:, BINS:])
    return jnp.log(dot_split(power, tables[0:BINS, bank], tables[BINS:, bank]) + 1e-06)


def log_mel_rows(starts, ends, samples, tables, frames_local):
    rows = frames_local * FRAME_ROWS
    frames_shard = starts.shape[1]

    def kernel(start_ref, end_ref, wave, tables_ref, out, held):
        held[0:rows, :] = wave[...]
        held[rows : rows + 8, :] = jnp.zeros((8, LANES), jnp.float32)
        lines = [held[pl.ds(j, frames_local, stride=FRAME_ROWS), :] for j in range(FRAME_ROWS + 2)]
        windows = []
        for sub in range(SUB):
            line, lane = divmod(sub * HOP, LANES)
            taken = jnp.concatenate(lines[line : line + WIDE // LANES], axis=1)
            windows.append(pltpu.roll(taken, WIDE - lane, axis=1) if lane else taken)
        extras = []
        for taken in (range(rows - TAIL_LINES, rows), range(HEAD_LINES)):
            line = jnp.concatenate([held[row : row + 1, :] for row in taken], axis=1)
            high = line.astype(jnp.bfloat16).astype(jnp.float32)
            extras += [padded_row(high), padded_row(line - high)]
        for ref in (start_ref, end_ref):
            edge = jnp.concatenate([ref[:, :HALO], ref[:, frames_shard - HALO :]], axis=1)
            high = edge // DIGIT
            low = edge - high * DIGIT
            extras += [padded_row(digit.astype(jnp.float32)) for digit in (high, low)]
        out[0, frames_local:, :] = jnp.concatenate(extras, axis=0).astype(jnp.bfloat16)
        mel = log_mel(jnp.concatenate(windows, axis=0), tables_ref)
        for sub in range(SUB):
            out[0, 0:frames_local, sub * NMEL : (sub + 1) * NMEL] = mel[
                sub * frames_local : (sub + 1) * frames_local
            ].astype(jnp.bfloat16)

    return call(
        kernel,
        jax.ShapeDtypeStruct((1, frames_local + EXTRA, SUB * NMEL), jnp.bfloat16),
        (starts, ends, samples, tables),
        scratch=[pltpu.VMEM((rows + 8, LANES), jnp.float32)],
        micros=1.0,
    )


def boundary_rows(places, starts, ends, stacks, tables, frames_local):
    counts = [stack.shape[0] for stack in stacks]
    slots = len(places)
    rows = -(-slots // HALO) * HALO
    frames_shard = starts.shape[1]
    parts = lax.axis_size("mp")
    final = lax.axis_size("tm") * parts - 1

    def kernel(start_ref, end_ref, *refs):
        stack_refs, refs = refs[: len(counts)], refs[len(counts) :]
        tables_ref, out, bounds, tails, heads, nexts, edges = refs
        time_index, model_index = lax.axis_index("tm"), lax.axis_index("mp")
        tails[...] = jnp.zeros_like(tails)
        nexts[...] = jnp.zeros_like(nexts)
        slot = 0
        for stack_ref, count in zip(stack_refs, counts):
            for block in range(count):
                kept = stack_ref[block, frames_local:, :].astype(jnp.float32)
                here = slice(slot, slot + 1)
                tails[here, :] = (kept[0:1] + kept[1:2])[:, : TAIL_LINES * LANES]
                heads[here, :] = (kept[2:3] + kept[3:4])[:, : HEAD_LINES * LANES]
                for line in range(2):
                    edge = kept[4 + 2 * line : 5 + 2 * line] * DIGIT + kept[5 + 2 * line : 6 + 2 * line]
                    edges[line, here, :] = edge[:, :LANES]
                slot += 1
        for slot, (slot_tm, slot_mp) in enumerate(places):
            following = slot_tm(time_index) * parts + (model_index ^ slot_mp) + 1
            found = slot_of(places, following // parts, lax.rem(following, parts))
            taken = heads[pl.ds(found, 1), :]
            nexts[slot : slot + 1, :] = jnp.where(following > final, 0.0, taken)
        line = jnp.concatenate([tails[...], nexts[...]], axis=1)
        windows = []
        for sub in range(SUB - 2, SUB):
            skip, lane = divmod(sub * HOP - (FRAME_ROWS - TAIL_LINES) * LANES, LANES)
            windows.append(
                pltpu.roll(line[:, skip * LANES : skip * LANES + WIDE], WIDE - lane, axis=1)
            )
        mel = log_mel(jnp.concatenate(windows, axis=0), tables_ref).astype(jnp.bfloat16)
        for number in range(2):
            lane = number * NMEL
            out[:, lane : lane + NMEL] = mel[number * rows : (number + 1) * rows]
        left = slot_of(places, time_index - 1, model_index)
        right = slot_of(places, time_index + 1, model_index)
        for number, ref in enumerate((start_ref, end_ref)):
            bounds[number : number + 1, :] = jnp.concatenate(
                [
                    edges[number, pl.ds(left, 1), :][:, HALO : 2 * HALO],
                    ref[...].astype(jnp.float32),
                    edges[number, pl.ds(right, 1), :][:, 0:HALO],
                ],
                axis=1,
            )

    return call(
        kernel,
        (
            jax.ShapeDtypeStruct((rows, 2 * NMEL), jnp.bfloat16),
            jax.ShapeDtypeStruct((2, frames_shard + 2 * HALO), jnp.float32),
        ),
        (starts, ends, *stacks, tables),
        scratch=[
            pltpu.VMEM((rows, TAIL_LINES * LANES), jnp.float32),
            pltpu.VMEM((rows, HEAD_LINES * LANES), jnp.float32),
            pltpu.VMEM((rows, HEAD_LINES * LANES), jnp.float32),
            pltpu.VMEM((2, rows, LANES), jnp.float32),
        ],
        micros=0.9,
    )


def last_rows(stack_refs, counts, frames_local, fixed, rows):
    lasts = []
    for stack_ref, count in zip(stack_refs, counts):
        for block in range(count):
            kept = stack_ref[block, frames_local - HALO : frames_local, 0 : 2 * NMEL]
            lasts.append(kept.astype(jnp.float32)[HALO - 1 : HALO])
    if len(lasts) < rows:
        lasts.append(jnp.zeros((rows - len(lasts), 2 * NMEL), jnp.float32))
    return jnp.concatenate([jnp.concatenate(lasts, axis=0).astype(jnp.bfloat16), fixed], axis=1)


def patch(held, fixed, slots, frames_local):
    fixed = fixed.astype(jnp.float32)
    for slot in range(slots):
        here = slice((slot + 1) * frames_local - HALO, (slot + 1) * frames_local)
        kept = held[here, :].astype(jnp.float32)
        last = lax.broadcasted_iota(jnp.int32, kept.shape, 0) == HALO - 1
        held[here, :] = jnp.where(last, fixed[slot : slot + 1, :], kept).astype(held.dtype)


def assemble(parts, after=()):
    counts = [part.shape[0] for part in parts]

    def kernel(*refs):
        begin = 0
        for ref, count in zip(refs, counts):
            refs[-1][begin : begin + count] = ref[...]
            begin += count

    shape = jax.ShapeDtypeStruct((sum(counts), *parts[0].shape[1:]), parts[0].dtype)
    return call(kernel, shape, (*parts, *after))


def project_rows(stack, w_subsample, w_attention, frames_local, every=(), fixed=None):
    count = stack.shape[0]
    rows, width = count * frames_local, w_attention.shape[2]
    model = w_subsample.shape[1]
    counts = [block.shape[0] for block in every]
    sizes = [rows] if fixed is None else [rows, fixed.shape[0]]

    def kernel(stack_ref, w_sub, w_att, *refs):
        stack_rows = [stack_ref[block, 0:frames_local, :] for block in range(count)]
        if fixed is not None:
            every_refs, fixed_ref, refs = refs[: len(every)], refs[len(every)], refs[len(every) + 1 :]
            stack_rows.append(
                last_rows(every_refs, counts, frames_local, fixed_ref[...], sizes[1])
            )
        features = dot32(jnp.concatenate(stack_rows, axis=0), w_sub[...]).astype(jnp.bfloat16)
        normed = normalize(features.astype(jnp.float32)).astype(jnp.bfloat16)
        for part in range(3):
            projected = dot32(normed, w_att[part]).astype(jnp.bfloat16)
            begin = 0
            for number, size in enumerate(sizes):
                refs[3 * number + part][...] = projected[begin : begin + size]
                begin += size

    return call(
        kernel,
        [jax.ShapeDtypeStruct((size, width), jnp.bfloat16) for size in sizes for _ in range(3)],
        (stack, w_subsample, w_attention) + (() if fixed is None else (*every, fixed)),
        micros=0.5 + 0.007 * sum(sizes),
    )


def slot_of(places, tm, mp):
    found = jnp.int32(0)
    for slot, (slot_tm, slot_mp) in enumerate(places):
        here = (slot_tm(lax.axis_index("tm")) == tm) & (lax.axis_index("mp") ^ slot_mp == mp)
        found = jnp.where(here, slot, found)
    return found


def gather_rows(places, bounds, queries, keys, values, fixed, frames_local, window, outs):
    q_rows, k_all, v_all, q_all, first, last = outs
    parts = lax.axis_size("mp")
    frames_shard = frames_local * parts
    for held, sources, fixed_ref in zip((q_all, k_all, v_all), (queries, keys, values), fixed):
        begin = 0
        for source in sources:
            held[begin : begin + source.shape[0], :] = source[...]
            begin += source.shape[0]
        patch(held, fixed_ref[...], len(places), frames_local)
    time_index = lax.axis_index("tm")

    def source(tm, mp, offset, count):
        start = pl.multiple_of(slot_of(places, tm, mp) * frames_local + offset, HALO)
        return q_all[pl.ds(start, count), :]

    q_rows[0:HALO, :] = source(time_index - 1, parts - 1, frames_local - HALO, HALO)
    for part in range(parts):
        begin = HALO + part * frames_local
        q_rows[begin : begin + frames_local, :] = source(time_index, part, 0, frames_local)
    q_rows[HALO + frames_shard :, :] = source(time_index + 1, 0, 0, HALO)
    for line, ref in enumerate((first, last)):
        row = bounds[line : line + 1, :]
        ref[...] = jnp.transpose(jnp.broadcast_to(row, (LANES, row.shape[1])))


def attend_rows(places, begin, q_rows, k_all, v_all, first, last, frames_local, result, bias):
    count, width = result.shape
    rows = k_all.shape[0]
    time_index, model_index = lax.axis_index("tm"), lax.axis_index("mp")
    frames_shard = frames_local * lax.axis_size("mp")
    lows, highs = first[pl.ds(begin, count), :], last[pl.ds(begin, count), :]
    lanes = lax.broadcasted_iota(jnp.int32, (1, LANES), 1)
    for lane in range(0, rows, LANES):
        at = jnp.zeros((1, LANES), jnp.int32)
        for slot in range(lane // frames_local, -(-(lane + LANES) // frames_local)):
            if slot < len(places):
                slot_tm, slot_mp = places[slot]
                base = slot_tm(time_index) * frames_shard
                base += (model_index ^ slot_mp) * frames_local - slot * frames_local + lane
                at = jnp.where(lanes >= slot * frames_local - lane, lanes + base, at)
        at = at.astype(jnp.float32)
        bias[:, lane : lane + LANES] = jnp.where((at >= lows) & (at < highs), 0.0, -1e30)
    for lane in range(0, width, LANES):
        span = min(LANES, width - lane)
        q_pair = q_rows[pl.ds(begin, count), lane : lane + span]
        k_pair = k_all[:, lane : lane + span]
        v_pair = v_all[:, lane : lane + span]
        head_of = lax.broadcasted_iota(jnp.int32, (count, span), 1) // HD
        merged = jnp.zeros((count, span), jnp.float32)
        for head in range(span // HD):
            mine = head_of == head
            q_head = jnp.where(mine, q_pair, jnp.zeros_like(q_pair)) * jnp.bfloat16(
                1.0 / math.sqrt(HD)
            )
            scores = lax.dot_general(
                q_head, k_pair, (((1,), (1,)), ((), ())), preferred_element_type=jnp.float32
            )
            scores = scores + bias[...]
            weights = jnp.exp(scores - jnp.max(scores, axis=1, keepdims=True))
            total = jnp.sum(weights, axis=1, keepdims=True)
            numerator = dot32(weights.astype(jnp.bfloat16), v_pair)
            merged = jnp.where(mine, numerator / total, merged)
        result[:, lane : lane + span] = merged.astype(jnp.bfloat16)


def split_pair(model_index, result, mine, other, frames_local):
    window = mine.shape[0]
    place = lax.rem(model_index, 2) * frames_local
    mine[...] = result[pl.ds(pl.multiple_of(place, HALO), window), :]
    place = frames_local - place
    other[...] = result[pl.ds(pl.multiple_of(place, HALO), window), :]


def attend_far(places, far, bounds, queries, keys, values, fixed, frames_local):
    counts = [q.shape[0] for q in queries]
    rows, width = sum(counts), queries[0].shape[1]
    groups = len(counts)
    extended = frames_local * lax.axis_size("mp") + 2 * HALO
    window = frames_local + 2 * HALO
    pair = 2 * frames_local + 2 * HALO

    def kernel(bound_ref, *refs):
        sources, refs = refs[: 3 * groups], refs[3 * groups :]
        fixed_refs, refs = refs[:3], refs[3:]
        windows, refs = refs[: 2 * len(far)], refs[2 * len(far) :]
        q_rows, k_all, v_all, first, last, q_all, result, bias = refs
        gather_rows(
            places,
            bound_ref,
            sources[:groups],
            sources[groups : 2 * groups],
            sources[2 * groups :],
            fixed_refs,
            frames_local,
            window,
            (q_rows, k_all, v_all, q_all, first, last),
        )
        model_index = lax.axis_index("mp")
        for number, bit in enumerate(far):
            begin = pl.multiple_of((model_index ^ bit) // 2 * (2 * frames_local), HALO)
            attend_rows(
                places, begin, q_rows, k_all, v_all, first, last, frames_local, result, bias
            )
            split_pair(
                model_index, result, windows[2 * number], windows[2 * number + 1], frames_local
            )

    def shape(count, wide=width, dtype=jnp.bfloat16):
        return jax.ShapeDtypeStruct((count, wide), dtype)

    return call(
        kernel,
        [shape(window)] * (2 * len(far))
        + [shape(extended), shape(rows), shape(rows)]
        + [shape(extended, LANES, jnp.float32)] * 2,
        (bounds, *queries, *keys, *values, *fixed),
        scratch=[
            pltpu.VMEM((rows, width), jnp.bfloat16),
            pltpu.VMEM((pair, width), jnp.bfloat16),
            pltpu.VMEM((pair, rows), jnp.float32),
        ],
        micros=2.5 * len(far),
        vmem=16 + pair * rows * 20 // 1024 // 1024,
    )


def attend_near(places, after, q_rows, k_all, v_all, first, last, frames_local):
    rows, width = k_all.shape
    window = frames_local + 2 * HALO
    pair = 2 * frames_local + 2 * HALO

    def kernel(_, q_ref, k_ref, v_ref, first_ref, last_ref, mine, other, result, bias):
        model_index = lax.axis_index("mp")
        begin = pl.multiple_of(model_index // 2 * (2 * frames_local), HALO)
        attend_rows(
            places, begin, q_ref, k_ref, v_ref, first_ref, last_ref, frames_local, result, bias
        )
        split_pair(model_index, result, mine, other, frames_local)

    return call(
        kernel,
        [jax.ShapeDtypeStruct((window, width), jnp.bfloat16)] * 2,
        (after, q_rows, k_all, v_all, first, last),
        scratch=[
            pltpu.VMEM((pair, width), jnp.bfloat16),
            pltpu.VMEM((pair, rows), jnp.float32),
        ],
        micros=2.0,
        vmem=16 + pair * rows * 20 // 1024 // 1024,
    )


def far_branch(windows, w_rows):
    count = len(windows) // 2

    def kernel(*refs):
        windows, (w_own, w_near), outs = refs[: 2 * count], refs[2 * count :][:2], refs[-count:]
        for number in range(count):
            own, near = windows[2 * number : 2 * number + 2]
            share = dot32(own[...], w_own[...]) + dot32(near[...], w_near[...])
            outs[number][...] = share.astype(jnp.bfloat16)

    shape = jax.ShapeDtypeStruct((windows[0].shape[0], w_rows[0].shape[1]), jnp.bfloat16)
    return call(kernel, [shape] * count, (*windows, *w_rows), micros=0.9 * count)


def near_branch(places, windows, w_rows, stacks, fixed, w_subsample, frames_local):
    counts = [stack.shape[0] for stack in stacks]
    depth, model = w_subsample.shape
    window = frames_local + 2 * HALO
    slots = len(places)

    def kernel(own, near, w_own, w_near, *refs):
        stack_refs, (fixed_ref, w_sub, out, held, taken) = refs[: len(counts)], refs[len(counts) :]
        begin = 0
        for stack_ref, count in zip(stack_refs, counts):
            for block in range(count):
                held[begin : begin + frames_local, :] = stack_ref[block, 0:frames_local, :]
                begin += frames_local
        rows = last_rows(stack_refs, counts, frames_local, fixed_ref[...], fixed.shape[0])
        patch(held, rows, slots, frames_local)
        parts = lax.axis_size("mp")
        block = lax.axis_index("tm") * parts + lax.axis_index("mp") + parts

        def source(number, offset, count):
            slot = slot_of(places, number // parts - 1, lax.rem(number, parts))
            start = pl.multiple_of(slot * frames_local + offset, HALO)
            return held[pl.ds(start, count), :]

        taken[0:HALO, :] = source(block - 1, frames_local - HALO, HALO)
        taken[HALO : HALO + frames_local, :] = source(block, 0, frames_local)
        taken[HALO + frames_local : window, :] = source(block + 1, 0, HALO)
        features = dot32(taken[...], w_sub[...]).astype(jnp.bfloat16).astype(jnp.float32)
        share = dot32(own[...], w_own[...]) + dot32(near[...], w_near[...])
        out[...] = features + share

    return call(
        kernel,
        jax.ShapeDtypeStruct((window, model), jnp.float32),
        (*windows, *w_rows, *stacks, fixed, w_subsample),
        scratch=[
            pltpu.VMEM((slots * frames_local, depth), jnp.bfloat16),
            pltpu.VMEM((window, depth), jnp.bfloat16),
        ],
        micros=1.2,
    )


def finish_rows(base, shares, gain, taps, frames_local):
    count = len(shares)
    parts = lax.axis_size("mp")
    window, model = base.shape
    chunk = 2 * LANES
    offset = HALO - KERNEL // 2

    def kernel(base_ref, *refs):
        share_refs, (gain_ref, tap_ref, out, held, mixed_rows) = refs[:count], refs[count:]
        mixed = base_ref[...]
        for share_ref in share_refs:
            mixed += share_ref[...].astype(jnp.float32)
        mixed = mixed.astype(jnp.bfloat16).astype(jnp.float32)
        mixed_rows[...] = mixed[HALO : HALO + frames_local]
        conv_in = (normalize(mixed) * gain_ref[...]).astype(jnp.bfloat16).astype(jnp.float32)
        held[HALO : HALO + frames_local, :] = conv_in[HALO : HALO + frames_local]
        block = lax.axis_index("tm") * parts + lax.axis_index("mp")
        before = block > 0
        held[0:HALO, :] = jnp.where(before, conv_in[0:HALO], 0.0)
        after = block < lax.axis_size("tm") * parts - 1
        held[HALO + frames_local : window, :] = jnp.where(after, conv_in[HALO + frames_local :], 0.0)
        for lane in range(0, model, chunk):
            here = slice(lane, lane + chunk)
            total = jnp.zeros((frames_local, chunk), jnp.float32)
            tap_rows = tap_ref[:, here].astype(jnp.float32)
            for phase in range(8):
                taken = [tap for tap in range(KERNEL) if (tap + offset) % 8 == phase]
                reach = (taken[-1] + offset) // 8 * 8 + frames_local
                moved = held[pl.ds(phase, reach), here]
                for tap in taken:
                    begin = (tap + offset) // 8 * 8
                    total += moved[begin : begin + frames_local] * tap_rows[tap : tap + 1]
            silu = total / (1.0 + jnp.exp(-total))
            out[:, here] = (mixed_rows[:, here] + silu).astype(jnp.bfloat16)

    return call(
        kernel,
        jax.ShapeDtypeStruct((frames_local, model), jnp.bfloat16),
        (base, *shares, gain, taps),
        scratch=[
            pltpu.VMEM((window, model), jnp.float32),
            pltpu.VMEM((frames_local, model), jnp.float32),
        ],
        micros=2.8,
    )


def exchange(block, axis, bit):
    return lax.ppermute(block, axis, [(i, i ^ bit) for i in range(lax.axis_size(axis))])


def shifted(block, axis, distance):
    count = lax.axis_size(axis)
    route = [(i - distance, i) for i in range(count) if 0 <= i - distance < count]
    return lax.ppermute(block, axis, route)


def shards(
    waveform,
    segment_start,
    segment_end,
    w_subsample,
    w_attention,
    w_output,
    gain_convolution,
    w_depthwise,
):
    frames_local = waveform.shape[0] // (SUB * HOP)
    frames_shard = segment_start.shape[0]
    parts, shards_total = lax.axis_size("mp"), lax.axis_size("tm")
    bits = [1 << b for b in reversed(range((parts - 1).bit_length()))]

    samples = waveform.reshape(-1, LANES)
    starts, ends = segment_start[None, :], segment_end[None, :]
    tables = jnp.asarray(front_tables())
    stacked = log_mel_rows(starts, ends, samples, tables, frames_local)
    w_subsample, w_attention = fetch(stacked, (w_subsample, w_attention))

    w_near = exchange(w_output, "mp", bits[-1])

    reach = min((SEG_MAX + HALO - 2) // frames_shard + 1, shards_total - 1)
    whole = reach == shards_total - 1 and shards_total & (shards_total - 1) == 0
    if whole:
        moves = [lambda tm, bit=bit: tm ^ bit for bit in range(1, shards_total)]
        column = [exchange(stacked, "tm", bit) for bit in range(1, shards_total)]
    else:
        steps = [sign * d for d in range(1, reach + 1) for sign in (1, -1)]
        moves = [lambda tm, step=step: tm - step for step in steps]
        column = [shifted(stacked, "tm", step) for step in steps]
    early = [(stacked, [(lambda tm: tm, 0)])]
    late = [(assemble(column, (w_subsample,)), [(move, 0) for move in moves])]

    def across(blocks, bit):
        return [
            (exchange(block, "mp", bit), [(move, mp ^ bit) for move, mp in held])
            for block, held in blocks
        ]

    for bit in bits[:-1]:
        early, late = early + across(early, bit), late + across(late, bit)
    ready = early + late[:1]
    joined = (assemble([block for block, _ in ready]), sum([held for _, held in ready], []))
    groups = [joined] + across([joined], bits[-1]) + late[1:] + across(late[1:], bits[-1])
    stacks, held = zip(*groups)
    places = sum(held, [])
    projected = [
        project_rows(block, w_subsample, w_attention, frames_local) for block in stacks[:-1]
    ]
    fixed, bounds = boundary_rows(places, starts, ends, stacks, tables, frames_local)
    *outs, fixed_query, fixed_key, fixed_value = project_rows(
        stacks[-1], w_subsample, w_attention, frames_local, stacks, fixed
    )
    queries, keys, values = zip(*projected, outs)
    fixed_rows = (fixed_query, fixed_key, fixed_value)

    far = list(range(2, parts, 2))
    outs = attend_far(places, far, bounds, queries, keys, values, fixed_rows, frames_local)
    windows, shared = outs[: 2 * len(far)], outs[2 * len(far) :]
    windows = [
        exchange(block, "mp", 1) if number % 2 else block for number, block in enumerate(windows)
    ]
    w_rows = (w_output, w_near)
    shares = far_branch(windows, w_rows)
    mine, other = attend_near(places, shares[0], *shared, frames_local)
    shares = [exchange(share, "mp", bit) for share, bit in zip(shares, far)]
    base = near_branch(
        places, (mine, exchange(other, "mp", 1)), w_rows, stacks, fixed, w_subsample, frames_local
    )
    return finish_rows(base, shares, gain_convolution[None, :], w_depthwise, frames_local)


def solution(mesh):
    placed = (
        P(("groups", "tm", "mp")),
        P(("groups", "tm")),
        P(("groups", "tm")),
        P(),
        P(None, None, "mp"),
        P("mp", None),
        P(),
        P(),
    )
    return jax.shard_map(
        shards,
        mesh=mesh,
        in_specs=placed,
        out_specs=P(("groups", "tm", "mp"), None),
        check_vma=False,
    )
```

time: 53 us -> 46.9 us (0.88)
  starting transfers between devices: 15.1 us -> 11.3 us
  Pallas kernels: 22.5 us -> 21.1 us
  waiting for transfers between devices: 10.4 us -> 9.21 us
  local copies, waits for them, and re-layouts: 4.33 us -> 4.99 us
    ppermute x3 -> x0, starting transfers between devices: 3.62 us -> none  [spread_piece(): pieces.append(lax.ppermute(piece, tuple(axes), route))]
    ppermute x3 -> x0, waiting for transfers between devices: 2.27 us -> none  [spread_piece(): pieces.append(lax.ppermute(piece, tuple(axes), route))]
    pallas_call x12 -> x14, Pallas kernels: 22.5 us -> 21.1 us  [call(): pl.pallas_call(kernel, out_shape=out_shape, in_specs=specs, out_specs=jax...]
    ppermute x13 -> x11, waiting for transfers between devices: 8.12 us -> 9.21 us  [exchange(): lax.ppermute(block, axis, [(i, i ^ bit) for i in range(lax.axis_size(axis...]
    unnamed x24, local copies, waits for them, and re-layouts: 4.32 us -> 4.99 us
    ppermute x13 -> x11, starting transfers between devices: 11.5 us -> 11.3 us  [exchange(): lax.ppermute(block, axis, [(i, i ^ bit) for i in range(lax.axis_size(axis...]
  transfers between devices with their start and end apart: 16 -> 11, of which waited for: 6 -> 6; matrix products, arithmetic and copies ran while one was open for 0% -> 0% of each run, Pallas kernels for 28% -> 36%
where the time goes in v3:
time: 46.9 us; the launch traced here: 46.7 us
  Pallas kernels  21.1 us (45%)
  starting transfers between devices  11.3 us (24%)
  waiting for transfers between devices  9.21 us (20%)
  local copies, waits for them, and re-layouts  4.99 us (11%)
    pallas_call x14, Pallas kernels, call(): pl.pallas_call(kernel, out_shape=out_shape, in_specs=specs, out_specs=jax...  21.1 us
    ppermute x11, starting transfers between devices, exchange(): lax.ppermute(block, axis, [(i, i ^ bit) for i in range(lax.axis_size(axis...  11.3 us
    ppermute x11, waiting for transfers between devices, exchange(): lax.ppermute(block, axis, [(i, i ^ bit) for i in range(lax.axis_size(axis...  9.21 us
    unnamed x24, local copies, waits for them, and re-layouts  4.99 us
  transfers between devices with their start and end apart: 11, of which 6 were waited for; matrix products, arithmetic and copies ran while one was open for 0% of the time, Pallas kernels for 36%

profile of v3, /device:TPU:0, one launch (start us, length us, event | category | flops | bytes accessed | tf_op | source)
XLA Modules:
  0.0 46.7 jit_solution(11397514521968137912)
XLA Ops:
  0.0 0.9 %copy-done.3 = f32[40960]{0:T(1024)S(1)} copy-done((f32[40960]{0:T(1024)S(1)}, f32[40960]{0:T(1024)}, u32[]{:S(2)}) %copy-start.3) | copy-done | bytes 163864
  0.9 0.7 %copy-done.5 = s32[256]{0:T(256)S(1)} copy-done((s32[256]{0:T(256)S(1)}, s32[256]{0:T(256)}, u32[]{:S(2)}) %copy-start.5) | copy-done | bytes 1048
  1.6 0.7 %copy-done.7 = s32[256]{0:T(256)S(1)} copy-done((s32[256]{0:T(256)S(1)}, s32[256]{0:T(256)}, u32[]{:S(2)}) %copy-start.7) | copy-done | bytes 1048
  2.3 1.3 %copy-done.9 = bf16[512,1152]{1,0:T(8,128)(2,1)S(1)} copy-done((bf16[512,1152]{1,0:T(8,128)(2,1)S(1)}, bf16[512,1152]{1,0:T(8,128)(2,1)}, u32[]{:S(2)}) %copy-start.9) | copy-done | bytes 1179672
  3.5 0.9 %shard_map.91._.refs_0_ = bf16[1,72,512]{2,1,0:T(8,128)(2,1)S(1)} custom-call(s32[1,256]{1,0:T(1,128)S(1)} %bitcast.4, s32[1,256]{1,0:T(1,128)S(1)} %bitcast.6, f32[320,128]{1,0:T(8,128)S(1)} %bitcast.3, bf16[512,1152]{1,0:T(8,128)(2,1)S(1)} %copy-done.9), custom_call_target="tpu_custom_call" | custom-call | flops 1000000000 | bytes 1000000 | tf_op jit(solution)/shard_map/pallas_call | solution.py:85
  4.4 3.1 %collective-permute-start.1 = (bf16[1,72,512]{2,1,0:T(8,128)(2,1)S(1)}, bf16[1,72,512]{2,1,0:T(8,128)(2,1)S(1)}, u32[]{:S(2)}, u32[]{:S(2)}) collective-permute-start(bf16[1,72,512]{2,1,0:T(8,128)(2,1)S(1)} %shard_map.91._.refs_0_), channel_id=1, source_target_pairs={{0,4},{4,0},{8,12},{12,8},{1,5},{5,1},{9,13},{13,9},{2,6},{6,2},{1... | collective-permute-start | bytes 221192 | tf_op jit(solution)/shard_map/ppermute | solution.py:570
  7.5 2.6 %collective-permute-start.2 = (bf16[1,72,512]{2,1,0:T(8,128)(2,1)S(1)}, bf16[1,72,512]{2,1,0:T(8,128)(2,1)S(1)}, u32[]{:S(2)}, u32[]{:S(2)}) collective-permute-start(bf16[1,72,512]{2,1,0:T(8,128)(2,1)S(1)} %shard_map.91._.refs_0_), channel_id=1, source_target_pairs={{0,8},{4,12},{8,0},{12,4},{1,9},{5,13},{9,1},{13,5},{2,10},{6,14},... | collective-permute-start | bytes 221192 | tf_op jit(solution)/shard_map/ppermute | solution.py:570
  10.1 0.0 collective-permute-start.3
  10.1 1.7 %collective-permute-start = (bf16[1,72,512]{2,1,0:T(8,128)(2,1)S(1)}, bf16[1,72,512]{2,1,0:T(8,128)(2,1)S(1)}, u32[]{:S(2)}, u32[]{:S(2)}) collective-permute-start(bf16[1,72,512]{2,1,0:T(8,128)(2,1)S(1)} %shard_map.91._.refs_0_), channel_id=1, source_target_pairs={{0,2},{1,3},{2,0},{3,1},{4,6},{5,7},{6,4},{7,5},{8,10},{9,11},{10,... | collective-permute-start | bytes 221192 | tf_op jit(solution)/shard_map/ppermute | solution.py:570
  11.8 0.0 collective-permute-start.8
  11.8 0.0 copy-done
  11.8 1.4 %copy-done.1 = bf16[512,1536]{1,0:T(8,128)(2,1)S(1)} copy-done((bf16[512,1536]{1,0:T(8,128)(2,1)S(1)}, bf16[512,1536]{1,0:T(8,128)(2,1)}, u32[]{:S(2)}) %copy-start.1) | copy-done | bytes 1572888
  13.2 0.5 %shard_map.92 = (bf16[512,1536]{1,0:T(8,128)(2,1)S(1)}, bf16[3,1536,384]{2,1,0:T(8,128)(2,1)S(1)}) custom-call(bf16[1,72,512]{2,1,0:T(8,128)(2,1)S(1)} %shard_map.91._.refs_0_, bf16[512,1536]{1,0:T(8,128)(2,1)S(1)} %copy-done.1, bf16[3,1536,384]{2,1,0:T(8,128)(2,1)S(1)} %copy-done), custom_call_target="tpu_custom_call" | custom-call | flops 1000000000 | bytes 1000000 | tf_op jit(solution)/shard_map/pallas_call | solution.py:85
  13.8 0.0 collective-permute-done.1.refs_0_
  13.8 1.5 %collective-permute-done.2.refs_1_ = bf16[1,72,512]{2,1,0:T(8,128)(2,1)S(1)} collective-permute-done((bf16[1,72,512]{2,1,0:T(8,128)(2,1)S(1)}, bf16[1,72,512]{2,1,0:T(8,128)(2,1)S(1)}, u32[]{:S(2)}, u32[]{:S(2)}) %collective-permute-start.2) | collective-permute-done | bytes 73760 | tf_op jit(solution)/shard_map/ppermute | solution.py:570
  15.3 1.1 %collective-permute-done.3.refs_2_ = bf16[1,72,512]{2,1,0:T(8,128)(2,1)S(1)} collective-permute-done((bf16[1,72,512]{2,1,0:T(8,128)(2,1)S(1)}, bf16[1,72,512]{2,1,0:T(8,128)(2,1)S(1)}, u32[]{:S(2)}, u32[]{:S(2)}) %collective-permute-start.3) | collective-permute-done | bytes 73760 | tf_op jit(solution)/shard_map/ppermute | solution.py:570
  16.4 1.6 %collective-permute-start.5 = (bf16[3,72,512]{2,1,0:T(8,128)(2,1)S(1)}, bf16[3,72,512]{2,1,0:T(8,128)(2,1)S(1)}, u32[]{:S(2)}, u32[]{:S(2)}) collective-permute-start(bf16[3,72,512]{2,1,0:T(8,128)(2,1)S(1)} %shard_map.93.refs_2_), channel_id=1, source_target_pairs={{0,2},{1,3},{2,0},{3,1},{4,6},{5,7},{6,4},{7,5},{8,10},{9,11},{10,... | collective-permute-start | bytes 663560 | tf_op jit(solution)/shard_map/ppermute | solution.py:570
  18.0 0.0 collective-permute-done.refs_1_
  18.0 0.1 collective-permute-start.4
  18.1 2.7 %shard_map.96 = (bf16[320,384]{1,0:T(8,128)(2,1)S(1)}, bf16[320,384]{1,0:T(8,128)(2,1)S(1)}, bf16[320,384]{1,0:T(8,128)(2,1)S(1)}) custom-call(bf16[5,72,512]{2,1,0:T(8,128)(2,1)S(1)} %shard_map.94.refs_0_.stack_ref, bf16[512,1536]{1,0:T(8,128)(2,1)S(1)} %get-tuple-element.33.refs_3_.w_sub.refs_5_, bf16[3,1536,384]{2,1,0:T(8,128)(2,1)S(1)} %get-tuple-element.35.w_att), custom_call_target="tpu_custom_call" | custom-call | flops 2740000000 | bytes 1000000 | tf_op jit(solution)/shard_map/pallas_call | solution.py:85
  20.8 1.6 %collective-permute-done.5.refs_2_.stack_ref = bf16[3,72,512]{2,1,0:T(8,128)(2,1)S(1)} collective-permute-done((bf16[3,72,512]{2,1,0:T(8,128)(2,1)S(1)}, bf16[3,72,512]{2,1,0:T(8,128)(2,1)S(1)}, u32[]{:S(2)}, u32[]{:S(2)}) %collective-permute-start.5) | collective-permute-done | bytes 221216 | tf_op jit(solution)/shard_map/ppermute | solution.py:570
  22.4 0.0 collective-permute-start.6
  22.4 1.8 %shard_map.98 = (bf16[192,384]{1,0:T(8,128)(2,1)S(1)}, bf16[192,384]{1,0:T(8,128)(2,1)S(1)}, bf16[192,384]{1,0:T(8,128)(2,1)S(1)}) custom-call(bf16[3,72,512]{2,1,0:T(8,128)(2,1)S(1)} %collective-permute-done.5.refs_2_.stack_ref, bf16[512,1536]{1,0:T(8,128)(2,1)S(1)} %get-tuple-element.33.refs_3_.w_sub.refs_5_, bf16[3,1536,384]{2,1,0:T(8,128)(2,1)S(1)} %get-tuple-element.35.w_att), custom_call_target="tpu_custom_call" | custom-call | flops 1844000000 | bytes 1000000 | tf_op jit(solution)/shard_map/pallas_call | solution.py:85
  24.2 0.0 copy-start.6
  24.2 0.0 copy-start.8
  24.3 0.0 copy-start.10
  24.3 0.0 collective-permute-done.4.refs_1_.stack_ref
  24.3 2.7 %shard_map.97 = (bf16[320,384]{1,0:T(8,128)(2,1)S(1)}, bf16[320,384]{1,0:T(8,128)(2,1)S(1)}, bf16[320,384]{1,0:T(8,128)(2,1)S(1)}) custom-call(bf16[5,72,512]{2,1,0:T(8,128)(2,1)S(1)} %collective-permute-done.4.refs_1_.stack_ref, bf16[512,1536]{1,0:T(8,128)(2,1)S(1)} %get-tuple-element.33.refs_3_.w_sub.refs_5_, bf16[3,1536,384]{2,1,0:T(8,128)(2,1)S(1)} %get-tuple-element.35.w_att), custom_call_target="tpu_custom_call" | custom-call | flops 2740000000 | bytes 1000000 | tf_op jit(solution)/shard_map/pallas_call | solution.py:85
  27.0 0.0 collective-permute-done.6.refs_3_.stack_ref
  27.0 0.0 copy-done.6
  27.0 0.0 copy-done.8
  27.0 0.0 copy-done.10
  27.0 0.8 %shard_map.95 = (bf16[16,256]{1,0:T(8,128)(2,1)S(1)}, f32[2,288]{1,0:T(2,128)S(1)}) custom-call(s32[1,256]{1,0:T(1,128)S(1)} %bitcast.5, s32[1,256]{1,0:T(1,128)S(1)} %bitcast.7, bf16[5,72,512]{2,1,0:T(8,128)(2,1)S(1)} %shard_map.94.refs_0_.stack_ref, bf16[5,72,512]{2,1,0:T(8,128)(2,1)S(1)} %collective-permute-done.4.refs_1_.stack_ref, ...), custom_call_target="tpu_custom_call" | custom-call | flops 900000000 | bytes 1000000 | tf_op jit(solution)/shard_map/pallas_call | solution.py:85
  27.9 1.9 %shard_map.99 = (bf16[192,384]{1,0:T(8,128)(2,1)S(1)}, bf16[192,384]{1,0:T(8,128)(2,1)S(1)}, bf16[192,384]{1,0:T(8,128)(2,1)S(1)}, bf16[16,384]{1,0:T(8,128)(2,1...) custom-call(bf16[3,72,512]{2,1,0:T(8,128)(2,1)S(1)} %collective-permute-done.6.refs_3_.stack_ref, ...), custom_call_target="tpu_custom_call" | custom-call | flops 1956000000 | bytes 1000000 | tf_op jit(solution)/shard_map/pallas_call | solution.py:85
  29.8 0.0 copy-start.2
  29.8 2.8 %shard_map.100 = (bf16[96,384]{1,0:T(8,128)(2,1)S(1)}, bf16[96,384]{1,0:T(8,128)(2,1)S(1)}, bf16[288,384]{1,0:T(8,128)(2,1)S(1)}, bf16[1024,384]{1,0:T(8,128)(2,...) custom-call(f32[2,288]{1,0:T(2,128)S(1)} %get-tuple-element.34.bound_ref, ...), custom_call_target="tpu_custom_call" | custom-call | flops 2500000000 | bytes 1000000 | tf_op jit(solution)/shard_map/pallas_call | solution.py:85
  32.6 0.6 %collective-permute-start.7 = (bf16[96,384]{1,0:T(8,128)(2,1)S(1)}, bf16[96,384]{1,0:T(8,128)(2,1)S(1)}, u32[]{:S(2)}, u32[]{:S(2)}) collective-permute-start(bf16[96,384]{1,0:T(8,128)(2,1)S(1)} %get-tuple-element.53), channel_id=1, source_target_pairs={{0,1},{1,0},{2,3},{3,2},{4,5},{5,4},{6,7},{7,6},{8,9},{9,8},{10,11... | collective-permute-start | bytes 221192 | tf_op jit(solution)/shard_map/ppermute | solution.py:570
  33.2 0.9 %collective-permute-done.7.refs_1_ = bf16[96,384]{1,0:T(8,128)(2,1)S(1)} collective-permute-done((bf16[96,384]{1,0:T(8,128)(2,1)S(1)}, bf16[96,384]{1,0:T(8,128)(2,1)S(1)}, u32[]{:S(2)}, u32[]{:S(2)}) %collective-permute-start.7) | collective-permute-done | bytes 73760 | tf_op jit(solution)/shard_map/ppermute | solution.py:570
  34.1 0.0 collective-permute-done.8.refs_3_.w_near
  34.1 0.6 %shard_map.101._ = bf16[96,1536]{1,0:T(8,128)(2,1)S(1)} custom-call(bf16[96,384]{1,0:T(8,128)(2,1)S(1)} %get-tuple-element.52.refs_0_, bf16[96,384]{1,0:T(8,128)(2,1)S(1)} %collective-permute-done.7.refs_1_, bf16[384,1536]{1,0:T(8,128)(2,1)S(1)} %copy-done.2, bf16[384,1536]{1,0:T(8,128)(2,1)S(1)} %collective-permute-done.8.refs_3_.w_near), custom_call_target="tpu_custom_call" | custom-call | flops 900000000 | bytes 1000000 | tf_op jit(solution)/shard_map/pallas_call | solution.py:85
  34.7 1.6 %collective-permute-start.10 = (bf16[96,1536]{1,0:T(8,128)(2,1)S(1)}, bf16[96,1536]{1,0:T(8,128)(2,1)S(1)}, u32[]{:S(2)}, u32[]{:S(2)}) collective-permute-start(bf16[96,1536]{1,0:T(8,128)(2,1)S(1)} %shard_map.101._), channel_id=1, source_target_pairs={{0,2},{1,3},{2,0},{3,1},{4,6},{5,7},{6,4},{7,5},{8,10},{9,11},{10,... | collective-permute-start | bytes 884744 | tf_op jit(solution)/shard_map/ppermute | solution.py:570
  36.2 2.7 %shard_map.102 = (bf16[96,384]{1,0:T(8,128)(2,1)S(1)}, bf16[96,384]{1,0:T(8,128)(2,1)S(1)}) custom-call(bf16[96,1536]{1,0:T(8,128)(2,1)S(1)} %shard_map.101._, bf16[288,384]{1,0:T(8,128)(2,1)S(1)} %get-tuple-element.54.q_ref, bf16[1024,384]{1,0:T(8,128)(2,1)S(1)} %get-tuple-element.55.k_ref, bf16[1024,384]{1,0:T(8,128)(2,1)S(1)} %get-tuple-element.56.v_ref, ...), custom_call_target="tpu_custom_call" | custom-call | flops 2000000000 | bytes 1000000 | tf_op jit(solution)/shard_map/pallas_call | solution.py:85
  38.9 0.1 collective-permute-start.9
  39.0 1.2 %collective-permute-done.9.near = bf16[96,384]{1,0:T(8,128)(2,1)S(1)} collective-permute-done((bf16[96,384]{1,0:T(8,128)(2,1)S(1)}, bf16[96,384]{1,0:T(8,128)(2,1)S(1)}, u32[]{:S(2)}, u32[]{:S(2)}) %collective-permute-start.9) | collective-permute-done | bytes 73760 | tf_op jit(solution)/shard_map/ppermute | solution.py:570
  40.2 0.9 %shard_map.103.base_ref = f32[96,1536]{1,0:T(8,128)S(1)} custom-call(bf16[96,384]{1,0:T(8,128)(2,1)S(1)} %get-tuple-element.59.own, bf16[96,384]{1,0:T(8,128)(2,1)S(1)} %collective-permute-done.9.near, bf16[384,1536]{1,0:T(8,128)(2,1)S(1)} %copy-done.2, bf16[384,1536]{1,0:T(8,128)(2,1)S(1)} %collective-permute-done.8.refs_3_.w_near, ...), custom_call_target="tpu_custom_call" | custom-call | flops 1200000000 | bytes 1000000 | tf_op jit(solution)/shard_map/pallas_call | solution.py:85
  41.1 2.9 %collective-permute-done.10.refs_0_ = bf16[96,1536]{1,0:T(8,128)(2,1)S(1)} collective-permute-done((bf16[96,1536]{1,0:T(8,128)(2,1)S(1)}, bf16[96,1536]{1,0:T(8,128)(2,1)S(1)}, u32[]{:S(2)}, u32[]{:S(2)}) %collective-permute-start.10) | collective-permute-done | bytes 294944 | tf_op jit(solution)/shard_map/ppermute | solution.py:570
  44.0 0.0 copy-done.4
  44.0 2.7 %shard_map.104 = bf16[64,1536]{1,0:T(8,128)(2,1)} custom-call(f32[96,1536]{1,0:T(8,128)S(1)} %shard_map.103.base_ref, bf16[96,1536]{1,0:T(8,128)(2,1)S(1)} %collective-permute-done.10.refs_0_, f32[1,1536]{1,0:T(1,128)S(1)} %broadcast_in_dim.11.refs_1_, bf16[31,1536]{1,0:T(8,128)(2,1)S(1)} %copy-done.4), custom_call_target="tpu_custom_call" | custom-call | flops 2800000000 | bytes 1000000 | tf_op jit(solution)/shard_map/pallas_call | solution.py:85
  (13 shorter events, 0.1 us)
Async XLA Ops:
  0.0 0.9 %copy-start.3 = (f32[40960]{0:T(1024)S(1)}, f32[40960]{0:T(1024)}, u32[]{:S(2)}) copy-start(f32[40960]{0:T(1024)} %param.9) | copy-start | bytes 491524
  0.9 0.7 %copy-start.5 = (s32[256]{0:T(256)S(1)}, s32[256]{0:T(256)}, u32[]{:S(2)}) copy-start(s32[256]{0:T(256)} %param.10) | copy-start | bytes 3076
  1.6 0.7 %copy-start.7 = (s32[256]{0:T(256)S(1)}, s32[256]{0:T(256)}, u32[]{:S(2)}) copy-start(s32[256]{0:T(256)} %param.11) | copy-start | bytes 3076
  2.3 1.3 %copy-start.9 = (bf16[512,1152]{1,0:T(8,128)(2,1)S(1)}, bf16[512,1152]{1,0:T(8,128)(2,1)}, u32[]{:S(2)}) copy-start(bf16[512,1152]{1,0:T(8,128)(2,1)} %constant.2.clone.tables_ref.refs_4_) | copy-start | bytes 3538948
  3.5 8.3 %copy-start = (bf16[3,1536,384]{2,1,0:T(8,128)(2,1)S(1)}, bf16[3,1536,384]{2,1,0:T(8,128)(2,1)}, u32[]{:S(2)}) copy-start(bf16[3,1536,384]{2,1,0:T(8,128)(2,1)} %refs_1_.1) | copy-start | bytes 10616836
  4.4 9.3 %collective-permute-start.1 = (bf16[1,72,512]{2,1,0:T(8,128)(2,1)S(1)}, bf16[1,72,512]{2,1,0:T(8,128)(2,1)S(1)}, u32[]{:S(2)}, u32[]{:S(2)}) collective-permute-start(bf16[1,72,512]{2,1,0:T(8,128)(2,1)S(1)} %shard_map.91._.refs_0_), channel_id=1, source_target_pairs={{0,4},{4,0},{8,12},{12,8},{1,5},{5,1},{9,13},{13,9},{2,6},{6,2},{1... | collective-permute-start | bytes 221192 | tf_op jit(solution)/shard_map/ppermute | solution.py:570
  7.5 7.8 %collective-permute-start.2 = (bf16[1,72,512]{2,1,0:T(8,128)(2,1)S(1)}, bf16[1,72,512]{2,1,0:T(8,128)(2,1)S(1)}, u32[]{:S(2)}, u32[]{:S(2)}) collective-permute-start(bf16[1,72,512]{2,1,0:T(8,128)(2,1)S(1)} %shard_map.91._.refs_0_), channel_id=1, source_target_pairs={{0,8},{4,12},{8,0},{12,4},{1,9},{5,13},{9,1},{13,5},{2,10},{6,14},... | collective-permute-start | bytes 221192 | tf_op jit(solution)/shard_map/ppermute | solution.py:570
  10.1 6.3 %collective-permute-start.3 = (bf16[1,72,512]{2,1,0:T(8,128)(2,1)S(1)}, bf16[1,72,512]{2,1,0:T(8,128)(2,1)S(1)}, u32[]{:S(2)}, u32[]{:S(2)}) collective-permute-start(bf16[1,72,512]{2,1,0:T(8,128)(2,1)S(1)} %shard_map.91._.refs_0_), channel_id=1, source_target_pairs={{0,12},{4,8},{8,4},{12,0},{1,13},{5,9},{9,5},{13,1},{2,14},{6,10},... | collective-permute-start | bytes 221192 | tf_op jit(solution)/shard_map/ppermute | solution.py:570
  10.1 7.8 %collective-permute-start = (bf16[1,72,512]{2,1,0:T(8,128)(2,1)S(1)}, bf16[1,72,512]{2,1,0:T(8,128)(2,1)S(1)}, u32[]{:S(2)}, u32[]{:S(2)}) collective-permute-start(bf16[1,72,512]{2,1,0:T(8,128)(2,1)S(1)} %shard_map.91._.refs_0_), channel_id=1, source_target_pairs={{0,2},{1,3},{2,0},{3,1},{4,6},{5,7},{6,4},{7,5},{8,10},{9,11},{10,... | collective-permute-start | bytes 221192 | tf_op jit(solution)/shard_map/ppermute | solution.py:570
  11.8 22.3 %collective-permute-start.8 = (bf16[384,1536]{1,0:T(8,128)(2,1)}, bf16[384,1536]{1,0:T(8,128)(2,1)S(1)}, u32[]{:S(2)}, u32[]{:S(2)}) collective-permute-start(bf16[384,1536]{1,0:T(8,128)(2,1)} %w_own.1), channel_id=1, source_target_pairs={{0,1},{1,0},{2,3},{3,2},{4,5},{5,4},{6,7},{7,6},{8,9},{9,8},{10,11... | collective-permute-start | bytes 3538952 | tf_op jit(solution)/shard_map/ppermute | solution.py:570
  11.8 1.4 %copy-start.1 = (bf16[512,1536]{1,0:T(8,128)(2,1)S(1)}, bf16[512,1536]{1,0:T(8,128)(2,1)}, u32[]{:S(2)}) copy-start(bf16[512,1536]{1,0:T(8,128)(2,1)} %refs_0_.1) | copy-start | bytes 4718596
  16.4 6.0 %collective-permute-start.5 = (bf16[3,72,512]{2,1,0:T(8,128)(2,1)S(1)}, bf16[3,72,512]{2,1,0:T(8,128)(2,1)S(1)}, u32[]{:S(2)}, u32[]{:S(2)}) collective-permute-start(bf16[3,72,512]{2,1,0:T(8,128)(2,1)S(1)} %shard_map.93.refs_2_), channel_id=1, source_target_pairs={{0,2},{1,3},{2,0},{3,1},{4,6},{5,7},{6,4},{7,5},{8,10},{9,11},{10,... | collective-permute-start | bytes 663560 | tf_op jit(solution)/shard_map/ppermute | solution.py:570
  18.0 6.3 %collective-permute-start.4 = (bf16[5,72,512]{2,1,0:T(8,128)(2,1)S(1)}, bf16[5,72,512]{2,1,0:T(8,128)(2,1)S(1)}, u32[]{:S(2)}, u32[]{:S(2)}) collective-permute-start(bf16[5,72,512]{2,1,0:T(8,128)(2,1)S(1)} %shard_map.94.refs_0_.stack_ref), channel_id=1, source_target_pairs={{0,1},{1,0},{2,3},{3,2},{4,5},{5,4},{6,7},{7,6},{8,9},{9,8},{10,11... | collective-permute-start | bytes 1105928 | tf_op jit(solution)/shard_map/ppermute | solution.py:570
  22.4 4.6 %collective-permute-start.6 = (bf16[3,72,512]{2,1,0:T(8,128)(2,1)S(1)}, bf16[3,72,512]{2,1,0:T(8,128)(2,1)S(1)}, u32[]{:S(2)}, u32[]{:S(2)}) collective-permute-start(bf16[3,72,512]{2,1,0:T(8,128)(2,1)S(1)} %collective-permute-done.5.refs_2_.stack_ref), channel_id=1, source_target_pairs={{0,1},{1,0},{2,3},{3,2},{4,5},{5,4},{6,7},{7,6},{8,9},{9,8},{10,11... | collective-permute-start | bytes 663560 | tf_op jit(solution)/shard_map/ppermute | solution.py:570
  24.2 2.8 %copy-start.6 = (s32[256]{0:T(256)S(1)}, s32[256]{0:T(256)}, u32[]{:S(2)}) copy-start(s32[256]{0:T(256)} %param.10) | copy-start | bytes 3076
  24.2 2.8 %copy-start.8 = (s32[256]{0:T(256)S(1)}, s32[256]{0:T(256)}, u32[]{:S(2)}) copy-start(s32[256]{0:T(256)} %param.11) | copy-start | bytes 3076
  24.3 2.8 %copy-start.10 = (bf16[512,1152]{1,0:T(8,128)(2,1)S(1)}, bf16[512,1152]{1,0:T(8,128)(2,1)}, u32[]{:S(2)}) copy-start(bf16[512,1152]{1,0:T(8,128)(2,1)} %constant.2.clone.tables_ref.refs_4_) | copy-start | bytes 3538948
  29.8 4.3 %copy-start.2 = (bf16[384,1536]{1,0:T(8,128)(2,1)S(1)}, bf16[384,1536]{1,0:T(8,128)(2,1)}, u32[]{:S(2)}) copy-start(bf16[384,1536]{1,0:T(8,128)(2,1)} %w_own.1) | copy-start | bytes 3538948
  32.6 1.5 %collective-permute-start.7 = (bf16[96,384]{1,0:T(8,128)(2,1)S(1)}, bf16[96,384]{1,0:T(8,128)(2,1)S(1)}, u32[]{:S(2)}, u32[]{:S(2)}) collective-permute-start(bf16[96,384]{1,0:T(8,128)(2,1)S(1)} %get-tuple-element.53), channel_id=1, source_target_pairs={{0,1},{1,0},{2,3},{3,2},{4,5},{5,4},{6,7},{7,6},{8,9},{9,8},{10,11... | collective-permute-start | bytes 221192 | tf_op jit(solution)/shard_map/ppermute | solution.py:570
  34.7 9.3 %collective-permute-start.10 = (bf16[96,1536]{1,0:T(8,128)(2,1)S(1)}, bf16[96,1536]{1,0:T(8,128)(2,1)S(1)}, u32[]{:S(2)}, u32[]{:S(2)}) collective-permute-start(bf16[96,1536]{1,0:T(8,128)(2,1)S(1)} %shard_map.101._), channel_id=1, source_target_pairs={{0,2},{1,3},{2,0},{3,1},{4,6},{5,7},{6,4},{7,5},{8,10},{9,11},{10,... | collective-permute-start | bytes 884744 | tf_op jit(solution)/shard_map/ppermute | solution.py:570
  36.2 2.8 %copy-start.11 = (f32[1536]{0:T(1024)S(1)}, f32[1536]{0:T(1024)}, u32[]{:S(2)}) copy-start(f32[1536]{0:T(1024)} %param.15) | copy-start | bytes 18436
  38.9 1.3 %collective-permute-start.9 = (bf16[96,384]{1,0:T(8,128)(2,1)S(1)}, bf16[96,384]{1,0:T(8,128)(2,1)S(1)}, u32[]{:S(2)}, u32[]{:S(2)}) collective-permute-start(bf16[96,384]{1,0:T(8,128)(2,1)S(1)} %get-tuple-element.60), channel_id=1, source_target_pairs={{0,1},{1,0},{2,3},{3,2},{4,5},{5,4},{6,7},{7,6},{8,9},{9,8},{10,11... | collective-permute-start | bytes 221192 | tf_op jit(solution)/shard_map/ppermute | solution.py:570
  40.2 3.8 %copy-start.4 = (bf16[31,1536]{1,0:T(8,128)(2,1)S(1)}, bf16[31,1536]{1,0:T(8,128)(2,1)}, u32[]{:S(2)}) copy-start(bf16[31,1536]{1,0:T(8,128)(2,1)} %refs_2_.3) | copy-start | bytes 285700

commit v4 on v3

--- a/solution.py
+++ b/solution.py
@@ -95,26 +95,30 @@
     )(*operands)
 
 
-def fetch(after, arrays):
-    count = len(arrays)
-
-    def kernel(_, *refs):
-        sources, outs, sems = refs[:count], refs[count:-1], refs[-1]
+def fetch(after, w_subsample, w_attention):
+    parts, _, width = w_attention.shape
+
+    def kernel(_, w_sub, w_att, out_sub, out_att, sums, sems):
         copies = [
-            pltpu.make_async_copy(source, target, sems.at[slot])
-            for slot, (source, target) in enumerate(zip(sources, outs))
+            pltpu.make_async_copy(w_att, out_att, sems.at[0]),
+            pltpu.make_async_copy(w_sub, out_sub, sems.at[1]),
         ]
         for copy in copies:
             copy.start()
         for copy in copies:
             copy.wait()
+        sums[...] = jnp.zeros_like(sums)
+        for part in range(parts):
+            columns = out_att[part].astype(jnp.float32)
+            sums[part : part + 1, :] = jnp.sum(columns, axis=0, keepdims=True)
 
     return call(
         kernel,
-        [jax.ShapeDtypeStruct(array.shape, array.dtype) for array in arrays],
-        (after, *arrays),
-        scratch=[pltpu.SemaphoreType.DMA((count,))],
-        remote=count,
+        [jax.ShapeDtypeStruct(array.shape, array.dtype) for array in (w_subsample, w_attention)]
+        + [jax.ShapeDtypeStruct((8, width), jnp.float32)],
+        (after, w_subsample, w_attention),
+        scratch=[pltpu.SemaphoreType.DMA((2,))],
+        remote=2,
     )
 
 
@@ -251,8 +255,8 @@
 
 def patch(held, fixed, slots, frames_local):
     fixed = fixed.astype(jnp.float32)
-    for slot in range(slots):
-        here = slice((slot + 1) * frames_local - HALO, (slot + 1) * frames_local)
+    for number, slot in enumerate(slots):
+        here = slice((number + 1) * frames_local - HALO, (number + 1) * frames_local)
         kept = held[here, :].astype(jnp.float32)
         last = lax.broadcasted_iota(jnp.int32, kept.shape, 0) == HALO - 1
         held[here, :] = jnp.where(last, fixed[slot : slot + 1, :], kept).astype(held.dtype)
@@ -269,37 +273,6 @@
 
     shape = jax.ShapeDtypeStruct((sum(counts), *parts[0].shape[1:]), parts[0].dtype)
     return call(kernel, shape, (*parts, *after))
-
-
-def project_rows(stack, w_subsample, w_attention, frames_local, every=(), fixed=None):
-    count = stack.shape[0]
-    rows, width = count * frames_local, w_attention.shape[2]
-    model = w_subsample.shape[1]
-    counts = [block.shape[0] for block in every]
-    sizes = [rows] if fixed is None else [rows, fixed.shape[0]]
-
-    def kernel(stack_ref, w_sub, w_att, *refs):
-        stack_rows = [stack_ref[block, 0:frames_local, :] for block in range(count)]
-        if fixed is not None:
-            every_refs, fixed_ref, refs = refs[: len(every)], refs[len(every)], refs[len(every) + 1 :]
-            stack_rows.append(
-                last_rows(every_refs, counts, frames_local, fixed_ref[...], sizes[1])
-            )
-        features = dot32(jnp.concatenate(stack_rows, axis=0), w_sub[...]).astype(jnp.bfloat16)
-        normed = normalize(features.astype(jnp.float32)).astype(jnp.bfloat16)
-        for part in range(3):
-            projected = dot32(normed, w_att[part]).astype(jnp.bfloat16)
-            begin = 0
-            for number, size in enumerate(sizes):
-                refs[3 * number + part][...] = projected[begin : begin + size]
-                begin += size
-
-    return call(
-        kernel,
-        [jax.ShapeDtypeStruct((size, width), jnp.bfloat16) for size in sizes for _ in range(3)],
-        (stack, w_subsample, w_attention) + (() if fixed is None else (*every, fixed)),
-        micros=0.5 + 0.007 * sum(sizes),
-    )
 
 
 def slot_of(places, tm, mp):
@@ -310,27 +283,105 @@
     return found
 
 
-def gather_rows(places, bounds, queries, keys, values, fixed, frames_local, window, outs):
+def project_rows(stack, weights, frames_local, query_blocks, boundary=None):
+    count = stack.shape[0]
+    rows, width = count * frames_local, weights[1].shape[2]
+    query_rows = query_blocks * frames_local
+    places, every, fixed = boundary or ((), (), jnp.zeros((0, 2 * NMEL), jnp.bfloat16))
+    counts = [block.shape[0] for block in every]
+    last_count = fixed.shape[0]
+    extra_rows = last_count + 2 * HALO if boundary else 0
+
+    def boundary_stack(every_refs, fixed_ref, lasts, heads, tails):
+        lasts[...] = last_rows(
+            every_refs, counts, frames_local, fixed_ref[...], last_count
+        ).astype(jnp.float32)
+        slot = 0
+        for ref, blocks in zip(every_refs, counts):
+            for block in range(blocks):
+                heads[slot] = ref[block, 0:HALO, :]
+                tails[slot] = ref[block, frames_local - HALO : frames_local, :]
+                slot += 1
+        time_index, parts = lax.axis_index("tm"), lax.axis_size("mp")
+        left = slot_of(places, time_index - 1, parts - 1)
+        right = slot_of(places, time_index + 1, 0)
+        tail = tails[left].astype(jnp.float32)
+        final = lax.broadcasted_iota(jnp.int32, tail.shape, 0) == HALO - 1
+        tail = jnp.where(final, lasts[pl.ds(left, 1), :], tail).astype(jnp.bfloat16)
+        return [lasts[...].astype(jnp.bfloat16), tail, heads[right]]
+
+    def kernel(stack_ref, w_sub, w_att, sums, *refs):
+        stack_rows = [stack_ref[block, 0:frames_local, :] for block in range(count)]
+        if boundary:
+            every_refs, refs = refs[: len(every)], refs[len(every) :]
+            fixed_ref, *refs = refs
+            refs, scratch = refs[:-3], refs[-3:]
+            stack_rows += boundary_stack(every_refs, fixed_ref, *scratch)
+        features = dot32(jnp.concatenate(stack_rows, axis=0), w_sub[...]).astype(jnp.bfloat16)
+        wide = features.astype(jnp.float32)
+        center = jnp.mean(wide, axis=-1, keepdims=True)
+        spread = jnp.mean(jnp.square(wide - center), axis=-1, keepdims=True)
+        scale = lax.rsqrt(spread + 1e-05)
+
+        def projected(part, begin, end):
+            product = dot32(features[begin:end], w_att[part])
+            shifted = product - center[begin:end] * sums[part : part + 1, :]
+            return (shifted * scale[begin:end]).astype(jnp.bfloat16)
+
+        refs = list(refs)
+        if query_rows:
+            refs.pop(0)[...] = projected(0, 0, query_rows)
+        if extra_rows:
+            refs.pop(0)[...] = projected(0, rows, rows + extra_rows)
+        for part in (1, 2):
+            both = projected(part, 0, rows + extra_rows)
+            refs.pop(0)[...] = both[:rows]
+            if extra_rows:
+                refs.pop(0)[...] = both[rows:]
+
+    def shape(size):
+        return jax.ShapeDtypeStruct((size, width), jnp.bfloat16)
+
+    shapes = [shape(query_rows)] * bool(query_rows) + [shape(extra_rows)] * bool(extra_rows)
+    shapes += ([shape(rows)] + [shape(extra_rows)] * bool(extra_rows)) * 2
+    depth = stack.shape[2]
+    return call(
+        kernel,
+        shapes,
+        (stack, *weights, *every) + ((fixed,) if boundary else ()),
+        scratch=[
+            pltpu.VMEM((last_count, depth), jnp.float32),
+            pltpu.VMEM((len(places), HALO, depth), jnp.bfloat16),
+            pltpu.VMEM((len(places), HALO, depth), jnp.bfloat16),
+        ]
+        if boundary
+        else [],
+        micros=0.5 + 0.006 * (rows + extra_rows),
+    )
+
+
+def gather_rows(places, query_slots, bounds, sources, extras, frames_local, outs):
     q_rows, k_all, v_all, q_all, first, last = outs
     parts = lax.axis_size("mp")
     frames_shard = frames_local * parts
-    for held, sources, fixed_ref in zip((q_all, k_all, v_all), (queries, keys, values), fixed):
+    last_count = extras[0].shape[0] - 2 * HALO
+    slots = range(len(places))
+    for held, group, extra, held_slots in zip(
+        (q_all, k_all, v_all), sources, extras, (query_slots, slots, slots)
+    ):
         begin = 0
-        for source in sources:
+        for source in group:
             held[begin : begin + source.shape[0], :] = source[...]
             begin += source.shape[0]
-        patch(held, fixed_ref[...], len(places), frames_local)
-    time_index = lax.axis_index("tm")
-
-    def source(tm, mp, offset, count):
-        start = pl.multiple_of(slot_of(places, tm, mp) * frames_local + offset, HALO)
-        return q_all[pl.ds(start, count), :]
-
-    q_rows[0:HALO, :] = source(time_index - 1, parts - 1, frames_local - HALO, HALO)
+        patch(held, extra[0:last_count, :], held_slots, frames_local)
+    query_places = [places[slot] for slot in query_slots]
+    q_rows[0:HALO, :] = extras[0][last_count : last_count + HALO, :]
     for part in range(parts):
         begin = HALO + part * frames_local
-        q_rows[begin : begin + frames_local, :] = source(time_index, part, 0, frames_local)
-    q_rows[HALO + frames_shard :, :] = source(time_index + 1, 0, 0, HALO)
+        slot = slot_of(query_places, lax.axis_index("tm"), part)
+        start = pl.multiple_of(slot * frames_local, HALO)
+        q_rows[begin : begin + frames_local, :] = q_all[pl.ds(start, frames_local), :]
+    q_rows[HALO + frames_shard :, :] = extras[0][last_count + HALO :, :]
     for line, ref in enumerate((first, last)):
         row = bounds[line : line + 1, :]
         ref[...] = jnp.transpose(jnp.broadcast_to(row, (LANES, row.shape[1])))
@@ -358,21 +409,23 @@
         q_pair = q_rows[pl.ds(begin, count), lane : lane + span]
         k_pair = k_all[:, lane : lane + span]
         v_pair = v_all[:, lane : lane + span]
+        heads = span // HD
         head_of = lax.broadcasted_iota(jnp.int32, (count, span), 1) // HD
-        merged = jnp.zeros((count, span), jnp.float32)
-        for head in range(span // HD):
-            mine = head_of == head
-            q_head = jnp.where(mine, q_pair, jnp.zeros_like(q_pair)) * jnp.bfloat16(
-                1.0 / math.sqrt(HD)
-            )
-            scores = lax.dot_general(
-                q_head, k_pair, (((1,), (1,)), ((), ())), preferred_element_type=jnp.float32
-            )
-            scores = scores + bias[...]
-            weights = jnp.exp(scores - jnp.max(scores, axis=1, keepdims=True))
-            total = jnp.sum(weights, axis=1, keepdims=True)
-            numerator = dot32(weights.astype(jnp.bfloat16), v_pair)
-            merged = jnp.where(mine, numerator / total, merged)
+        scaled = q_pair * jnp.bfloat16(1.0 / math.sqrt(HD))
+        stacked = jnp.concatenate(
+            [jnp.where(head_of == head, scaled, jnp.zeros_like(scaled)) for head in range(heads)],
+            axis=0,
+        )
+        scores = lax.dot_general(
+            stacked, k_pair, (((1,), (1,)), ((), ())), preferred_element_type=jnp.float32
+        )
+        scores = scores + jnp.concatenate([bias[...]] * heads, axis=0)
+        weights = jnp.exp(scores - jnp.max(scores, axis=1, keepdims=True))
+        total = jnp.sum(weights, axis=1, keepdims=True)
+        ratio = dot32(weights.astype(jnp.bfloat16), v_pair) / total
+        merged = ratio[0:count]
+        for head in range(1, heads):
+            merged = jnp.where(head_of == head, ratio[head * count : (head + 1) * count], merged)
         result[:, lane : lane + span] = merged.astype(jnp.bfloat16)
 
 
@@ -384,28 +437,29 @@
     other[...] = result[pl.ds(pl.multiple_of(place, HALO), window), :]
 
 
-def attend_far(places, far, bounds, queries, keys, values, fixed, frames_local):
-    counts = [q.shape[0] for q in queries]
-    rows, width = sum(counts), queries[0].shape[1]
-    groups = len(counts)
+def attend_far(places, query_slots, far, bounds, sources, extras, frames_local):
+    width = sources[0][0].shape[1]
+    query_count, rows = (sum(group.shape[0] for group in groups) for groups in sources[:2])
+    sizes = [len(groups) for groups in sources]
     extended = frames_local * lax.axis_size("mp") + 2 * HALO
     window = frames_local + 2 * HALO
     pair = 2 * frames_local + 2 * HALO
 
     def kernel(bound_ref, *refs):
-        sources, refs = refs[: 3 * groups], refs[3 * groups :]
-        fixed_refs, refs = refs[:3], refs[3:]
+        groups = []
+        for size in sizes:
+            groups.append(refs[:size])
+            refs = refs[size:]
+        extra_refs, refs = refs[:3], refs[3:]
         windows, refs = refs[: 2 * len(far)], refs[2 * len(far) :]
         q_rows, k_all, v_all, first, last, q_all, result, bias = refs
         gather_rows(
             places,
+            query_slots,
             bound_ref,
-            sources[:groups],
-            sources[groups : 2 * groups],
-            sources[2 * groups :],
-            fixed_refs,
+            groups,
+            extra_refs,
             frames_local,
-            window,
             (q_rows, k_all, v_all, q_all, first, last),
         )
         model_index = lax.axis_index("mp")
@@ -426,9 +480,9 @@
         [shape(window)] * (2 * len(far))
         + [shape(extended), shape(rows), shape(rows)]
         + [shape(extended, LANES, jnp.float32)] * 2,
-        (bounds, *queries, *keys, *values, *fixed),
+        (bounds, *(array for groups in sources for array in groups), *extras),
         scratch=[
-            pltpu.VMEM((rows, width), jnp.bfloat16),
+            pltpu.VMEM((query_count, width), jnp.bfloat16),
             pltpu.VMEM((pair, width), jnp.bfloat16),
             pltpu.VMEM((pair, rows), jnp.float32),
         ],
@@ -491,7 +545,7 @@
                 held[begin : begin + frames_local, :] = stack_ref[block, 0:frames_local, :]
                 begin += frames_local
         rows = last_rows(stack_refs, counts, frames_local, fixed_ref[...], fixed.shape[0])
-        patch(held, rows, slots, frames_local)
+        patch(held, rows, range(slots), frames_local)
         parts = lax.axis_size("mp")
         block = lax.axis_index("tm") * parts + lax.axis_index("mp") + parts
 
@@ -544,13 +598,16 @@
             here = slice(lane, lane + chunk)
             total = jnp.zeros((frames_local, chunk), jnp.float32)
             tap_rows = tap_ref[:, here].astype(jnp.float32)
+            rows = held[:, here]
+            reach = frames_local + 8
             for phase in range(8):
-                taken = [tap for tap in range(KERNEL) if (tap + offset) % 8 == phase]
-                reach = (taken[-1] + offset) // 8 * 8 + frames_local
-                moved = held[pl.ds(phase, reach), here]
-                for tap in taken:
-                    begin = (tap + offset) // 8 * 8
-                    total += moved[begin : begin + frames_local] * tap_rows[tap : tap + 1]
+                share = jnp.zeros((reach, chunk), jnp.float32)
+                for tap in range(KERNEL):
+                    if (tap + offset) % 8 == phase:
+                        begin = (tap + offset) // 8 * 8
+                        share += rows[begin : begin + reach] * tap_rows[tap : tap + 1]
+                moved = pltpu.roll(share, reach - phase, axis=0) if phase else share
+                total += moved[0:frames_local]
             silu = total / (1.0 + jnp.exp(-total))
             out[:, here] = (mixed_rows[:, here] + silu).astype(jnp.bfloat16)
 
@@ -595,7 +652,7 @@
     starts, ends = segment_start[None, :], segment_end[None, :]
     tables = jnp.asarray(front_tables())
     stacked = log_mel_rows(starts, ends, samples, tables, frames_local)
-    w_subsample, w_attention = fetch(stacked, (w_subsample, w_attention))
+    weights = fetch(stacked, w_subsample, w_attention)
 
     w_near = exchange(w_output, "mp", bits[-1])
 
@@ -609,7 +666,7 @@
         moves = [lambda tm, step=step: tm - step for step in steps]
         column = [shifted(stacked, "tm", step) for step in steps]
     early = [(stacked, [(lambda tm: tm, 0)])]
-    late = [(assemble(column, (w_subsample,)), [(move, 0) for move in moves])]
+    late = [(assemble(column, weights[-1:]), [(move, 0) for move in moves])]
 
     def across(blocks, bit):
         return [
@@ -624,18 +681,28 @@
     groups = [joined] + across([joined], bits[-1]) + late[1:] + across(late[1:], bits[-1])
     stacks, held = zip(*groups)
     places = sum(held, [])
+    joined_slots = range(len(joined[1]), 2 * len(joined[1]))
+    query_slots = [*range(len(early)), *joined_slots[: len(early)]]
+    fixed, bounds = boundary_rows(places, starts, ends, stacks, tables, frames_local)
     projected = [
-        project_rows(block, w_subsample, w_attention, frames_local) for block in stacks[:-1]
+        project_rows(block, weights, frames_local, len(early) if number < 2 else 0)
+        for number, block in enumerate(stacks[:-1])
     ]
-    fixed, bounds = boundary_rows(places, starts, ends, stacks, tables, frames_local)
-    *outs, fixed_query, fixed_key, fixed_value = project_rows(
-        stacks[-1], w_subsample, w_attention, frames_local, stacks, fixed
-    )
-    queries, keys, values = zip(*projected, outs)
-    fixed_rows = (fixed_query, fixed_key, fixed_value)
+    boundary = (places, stacks, fixed)
+    if len(stacks) > 2:
+        outs = project_rows(stacks[-1], weights, frames_local, 0, boundary)
+    else:
+        query, *outs = project_rows(stacks[-1], weights, frames_local, len(early), boundary)
+        projected.append([query])
+    extras = (outs[0], outs[2], outs[4])
+    queries = [group[0] for group in projected[:2]]
+    keys = [*(group[-2] for group in projected if len(group) > 1), outs[1]]
+    values = [*(group[-1] for group in projected if len(group) > 1), outs[3]]
 
     far = list(range(2, parts, 2))
-    outs = attend_far(places, far, bounds, queries, keys, values, fixed_rows, frames_local)
+    outs = attend_far(
+        places, query_slots, far, bounds, (queries, keys, values), extras, frames_local
+    )
     windows, shared = outs[: 2 * len(far)], outs[2 * len(far) :]
     windows = [
         exchange(block, "mp", 1) if number % 2 else block for number, block in enumerate(windows)
@@ -645,7 +712,7 @@
     mine, other = attend_near(places, shares[0], *shared, frames_local)
     shares = [exchange(share, "mp", bit) for share, bit in zip(shares, far)]
     base = near_branch(
-        places, (mine, exchange(other, "mp", 1)), w_rows, stacks, fixed, w_subsample, frames_local
+        places, (mine, exchange(other, "mp", 1)), w_rows, stacks, fixed, weights[0], frames_local
     )
     return finish_rows(base, shares, gain_convolution[None, :], w_depthwise, frames_local)
 

time: 46.9 us -> 44.4 us (0.947)
  Pallas kernels: 21.1 us -> 17.9 us
  waiting for transfers between devices: 9.21 us -> 9.85 us
    pallas_call x14, Pallas kernels: 21.1 us -> 17.9 us  [call(): pl.pallas_call(kernel, out_shape=out_shape, in_specs=specs, out_specs=jax...]
    ppermute x11, waiting for transfers between devices: 9.21 us -> 9.85 us  [exchange(): lax.ppermute(block, axis, [(i, i ^ bit) for i in range(lax.axis_size(axis...]
    unnamed x24 -> x20, local copies, waits for them, and re-layouts: 4.99 us -> 4.97 us
  transfers between devices with their start and end apart: 11 -> 11, of which waited for: 6 -> 6; matrix products, arithmetic and copies ran while one was open for 0% -> 0% of each run, Pallas kernels for 36% -> 32%
where the time goes in v4:
time: 44.4 us; the launch traced here: 44.2 us
  Pallas kernels  17.9 us (40%)
  starting transfers between devices  11.3 us (25%)
  waiting for transfers between devices  9.85 us (22%)
  local copies, waits for them, and re-layouts  4.98 us (11%)
    pallas_call x14, Pallas kernels, call(): pl.pallas_call(kernel, out_shape=out_shape, in_specs=specs, out_specs=jax...  17.9 us
    ppermute x11, starting transfers between devices, exchange(): lax.ppermute(block, axis, [(i, i ^ bit) for i in range(lax.axis_size(axis...  11.3 us
    ppermute x11, waiting for transfers between devices, exchange(): lax.ppermute(block, axis, [(i, i ^ bit) for i in range(lax.axis_size(axis...  9.85 us
    unnamed x20, local copies, waits for them, and re-layouts  4.97 us
  transfers between devices with their start and end apart: 11, of which 6 were waited for; matrix products, arithmetic and copies ran while one was open for 0% of the time, Pallas kernels for 32%

profile of v4, /device:TPU:0, one launch (start us, length us, event | category | flops | bytes accessed | tf_op | source)
XLA Modules:
  0.0 44.2 jit_solution(11133253875834787732)
XLA Ops:
  0.0 0.0 copy-start.3
  0.0 0.9 %copy-done.3 = f32[40960]{0:T(1024)S(1)} copy-done((f32[40960]{0:T(1024)S(1)}, f32[40960]{0:T(1024)}, u32[]{:S(2)}) %copy-start.3) | copy-done | bytes 163864
  0.9 0.0 copy-start.5
  0.9 0.7 %copy-done.5 = s32[256]{0:T(256)S(1)} copy-done((s32[256]{0:T(256)S(1)}, s32[256]{0:T(256)}, u32[]{:S(2)}) %copy-start.5) | copy-done | bytes 1048
  1.6 0.7 %copy-done.6 = s32[256]{0:T(256)S(1)} copy-done((s32[256]{0:T(256)S(1)}, s32[256]{0:T(256)}, u32[]{:S(2)}) %copy-start.6) | copy-done | bytes 1048
  2.3 1.3 %copy-done.7 = bf16[512,1152]{1,0:T(8,128)(2,1)S(1)} copy-done((bf16[512,1152]{1,0:T(8,128)(2,1)S(1)}, bf16[512,1152]{1,0:T(8,128)(2,1)}, u32[]{:S(2)}) %copy-start.7) | copy-done | bytes 1179672
  3.5 0.9 %shard_map.91._.refs_0_ = bf16[1,72,512]{2,1,0:T(8,128)(2,1)S(1)} custom-call(s32[1,256]{1,0:T(1,128)S(1)} %bitcast.4, s32[1,256]{1,0:T(1,128)S(1)} %bitcast.6, f32[320,128]{1,0:T(8,128)S(1)} %bitcast.3, bf16[512,1152]{1,0:T(8,128)(2,1)S(1)} %copy-done.7), custom_call_target="tpu_custom_call" | custom-call | flops 1000000000 | bytes 1000000 | tf_op jit(solution)/shard_map/pallas_call | solution.py:85
  4.4 3.1 %collective-permute-start.1 = (bf16[1,72,512]{2,1,0:T(8,128)(2,1)S(1)}, bf16[1,72,512]{2,1,0:T(8,128)(2,1)S(1)}, u32[]{:S(2)}, u32[]{:S(2)}) collective-permute-start(bf16[1,72,512]{2,1,0:T(8,128)(2,1)S(1)} %shard_map.91._.refs_0_), channel_id=1, source_target_pairs={{0,4},{4,0},{8,12},{12,8},{1,5},{5,1},{9,13},{13,9},{2,6},{6,2},{1... | collective-permute-start | bytes 221192 | tf_op jit(solution)/shard_map/ppermute | solution.py:627
  7.5 2.6 %collective-permute-start.2 = (bf16[1,72,512]{2,1,0:T(8,128)(2,1)S(1)}, bf16[1,72,512]{2,1,0:T(8,128)(2,1)S(1)}, u32[]{:S(2)}, u32[]{:S(2)}) collective-permute-start(bf16[1,72,512]{2,1,0:T(8,128)(2,1)S(1)} %shard_map.91._.refs_0_), channel_id=1, source_target_pairs={{0,8},{4,12},{8,0},{12,4},{1,9},{5,13},{9,1},{13,5},{2,10},{6,14},... | collective-permute-start | bytes 221192 | tf_op jit(solution)/shard_map/ppermute | solution.py:627
  10.1 0.0 collective-permute-start.3
  10.1 1.7 %collective-permute-start = (bf16[1,72,512]{2,1,0:T(8,128)(2,1)S(1)}, bf16[1,72,512]{2,1,0:T(8,128)(2,1)S(1)}, u32[]{:S(2)}, u32[]{:S(2)}) collective-permute-start(bf16[1,72,512]{2,1,0:T(8,128)(2,1)S(1)} %shard_map.91._.refs_0_), channel_id=1, source_target_pairs={{0,2},{1,3},{2,0},{3,1},{4,6},{5,7},{6,4},{7,5},{8,10},{9,11},{10,... | collective-permute-start | bytes 221192 | tf_op jit(solution)/shard_map/ppermute | solution.py:627
  11.8 0.0 collective-permute-start.8
  11.8 0.0 copy-done
  11.8 1.4 %copy-done.1 = bf16[512,1536]{1,0:T(8,128)(2,1)S(1)} copy-done((bf16[512,1536]{1,0:T(8,128)(2,1)S(1)}, bf16[512,1536]{1,0:T(8,128)(2,1)}, u32[]{:S(2)}) %copy-start.1) | copy-done | bytes 1572888
  13.2 1.1 %shard_map.92 = (bf16[512,1536]{1,0:T(8,128)(2,1)S(1)}, bf16[3,1536,384]{2,1,0:T(8,128)(2,1)S(1)}, f32[8,384]{1,0:T(8,128)S(1)}) custom-call(bf16[1,72,512]{2,1,0:T(8,128)(2,1)S(1)} %shard_map.91._.refs_0_, bf16[512,1536]{1,0:T(8,128)(2,1)S(1)} %copy-done.1, bf16[3,1536,384]{2,1,0:T(8,128)(2,1)S(1)} %copy-done), custom_call_target="tpu_custom_call" | custom-call | flops 1000000000 | bytes 1000000 | tf_op jit(solution)/shard_map/pallas_call | solution.py:85
  14.4 0.0 collective-permute-done.1.refs_0_
  14.4 0.9 %collective-permute-done.2.refs_1_ = bf16[1,72,512]{2,1,0:T(8,128)(2,1)S(1)} collective-permute-done((bf16[1,72,512]{2,1,0:T(8,128)(2,1)S(1)}, bf16[1,72,512]{2,1,0:T(8,128)(2,1)S(1)}, u32[]{:S(2)}, u32[]{:S(2)}) %collective-permute-start.2) | collective-permute-done | bytes 73760 | tf_op jit(solution)/shard_map/ppermute | solution.py:627
  15.3 1.1 %collective-permute-done.3.refs_2_ = bf16[1,72,512]{2,1,0:T(8,128)(2,1)S(1)} collective-permute-done((bf16[1,72,512]{2,1,0:T(8,128)(2,1)S(1)}, bf16[1,72,512]{2,1,0:T(8,128)(2,1)S(1)}, u32[]{:S(2)}, u32[]{:S(2)}) %collective-permute-start.3) | collective-permute-done | bytes 73760 | tf_op jit(solution)/shard_map/ppermute | solution.py:627
  16.4 1.6 %collective-permute-start.5 = (bf16[3,72,512]{2,1,0:T(8,128)(2,1)S(1)}, bf16[3,72,512]{2,1,0:T(8,128)(2,1)S(1)}, u32[]{:S(2)}, u32[]{:S(2)}) collective-permute-start(bf16[3,72,512]{2,1,0:T(8,128)(2,1)S(1)} %shard_map.93.refs_2_), channel_id=1, source_target_pairs={{0,2},{1,3},{2,0},{3,1},{4,6},{5,7},{6,4},{7,5},{8,10},{9,11},{10,... | collective-permute-start | bytes 663560 | tf_op jit(solution)/shard_map/ppermute | solution.py:627
  18.0 0.0 collective-permute-done.refs_1_
  18.0 0.1 collective-permute-start.4
  18.1 2.1 %shard_map.96 = (bf16[128,384]{1,0:T(8,128)(2,1)S(1)}, bf16[320,384]{1,0:T(8,128)(2,1)S(1)}, bf16[320,384]{1,0:T(8,128)(2,1)S(1)}) custom-call(bf16[5,72,512]{2,1,0:T(8,128)(2,1)S(1)} %shard_map.94.refs_0_.stack_ref, bf16[512,1536]{1,0:T(8,128)(2,1)S(1)} %get-tuple-element.34.w_sub.refs_5_, bf16[3,1536,384]{2,1,0:T(8,128)(2,1)S(1)} %get-tuple-element.35.w_att, ...), custom_call_target="tpu_custom_call" | custom-call | flops 2420000000 | bytes 1000000 | tf_op jit(solution)/shard_map/pallas_call | solution.py:85
  20.2 2.2 %collective-permute-done.5.refs_2_.stack_ref = bf16[3,72,512]{2,1,0:T(8,128)(2,1)S(1)} collective-permute-done((bf16[3,72,512]{2,1,0:T(8,128)(2,1)S(1)}, bf16[3,72,512]{2,1,0:T(8,128)(2,1)S(1)}, u32[]{:S(2)}, u32[]{:S(2)}) %collective-permute-start.5) | collective-permute-done | bytes 221216 | tf_op jit(solution)/shard_map/ppermute | solution.py:627
  22.4 0.0 collective-permute-start.6
  22.4 1.2 %shard_map.98 = (bf16[192,384]{1,0:T(8,128)(2,1)S(1)}, bf16[192,384]{1,0:T(8,128)(2,1)S(1)}) custom-call(bf16[3,72,512]{2,1,0:T(8,128)(2,1)S(1)} %collective-permute-done.5.refs_2_.stack_ref, bf16[512,1536]{1,0:T(8,128)(2,1)S(1)} %get-tuple-element.34.w_sub.refs_5_, bf16[3,1536,384]{2,1,0:T(8,128)(2,1)S(1)} %get-tuple-element.35.w_att, ...), custom_call_target="tpu_custom_call" | custom-call | flops 1652000000 | bytes 1000000 | tf_op jit(solution)/shard_map/pallas_call | solution.py:85
  23.6 0.0 copy-start.8
  23.6 0.0 collective-permute-done.4.refs_1_.stack_ref
  23.7 2.1 %shard_map.97 = (bf16[128,384]{1,0:T(8,128)(2,1)S(1)}, bf16[320,384]{1,0:T(8,128)(2,1)S(1)}, bf16[320,384]{1,0:T(8,128)(2,1)S(1)}) custom-call(bf16[5,72,512]{2,1,0:T(8,128)(2,1)S(1)} %collective-permute-done.4.refs_1_.stack_ref, bf16[512,1536]{1,0:T(8,128)(2,1)S(1)} %get-tuple-element.34.w_sub.refs_5_, bf16[3,1536,384]{2,1,0:T(8,128)(2,1)S(1)} %get-tuple-element.35.w_att, ...), custom_call_target="tpu_custom_call" | custom-call | flops 2420000000 | bytes 1000000 | tf_op jit(solution)/shard_map/pallas_call | solution.py:85
  25.8 0.0 collective-permute-done.6.refs_3_.stack_ref
  25.8 0.0 copy-done.8
  25.8 0.8 %shard_map.95 = (bf16[16,256]{1,0:T(8,128)(2,1)S(1)}, f32[2,288]{1,0:T(2,128)S(1)}) custom-call(s32[1,256]{1,0:T(1,128)S(1)} %bitcast.5, s32[1,256]{1,0:T(1,128)S(1)} %bitcast.7, bf16[5,72,512]{2,1,0:T(8,128)(2,1)S(1)} %shard_map.94.refs_0_.stack_ref, bf16[5,72,512]{2,1,0:T(8,128)(2,1)S(1)} %collective-permute-done.4.refs_1_.stack_ref, ...), custom_call_target="tpu_custom_call" | custom-call | flops 900000000 | bytes 1000000 | tf_op jit(solution)/shard_map/pallas_call | solution.py:85
  26.7 1.7 %shard_map.99 = (bf16[48,384]{1,0:T(8,128)(2,1)S(1)}, bf16[192,384]{1,0:T(8,128)(2,1)S(1)}, bf16[48,384]{1,0:T(8,128)(2,1)S(1)}, bf16[192,384]{1,0:T(8,128)(2,1)S(1)}, bf16[48,384]{1,0:T(8,128)(2,1)S(1)}) custom-call(bf16[3,72,512]{2,1,0:T(8,128)(2,1)S(1)} %collective-permute-done.6.refs_3_.stack_ref, bf16[512,1536]{1,0:T(8,128)(2,1)S(1)} %get-tuple-element.34.w_sub.refs_5_, ...), custom_call_target="tpu_custom_call" | custom-call | flops 1940000000 | bytes 1000000 | tf_op jit(solution)/shard_map/pallas_call | solution.py:85
  28.4 0.0 copy-start.2
  28.4 2.2 %shard_map.100 = (bf16[96,384]{1,0:T(8,128)(2,1)S(1)}, bf16[96,384]{1,0:T(8,128)(2,1)S(1)}, bf16[288,384]{1,0:T(8,128)(2,1)S(1)}, bf16[1024,384]{1,0:T(8,128)(2,...) custom-call(f32[2,288]{1,0:T(2,128)S(1)} %get-tuple-element.33.bound_ref, ...), custom_call_target="tpu_custom_call" | custom-call | flops 2500000000 | bytes 1000000 | tf_op jit(solution)/shard_map/pallas_call | solution.py:85
  30.6 0.6 %collective-permute-start.7 = (bf16[96,384]{1,0:T(8,128)(2,1)S(1)}, bf16[96,384]{1,0:T(8,128)(2,1)S(1)}, u32[]{:S(2)}, u32[]{:S(2)}) collective-permute-start(bf16[96,384]{1,0:T(8,128)(2,1)S(1)} %get-tuple-element.51), channel_id=1, source_target_pairs={{0,1},{1,0},{2,3},{3,2},{4,5},{5,4},{6,7},{7,6},{8,9},{9,8},{10,11... | collective-permute-start | bytes 221192 | tf_op jit(solution)/shard_map/ppermute | solution.py:627
  31.2 0.9 %collective-permute-done.7.refs_1_ = bf16[96,384]{1,0:T(8,128)(2,1)S(1)} collective-permute-done((bf16[96,384]{1,0:T(8,128)(2,1)S(1)}, bf16[96,384]{1,0:T(8,128)(2,1)S(1)}, u32[]{:S(2)}, u32[]{:S(2)}) %collective-permute-start.7) | collective-permute-done | bytes 73760 | tf_op jit(solution)/shard_map/ppermute | solution.py:627
  32.1 0.0 collective-permute-done.8.refs_3_.w_near
  32.1 0.0 copy-done.2
  32.1 0.6 %shard_map.101._ = bf16[96,1536]{1,0:T(8,128)(2,1)S(1)} custom-call(bf16[96,384]{1,0:T(8,128)(2,1)S(1)} %get-tuple-element.50.refs_0_, bf16[96,384]{1,0:T(8,128)(2,1)S(1)} %collective-permute-done.7.refs_1_, bf16[384,1536]{1,0:T(8,128)(2,1)S(1)} %copy-done.2, bf16[384,1536]{1,0:T(8,128)(2,1)S(1)} %collective-permute-done.8.refs_3_.w_near), custom_call_target="tpu_custom_call" | custom-call | flops 900000000 | bytes 1000000 | tf_op jit(solution)/shard_map/pallas_call | solution.py:85
  32.7 1.6 %collective-permute-start.10 = (bf16[96,1536]{1,0:T(8,128)(2,1)S(1)}, bf16[96,1536]{1,0:T(8,128)(2,1)S(1)}, u32[]{:S(2)}, u32[]{:S(2)}) collective-permute-start(bf16[96,1536]{1,0:T(8,128)(2,1)S(1)} %shard_map.101._), channel_id=1, source_target_pairs={{0,2},{1,3},{2,0},{3,1},{4,6},{5,7},{6,4},{7,5},{8,10},{9,11},{10,... | collective-permute-start | bytes 884744 | tf_op jit(solution)/shard_map/ppermute | solution.py:627
  34.2 1.9 %shard_map.102 = (bf16[96,384]{1,0:T(8,128)(2,1)S(1)}, bf16[96,384]{1,0:T(8,128)(2,1)S(1)}) custom-call(bf16[96,1536]{1,0:T(8,128)(2,1)S(1)} %shard_map.101._, bf16[288,384]{1,0:T(8,128)(2,1)S(1)} %get-tuple-element.52.q_ref, bf16[1024,384]{1,0:T(8,128)(2,1)S(1)} %get-tuple-element.53.k_ref, bf16[1024,384]{1,0:T(8,128)(2,1)S(1)} %get-tuple-element.54.v_ref, ...), custom_call_target="tpu_custom_call" | custom-call | flops 2000000000 | bytes 1000000 | tf_op jit(solution)/shard_map/pallas_call | solution.py:85
  36.2 0.1 collective-permute-start.9
  36.3 0.0 copy-done.9
  36.3 1.2 %collective-permute-done.9.near = bf16[96,384]{1,0:T(8,128)(2,1)S(1)} collective-permute-done((bf16[96,384]{1,0:T(8,128)(2,1)S(1)}, bf16[96,384]{1,0:T(8,128)(2,1)S(1)}, u32[]{:S(2)}, u32[]{:S(2)}) %collective-permute-start.9) | collective-permute-done | bytes 73760 | tf_op jit(solution)/shard_map/ppermute | solution.py:627
  37.5 0.9 %shard_map.103.base_ref = f32[96,1536]{1,0:T(8,128)S(1)} custom-call(bf16[96,384]{1,0:T(8,128)(2,1)S(1)} %get-tuple-element.57.own, bf16[96,384]{1,0:T(8,128)(2,1)S(1)} %collective-permute-done.9.near, bf16[384,1536]{1,0:T(8,128)(2,1)S(1)} %copy-done.2, bf16[384,1536]{1,0:T(8,128)(2,1)S(1)} %collective-permute-done.8.refs_3_.w_near, ...), custom_call_target="tpu_custom_call" | custom-call | flops 1200000000 | bytes 1000000 | tf_op jit(solution)/shard_map/pallas_call | solution.py:85
  38.4 3.6 %collective-permute-done.10.refs_0_ = bf16[96,1536]{1,0:T(8,128)(2,1)S(1)} collective-permute-done((bf16[96,1536]{1,0:T(8,128)(2,1)S(1)}, bf16[96,1536]{1,0:T(8,128)(2,1)S(1)}, u32[]{:S(2)}, u32[]{:S(2)}) %collective-permute-start.10) | collective-permute-done | bytes 294944 | tf_op jit(solution)/shard_map/ppermute | solution.py:627
  42.0 0.0 copy-done.4
  42.0 2.2 %shard_map.104 = bf16[64,1536]{1,0:T(8,128)(2,1)} custom-call(f32[96,1536]{1,0:T(8,128)S(1)} %shard_map.103.base_ref, bf16[96,1536]{1,0:T(8,128)(2,1)S(1)} %collective-permute-done.10.refs_0_, f32[1,1536]{1,0:T(1,128)S(1)} %broadcast_in_dim.11.refs_1_, bf16[31,1536]{1,0:T(8,128)(2,1)S(1)} %copy-done.4), custom_call_target="tpu_custom_call" | custom-call | flops 2800000000 | bytes 1000000 | tf_op jit(solution)/shard_map/pallas_call | solution.py:85
  (9 shorter events, 0.1 us)
Async XLA Ops:
  0.0 0.9 %copy-start.3 = (f32[40960]{0:T(1024)S(1)}, f32[40960]{0:T(1024)}, u32[]{:S(2)}) copy-start(f32[40960]{0:T(1024)} %param.9) | copy-start | bytes 491524
  0.9 0.7 %copy-start.5 = (s32[256]{0:T(256)S(1)}, s32[256]{0:T(256)}, u32[]{:S(2)}) copy-start(s32[256]{0:T(256)} %param.10) | copy-start | bytes 3076
  1.6 0.7 %copy-start.6 = (s32[256]{0:T(256)S(1)}, s32[256]{0:T(256)}, u32[]{:S(2)}) copy-start(s32[256]{0:T(256)} %param.11) | copy-start | bytes 3076
  2.3 1.3 %copy-start.7 = (bf16[512,1152]{1,0:T(8,128)(2,1)S(1)}, bf16[512,1152]{1,0:T(8,128)(2,1)}, u32[]{:S(2)}) copy-start(bf16[512,1152]{1,0:T(8,128)(2,1)} %constant.2.clone.tables_ref.refs_4_) | copy-start | bytes 3538948
  3.5 8.3 %copy-start = (bf16[3,1536,384]{2,1,0:T(8,128)(2,1)S(1)}, bf16[3,1536,384]{2,1,0:T(8,128)(2,1)}, u32[]{:S(2)}) copy-start(bf16[3,1536,384]{2,1,0:T(8,128)(2,1)} %w_att.1) | copy-start | bytes 10616836
  4.4 10.0 %collective-permute-start.1 = (bf16[1,72,512]{2,1,0:T(8,128)(2,1)S(1)}, bf16[1,72,512]{2,1,0:T(8,128)(2,1)S(1)}, u32[]{:S(2)}, u32[]{:S(2)}) collective-permute-start(bf16[1,72,512]{2,1,0:T(8,128)(2,1)S(1)} %shard_map.91._.refs_0_), channel_id=1, source_target_pairs={{0,4},{4,0},{8,12},{12,8},{1,5},{5,1},{9,13},{13,9},{2,6},{6,2},{1... | collective-permute-start | bytes 221192 | tf_op jit(solution)/shard_map/ppermute | solution.py:627
  7.5 7.8 %collective-permute-start.2 = (bf16[1,72,512]{2,1,0:T(8,128)(2,1)S(1)}, bf16[1,72,512]{2,1,0:T(8,128)(2,1)S(1)}, u32[]{:S(2)}, u32[]{:S(2)}) collective-permute-start(bf16[1,72,512]{2,1,0:T(8,128)(2,1)S(1)} %shard_map.91._.refs_0_), channel_id=1, source_target_pairs={{0,8},{4,12},{8,0},{12,4},{1,9},{5,13},{9,1},{13,5},{2,10},{6,14},... | collective-permute-start | bytes 221192 | tf_op jit(solution)/shard_map/ppermute | solution.py:627
  10.1 6.3 %collective-permute-start.3 = (bf16[1,72,512]{2,1,0:T(8,128)(2,1)S(1)}, bf16[1,72,512]{2,1,0:T(8,128)(2,1)S(1)}, u32[]{:S(2)}, u32[]{:S(2)}) collective-permute-start(bf16[1,72,512]{2,1,0:T(8,128)(2,1)S(1)} %shard_map.91._.refs_0_), channel_id=1, source_target_pairs={{0,12},{4,8},{8,4},{12,0},{1,13},{5,9},{9,5},{13,1},{2,14},{6,10},... | collective-permute-start | bytes 221192 | tf_op jit(solution)/shard_map/ppermute | solution.py:627
  10.1 7.8 %collective-permute-start = (bf16[1,72,512]{2,1,0:T(8,128)(2,1)S(1)}, bf16[1,72,512]{2,1,0:T(8,128)(2,1)S(1)}, u32[]{:S(2)}, u32[]{:S(2)}) collective-permute-start(bf16[1,72,512]{2,1,0:T(8,128)(2,1)S(1)} %shard_map.91._.refs_0_), channel_id=1, source_target_pairs={{0,2},{1,3},{2,0},{3,1},{4,6},{5,7},{6,4},{7,5},{8,10},{9,11},{10,... | collective-permute-start | bytes 221192 | tf_op jit(solution)/shard_map/ppermute | solution.py:627
  11.8 20.3 %collective-permute-start.8 = (bf16[384,1536]{1,0:T(8,128)(2,1)}, bf16[384,1536]{1,0:T(8,128)(2,1)S(1)}, u32[]{:S(2)}, u32[]{:S(2)}) collective-permute-start(bf16[384,1536]{1,0:T(8,128)(2,1)} %w_own.1), channel_id=1, source_target_pairs={{0,1},{1,0},{2,3},{3,2},{4,5},{5,4},{6,7},{7,6},{8,9},{9,8},{10,11... | collective-permute-start | bytes 3538952 | tf_op jit(solution)/shard_map/ppermute | solution.py:627
  11.8 1.4 %copy-start.1 = (bf16[512,1536]{1,0:T(8,128)(2,1)S(1)}, bf16[512,1536]{1,0:T(8,128)(2,1)}, u32[]{:S(2)}) copy-start(bf16[512,1536]{1,0:T(8,128)(2,1)} %w_sub.1) | copy-start | bytes 4718596
  16.4 6.0 %collective-permute-start.5 = (bf16[3,72,512]{2,1,0:T(8,128)(2,1)S(1)}, bf16[3,72,512]{2,1,0:T(8,128)(2,1)S(1)}, u32[]{:S(2)}, u32[]{:S(2)}) collective-permute-start(bf16[3,72,512]{2,1,0:T(8,128)(2,1)S(1)} %shard_map.93.refs_2_), channel_id=1, source_target_pairs={{0,2},{1,3},{2,0},{3,1},{4,6},{5,7},{6,4},{7,5},{8,10},{9,11},{10,... | collective-permute-start | bytes 663560 | tf_op jit(solution)/shard_map/ppermute | solution.py:627
  18.0 5.7 %collective-permute-start.4 = (bf16[5,72,512]{2,1,0:T(8,128)(2,1)S(1)}, bf16[5,72,512]{2,1,0:T(8,128)(2,1)S(1)}, u32[]{:S(2)}, u32[]{:S(2)}) collective-permute-start(bf16[5,72,512]{2,1,0:T(8,128)(2,1)S(1)} %shard_map.94.refs_0_.stack_ref), channel_id=1, source_target_pairs={{0,1},{1,0},{2,3},{3,2},{4,5},{5,4},{6,7},{7,6},{8,9},{9,8},{10,11... | collective-permute-start | bytes 1105928 | tf_op jit(solution)/shard_map/ppermute | solution.py:627
  22.4 3.4 %collective-permute-start.6 = (bf16[3,72,512]{2,1,0:T(8,128)(2,1)S(1)}, bf16[3,72,512]{2,1,0:T(8,128)(2,1)S(1)}, u32[]{:S(2)}, u32[]{:S(2)}) collective-permute-start(bf16[3,72,512]{2,1,0:T(8,128)(2,1)S(1)} %collective-permute-done.5.refs_2_.stack_ref), channel_id=1, source_target_pairs={{0,1},{1,0},{2,3},{3,2},{4,5},{5,4},{6,7},{7,6},{8,9},{9,8},{10,11... | collective-permute-start | bytes 663560 | tf_op jit(solution)/shard_map/ppermute | solution.py:627
  23.6 2.2 %copy-start.8 = (bf16[512,1152]{1,0:T(8,128)(2,1)S(1)}, bf16[512,1152]{1,0:T(8,128)(2,1)}, u32[]{:S(2)}) copy-start(bf16[512,1152]{1,0:T(8,128)(2,1)} %constant.2.clone.tables_ref.refs_4_) | copy-start | bytes 3538948
  28.4 3.7 %copy-start.2 = (bf16[384,1536]{1,0:T(8,128)(2,1)S(1)}, bf16[384,1536]{1,0:T(8,128)(2,1)}, u32[]{:S(2)}) copy-start(bf16[384,1536]{1,0:T(8,128)(2,1)} %w_own.1) | copy-start | bytes 3538948
  30.6 1.5 %collective-permute-start.7 = (bf16[96,384]{1,0:T(8,128)(2,1)S(1)}, bf16[96,384]{1,0:T(8,128)(2,1)S(1)}, u32[]{:S(2)}, u32[]{:S(2)}) collective-permute-start(bf16[96,384]{1,0:T(8,128)(2,1)S(1)} %get-tuple-element.51), channel_id=1, source_target_pairs={{0,1},{1,0},{2,3},{3,2},{4,5},{5,4},{6,7},{7,6},{8,9},{9,8},{10,11... | collective-permute-start | bytes 221192 | tf_op jit(solution)/shard_map/ppermute | solution.py:627
  32.7 9.3 %collective-permute-start.10 = (bf16[96,1536]{1,0:T(8,128)(2,1)S(1)}, bf16[96,1536]{1,0:T(8,128)(2,1)S(1)}, u32[]{:S(2)}, u32[]{:S(2)}) collective-permute-start(bf16[96,1536]{1,0:T(8,128)(2,1)S(1)} %shard_map.101._), channel_id=1, source_target_pairs={{0,2},{1,3},{2,0},{3,1},{4,6},{5,7},{6,4},{7,5},{8,10},{9,11},{10,... | collective-permute-start | bytes 884744 | tf_op jit(solution)/shard_map/ppermute | solution.py:627
  34.2 2.1 %copy-start.9 = (f32[1536]{0:T(1024)S(1)}, f32[1536]{0:T(1024)}, u32[]{:S(2)}) copy-start(f32[1536]{0:T(1024)} %param.15) | copy-start | bytes 18436
  36.2 1.3 %collective-permute-start.9 = (bf16[96,384]{1,0:T(8,128)(2,1)S(1)}, bf16[96,384]{1,0:T(8,128)(2,1)S(1)}, u32[]{:S(2)}, u32[]{:S(2)}) collective-permute-start(bf16[96,384]{1,0:T(8,128)(2,1)S(1)} %get-tuple-element.58), channel_id=1, source_target_pairs={{0,1},{1,0},{2,3},{3,2},{4,5},{5,4},{6,7},{7,6},{8,9},{9,8},{10,11... | collective-permute-start | bytes 221192 | tf_op jit(solution)/shard_map/ppermute | solution.py:627
  37.5 4.5 %copy-start.4 = (bf16[31,1536]{1,0:T(8,128)(2,1)S(1)}, bf16[31,1536]{1,0:T(8,128)(2,1)}, u32[]{:S(2)}) copy-start(bf16[31,1536]{1,0:T(8,128)(2,1)} %refs_2_.3) | copy-start | bytes 285700

commit v5 on v4

--- a/solution.py
+++ b/solution.py
@@ -20,7 +20,7 @@
 LANES = 128
 HALO = 16
 EXTRA = 8
-FLOPS_PER_MICRO = 1000000000
+FLOPS_PER_MICRO = 2000000000
 TAIL_LINES = 3
 HEAD_LINES = 2
 DIGIT = 128
@@ -95,10 +95,11 @@
     )(*operands)
 
 
-def fetch(after, w_subsample, w_attention):
+def fetch(stacked, w_subsample, w_attention):
     parts, _, width = w_attention.shape
 
-    def kernel(_, w_sub, w_att, out_sub, out_att, sums, sems):
+    def kernel(stack_ref, w_sub, w_att, out_sub, out_att, sums, out_stack, sems):
+        out_stack[...] = stack_ref[...]
         copies = [
             pltpu.make_async_copy(w_att, out_att, sems.at[0]),
             pltpu.make_async_copy(w_sub, out_sub, sems.at[1]),
@@ -115,8 +116,11 @@
     return call(
         kernel,
         [jax.ShapeDtypeStruct(array.shape, array.dtype) for array in (w_subsample, w_attention)]
-        + [jax.ShapeDtypeStruct((8, width), jnp.float32)],
-        (after, w_subsample, w_attention),
+        + [
+            jax.ShapeDtypeStruct((8, width), jnp.float32),
+            jax.ShapeDtypeStruct(stacked.shape, stacked.dtype),
+        ],
+        (stacked, w_subsample, w_attention),
         scratch=[pltpu.SemaphoreType.DMA((2,))],
         remote=2,
     )
@@ -512,7 +516,7 @@
             pltpu.VMEM((pair, width), jnp.bfloat16),
             pltpu.VMEM((pair, rows), jnp.float32),
         ],
-        micros=2.0,
+        micros=1.0,
         vmem=16 + pair * rows * 20 // 1024 // 1024,
     )
 
@@ -569,7 +573,7 @@
             pltpu.VMEM((slots * frames_local, depth), jnp.bfloat16),
             pltpu.VMEM((window, depth), jnp.bfloat16),
         ],
-        micros=1.2,
+        micros=0.6,
     )
 
 
@@ -652,7 +656,7 @@
     starts, ends = segment_start[None, :], segment_end[None, :]
     tables = jnp.asarray(front_tables())
     stacked = log_mel_rows(starts, ends, samples, tables, frames_local)
-    weights = fetch(stacked, w_subsample, w_attention)
+    *weights, kept = fetch(stacked, w_subsample, w_attention)
 
     w_near = exchange(w_output, "mp", bits[-1])
 
@@ -665,7 +669,7 @@
         steps = [sign * d for d in range(1, reach + 1) for sign in (1, -1)]
         moves = [lambda tm, step=step: tm - step for step in steps]
         column = [shifted(stacked, "tm", step) for step in steps]
-    early = [(stacked, [(lambda tm: tm, 0)])]
+    early = [(kept, [(lambda tm: tm, 0)])]
     late = [(assemble(column, weights[-1:]), [(move, 0) for move in moves])]
 
     def across(blocks, bit):
@@ -678,26 +682,24 @@
         early, late = early + across(early, bit), late + across(late, bit)
     ready = early + late[:1]
     joined = (assemble([block for block, _ in ready]), sum([held for _, held in ready], []))
-    groups = [joined] + across([joined], bits[-1]) + late[1:] + across(late[1:], bits[-1])
+    groups = [joined] + across([joined], bits[-1])
+    projected = [
+        project_rows(block, weights, frames_local, len(early)) for block, _ in groups
+    ]
+    done = [group[-1] for group in projected]
+    late = [(assemble([block], done), held) for block, held in late[1:]]
+    groups += late + across(late, bits[-1])
     stacks, held = zip(*groups)
     places = sum(held, [])
     joined_slots = range(len(joined[1]), 2 * len(joined[1]))
     query_slots = [*range(len(early)), *joined_slots[: len(early)]]
     fixed, bounds = boundary_rows(places, starts, ends, stacks, tables, frames_local)
-    projected = [
-        project_rows(block, weights, frames_local, len(early) if number < 2 else 0)
-        for number, block in enumerate(stacks[:-1])
-    ]
-    boundary = (places, stacks, fixed)
-    if len(stacks) > 2:
-        outs = project_rows(stacks[-1], weights, frames_local, 0, boundary)
-    else:
-        query, *outs = project_rows(stacks[-1], weights, frames_local, len(early), boundary)
-        projected.append([query])
+    projected += [project_rows(block, weights, frames_local, 0) for block in stacks[2:-1]]
+    outs = project_rows(stacks[-1], weights, frames_local, 0, (places, stacks, fixed))
     extras = (outs[0], outs[2], outs[4])
     queries = [group[0] for group in projected[:2]]
-    keys = [*(group[-2] for group in projected if len(group) > 1), outs[1]]
-    values = [*(group[-1] for group in projected if len(group) > 1), outs[3]]
+    keys = [*(group[-2] for group in projected), outs[1]]
+    values = [*(group[-1] for group in projected), outs[3]]
 
     far = list(range(2, parts, 2))
     outs = attend_far(

time: 44.4 us -> 42.5 us (0.957)
  local copies, waits for them, and re-layouts: 4.98 us -> 3.59 us
  waiting for transfers between devices: 9.85 us -> 9.38 us
    unnamed x20 -> x24, local copies, waits for them, and re-layouts: 4.97 us -> 3.58 us
    ppermute x11, waiting for transfers between devices: 9.85 us -> 9.38 us  [exchange(): lax.ppermute(block, axis, [(i, i ^ bit) for i in range(lax.axis_size(axis...]
    pallas_call x14 -> x15, Pallas kernels: 17.9 us -> 17.9 us  [call(): pl.pallas_call(kernel, out_shape=out_shape, in_specs=specs, out_specs=jax...]
  transfers between devices with their start and end apart: 11 -> 11, of which waited for: 6 -> 5; matrix products, arithmetic and copies ran while one was open for 0% -> 0% of each run, Pallas kernels for 32% -> 34%
where the time goes in v5:
time: 42.5 us; the launch traced here: 42.3 us
  Pallas kernels  17.9 us (42%)
  starting transfers between devices  11.3 us (27%)
  waiting for transfers between devices  9.38 us (22%)
  local copies, waits for them, and re-layouts  3.59 us (8%)
    pallas_call x15, Pallas kernels, call(): pl.pallas_call(kernel, out_shape=out_shape, in_specs=specs, out_specs=jax...  17.9 us
    ppermute x11, starting transfers between devices, exchange(): lax.ppermute(block, axis, [(i, i ^ bit) for i in range(lax.axis_size(axis...  11.3 us
    ppermute x11, waiting for transfers between devices, exchange(): lax.ppermute(block, axis, [(i, i ^ bit) for i in range(lax.axis_size(axis...  9.38 us
    unnamed x24, local copies, waits for them, and re-layouts  3.58 us
  transfers between devices with their start and end apart: 11, of which 5 were waited for; matrix products, arithmetic and copies ran while one was open for 0% of the time, Pallas kernels for 34%

profile of v5, /device:TPU:0, one launch (start us, length us, event | category | flops | bytes accessed | tf_op | source)
XLA Modules:
  0.0 42.3 jit_solution(9168365116437756715)
XLA Ops:
  0.0 0.9 %copy-done.3 = f32[40960]{0:T(1024)S(1)} copy-done((f32[40960]{0:T(1024)S(1)}, f32[40960]{0:T(1024)}, u32[]{:S(2)}) %copy-start.3) | copy-done | bytes 163864
  0.9 0.7 %copy-done.5 = s32[256]{0:T(256)S(1)} copy-done((s32[256]{0:T(256)S(1)}, s32[256]{0:T(256)}, u32[]{:S(2)}) %copy-start.5) | copy-done | bytes 1048
  1.6 0.7 %copy-done.7 = s32[256]{0:T(256)S(1)} copy-done((s32[256]{0:T(256)S(1)}, s32[256]{0:T(256)}, u32[]{:S(2)}) %copy-start.7) | copy-done | bytes 1048
  2.3 1.3 %copy-done.9 = bf16[512,1152]{1,0:T(8,128)(2,1)S(1)} copy-done((bf16[512,1152]{1,0:T(8,128)(2,1)S(1)}, bf16[512,1152]{1,0:T(8,128)(2,1)}, u32[]{:S(2)}) %copy-start.9) | copy-done | bytes 1179672
  3.6 0.9 %shard_map.91.stack_ref = bf16[1,72,512]{2,1,0:T(8,128)(2,1)S(1)} custom-call(s32[1,256]{1,0:T(1,128)S(1)} %bitcast.4, s32[1,256]{1,0:T(1,128)S(1)} %bitcast.6, f32[320,128]{1,0:T(8,128)S(1)} %bitcast.3, bf16[512,1152]{1,0:T(8,128)(2,1)S(1)} %copy-done.9), custom_call_target="tpu_custom_call" | custom-call | flops 2000000000 | bytes 1000000 | tf_op jit(solution)/shard_map/pallas_call | solution.py:85
  4.4 0.0 copy-start
  4.5 3.1 %collective-permute-start.1 = (bf16[1,72,512]{2,1,0:T(8,128)(2,1)S(1)}, bf16[1,72,512]{2,1,0:T(8,128)(2,1)S(1)}, u32[]{:S(2)}, u32[]{:S(2)}) collective-permute-start(bf16[1,72,512]{2,1,0:T(8,128)(2,1)S(1)} %shard_map.91.stack_ref), channel_id=1, source_target_pairs={{0,4},{4,0},{8,12},{12,8},{1,5},{5,1},{9,13},{13,9},{2,6},{6,2},{1... | collective-permute-start | bytes 221192 | tf_op jit(solution)/shard_map/ppermute | solution.py:631
  7.5 2.6 %collective-permute-start.2 = (bf16[1,72,512]{2,1,0:T(8,128)(2,1)S(1)}, bf16[1,72,512]{2,1,0:T(8,128)(2,1)S(1)}, u32[]{:S(2)}, u32[]{:S(2)}) collective-permute-start(bf16[1,72,512]{2,1,0:T(8,128)(2,1)S(1)} %shard_map.91.stack_ref), channel_id=1, source_target_pairs={{0,8},{4,12},{8,0},{12,4},{1,9},{5,13},{9,1},{13,5},{2,10},{6,14},... | collective-permute-start | bytes 221192 | tf_op jit(solution)/shard_map/ppermute | solution.py:631
  10.1 0.0 collective-permute-start.3
  10.1 0.0 copy-done.1
  10.1 0.0 copy-done.2
  10.1 1.2 %shard_map.92 = (bf16[512,1536]{1,0:T(8,128)(2,1)S(1)}, bf16[3,1536,384]{2,1,0:T(8,128)(2,1)S(1)}, f32[8,384]{1,0:T(8,128)S(1)}, bf16[1,72,512]{2,1,0:T(8,128)(2,1)S(1)}) custom-call(bf16[1,72,512]{2,1,0:T(8,128)(2,1)S(1)} %shard_map.91.stack_ref, bf16[512,1536]{1,0:T(8,128)(2,1)S(1)} %copy-done.2, bf16[3,1536,384]{2,1,0:T(8,128)(2,1)S(1)} %copy-done.1), custom_call_target="tpu_custom_call" | custom-call | flops 2000000000 | bytes 1000000 | tf_op jit(solution)/shard_map/pallas_call | solution.py:85
  11.3 1.8 %collective-permute-start = (bf16[1,72,512]{2,1,0:T(8,128)(2,1)S(1)}, bf16[1,72,512]{2,1,0:T(8,128)(2,1)S(1)}, u32[]{:S(2)}, u32[]{:S(2)}) collective-permute-start(bf16[1,72,512]{2,1,0:T(8,128)(2,1)S(1)} %get-tuple-element.33.refs_0_), channel_id=1, source_target_pairs={{0,2},{1,3},{2,0},{3,1},{4,6},{5,7},{6,4},{7,5},{8,10},{9,11},{10,... | collective-permute-start | bytes 221192 | tf_op jit(solution)/shard_map/ppermute | solution.py:631
  13.1 0.0 copy-done
  13.1 0.0 collective-permute-start.8
  13.1 0.0 collective-permute-done.1.refs_0_
  13.1 2.2 %collective-permute-done.2.refs_1_ = bf16[1,72,512]{2,1,0:T(8,128)(2,1)S(1)} collective-permute-done((bf16[1,72,512]{2,1,0:T(8,128)(2,1)S(1)}, bf16[1,72,512]{2,1,0:T(8,128)(2,1)S(1)}, u32[]{:S(2)}, u32[]{:S(2)}) %collective-permute-start.2) | collective-permute-done | bytes 73760 | tf_op jit(solution)/shard_map/ppermute | solution.py:631
  15.3 1.1 %collective-permute-done.3.refs_2_ = bf16[1,72,512]{2,1,0:T(8,128)(2,1)S(1)} collective-permute-done((bf16[1,72,512]{2,1,0:T(8,128)(2,1)S(1)}, bf16[1,72,512]{2,1,0:T(8,128)(2,1)S(1)}, u32[]{:S(2)}, u32[]{:S(2)}) %collective-permute-start.3) | collective-permute-done | bytes 73760 | tf_op jit(solution)/shard_map/ppermute | solution.py:631
  16.4 1.6 %collective-permute-start.5 = (bf16[3,72,512]{2,1,0:T(8,128)(2,1)S(1)}, bf16[3,72,512]{2,1,0:T(8,128)(2,1)S(1)}, u32[]{:S(2)}, u32[]{:S(2)}) collective-permute-start(bf16[3,72,512]{2,1,0:T(8,128)(2,1)S(1)} %shard_map.93.refs_2_), channel_id=1, source_target_pairs={{0,2},{1,3},{2,0},{3,1},{4,6},{5,7},{6,4},{7,5},{8,10},{9,11},{10,... | collective-permute-start | bytes 663560 | tf_op jit(solution)/shard_map/ppermute | solution.py:631
  18.0 0.0 collective-permute-done.refs_1_
  18.0 0.1 collective-permute-start.4
  18.1 2.2 %shard_map.95 = (bf16[128,384]{1,0:T(8,128)(2,1)S(1)}, bf16[320,384]{1,0:T(8,128)(2,1)S(1)}, bf16[320,384]{1,0:T(8,128)(2,1)S(1)}) custom-call(bf16[5,72,512]{2,1,0:T(8,128)(2,1)S(1)} %shard_map.94.stack_ref.refs_0_, bf16[512,1536]{1,0:T(8,128)(2,1)S(1)} %get-tuple-element.35.w_sub.refs_5_, bf16[3,1536,384]{2,1,0:T(8,128)(2,1)S(1)} %get-tuple-element.36.w_att, ...), custom_call_target="tpu_custom_call" | custom-call | flops 4840000000 | bytes 1000000 | tf_op jit(solution)/shard_map/pallas_call | solution.py:85
  20.2 0.0 collective-permute-done.4.stack_ref.refs_1_
  20.3 2.2 %shard_map.96 = (bf16[128,384]{1,0:T(8,128)(2,1)S(1)}, bf16[320,384]{1,0:T(8,128)(2,1)S(1)}, bf16[320,384]{1,0:T(8,128)(2,1)S(1)}) custom-call(bf16[5,72,512]{2,1,0:T(8,128)(2,1)S(1)} %collective-permute-done.4.stack_ref.refs_1_, bf16[512,1536]{1,0:T(8,128)(2,1)S(1)} %get-tuple-element.35.w_sub.refs_5_, bf16[3,1536,384]{2,1,0:T(8,128)(2,1)S(1)} %get-tuple-element.36.w_att, ...), custom_call_target="tpu_custom_call" | custom-call | flops 4840000000 | bytes 1000000 | tf_op jit(solution)/shard_map/pallas_call | solution.py:85
  22.4 0.0 collective-permute-done.5.refs_0_
  22.5 0.0 copy-start.6
  22.5 0.0 copy-start.8
  22.5 0.0 copy-start.10
  22.5 0.6 %collective-permute-start.6 = (bf16[3,72,512]{2,1,0:T(8,128)(2,1)S(1)}, bf16[3,72,512]{2,1,0:T(8,128)(2,1)S(1)}, u32[]{:S(2)}, u32[]{:S(2)}) collective-permute-start(bf16[3,72,512]{2,1,0:T(8,128)(2,1)S(1)} %shard_map.97.refs_2_.stack_ref), channel_id=1, source_target_pairs={{0,1},{1,0},{2,3},{3,2},{4,5},{5,4},{6,7},{7,6},{8,9},{9,8},{10,11... | collective-permute-start | bytes 663560 | tf_op jit(solution)/shard_map/ppermute | solution.py:631
  23.0 1.2 %shard_map.99 = (bf16[192,384]{1,0:T(8,128)(2,1)S(1)}, bf16[192,384]{1,0:T(8,128)(2,1)S(1)}) custom-call(bf16[3,72,512]{2,1,0:T(8,128)(2,1)S(1)} %shard_map.97.refs_2_.stack_ref, bf16[512,1536]{1,0:T(8,128)(2,1)S(1)} %get-tuple-element.35.w_sub.refs_5_, bf16[3,1536,384]{2,1,0:T(8,128)(2,1)S(1)} %get-tuple-element.36.w_att, ...), custom_call_target="tpu_custom_call" | custom-call | flops 3304000000 | bytes 1000000 | tf_op jit(solution)/shard_map/pallas_call | solution.py:85
  24.3 0.0 collective-permute-done.6.refs_3_.stack_ref
  24.3 0.0 copy-done.6
  24.3 0.0 copy-done.8
  24.3 0.0 copy-done.10
  24.3 0.8 %shard_map.98 = (bf16[16,256]{1,0:T(8,128)(2,1)S(1)}, f32[2,288]{1,0:T(2,128)S(1)}) custom-call(s32[1,256]{1,0:T(1,128)S(1)} %bitcast.5, s32[1,256]{1,0:T(1,128)S(1)} %bitcast.7, bf16[5,72,512]{2,1,0:T(8,128)(2,1)S(1)} %shard_map.94.stack_ref.refs_0_, bf16[5,72,512]{2,1,0:T(8,128)(2,1)S(1)} %collective-permute-done.4.stack_ref.refs_1_, ...), custom_call_target="tpu_custom_call" | custom-call | flops 1800000000 | bytes 1000000 | tf_op jit(solution)/shard_map/pallas_call | solution.py:85
  25.2 1.7 %shard_map.100 = (bf16[48,384]{1,0:T(8,128)(2,1)S(1)}, bf16[192,384]{1,0:T(8,128)(2,1)S(1)}, bf16[48,384]{1,0:T(8,128)(2,1)S(1)}, bf16[192,384]{1,0:T(8,128)(2,1)S(1)}, bf16[48,384]{1,0:T(8,128)(2,1)S(1)}) custom-call(bf16[3,72,512]{2,1,0:T(8,128)(2,1)S(1)} %collective-permute-done.6.refs_3_.stack_ref, ...), custom_call_target="tpu_custom_call" | custom-call | flops 3880000000 | bytes 1000000 | tf_op jit(solution)/shard_map/pallas_call | solution.py:85
  26.9 2.2 %shard_map.101 = (bf16[96,384]{1,0:T(8,128)(2,1)S(1)}, bf16[96,384]{1,0:T(8,128)(2,1)S(1)}, bf16[288,384]{1,0:T(8,128)(2,1)S(1)}, bf16[1024,384]{1,0:T(8,128)(2,...) custom-call(f32[2,288]{1,0:T(2,128)S(1)} %get-tuple-element.39.bound_ref, ...), custom_call_target="tpu_custom_call" | custom-call | flops 5000000000 | bytes 1000000 | tf_op jit(solution)/shard_map/pallas_call | solution.py:85
  29.1 0.3 collective-permute-start.7
  29.3 1.1 %collective-permute-done.7.refs_1_ = bf16[96,384]{1,0:T(8,128)(2,1)S(1)} collective-permute-done((bf16[96,384]{1,0:T(8,128)(2,1)S(1)}, bf16[96,384]{1,0:T(8,128)(2,1)S(1)}, u32[]{:S(2)}, u32[]{:S(2)}) %collective-permute-start.7) | collective-permute-done | bytes 73760 | tf_op jit(solution)/shard_map/ppermute | solution.py:631
  30.4 0.0 collective-permute-done.8.refs_3_.w_near
  30.4 0.5 %shard_map.102._ = bf16[96,1536]{1,0:T(8,128)(2,1)S(1)} custom-call(bf16[96,384]{1,0:T(8,128)(2,1)S(1)} %get-tuple-element.52.refs_0_, bf16[96,384]{1,0:T(8,128)(2,1)S(1)} %collective-permute-done.7.refs_1_, bf16[384,1536]{1,0:T(8,128)(2,1)S(1)} %copy-done, bf16[384,1536]{1,0:T(8,128)(2,1)S(1)} %collective-permute-done.8.refs_3_.w_near), custom_call_target="tpu_custom_call" | custom-call | flops 1800000000 | bytes 1000000 | tf_op jit(solution)/shard_map/pallas_call | solution.py:85
  30.9 1.2 %collective-permute-start.10 = (bf16[96,1536]{1,0:T(8,128)(2,1)S(1)}, bf16[96,1536]{1,0:T(8,128)(2,1)S(1)}, u32[]{:S(2)}, u32[]{:S(2)}) collective-permute-start(bf16[96,1536]{1,0:T(8,128)(2,1)S(1)} %shard_map.102._), channel_id=1, source_target_pairs={{0,2},{1,3},{2,0},{3,1},{4,6},{5,7},{6,4},{7,5},{8,10},{9,11},{10,... | collective-permute-start | bytes 884744 | tf_op jit(solution)/shard_map/ppermute | solution.py:631
  32.2 1.9 %shard_map.103 = (bf16[96,384]{1,0:T(8,128)(2,1)S(1)}, bf16[96,384]{1,0:T(8,128)(2,1)S(1)}) custom-call(bf16[96,1536]{1,0:T(8,128)(2,1)S(1)} %shard_map.102._, bf16[288,384]{1,0:T(8,128)(2,1)S(1)} %get-tuple-element.54.q_ref, bf16[1024,384]{1,0:T(8,128)(2,1)S(1)} %get-tuple-element.55.k_ref, bf16[1024,384]{1,0:T(8,128)(2,1)S(1)} %get-tuple-element.56.v_ref, ...), custom_call_target="tpu_custom_call" | custom-call | flops 2000000000 | bytes 1000000 | tf_op jit(solution)/shard_map/pallas_call | solution.py:85
  34.1 0.1 collective-permute-start.9
  34.2 1.2 %collective-permute-done.9.near = bf16[96,384]{1,0:T(8,128)(2,1)S(1)} collective-permute-done((bf16[96,384]{1,0:T(8,128)(2,1)S(1)}, bf16[96,384]{1,0:T(8,128)(2,1)S(1)}, u32[]{:S(2)}, u32[]{:S(2)}) %collective-permute-start.9) | collective-permute-done | bytes 73760 | tf_op jit(solution)/shard_map/ppermute | solution.py:631
  35.5 0.9 %shard_map.104.base_ref = f32[96,1536]{1,0:T(8,128)S(1)} custom-call(bf16[96,384]{1,0:T(8,128)(2,1)S(1)} %get-tuple-element.59.own, bf16[96,384]{1,0:T(8,128)(2,1)S(1)} %collective-permute-done.9.near, bf16[384,1536]{1,0:T(8,128)(2,1)S(1)} %copy-done, bf16[384,1536]{1,0:T(8,128)(2,1)S(1)} %collective-permute-done.8.refs_3_.w_near, ...), custom_call_target="tpu_custom_call" | custom-call | flops 1200000000 | bytes 1000000 | tf_op jit(solution)/shard_map/pallas_call | solution.py:85
  36.3 3.8 %collective-permute-done.10.refs_0_ = bf16[96,1536]{1,0:T(8,128)(2,1)S(1)} collective-permute-done((bf16[96,1536]{1,0:T(8,128)(2,1)S(1)}, bf16[96,1536]{1,0:T(8,128)(2,1)S(1)}, u32[]{:S(2)}, u32[]{:S(2)}) %collective-permute-start.10) | collective-permute-done | bytes 294944 | tf_op jit(solution)/shard_map/ppermute | solution.py:631
  40.1 2.2 %shard_map.105 = bf16[64,1536]{1,0:T(8,128)(2,1)} custom-call(f32[96,1536]{1,0:T(8,128)S(1)} %shard_map.104.base_ref, bf16[96,1536]{1,0:T(8,128)(2,1)S(1)} %collective-permute-done.10.refs_0_, f32[1,1536]{1,0:T(1,128)S(1)} %broadcast_in_dim.11.refs_1_, bf16[31,1536]{1,0:T(8,128)(2,1)S(1)} %copy-done.4), custom_call_target="tpu_custom_call" | custom-call | flops 5600000000 | bytes 1000000 | tf_op jit(solution)/shard_map/pallas_call | solution.py:85
  (14 shorter events, 0.1 us)
Async XLA Ops:
  0.0 0.9 %copy-start.3 = (f32[40960]{0:T(1024)S(1)}, f32[40960]{0:T(1024)}, u32[]{:S(2)}) copy-start(f32[40960]{0:T(1024)} %param.9) | copy-start | bytes 491524
  0.9 0.7 %copy-start.5 = (s32[256]{0:T(256)S(1)}, s32[256]{0:T(256)}, u32[]{:S(2)}) copy-start(s32[256]{0:T(256)} %param.10) | copy-start | bytes 3076
  1.6 0.7 %copy-start.7 = (s32[256]{0:T(256)S(1)}, s32[256]{0:T(256)}, u32[]{:S(2)}) copy-start(s32[256]{0:T(256)} %param.11) | copy-start | bytes 3076
  2.3 1.3 %copy-start.9 = (bf16[512,1152]{1,0:T(8,128)(2,1)S(1)}, bf16[512,1152]{1,0:T(8,128)(2,1)}, u32[]{:S(2)}) copy-start(bf16[512,1152]{1,0:T(8,128)(2,1)} %constant.2.clone.tables_ref.refs_4_) | copy-start | bytes 3538948
  3.5 6.6 %copy-start.1 = (bf16[3,1536,384]{2,1,0:T(8,128)(2,1)S(1)}, bf16[3,1536,384]{2,1,0:T(8,128)(2,1)}, u32[]{:S(2)}) copy-start(bf16[3,1536,384]{2,1,0:T(8,128)(2,1)} %w_att.1) | copy-start | bytes 10616836
  3.5 6.6 %copy-start.2 = (bf16[512,1536]{1,0:T(8,128)(2,1)S(1)}, bf16[512,1536]{1,0:T(8,128)(2,1)}, u32[]{:S(2)}) copy-start(bf16[512,1536]{1,0:T(8,128)(2,1)} %w_sub.1) | copy-start | bytes 4718596
  4.4 8.6 %copy-start = (bf16[384,1536]{1,0:T(8,128)(2,1)S(1)}, bf16[384,1536]{1,0:T(8,128)(2,1)}, u32[]{:S(2)}) copy-start(bf16[384,1536]{1,0:T(8,128)(2,1)} %w_own.1) | copy-start | bytes 3538948
  4.5 8.6 %collective-permute-start.1 = (bf16[1,72,512]{2,1,0:T(8,128)(2,1)S(1)}, bf16[1,72,512]{2,1,0:T(8,128)(2,1)S(1)}, u32[]{:S(2)}, u32[]{:S(2)}) collective-permute-start(bf16[1,72,512]{2,1,0:T(8,128)(2,1)S(1)} %shard_map.91.stack_ref), channel_id=1, source_target_pairs={{0,4},{4,0},{8,12},{12,8},{1,5},{5,1},{9,13},{13,9},{2,6},{6,2},{1... | collective-permute-start | bytes 221192 | tf_op jit(solution)/shard_map/ppermute | solution.py:631
  7.5 7.8 %collective-permute-start.2 = (bf16[1,72,512]{2,1,0:T(8,128)(2,1)S(1)}, bf16[1,72,512]{2,1,0:T(8,128)(2,1)S(1)}, u32[]{:S(2)}, u32[]{:S(2)}) collective-permute-start(bf16[1,72,512]{2,1,0:T(8,128)(2,1)S(1)} %shard_map.91.stack_ref), channel_id=1, source_target_pairs={{0,8},{4,12},{8,0},{12,4},{1,9},{5,13},{9,1},{13,5},{2,10},{6,14},... | collective-permute-start | bytes 221192 | tf_op jit(solution)/shard_map/ppermute | solution.py:631
  10.1 6.3 %collective-permute-start.3 = (bf16[1,72,512]{2,1,0:T(8,128)(2,1)S(1)}, bf16[1,72,512]{2,1,0:T(8,128)(2,1)S(1)}, u32[]{:S(2)}, u32[]{:S(2)}) collective-permute-start(bf16[1,72,512]{2,1,0:T(8,128)(2,1)S(1)} %shard_map.91.stack_ref), channel_id=1, source_target_pairs={{0,12},{4,8},{8,4},{12,0},{1,13},{5,9},{9,5},{13,1},{2,14},{6,10},... | collective-permute-start | bytes 221192 | tf_op jit(solution)/shard_map/ppermute | solution.py:631
  11.3 6.7 %collective-permute-start = (bf16[1,72,512]{2,1,0:T(8,128)(2,1)S(1)}, bf16[1,72,512]{2,1,0:T(8,128)(2,1)S(1)}, u32[]{:S(2)}, u32[]{:S(2)}) collective-permute-start(bf16[1,72,512]{2,1,0:T(8,128)(2,1)S(1)} %get-tuple-element.33.refs_0_), channel_id=1, source_target_pairs={{0,2},{1,3},{2,0},{3,1},{4,6},{5,7},{6,4},{7,5},{8,10},{9,11},{10,... | collective-permute-start | bytes 221192 | tf_op jit(solution)/shard_map/ppermute | solution.py:631
  13.1 17.3 %collective-permute-start.8 = (bf16[384,1536]{1,0:T(8,128)(2,1)S(1)}, bf16[384,1536]{1,0:T(8,128)(2,1)S(1)}, u32[]{:S(2)}, u32[]{:S(2)}) collective-permute-start(bf16[384,1536]{1,0:T(8,128)(2,1)S(1)} %copy-done), channel_id=1, source_target_pairs={{0,1},{1,0},{2,3},{3,2},{4,5},{5,4},{6,7},{7,6},{8,9},{9,8},{10,11... | collective-permute-start | bytes 3538952 | tf_op jit(solution)/shard_map/ppermute | solution.py:631
  16.4 6.0 %collective-permute-start.5 = (bf16[3,72,512]{2,1,0:T(8,128)(2,1)S(1)}, bf16[3,72,512]{2,1,0:T(8,128)(2,1)S(1)}, u32[]{:S(2)}, u32[]{:S(2)}) collective-permute-start(bf16[3,72,512]{2,1,0:T(8,128)(2,1)S(1)} %shard_map.93.refs_2_), channel_id=1, source_target_pairs={{0,2},{1,3},{2,0},{3,1},{4,6},{5,7},{6,4},{7,5},{8,10},{9,11},{10,... | collective-permute-start | bytes 663560 | tf_op jit(solution)/shard_map/ppermute | solution.py:631
  18.0 2.2 %collective-permute-start.4 = (bf16[5,72,512]{2,1,0:T(8,128)(2,1)S(1)}, bf16[5,72,512]{2,1,0:T(8,128)(2,1)S(1)}, u32[]{:S(2)}, u32[]{:S(2)}) collective-permute-start(bf16[5,72,512]{2,1,0:T(8,128)(2,1)S(1)} %shard_map.94.stack_ref.refs_0_), channel_id=1, source_target_pairs={{0,1},{1,0},{2,3},{3,2},{4,5},{5,4},{6,7},{7,6},{8,9},{9,8},{10,11... | collective-permute-start | bytes 1105928 | tf_op jit(solution)/shard_map/ppermute | solution.py:631
  22.5 1.8 %copy-start.6 = (s32[256]{0:T(256)S(1)}, s32[256]{0:T(256)}, u32[]{:S(2)}) copy-start(s32[256]{0:T(256)} %param.10) | copy-start | bytes 3076
  22.5 1.8 %copy-start.8 = (s32[256]{0:T(256)S(1)}, s32[256]{0:T(256)}, u32[]{:S(2)}) copy-start(s32[256]{0:T(256)} %param.11) | copy-start | bytes 3076
  22.5 1.8 %copy-start.10 = (bf16[512,1152]{1,0:T(8,128)(2,1)S(1)}, bf16[512,1152]{1,0:T(8,128)(2,1)}, u32[]{:S(2)}) copy-start(bf16[512,1152]{1,0:T(8,128)(2,1)} %constant.2.clone.tables_ref.refs_4_) | copy-start | bytes 3538948
  22.5 1.8 %collective-permute-start.6 = (bf16[3,72,512]{2,1,0:T(8,128)(2,1)S(1)}, bf16[3,72,512]{2,1,0:T(8,128)(2,1)S(1)}, u32[]{:S(2)}, u32[]{:S(2)}) collective-permute-start(bf16[3,72,512]{2,1,0:T(8,128)(2,1)S(1)} %shard_map.97.refs_2_.stack_ref), channel_id=1, source_target_pairs={{0,1},{1,0},{2,3},{3,2},{4,5},{5,4},{6,7},{7,6},{8,9},{9,8},{10,11... | collective-permute-start | bytes 663560 | tf_op jit(solution)/shard_map/ppermute | solution.py:631
  29.1 1.3 %collective-permute-start.7 = (bf16[96,384]{1,0:T(8,128)(2,1)S(1)}, bf16[96,384]{1,0:T(8,128)(2,1)S(1)}, u32[]{:S(2)}, u32[]{:S(2)}) collective-permute-start(bf16[96,384]{1,0:T(8,128)(2,1)S(1)} %get-tuple-element.53), channel_id=1, source_target_pairs={{0,1},{1,0},{2,3},{3,2},{4,5},{5,4},{6,7},{7,6},{8,9},{9,8},{10,11... | collective-permute-start | bytes 221192 | tf_op jit(solution)/shard_map/ppermute | solution.py:631
  30.9 9.2 %collective-permute-start.10 = (bf16[96,1536]{1,0:T(8,128)(2,1)S(1)}, bf16[96,1536]{1,0:T(8,128)(2,1)S(1)}, u32[]{:S(2)}, u32[]{:S(2)}) collective-permute-start(bf16[96,1536]{1,0:T(8,128)(2,1)S(1)} %shard_map.102._), channel_id=1, source_target_pairs={{0,2},{1,3},{2,0},{3,1},{4,6},{5,7},{6,4},{7,5},{8,10},{9,11},{10,... | collective-permute-start | bytes 884744 | tf_op jit(solution)/shard_map/ppermute | solution.py:631
  32.2 2.0 %copy-start.11 = (f32[1536]{0:T(1024)S(1)}, f32[1536]{0:T(1024)}, u32[]{:S(2)}) copy-start(f32[1536]{0:T(1024)} %param.15) | copy-start | bytes 18436
  34.1 1.3 %collective-permute-start.9 = (bf16[96,384]{1,0:T(8,128)(2,1)S(1)}, bf16[96,384]{1,0:T(8,128)(2,1)S(1)}, u32[]{:S(2)}, u32[]{:S(2)}) collective-permute-start(bf16[96,384]{1,0:T(8,128)(2,1)S(1)} %get-tuple-element.60), channel_id=1, source_target_pairs={{0,1},{1,0},{2,3},{3,2},{4,5},{5,4},{6,7},{7,6},{8,9},{9,8},{10,11... | collective-permute-start | bytes 221192 | tf_op jit(solution)/shard_map/ppermute | solution.py:631
  35.5 4.7 %copy-start.4 = (bf16[31,1536]{1,0:T(8,128)(2,1)S(1)}, bf16[31,1536]{1,0:T(8,128)(2,1)}, u32[]{:S(2)}) copy-start(bf16[31,1536]{1,0:T(8,128)(2,1)} %refs_2_.3) | copy-start | bytes 285700

commit v6 on v5

--- a/solution.py
+++ b/solution.py
@@ -69,7 +69,9 @@
 def dot_split(values, table_high, table_low):
     high = values.astype(jnp.bfloat16)
     low = (values - high.astype(jnp.float32)).astype(jnp.bfloat16)
-    return dot32(high, table_high) + (dot32(low, table_high) + dot32(high, table_low))
+    table = table_high()
+    large, small = dot32(high, table), dot32(low, table)
+    return large + (small + dot32(high, table_low()))
 
 
 def normalize(values):
@@ -79,14 +81,16 @@
     return shifted * lax.rsqrt(spread + 1e-05)
 
 
-def call(kernel, out_shape, operands, scratch=(), micros=1.0, remote=0, vmem=16):
+def call(
+    kernel, out_shape, operands, scratch=(), micros=1.0, remote=0, vmem=16, result=pltpu.VMEM
+):
     specs = [pl.BlockSpec(memory_space=pltpu.VMEM)] * (len(operands) - remote)
     specs += [pl.BlockSpec(memory_space=pltpu.HBM)] * remote
     return pl.pallas_call(
         kernel,
         out_shape=out_shape,
         in_specs=specs,
-        out_specs=jax.tree.map(lambda _: pl.BlockSpec(memory_space=pltpu.VMEM), out_shape),
+        out_specs=jax.tree.map(lambda _: pl.BlockSpec(memory_space=result), out_shape),
         scratch_shapes=list(scratch),
         compiler_params=pltpu.CompilerParams(vmem_limit_bytes=vmem * 1024 * 1024),
         cost_estimate=pl.CostEstimate(
@@ -130,20 +134,48 @@
     return jnp.concatenate([row, jnp.zeros((1, SUB * NMEL - row.shape[1]), row.dtype)], axis=1)
 
 
-def log_mel(windows, tables):
+def log_mel(windows, tables, copies=()):
     wide, bank = 2 * BINS, slice(4 * BINS, 4 * BINS + NMEL)
-    spectrum = dot_split(windows, tables[:, 0:wide], tables[:, wide : 2 * wide])
+
+    def fetched(number, rows, columns):
+        def load():
+            if copies:
+                copies[number].wait()
+            return tables[rows, columns]
+
+        return load
+
+    every = slice(None)
+    spectrum = dot_split(
+        windows, fetched(0, every, slice(0, wide)), fetched(1, every, slice(wide, 2 * wide))
+    )
     power = jnp.square(spectrum[:, :BINS]) + jnp.square(spectrum[:, BINS:])
-    return jnp.log(dot_split(power, tables[0:BINS, bank], tables[BINS:, bank]) + 1e-06)
+    bank_high = fetched(2, slice(0, BINS), bank)
+    return jnp.log(dot_split(power, bank_high, lambda: tables[BINS:, bank]) + 1e-06)
 
 
 def log_mel_rows(starts, ends, samples, tables, frames_local):
     rows = frames_local * FRAME_ROWS
     frames_shard = starts.shape[1]
 
-    def kernel(start_ref, end_ref, wave, tables_ref, out, held):
-        held[0:rows, :] = wave[...]
+    wide = 2 * BINS
+    spans = (slice(0, wide), slice(wide, 2 * wide), slice(2 * wide, tables.shape[1]))
+
+    def kernel(start, end, wave, table, out, held, start_ref, end_ref, tables_ref, sems):
+        pairs = (
+            (wave, held.at[pl.ds(0, rows)]),
+            (start, start_ref),
+            (end, end_ref),
+        ) + tuple((table.at[:, span], tables_ref.at[:, span]) for span in spans)
+        copies = [
+            pltpu.make_async_copy(source, target, sems.at[slot])
+            for slot, (source, target) in enumerate(pairs)
+        ]
+        for copy in copies:
+            copy.start()
         held[rows : rows + 8, :] = jnp.zeros((8, LANES), jnp.float32)
+        for copy in copies[:3]:
+            copy.wait()
         lines = [held[pl.ds(j, frames_local, stride=FRAME_ROWS), :] for j in range(FRAME_ROWS + 2)]
         windows = []
         for sub in range(SUB):
@@ -161,7 +193,7 @@
             low = edge - high * DIGIT
             extras += [padded_row(digit.astype(jnp.float32)) for digit in (high, low)]
         out[0, frames_local:, :] = jnp.concatenate(extras, axis=0).astype(jnp.bfloat16)
-        mel = log_mel(jnp.concatenate(windows, axis=0), tables_ref)
+        mel = log_mel(jnp.concatenate(windows, axis=0), tables_ref, copies[3:])
         for sub in range(SUB):
             out[0, 0:frames_local, sub * NMEL : (sub + 1) * NMEL] = mel[
                 sub * frames_local : (sub + 1) * frames_local
@@ -171,7 +203,15 @@
         kernel,
         jax.ShapeDtypeStruct((1, frames_local + EXTRA, SUB * NMEL), jnp.bfloat16),
         (starts, ends, samples, tables),
-        scratch=[pltpu.VMEM((rows + 8, LANES), jnp.float32)],
+        scratch=[
+            pltpu.VMEM((rows + 8, LANES), jnp.float32),
+            pltpu.VMEM(starts.shape, starts.dtype),
+            pltpu.VMEM(ends.shape, ends.dtype),
+            pltpu.VMEM(tables.shape, tables.dtype),
+            pltpu.SemaphoreType.DMA((6,)),
+        ],
+        remote=4,
+        vmem=54,
         micros=1.0,
     )
 
@@ -183,10 +223,11 @@
     frames_shard = starts.shape[1]
     parts = lax.axis_size("mp")
     final = lax.axis_size("tm") * parts - 1
+    shift = final + 1
 
     def kernel(start_ref, end_ref, *refs):
         stack_refs, refs = refs[: len(counts)], refs[len(counts) :]
-        tables_ref, out, bounds, tails, heads, nexts, edges = refs
+        tables_ref, out, bounds, tails, heads, nexts, edges, order = refs
         time_index, model_index = lax.axis_index("tm"), lax.axis_index("mp")
         tails[...] = jnp.zeros_like(tails)
         nexts[...] = jnp.zeros_like(nexts)
@@ -201,11 +242,16 @@
                     edge = kept[4 + 2 * line : 5 + 2 * line] * DIGIT + kept[5 + 2 * line : 6 + 2 * line]
                     edges[line, here, :] = edge[:, :LANES]
                 slot += 1
-        for slot, (slot_tm, slot_mp) in enumerate(places):
-            following = slot_tm(time_index) * parts + (model_index ^ slot_mp) + 1
-            found = slot_of(places, following // parts, lax.rem(following, parts))
-            taken = heads[pl.ds(found, 1), :]
-            nexts[slot : slot + 1, :] = jnp.where(following > final, 0.0, taken)
+        numbers = [
+            slot_tm(time_index) * parts + (model_index ^ slot_mp) for slot_tm, slot_mp in places
+        ]
+        for number in numbers:
+            order[number + 1 + shift] = jnp.int32(0)
+        for slot, number in enumerate(numbers):
+            order[number + shift] = jnp.int32(slot)
+        for slot, number in enumerate(numbers):
+            taken = heads[pl.ds(order[number + 1 + shift], 1), :]
+            nexts[slot : slot + 1, :] = jnp.where(number == final, 0.0, taken)
         line = jnp.concatenate([tails[...], nexts[...]], axis=1)
         windows = []
         for sub in range(SUB - 2, SUB):
@@ -241,6 +287,7 @@
             pltpu.VMEM((rows, HEAD_LINES * LANES), jnp.float32),
             pltpu.VMEM((rows, HEAD_LINES * LANES), jnp.float32),
             pltpu.VMEM((2, rows, LANES), jnp.float32),
+            pltpu.SMEM((3 * shift,), jnp.int32),
         ],
         micros=0.9,
     )
@@ -521,18 +568,35 @@
     )
 
 
-def far_branch(windows, w_rows):
-    count = len(windows) // 2
+def far_branch_own(windows, w_own):
+    count = len(windows)
 
     def kernel(*refs):
-        windows, (w_own, w_near), outs = refs[: 2 * count], refs[2 * count :][:2], refs[-count:]
-        for number in range(count):
-            own, near = windows[2 * number : 2 * number + 2]
-            share = dot32(own[...], w_own[...]) + dot32(near[...], w_near[...])
-            outs[number][...] = share.astype(jnp.bfloat16)
-
-    shape = jax.ShapeDtypeStruct((windows[0].shape[0], w_rows[0].shape[1]), jnp.bfloat16)
-    return call(kernel, [shape] * count, (*windows, *w_rows), micros=0.9 * count)
+        for window, out in zip(refs[:count], refs[count + 1 :]):
+            out[...] = dot32(window[...], refs[count][...])
+
+    shape = jax.ShapeDtypeStruct((windows[0].shape[0], w_own.shape[1]), jnp.float32)
+    return call(kernel, [shape] * count, (*windows, w_own), micros=0.4 * count)
+
+
+def far_branch(shares, windows, w_near, cut):
+    count = len(windows)
+
+    def kernel(*refs):
+        share_refs, window_refs, near, outs = (
+            refs[:count],
+            refs[count : 2 * count],
+            refs[2 * count],
+            refs[2 * count + 1 :],
+        )
+        for number, (share, window) in enumerate(zip(share_refs, window_refs)):
+            total = (share[...] + dot32(window[...], near[...])).astype(jnp.bfloat16)
+            outs[2 * number][...] = total[:cut]
+            outs[2 * number + 1][...] = total[cut:]
+
+    sizes = [cut, windows[0].shape[0] - cut] * count
+    shapes = [jax.ShapeDtypeStruct((size, w_near.shape[1]), jnp.bfloat16) for size in sizes]
+    return call(kernel, shapes, (*shares, *windows, w_near), micros=0.5 * count)
 
 
 def near_branch(places, windows, w_rows, stacks, fixed, w_subsample, frames_local):
@@ -577,53 +641,110 @@
     )
 
 
-def finish_rows(base, shares, gain, taps, frames_local):
+def convolve(held, taps, begin, count, here):
+    offset = HALO - KERNEL // 2
+    reach = count + 8
+    rows = held[begin : begin + count + 2 * HALO, here]
+    tap_rows = taps[:, here].astype(jnp.float32)
+    total = jnp.zeros((count, rows.shape[1]), jnp.float32)
+    for phase in range(8):
+        share = jnp.zeros((reach, rows.shape[1]), jnp.float32)
+        for tap in range(KERNEL):
+            if (tap + offset) % 8 == phase:
+                first = (tap + offset) // 8 * 8
+                share += rows[first : first + reach] * tap_rows[tap : tap + 1]
+        moved = pltpu.roll(share, reach - phase, axis=0) if phase else share
+        total += moved[0:count]
+    return total
+
+
+def mix(base, shares, gain):
+    mixed = base
+    for share in shares:
+        mixed += share[...].astype(jnp.float32)
+    mixed = mixed.astype(jnp.bfloat16).astype(jnp.float32)
+    return mixed, (normalize(mixed) * gain[...]).astype(jnp.bfloat16).astype(jnp.float32)
+
+
+def silu(values):
+    return values / (1.0 + jnp.exp(-values))
+
+
+def finish_first(base, shares, gain, taps):
     count = len(shares)
-    parts = lax.axis_size("mp")
-    window, model = base.shape
+    cut, model = shares[0].shape
+    done = cut - 2 * HALO
     chunk = 2 * LANES
-    offset = HALO - KERNEL // 2
 
     def kernel(base_ref, *refs):
         share_refs, (gain_ref, tap_ref, out, held, mixed_rows) = refs[:count], refs[count:]
-        mixed = base_ref[...]
-        for share_ref in share_refs:
-            mixed += share_ref[...].astype(jnp.float32)
-        mixed = mixed.astype(jnp.bfloat16).astype(jnp.float32)
-        mixed_rows[...] = mixed[HALO : HALO + frames_local]
-        conv_in = (normalize(mixed) * gain_ref[...]).astype(jnp.bfloat16).astype(jnp.float32)
-        held[HALO : HALO + frames_local, :] = conv_in[HALO : HALO + frames_local]
-        block = lax.axis_index("tm") * parts + lax.axis_index("mp")
-        before = block > 0
+        mixed, conv_in = mix(base_ref[0:cut, :], share_refs, gain_ref)
+        mixed_rows[...] = mixed
+        held[...] = conv_in
+        before = lax.axis_index("tm") * lax.axis_size("mp") + lax.axis_index("mp") > 0
         held[0:HALO, :] = jnp.where(before, conv_in[0:HALO], 0.0)
-        after = block < lax.axis_size("tm") * parts - 1
-        held[HALO + frames_local : window, :] = jnp.where(after, conv_in[HALO + frames_local :], 0.0)
         for lane in range(0, model, chunk):
             here = slice(lane, lane + chunk)
-            total = jnp.zeros((frames_local, chunk), jnp.float32)
-            tap_rows = tap_ref[:, here].astype(jnp.float32)
-            rows = held[:, here]
-            reach = frames_local + 8
-            for phase in range(8):
-                share = jnp.zeros((reach, chunk), jnp.float32)
-                for tap in range(KERNEL):
-                    if (tap + offset) % 8 == phase:
-                        begin = (tap + offset) // 8 * 8
-                        share += rows[begin : begin + reach] * tap_rows[tap : tap + 1]
-                moved = pltpu.roll(share, reach - phase, axis=0) if phase else share
-                total += moved[0:frames_local]
-            silu = total / (1.0 + jnp.exp(-total))
-            out[:, here] = (mixed_rows[:, here] + silu).astype(jnp.bfloat16)
-
+            total = convolve(held, tap_ref, 0, done, here)
+            out[:, here] = (mixed_rows[HALO : HALO + done, here] + silu(total)).astype(jnp.bfloat16)
+
+    rows = jax.ShapeDtypeStruct((cut, model), jnp.float32)
     return call(
         kernel,
+        (jax.ShapeDtypeStruct((done, model), jnp.bfloat16), rows, rows),
+        (base, *shares, gain, taps),
+        micros=0.5,
+    )
+
+
+def finish_last(base, shares, first, gain, taps, frames_local):
+    count = len(shares)
+    window, model = base.shape
+    cut, done = first[1].shape[0], first[0].shape[0]
+    left = frames_local - done
+    chunk = 2 * LANES
+    chunks = model // chunk
+
+    def kernel(base_ref, *refs):
+        share_refs, refs = refs[:count], refs[count:]
+        out_ref, held_ref, mixed_ref, gain_ref, tap_ref, result, held, mixed_rows, staged, sems = refs
+        copies = [pltpu.make_async_copy(out_ref, result.at[pl.ds(0, done)], sems.at[chunks])]
+        copies[0].start()
+        mixed, conv_in = mix(base_ref[cut:window, :], share_refs, gain_ref)
+        mixed_rows[0:cut, :] = mixed_ref[...]
+        mixed_rows[cut:window, :] = mixed
+        held[0:cut, :] = held_ref[...]
+        held[cut:window, :] = conv_in
+        parts = lax.axis_size("mp")
+        block = lax.axis_index("tm") * parts + lax.axis_index("mp")
+        after = block < lax.axis_size("tm") * parts - 1
+        held[window - HALO : window, :] = jnp.where(after, conv_in[window - HALO - cut :], 0.0)
+        for number in range(chunks):
+            here = slice(number * chunk, (number + 1) * chunk)
+            total = convolve(held, tap_ref, done, left, here)
+            kept = mixed_rows[HALO + done : HALO + frames_local, here]
+            staged[:, here] = (kept + silu(total)).astype(jnp.bfloat16)
+            copies.append(
+                pltpu.make_async_copy(
+                    staged.at[:, here], result.at[pl.ds(done, left), here], sems.at[number]
+                )
+            )
+            copies[-1].start()
+        for copy in copies:
+            copy.wait()
+
+    return call(
+        kernel,
         jax.ShapeDtypeStruct((frames_local, model), jnp.bfloat16),
-        (base, *shares, gain, taps),
+        (base, *shares, *first, gain, taps),
         scratch=[
             pltpu.VMEM((window, model), jnp.float32),
-            pltpu.VMEM((frames_local, model), jnp.float32),
+            pltpu.VMEM((window, model), jnp.float32),
+            pltpu.VMEM((left, model), jnp.bfloat16),
+            pltpu.SemaphoreType.DMA((chunks + 1,)),
         ],
-        micros=2.8,
+        micros=1.5,
+        result=pltpu.HBM,
     )
 
 
@@ -706,17 +827,18 @@
         places, query_slots, far, bounds, (queries, keys, values), extras, frames_local
     )
     windows, shared = outs[: 2 * len(far)], outs[2 * len(far) :]
-    windows = [
-        exchange(block, "mp", 1) if number % 2 else block for number, block in enumerate(windows)
-    ]
+    arrived = [exchange(window, "mp", 1) for window in windows[1::2]]
     w_rows = (w_output, w_near)
-    shares = far_branch(windows, w_rows)
+    shares = far_branch_own(windows[0::2], w_output)
+    shares = far_branch(shares, arrived, w_near, frames_local + HALO)
     mine, other = attend_near(places, shares[0], *shared, frames_local)
-    shares = [exchange(share, "mp", bit) for share, bit in zip(shares, far)]
+    shares = [exchange(share, "mp", far[number // 2]) for number, share in enumerate(shares)]
     base = near_branch(
         places, (mine, exchange(other, "mp", 1)), w_rows, stacks, fixed, weights[0], frames_local
     )
-    return finish_rows(base, shares, gain_convolution[None, :], w_depthwise, frames_local)
+    gain = gain_convolution[None, :]
+    first = finish_first(base, shares[0::2], gain, w_depthwise)
+    return finish_last(base, shares[1::2], first, gain, w_depthwise, frames_local)
 
 
 def solution(mesh):

time: 42.5 us -> 40.7 us (0.958)
  local copies, waits for them, and re-layouts: 3.59 us -> 0.98 us
  waiting for transfers between devices: 9.38 us -> 6.93 us
  Pallas kernels: 17.9 us -> 20.2 us
  starting transfers between devices: 11.3 us -> 12.1 us
    unnamed x24 -> x18, local copies, waits for them, and re-layouts: 3.58 us -> 0.97 us
    ppermute x11 -> x12, waiting for transfers between devices: 9.38 us -> 6.93 us  [exchange(): lax.ppermute(block, axis, [(i, i ^ bit) for i in range(lax.axis_size(axis...]
    pallas_call x15 -> x17, Pallas kernels: 17.9 us -> 20.2 us  [call(): pl.pallas_call(kernel, out_shape=out_shape, in_specs=specs, out_specs=jax...]
    ppermute x11 -> x12, starting transfers between devices: 11.3 us -> 12.1 us  [exchange(): lax.ppermute(block, axis, [(i, i ^ bit) for i in range(lax.axis_size(axis...]
  transfers between devices with their start and end apart: 11 -> 12, of which waited for: 5 -> 5; matrix products, arithmetic and copies ran while one was open for 0% -> 0% of each run, Pallas kernels for 34% -> 38%
where the time goes in v6:
time: 40.7 us; the launch traced here: 40.5 us
  Pallas kernels  20.2 us (50%)
  starting transfers between devices  12.1 us (30%)
  waiting for transfers between devices  6.93 us (17%)
  local copies, waits for them, and re-layouts  0.98 us (2%)
    pallas_call x17, Pallas kernels, call(): pl.pallas_call(kernel, out_shape=out_shape, in_specs=specs, out_specs=jax...  20.2 us
    ppermute x12, starting transfers between devices, exchange(): lax.ppermute(block, axis, [(i, i ^ bit) for i in range(lax.axis_size(axis...  12.1 us
    ppermute x12, waiting for transfers between devices, exchange(): lax.ppermute(block, axis, [(i, i ^ bit) for i in range(lax.axis_size(axis...  6.93 us
    unnamed x18, local copies, waits for them, and re-layouts  0.97 us
  transfers between devices with their start and end apart: 12, of which 5 were waited for; matrix products, arithmetic and copies ran while one was open for 0% of the time, Pallas kernels for 38%

profile of v6, /device:TPU:0, one launch (start us, length us, event | category | flops | bytes accessed | tf_op | source)
XLA Modules:
  0.0 40.5 jit_solution(4142821903865753079)
XLA Ops:
  0.0 3.1 %shard_map.91.stack_ref = bf16[1,72,512]{2,1,0:T(8,128)(2,1)} custom-call(s32[1,256]{1,0:T(1,128)} %bitcast.3, s32[1,256]{1,0:T(1,128)} %bitcast.5, f32[320,128]{1,0:T(8,128)} %bitcast.7, bf16[512,1152]{1,0:T(8,128)(2,1)} %constant.2.clone.table.refs_4_), custom_call_target="tpu_custom_call" | custom-call | flops 2000000000 | bytes 1000000 | tf_op jit(solution)/shard_map/pallas_call | solution.py:89
  3.1 0.0 copy-start
  3.1 3.1 %collective-permute-start.1 = (bf16[1,72,512]{2,1,0:T(8,128)(2,1)}, bf16[1,72,512]{2,1,0:T(8,128)(2,1)S(1)}, u32[]{:S(2)}, u32[]{:S(2)}) collective-permute-start(bf16[1,72,512]{2,1,0:T(8,128)(2,1)} %shard_map.91.stack_ref), channel_id=1, source_target_pairs={{0,4},{4,0},{8,12},{12,8},{1,5},{5,1},{9,13},{13,9},{2,6},{6,2},{1... | collective-permute-start | bytes 221192 | tf_op jit(solution)/shard_map/ppermute | solution.py:752
  6.2 2.6 %collective-permute-start.2 = (bf16[1,72,512]{2,1,0:T(8,128)(2,1)}, bf16[1,72,512]{2,1,0:T(8,128)(2,1)S(1)}, u32[]{:S(2)}, u32[]{:S(2)}) collective-permute-start(bf16[1,72,512]{2,1,0:T(8,128)(2,1)} %shard_map.91.stack_ref), channel_id=1, source_target_pairs={{0,8},{4,12},{8,0},{12,4},{1,9},{5,13},{9,1},{13,5},{2,10},{6,14},... | collective-permute-start | bytes 221192 | tf_op jit(solution)/shard_map/ppermute | solution.py:752
  8.8 0.0 collective-permute-start.3
  8.8 0.0 copy-done.2
  8.8 0.0 copy-start.4
  8.8 0.9 %copy-done.4 = bf16[1,72,512]{2,1,0:T(8,128)(2,1)S(1)} copy-done((bf16[1,72,512]{2,1,0:T(8,128)(2,1)S(1)}, bf16[1,72,512]{2,1,0:T(8,128)(2,1)}, u32[]{:S(2)}) %copy-start.4) | copy-done | bytes 73752
  9.7 1.2 %shard_map.92 = (bf16[512,1536]{1,0:T(8,128)(2,1)S(1)}, bf16[3,1536,384]{2,1,0:T(8,128)(2,1)S(1)}, f32[8,384]{1,0:T(8,128)S(1)}, bf16[1,72,512]{2,1,0:T(8,128)(2,1)S(1)}) custom-call(bf16[1,72,512]{2,1,0:T(8,128)(2,1)S(1)} %copy-done.4, bf16[512,1536]{1,0:T(8,128)(2,1)S(1)} %copy-done.2, bf16[3,1536,384]{2,1,0:T(8,128)(2,1)S(1)} %copy-done.1), custom_call_target="tpu_custom_call" | custom-call | flops 2000000000 | bytes 1000000 | tf_op jit(solution)/shard_map/pallas_call | solution.py:89
  10.9 1.7 %collective-permute-start = (bf16[1,72,512]{2,1,0:T(8,128)(2,1)S(1)}, bf16[1,72,512]{2,1,0:T(8,128)(2,1)S(1)}, u32[]{:S(2)}, u32[]{:S(2)}) collective-permute-start(bf16[1,72,512]{2,1,0:T(8,128)(2,1)S(1)} %get-tuple-element.38.refs_0_), channel_id=1, source_target_pairs={{0,2},{1,3},{2,0},{3,1},{4,6},{5,7},{6,4},{7,5},{8,10},{9,11},{10,... | collective-permute-start | bytes 221192 | tf_op jit(solution)/shard_map/ppermute | solution.py:752
  12.6 0.0 collective-permute-start.8
  12.6 0.0 collective-permute-done.1.refs_0_
  12.6 1.6 %collective-permute-done.2.refs_1_ = bf16[1,72,512]{2,1,0:T(8,128)(2,1)S(1)} collective-permute-done((bf16[1,72,512]{2,1,0:T(8,128)(2,1)}, bf16[1,72,512]{2,1,0:T(8,128)(2,1)S(1)}, u32[]{:S(2)}, u32[]{:S(2)}) %collective-permute-start.2) | collective-permute-done | bytes 73760 | tf_op jit(solution)/shard_map/ppermute | solution.py:752
  14.2 1.0 %collective-permute-done.3.refs_2_ = bf16[1,72,512]{2,1,0:T(8,128)(2,1)S(1)} collective-permute-done((bf16[1,72,512]{2,1,0:T(8,128)(2,1)}, bf16[1,72,512]{2,1,0:T(8,128)(2,1)S(1)}, u32[]{:S(2)}, u32[]{:S(2)}) %collective-permute-start.3) | collective-permute-done | bytes 73760 | tf_op jit(solution)/shard_map/ppermute | solution.py:752
  15.3 1.6 %collective-permute-start.5 = (bf16[3,72,512]{2,1,0:T(8,128)(2,1)S(1)}, bf16[3,72,512]{2,1,0:T(8,128)(2,1)S(1)}, u32[]{:S(2)}, u32[]{:S(2)}) collective-permute-start(bf16[3,72,512]{2,1,0:T(8,128)(2,1)S(1)} %shard_map.93.refs_2_), channel_id=1, source_target_pairs={{0,2},{1,3},{2,0},{3,1},{4,6},{5,7},{6,4},{7,5},{8,10},{9,11},{10,... | collective-permute-start | bytes 663560 | tf_op jit(solution)/shard_map/ppermute | solution.py:752
  16.8 0.0 collective-permute-done.refs_1_
  16.8 0.1 collective-permute-start.4
  16.9 2.1 %shard_map.95 = (bf16[128,384]{1,0:T(8,128)(2,1)S(1)}, bf16[320,384]{1,0:T(8,128)(2,1)S(1)}, bf16[320,384]{1,0:T(8,128)(2,1)S(1)}) custom-call(bf16[5,72,512]{2,1,0:T(8,128)(2,1)S(1)} %shard_map.94.stack_ref.refs_0_, bf16[512,1536]{1,0:T(8,128)(2,1)S(1)} %get-tuple-element.40.w_sub.refs_5_, bf16[3,1536,384]{2,1,0:T(8,128)(2,1)S(1)} %get-tuple-element.41.w_att, ...), custom_call_target="tpu_custom_call" | custom-call | flops 4840000000 | bytes 1000000 | tf_op jit(solution)/shard_map/pallas_call | solution.py:89
  19.1 0.0 collective-permute-done.4.stack_ref.refs_1_
  19.1 2.1 %shard_map.96 = (bf16[128,384]{1,0:T(8,128)(2,1)S(1)}, bf16[320,384]{1,0:T(8,128)(2,1)S(1)}, bf16[320,384]{1,0:T(8,128)(2,1)S(1)}) custom-call(bf16[5,72,512]{2,1,0:T(8,128)(2,1)S(1)} %collective-permute-done.4.stack_ref.refs_1_, bf16[512,1536]{1,0:T(8,128)(2,1)S(1)} %get-tuple-element.40.w_sub.refs_5_, bf16[3,1536,384]{2,1,0:T(8,128)(2,1)S(1)} %get-tuple-element.41.w_att, ...), custom_call_target="tpu_custom_call" | custom-call | flops 4840000000 | bytes 1000000 | tf_op jit(solution)/shard_map/pallas_call | solution.py:89
  21.2 0.0 collective-permute-done.5.refs_0_
  21.3 0.0 copy-start.5
  21.3 0.0 copy-start.6
  21.3 0.0 copy-start.7
  21.3 0.6 %collective-permute-start.6 = (bf16[3,72,512]{2,1,0:T(8,128)(2,1)S(1)}, bf16[3,72,512]{2,1,0:T(8,128)(2,1)S(1)}, u32[]{:S(2)}, u32[]{:S(2)}) collective-permute-start(bf16[3,72,512]{2,1,0:T(8,128)(2,1)S(1)} %shard_map.97.refs_2_.stack_ref), channel_id=1, source_target_pairs={{0,1},{1,0},{2,3},{3,2},{4,5},{5,4},{6,7},{7,6},{8,9},{9,8},{10,11... | collective-permute-start | bytes 663560 | tf_op jit(solution)/shard_map/ppermute | solution.py:752
  21.9 1.2 %shard_map.99 = (bf16[192,384]{1,0:T(8,128)(2,1)S(1)}, bf16[192,384]{1,0:T(8,128)(2,1)S(1)}) custom-call(bf16[3,72,512]{2,1,0:T(8,128)(2,1)S(1)} %shard_map.97.refs_2_.stack_ref, bf16[512,1536]{1,0:T(8,128)(2,1)S(1)} %get-tuple-element.40.w_sub.refs_5_, bf16[3,1536,384]{2,1,0:T(8,128)(2,1)S(1)} %get-tuple-element.41.w_att, ...), custom_call_target="tpu_custom_call" | custom-call | flops 3304000000 | bytes 1000000 | tf_op jit(solution)/shard_map/pallas_call | solution.py:89
  23.1 0.0 collective-permute-done.6.refs_3_.stack_ref
  23.1 0.0 copy-done.5
  23.1 0.0 copy-done.6
  23.1 0.0 copy-done.7
  23.1 0.7 %shard_map.98 = (bf16[16,256]{1,0:T(8,128)(2,1)S(1)}, f32[2,288]{1,0:T(2,128)S(1)}) custom-call(s32[1,256]{1,0:T(1,128)S(1)} %bitcast.4, s32[1,256]{1,0:T(1,128)S(1)} %bitcast.6, bf16[5,72,512]{2,1,0:T(8,128)(2,1)S(1)} %shard_map.94.stack_ref.refs_0_, bf16[5,72,512]{2,1,0:T(8,128)(2,1)S(1)} %collective-permute-done.4.stack_ref.refs_1_, ...), custom_call_target="tpu_custom_call" | custom-call | flops 1800000000 | bytes 1000000 | tf_op jit(solution)/shard_map/pallas_call | solution.py:89
  23.8 1.7 %shard_map.100 = (bf16[48,384]{1,0:T(8,128)(2,1)S(1)}, bf16[192,384]{1,0:T(8,128)(2,1)S(1)}, bf16[48,384]{1,0:T(8,128)(2,1)S(1)}, bf16[192,384]{1,0:T(8,128)(2,1)S(1)}, bf16[48,384]{1,0:T(8,128)(2,1)S(1)}) custom-call(bf16[3,72,512]{2,1,0:T(8,128)(2,1)S(1)} %collective-permute-done.6.refs_3_.stack_ref, ...), custom_call_target="tpu_custom_call" | custom-call | flops 3880000000 | bytes 1000000 | tf_op jit(solution)/shard_map/pallas_call | solution.py:89
  25.5 2.2 %shard_map.101 = (bf16[96,384]{1,0:T(8,128)(2,1)S(1)}, bf16[96,384]{1,0:T(8,128)(2,1)S(1)}, bf16[288,384]{1,0:T(8,128)(2,1)S(1)}, bf16[1024,384]{1,0:T(8,128)(2,...) custom-call(f32[2,288]{1,0:T(2,128)S(1)} %get-tuple-element.44.bound_ref, ...), custom_call_target="tpu_custom_call" | custom-call | flops 5000000000 | bytes 1000000 | tf_op jit(solution)/shard_map/pallas_call | solution.py:89
  27.6 0.3 collective-permute-start.7
  27.9 0.4 shard_map.102.refs_0_
  28.3 0.7 %collective-permute-done.7.refs_1_ = bf16[96,384]{1,0:T(8,128)(2,1)S(1)} collective-permute-done((bf16[96,384]{1,0:T(8,128)(2,1)S(1)}, bf16[96,384]{1,0:T(8,128)(2,1)S(1)}, u32[]{:S(2)}, u32[]{:S(2)}) %collective-permute-start.7) | collective-permute-done | bytes 73760 | tf_op jit(solution)/shard_map/ppermute | solution.py:752
  29.0 0.0 collective-permute-done.8.refs_2_.w_near
  29.0 0.4 shard_map.103
  29.3 1.3 %collective-permute-start.11 = (bf16[80,1536]{1,0:T(8,128)(2,1)S(1)}, bf16[80,1536]{1,0:T(8,128)(2,1)S(1)}, u32[]{:S(2)}, u32[]{:S(2)}) collective-permute-start(bf16[80,1536]{1,0:T(8,128)(2,1)S(1)} %get-tuple-element.59._), channel_id=1, source_target_pairs={{0,2},{1,3},{2,0},{3,1},{4,6},{5,7},{6,4},{7,5},{8,10},{9,11},{10,... | collective-permute-start | bytes 737288 | tf_op jit(solution)/shard_map/ppermute | solution.py:752
  30.6 1.9 %shard_map.104 = (bf16[96,384]{1,0:T(8,128)(2,1)S(1)}, bf16[96,384]{1,0:T(8,128)(2,1)S(1)}) custom-call(bf16[80,1536]{1,0:T(8,128)(2,1)S(1)} %get-tuple-element.59._, bf16[288,384]{1,0:T(8,128)(2,1)S(1)} %get-tuple-element.60.q_ref, bf16[1024,384]{1,0:T(8,128)(2,1)S(1)} %get-tuple-element.61.k_ref, bf16[1024,384]{1,0:T(8,128)(2,1)S(1)} %get-tuple-element.62.v_ref, ...), custom_call_target="tpu_custom_call" | custom-call | flops 2000000000 | bytes 1000000 | tf_op jit(solution)/shard_map/pallas_call | solution.py:89
  32.5 0.1 collective-permute-start.9
  32.6 0.9 %collective-permute-start.10 = (bf16[16,1536]{1,0:T(8,128)(2,1)S(1)}, bf16[16,1536]{1,0:T(8,128)(2,1)S(1)}, u32[]{:S(2)}, u32[]{:S(2)}) collective-permute-start(bf16[16,1536]{1,0:T(8,128)(2,1)S(1)} %get-tuple-element.67), channel_id=1, source_target_pairs={{0,2},{1,3},{2,0},{3,1},{4,6},{5,7},{6,4},{7,5},{8,10},{9,11},{10,... | collective-permute-start | bytes 147464 | tf_op jit(solution)/shard_map/ppermute | solution.py:752
  33.5 0.4 collective-permute-done.9.near
  33.9 0.9 %shard_map.105.base_ref = f32[96,1536]{1,0:T(8,128)S(1)} custom-call(bf16[96,384]{1,0:T(8,128)(2,1)S(1)} %get-tuple-element.65.own, bf16[96,384]{1,0:T(8,128)(2,1)S(1)} %collective-permute-done.9.near, bf16[384,1536]{1,0:T(8,128)(2,1)S(1)} %copy-done, bf16[384,1536]{1,0:T(8,128)(2,1)S(1)} %collective-permute-done.8.refs_2_.w_near, ...), custom_call_target="tpu_custom_call" | custom-call | flops 1200000000 | bytes 1000000 | tf_op jit(solution)/shard_map/pallas_call | solution.py:89
  34.7 3.3 %collective-permute-done.11.refs_0_ = bf16[80,1536]{1,0:T(8,128)(2,1)S(1)} collective-permute-done((bf16[80,1536]{1,0:T(8,128)(2,1)S(1)}, bf16[80,1536]{1,0:T(8,128)(2,1)S(1)}, u32[]{:S(2)}, u32[]{:S(2)}) %collective-permute-start.11) | collective-permute-done | bytes 245792 | tf_op jit(solution)/shard_map/ppermute | solution.py:752
  38.0 1.2 %shard_map.106 = (bf16[48,1536]{1,0:T(8,128)(2,1)S(1)}, f32[80,1536]{1,0:T(8,128)S(1)}, f32[80,1536]{1,0:T(8,128)S(1)}) custom-call(f32[96,1536]{1,0:T(8,128)S(1)} %shard_map.105.base_ref, bf16[80,1536]{1,0:T(8,128)(2,1)S(1)} %collective-permute-done.11.refs_0_, f32[1,1536]{1,0:T(1,128)S(1)} %broadcast_in_dim.11.refs_1_.refs_4_, bf16[31,1536]{1,0:T(8,128)(2,1)S(1)} %copy-done.3), custom_call_target="tpu_custom_call" | custom-call | flops 1000000000 | bytes 1000000 | tf_op jit(solution)/shard_map/pallas_call | solution.py:89
  39.3 0.0 collective-permute-done.10.refs_0_
  39.3 1.3 %shard_map.107 = bf16[64,1536]{1,0:T(8,128)(2,1)} custom-call(f32[96,1536]{1,0:T(8,128)S(1)} %shard_map.105.base_ref, bf16[16,1536]{1,0:T(8,128)(2,1)S(1)} %collective-permute-done.10.refs_0_, bf16[48,1536]{1,0:T(8,128)(2,1)S(1)} %get-tuple-element.68.refs_1_, f32[80,1536]{1,0:T(8,128)S(1)} %get-tuple-element.69.refs_2_, ...), custom_call_target="tpu_custom_call" | custom-call | flops 3000000000 | bytes 1000000 | tf_op jit(solution)/shard_map/pallas_call | solution.py:89
  (12 shorter events, 0.1 us)
Async XLA Ops:
  0.0 8.8 %copy-start.1 = (bf16[3,1536,384]{2,1,0:T(8,128)(2,1)S(1)}, bf16[3,1536,384]{2,1,0:T(8,128)(2,1)}, u32[]{:S(2)}) copy-start(bf16[3,1536,384]{2,1,0:T(8,128)(2,1)} %w_att.1) | copy-start | bytes 10616836
  0.0 8.8 %copy-start.2 = (bf16[512,1536]{1,0:T(8,128)(2,1)S(1)}, bf16[512,1536]{1,0:T(8,128)(2,1)}, u32[]{:S(2)}) copy-start(bf16[512,1536]{1,0:T(8,128)(2,1)} %w_sub.1) | copy-start | bytes 4718596
  3.1 9.5 %copy-start = (bf16[384,1536]{1,0:T(8,128)(2,1)S(1)}, bf16[384,1536]{1,0:T(8,128)(2,1)}, u32[]{:S(2)}) copy-start(bf16[384,1536]{1,0:T(8,128)(2,1)} %w_own.1) | copy-start | bytes 3538948
  3.1 9.5 %collective-permute-start.1 = (bf16[1,72,512]{2,1,0:T(8,128)(2,1)}, bf16[1,72,512]{2,1,0:T(8,128)(2,1)S(1)}, u32[]{:S(2)}, u32[]{:S(2)}) collective-permute-start(bf16[1,72,512]{2,1,0:T(8,128)(2,1)} %shard_map.91.stack_ref), channel_id=1, source_target_pairs={{0,4},{4,0},{8,12},{12,8},{1,5},{5,1},{9,13},{13,9},{2,6},{6,2},{1... | collective-permute-start | bytes 221192 | tf_op jit(solution)/shard_map/ppermute | solution.py:752
  6.2 8.0 %collective-permute-start.2 = (bf16[1,72,512]{2,1,0:T(8,128)(2,1)}, bf16[1,72,512]{2,1,0:T(8,128)(2,1)S(1)}, u32[]{:S(2)}, u32[]{:S(2)}) collective-permute-start(bf16[1,72,512]{2,1,0:T(8,128)(2,1)} %shard_map.91.stack_ref), channel_id=1, source_target_pairs={{0,8},{4,12},{8,0},{12,4},{1,9},{5,13},{9,1},{13,5},{2,10},{6,14},... | collective-permute-start | bytes 221192 | tf_op jit(solution)/shard_map/ppermute | solution.py:752
  8.8 6.5 %collective-permute-start.3 = (bf16[1,72,512]{2,1,0:T(8,128)(2,1)}, bf16[1,72,512]{2,1,0:T(8,128)(2,1)S(1)}, u32[]{:S(2)}, u32[]{:S(2)}) collective-permute-start(bf16[1,72,512]{2,1,0:T(8,128)(2,1)} %shard_map.91.stack_ref), channel_id=1, source_target_pairs={{0,12},{4,8},{8,4},{12,0},{1,13},{5,9},{9,5},{13,1},{2,14},{6,10},... | collective-permute-start | bytes 221192 | tf_op jit(solution)/shard_map/ppermute | solution.py:752
  8.8 0.9 %copy-start.4 = (bf16[1,72,512]{2,1,0:T(8,128)(2,1)S(1)}, bf16[1,72,512]{2,1,0:T(8,128)(2,1)}, u32[]{:S(2)}) copy-start(bf16[1,72,512]{2,1,0:T(8,128)(2,1)} %shard_map.91.stack_ref) | copy-start | bytes 221188
  10.9 5.9 %collective-permute-start = (bf16[1,72,512]{2,1,0:T(8,128)(2,1)S(1)}, bf16[1,72,512]{2,1,0:T(8,128)(2,1)S(1)}, u32[]{:S(2)}, u32[]{:S(2)}) collective-permute-start(bf16[1,72,512]{2,1,0:T(8,128)(2,1)S(1)} %get-tuple-element.38.refs_0_), channel_id=1, source_target_pairs={{0,2},{1,3},{2,0},{3,1},{4,6},{5,7},{6,4},{7,5},{8,10},{9,11},{10,... | collective-permute-start | bytes 221192 | tf_op jit(solution)/shard_map/ppermute | solution.py:752
  12.6 16.4 %collective-permute-start.8 = (bf16[384,1536]{1,0:T(8,128)(2,1)S(1)}, bf16[384,1536]{1,0:T(8,128)(2,1)S(1)}, u32[]{:S(2)}, u32[]{:S(2)}) collective-permute-start(bf16[384,1536]{1,0:T(8,128)(2,1)S(1)} %copy-done), channel_id=1, source_target_pairs={{0,1},{1,0},{2,3},{3,2},{4,5},{5,4},{6,7},{7,6},{8,9},{9,8},{10,11... | collective-permute-start | bytes 3538952 | tf_op jit(solution)/shard_map/ppermute | solution.py:752
  15.3 6.0 %collective-permute-start.5 = (bf16[3,72,512]{2,1,0:T(8,128)(2,1)S(1)}, bf16[3,72,512]{2,1,0:T(8,128)(2,1)S(1)}, u32[]{:S(2)}, u32[]{:S(2)}) collective-permute-start(bf16[3,72,512]{2,1,0:T(8,128)(2,1)S(1)} %shard_map.93.refs_2_), channel_id=1, source_target_pairs={{0,2},{1,3},{2,0},{3,1},{4,6},{5,7},{6,4},{7,5},{8,10},{9,11},{10,... | collective-permute-start | bytes 663560 | tf_op jit(solution)/shard_map/ppermute | solution.py:752
  16.8 2.2 %collective-permute-start.4 = (bf16[5,72,512]{2,1,0:T(8,128)(2,1)S(1)}, bf16[5,72,512]{2,1,0:T(8,128)(2,1)S(1)}, u32[]{:S(2)}, u32[]{:S(2)}) collective-permute-start(bf16[5,72,512]{2,1,0:T(8,128)(2,1)S(1)} %shard_map.94.stack_ref.refs_0_), channel_id=1, source_target_pairs={{0,1},{1,0},{2,3},{3,2},{4,5},{5,4},{6,7},{7,6},{8,9},{9,8},{10,11... | collective-permute-start | bytes 1105928 | tf_op jit(solution)/shard_map/ppermute | solution.py:752
  21.3 1.8 %copy-start.5 = (s32[256]{0:T(256)S(1)}, s32[256]{0:T(256)}, u32[]{:S(2)}) copy-start(s32[256]{0:T(256)} %param.10) | copy-start | bytes 3076
  21.3 1.8 %copy-start.6 = (s32[256]{0:T(256)S(1)}, s32[256]{0:T(256)}, u32[]{:S(2)}) copy-start(s32[256]{0:T(256)} %param.11) | copy-start | bytes 3076
  21.3 1.8 %copy-start.7 = (bf16[512,1152]{1,0:T(8,128)(2,1)S(1)}, bf16[512,1152]{1,0:T(8,128)(2,1)}, u32[]{:S(2)}) copy-start(bf16[512,1152]{1,0:T(8,128)(2,1)} %constant.2.clone.table.refs_4_) | copy-start | bytes 3538948
  21.3 1.8 %collective-permute-start.6 = (bf16[3,72,512]{2,1,0:T(8,128)(2,1)S(1)}, bf16[3,72,512]{2,1,0:T(8,128)(2,1)S(1)}, u32[]{:S(2)}, u32[]{:S(2)}) collective-permute-start(bf16[3,72,512]{2,1,0:T(8,128)(2,1)S(1)} %shard_map.97.refs_2_.stack_ref), channel_id=1, source_target_pairs={{0,1},{1,0},{2,3},{3,2},{4,5},{5,4},{6,7},{7,6},{8,9},{9,8},{10,11... | collective-permute-start | bytes 663560 | tf_op jit(solution)/shard_map/ppermute | solution.py:752
  27.6 1.3 %collective-permute-start.7 = (bf16[96,384]{1,0:T(8,128)(2,1)S(1)}, bf16[96,384]{1,0:T(8,128)(2,1)S(1)}, u32[]{:S(2)}, u32[]{:S(2)}) collective-permute-start(bf16[96,384]{1,0:T(8,128)(2,1)S(1)} %get-tuple-element.58), channel_id=1, source_target_pairs={{0,1},{1,0},{2,3},{3,2},{4,5},{5,4},{6,7},{7,6},{8,9},{9,8},{10,11... | collective-permute-start | bytes 221192 | tf_op jit(solution)/shard_map/ppermute | solution.py:752
  29.3 8.7 %collective-permute-start.11 = (bf16[80,1536]{1,0:T(8,128)(2,1)S(1)}, bf16[80,1536]{1,0:T(8,128)(2,1)S(1)}, u32[]{:S(2)}, u32[]{:S(2)}) collective-permute-start(bf16[80,1536]{1,0:T(8,128)(2,1)S(1)} %get-tuple-element.59._), channel_id=1, source_target_pairs={{0,2},{1,3},{2,0},{3,1},{4,6},{5,7},{6,4},{7,5},{8,10},{9,11},{10,... | collective-permute-start | bytes 737288 | tf_op jit(solution)/shard_map/ppermute | solution.py:752
  30.6 2.0 %copy-start.8 = (f32[1536]{0:T(1024)S(1)}, f32[1536]{0:T(1024)}, u32[]{:S(2)}) copy-start(f32[1536]{0:T(1024)} %param.15) | copy-start | bytes 18436
  32.5 1.3 %collective-permute-start.9 = (bf16[96,384]{1,0:T(8,128)(2,1)S(1)}, bf16[96,384]{1,0:T(8,128)(2,1)S(1)}, u32[]{:S(2)}, u32[]{:S(2)}) collective-permute-start(bf16[96,384]{1,0:T(8,128)(2,1)S(1)} %get-tuple-element.66), channel_id=1, source_target_pairs={{0,1},{1,0},{2,3},{3,2},{4,5},{5,4},{6,7},{7,6},{8,9},{9,8},{10,11... | collective-permute-start | bytes 221192 | tf_op jit(solution)/shard_map/ppermute | solution.py:752
  32.6 6.6 %collective-permute-start.10 = (bf16[16,1536]{1,0:T(8,128)(2,1)S(1)}, bf16[16,1536]{1,0:T(8,128)(2,1)S(1)}, u32[]{:S(2)}, u32[]{:S(2)}) collective-permute-start(bf16[16,1536]{1,0:T(8,128)(2,1)S(1)} %get-tuple-element.67), channel_id=1, source_target_pairs={{0,2},{1,3},{2,0},{3,1},{4,6},{5,7},{6,4},{7,5},{8,10},{9,11},{10,... | collective-permute-start | bytes 147464 | tf_op jit(solution)/shard_map/ppermute | solution.py:752
  33.9 4.2 %copy-start.3 = (bf16[31,1536]{1,0:T(8,128)(2,1)S(1)}, bf16[31,1536]{1,0:T(8,128)(2,1)}, u32[]{:S(2)}) copy-start(bf16[31,1536]{1,0:T(8,128)(2,1)} %refs_5_.1) | copy-start | bytes 285700

commit v7 on v6

--- a/solution.py
+++ b/solution.py
@@ -784,8 +784,9 @@
     reach = min((SEG_MAX + HALO - 2) // frames_shard + 1, shards_total - 1)
     whole = reach == shards_total - 1 and shards_total & (shards_total - 1) == 0
     if whole:
-        moves = [lambda tm, bit=bit: tm ^ bit for bit in range(1, shards_total)]
-        column = [exchange(stacked, "tm", bit) for bit in range(1, shards_total)]
+        order = [shards_total - 1, *range(1, shards_total - 1)]
+        moves = [lambda tm, bit=bit: tm ^ bit for bit in order]
+        column = [exchange(stacked, "tm", bit) for bit in order]
     else:
         steps = [sign * d for d in range(1, reach + 1) for sign in (1, -1)]
         moves = [lambda tm, step=step: tm - step for step in steps]

time: 40.7 us -> 39.8 us (0.978)
  waiting for transfers between devices: 6.93 us -> 6.16 us
    ppermute x12, waiting for transfers between devices: 6.93 us -> 6.16 us  [exchange(): lax.ppermute(block, axis, [(i, i ^ bit) for i in range(lax.axis_size(axis...]
  transfers between devices with their start and end apart: 12 -> 12, of which waited for: 5 -> 6; matrix products, arithmetic and copies ran while one was open for 0% -> 0% of each run, Pallas kernels for 38% -> 39%
where the time goes in v7:
time: 39.8 us; the launch traced here: 39.6 us
  Pallas kernels  20.3 us (51%)
  starting transfers between devices  12 us (30%)
  waiting for transfers between devices  6.16 us (15%)
  local copies, waits for them, and re-layouts  0.96 us (2%)
    pallas_call x17, Pallas kernels, call(): pl.pallas_call(kernel, out_shape=out_shape, in_specs=specs, out_specs=jax...  20.3 us
    ppermute x12, starting transfers between devices, exchange(): lax.ppermute(block, axis, [(i, i ^ bit) for i in range(lax.axis_size(axis...  12 us
    ppermute x12, waiting for transfers between devices, exchange(): lax.ppermute(block, axis, [(i, i ^ bit) for i in range(lax.axis_size(axis...  6.16 us
    unnamed x18, local copies, waits for them, and re-layouts  0.95 us
  transfers between devices with their start and end apart: 12, of which 6 were waited for; matrix products, arithmetic and copies ran while one was open for 0% of the time, Pallas kernels for 39%

profile of v7, /device:TPU:0, one launch (start us, length us, event | category | flops | bytes accessed | tf_op | source)
XLA Modules:
  0.0 39.6 jit_solution(547220112740570981)
XLA Ops:
  0.0 3.1 %shard_map.91.stack_ref = bf16[1,72,512]{2,1,0:T(8,128)(2,1)} custom-call(s32[1,256]{1,0:T(1,128)} %bitcast.3, s32[1,256]{1,0:T(1,128)} %bitcast.5, f32[320,128]{1,0:T(8,128)} %bitcast.7, bf16[512,1152]{1,0:T(8,128)(2,1)} %constant.2.clone.table.refs_4_), custom_call_target="tpu_custom_call" | custom-call | flops 2000000000 | bytes 1000000 | tf_op jit(solution)/shard_map/pallas_call | solution.py:89
  3.1 0.0 copy-start
  3.1 5.1 %collective-permute-start.1 = (bf16[1,72,512]{2,1,0:T(8,128)(2,1)}, bf16[1,72,512]{2,1,0:T(8,128)(2,1)S(1)}, u32[]{:S(2)}, u32[]{:S(2)}) collective-permute-start(bf16[1,72,512]{2,1,0:T(8,128)(2,1)} %shard_map.91.stack_ref), channel_id=1, source_target_pairs={{0,12},{4,8},{8,4},{12,0},{1,13},{5,9},{9,5},{13,1},{2,14},{6,10},... | collective-permute-start | bytes 221192 | tf_op jit(solution)/shard_map/ppermute | solution.py:752
  8.2 0.0 collective-permute-start.2
  8.2 0.6 %collective-permute-start.3 = (bf16[1,72,512]{2,1,0:T(8,128)(2,1)}, bf16[1,72,512]{2,1,0:T(8,128)(2,1)S(1)}, u32[]{:S(2)}, u32[]{:S(2)}) collective-permute-start(bf16[1,72,512]{2,1,0:T(8,128)(2,1)} %shard_map.91.stack_ref), channel_id=1, source_target_pairs={{0,8},{4,12},{8,0},{12,4},{1,9},{5,13},{9,1},{13,5},{2,10},{6,14},... | collective-permute-start | bytes 221192 | tf_op jit(solution)/shard_map/ppermute | solution.py:752
  8.8 0.0 copy-done.1
  8.8 0.0 copy-done.2
  8.8 0.9 %copy-done.4 = bf16[1,72,512]{2,1,0:T(8,128)(2,1)S(1)} copy-done((bf16[1,72,512]{2,1,0:T(8,128)(2,1)S(1)}, bf16[1,72,512]{2,1,0:T(8,128)(2,1)}, u32[]{:S(2)}) %copy-start.4) | copy-done | bytes 73752
  9.8 1.2 %shard_map.92 = (bf16[512,1536]{1,0:T(8,128)(2,1)S(1)}, bf16[3,1536,384]{2,1,0:T(8,128)(2,1)S(1)}, f32[8,384]{1,0:T(8,128)S(1)}, bf16[1,72,512]{2,1,0:T(8,128)(2,1)S(1)}) custom-call(bf16[1,72,512]{2,1,0:T(8,128)(2,1)S(1)} %copy-done.4, bf16[512,1536]{1,0:T(8,128)(2,1)S(1)} %copy-done.2, bf16[3,1536,384]{2,1,0:T(8,128)(2,1)S(1)} %copy-done.1), custom_call_target="tpu_custom_call" | custom-call | flops 2000000000 | bytes 1000000 | tf_op jit(solution)/shard_map/pallas_call | solution.py:89
  10.9 1.7 %collective-permute-start = (bf16[1,72,512]{2,1,0:T(8,128)(2,1)S(1)}, bf16[1,72,512]{2,1,0:T(8,128)(2,1)S(1)}, u32[]{:S(2)}, u32[]{:S(2)}) collective-permute-start(bf16[1,72,512]{2,1,0:T(8,128)(2,1)S(1)} %get-tuple-element.38.refs_0_), channel_id=1, source_target_pairs={{0,2},{1,3},{2,0},{3,1},{4,6},{5,7},{6,4},{7,5},{8,10},{9,11},{10,... | collective-permute-start | bytes 221192 | tf_op jit(solution)/shard_map/ppermute | solution.py:752
  12.6 0.0 copy-done
  12.6 0.0 collective-permute-start.8
  12.6 0.0 collective-permute-done.1.refs_0_
  12.6 0.8 %collective-permute-done.2.refs_1_ = bf16[1,72,512]{2,1,0:T(8,128)(2,1)S(1)} collective-permute-done((bf16[1,72,512]{2,1,0:T(8,128)(2,1)}, bf16[1,72,512]{2,1,0:T(8,128)(2,1)S(1)}, u32[]{:S(2)}, u32[]{:S(2)}) %collective-permute-start.2) | collective-permute-done | bytes 73760 | tf_op jit(solution)/shard_map/ppermute | solution.py:752
  13.5 0.8 %collective-permute-done.3.refs_2_ = bf16[1,72,512]{2,1,0:T(8,128)(2,1)S(1)} collective-permute-done((bf16[1,72,512]{2,1,0:T(8,128)(2,1)}, bf16[1,72,512]{2,1,0:T(8,128)(2,1)S(1)}, u32[]{:S(2)}, u32[]{:S(2)}) %collective-permute-start.3) | collective-permute-done | bytes 73760 | tf_op jit(solution)/shard_map/ppermute | solution.py:752
  14.2 1.7 %collective-permute-start.5 = (bf16[3,72,512]{2,1,0:T(8,128)(2,1)S(1)}, bf16[3,72,512]{2,1,0:T(8,128)(2,1)S(1)}, u32[]{:S(2)}, u32[]{:S(2)}) collective-permute-start(bf16[3,72,512]{2,1,0:T(8,128)(2,1)S(1)} %shard_map.93.refs_2_), channel_id=1, source_target_pairs={{0,2},{1,3},{2,0},{3,1},{4,6},{5,7},{6,4},{7,5},{8,10},{9,11},{10,... | collective-permute-start | bytes 663560 | tf_op jit(solution)/shard_map/ppermute | solution.py:752
  15.9 0.0 collective-permute-done.refs_1_
  15.9 0.1 collective-permute-start.4
  16.0 2.1 %shard_map.95 = (bf16[128,384]{1,0:T(8,128)(2,1)S(1)}, bf16[320,384]{1,0:T(8,128)(2,1)S(1)}, bf16[320,384]{1,0:T(8,128)(2,1)S(1)}) custom-call(bf16[5,72,512]{2,1,0:T(8,128)(2,1)S(1)} %shard_map.94.stack_ref.refs_0_, bf16[512,1536]{1,0:T(8,128)(2,1)S(1)} %get-tuple-element.40.w_sub.refs_5_, bf16[3,1536,384]{2,1,0:T(8,128)(2,1)S(1)} %get-tuple-element.41.w_att, ...), custom_call_target="tpu_custom_call" | custom-call | flops 4840000000 | bytes 1000000 | tf_op jit(solution)/shard_map/pallas_call | solution.py:89
  18.2 0.0 collective-permute-done.4.stack_ref.refs_1_
  18.2 2.1 %shard_map.96 = (bf16[128,384]{1,0:T(8,128)(2,1)S(1)}, bf16[320,384]{1,0:T(8,128)(2,1)S(1)}, bf16[320,384]{1,0:T(8,128)(2,1)S(1)}) custom-call(bf16[5,72,512]{2,1,0:T(8,128)(2,1)S(1)} %collective-permute-done.4.stack_ref.refs_1_, bf16[512,1536]{1,0:T(8,128)(2,1)S(1)} %get-tuple-element.40.w_sub.refs_5_, bf16[3,1536,384]{2,1,0:T(8,128)(2,1)S(1)} %get-tuple-element.41.w_att, ...), custom_call_target="tpu_custom_call" | custom-call | flops 4840000000 | bytes 1000000 | tf_op jit(solution)/shard_map/pallas_call | solution.py:89
  20.3 0.2 collective-permute-done.5.refs_0_
  20.6 0.0 copy-start.5
  20.6 0.0 copy-start.6
  20.6 0.0 copy-start.7
  20.6 0.3 collective-permute-start.6
  21.0 1.2 %shard_map.99 = (bf16[192,384]{1,0:T(8,128)(2,1)S(1)}, bf16[192,384]{1,0:T(8,128)(2,1)S(1)}) custom-call(bf16[3,72,512]{2,1,0:T(8,128)(2,1)S(1)} %shard_map.97.refs_2_.stack_ref, bf16[512,1536]{1,0:T(8,128)(2,1)S(1)} %get-tuple-element.40.w_sub.refs_5_, bf16[3,1536,384]{2,1,0:T(8,128)(2,1)S(1)} %get-tuple-element.41.w_att, ...), custom_call_target="tpu_custom_call" | custom-call | flops 3304000000 | bytes 1000000 | tf_op jit(solution)/shard_map/pallas_call | solution.py:89
  22.2 0.0 collective-permute-done.6.refs_3_.stack_ref
  22.2 0.0 copy-done.5
  22.2 0.7 %shard_map.98 = (bf16[16,256]{1,0:T(8,128)(2,1)S(1)}, f32[2,288]{1,0:T(2,128)S(1)}) custom-call(s32[1,256]{1,0:T(1,128)S(1)} %bitcast.4, s32[1,256]{1,0:T(1,128)S(1)} %bitcast.6, bf16[5,72,512]{2,1,0:T(8,128)(2,1)S(1)} %shard_map.94.stack_ref.refs_0_, bf16[5,72,512]{2,1,0:T(8,128)(2,1)S(1)} %collective-permute-done.4.stack_ref.refs_1_, ...), custom_call_target="tpu_custom_call" | custom-call | flops 1800000000 | bytes 1000000 | tf_op jit(solution)/shard_map/pallas_call | solution.py:89
  22.9 1.7 %shard_map.100 = (bf16[48,384]{1,0:T(8,128)(2,1)S(1)}, bf16[192,384]{1,0:T(8,128)(2,1)S(1)}, bf16[48,384]{1,0:T(8,128)(2,1)S(1)}, bf16[192,384]{1,0:T(8,128)(2,1)S(1)}, bf16[48,384]{1,0:T(8,128)(2,1)S(1)}) custom-call(bf16[3,72,512]{2,1,0:T(8,128)(2,1)S(1)} %collective-permute-done.6.refs_3_.stack_ref, ...), custom_call_target="tpu_custom_call" | custom-call | flops 3880000000 | bytes 1000000 | tf_op jit(solution)/shard_map/pallas_call | solution.py:89
  24.6 2.2 %shard_map.101 = (bf16[96,384]{1,0:T(8,128)(2,1)S(1)}, bf16[96,384]{1,0:T(8,128)(2,1)S(1)}, bf16[288,384]{1,0:T(8,128)(2,1)S(1)}, bf16[1024,384]{1,0:T(8,128)(2,...) custom-call(f32[2,288]{1,0:T(2,128)S(1)} %get-tuple-element.44.bound_ref, ...), custom_call_target="tpu_custom_call" | custom-call | flops 5000000000 | bytes 1000000 | tf_op jit(solution)/shard_map/pallas_call | solution.py:89
  26.7 0.3 collective-permute-start.7
  27.0 0.3 shard_map.102.refs_0_
  27.4 0.7 %collective-permute-done.7.refs_1_ = bf16[96,384]{1,0:T(8,128)(2,1)S(1)} collective-permute-done((bf16[96,384]{1,0:T(8,128)(2,1)S(1)}, bf16[96,384]{1,0:T(8,128)(2,1)S(1)}, u32[]{:S(2)}, u32[]{:S(2)}) %collective-permute-start.7) | collective-permute-done | bytes 73760 | tf_op jit(solution)/shard_map/ppermute | solution.py:752
  28.1 0.0 collective-permute-done.8.refs_2_.w_near
  28.1 0.4 shard_map.103
  28.4 1.5 %collective-permute-start.11 = (bf16[80,1536]{1,0:T(8,128)(2,1)S(1)}, bf16[80,1536]{1,0:T(8,128)(2,1)S(1)}, u32[]{:S(2)}, u32[]{:S(2)}) collective-permute-start(bf16[80,1536]{1,0:T(8,128)(2,1)S(1)} %get-tuple-element.59._), channel_id=1, source_target_pairs={{0,2},{1,3},{2,0},{3,1},{4,6},{5,7},{6,4},{7,5},{8,10},{9,11},{10,... | collective-permute-start | bytes 737288 | tf_op jit(solution)/shard_map/ppermute | solution.py:752
  30.0 1.9 %shard_map.104 = (bf16[96,384]{1,0:T(8,128)(2,1)S(1)}, bf16[96,384]{1,0:T(8,128)(2,1)S(1)}) custom-call(bf16[80,1536]{1,0:T(8,128)(2,1)S(1)} %get-tuple-element.59._, bf16[288,384]{1,0:T(8,128)(2,1)S(1)} %get-tuple-element.60.q_ref, bf16[1024,384]{1,0:T(8,128)(2,1)S(1)} %get-tuple-element.61.k_ref, bf16[1024,384]{1,0:T(8,128)(2,1)S(1)} %get-tuple-element.62.v_ref, ...), custom_call_target="tpu_custom_call" | custom-call | flops 2000000000 | bytes 1000000 | tf_op jit(solution)/shard_map/pallas_call | solution.py:89
  31.9 0.1 collective-permute-start.9
  32.0 0.0 copy-done.8
  32.0 0.6 %collective-permute-start.10 = (bf16[16,1536]{1,0:T(8,128)(2,1)S(1)}, bf16[16,1536]{1,0:T(8,128)(2,1)S(1)}, u32[]{:S(2)}, u32[]{:S(2)}) collective-permute-start(bf16[16,1536]{1,0:T(8,128)(2,1)S(1)} %get-tuple-element.67), channel_id=1, source_target_pairs={{0,2},{1,3},{2,0},{3,1},{4,6},{5,7},{6,4},{7,5},{8,10},{9,11},{10,... | collective-permute-start | bytes 147464 | tf_op jit(solution)/shard_map/ppermute | solution.py:752
  32.6 0.6 %collective-permute-done.9.near = bf16[96,384]{1,0:T(8,128)(2,1)S(1)} collective-permute-done((bf16[96,384]{1,0:T(8,128)(2,1)S(1)}, bf16[96,384]{1,0:T(8,128)(2,1)S(1)}, u32[]{:S(2)}, u32[]{:S(2)}) %collective-permute-start.9) | collective-permute-done | bytes 73760 | tf_op jit(solution)/shard_map/ppermute | solution.py:752
  33.2 0.9 %shard_map.105.base_ref = f32[96,1536]{1,0:T(8,128)S(1)} custom-call(bf16[96,384]{1,0:T(8,128)(2,1)S(1)} %get-tuple-element.65.own, bf16[96,384]{1,0:T(8,128)(2,1)S(1)} %collective-permute-done.9.near, bf16[384,1536]{1,0:T(8,128)(2,1)S(1)} %copy-done, bf16[384,1536]{1,0:T(8,128)(2,1)S(1)} %collective-permute-done.8.refs_2_.w_near, ...), custom_call_target="tpu_custom_call" | custom-call | flops 1200000000 | bytes 1000000 | tf_op jit(solution)/shard_map/pallas_call | solution.py:89
  34.1 3.0 %collective-permute-done.11.refs_0_ = bf16[80,1536]{1,0:T(8,128)(2,1)S(1)} collective-permute-done((bf16[80,1536]{1,0:T(8,128)(2,1)S(1)}, bf16[80,1536]{1,0:T(8,128)(2,1)S(1)}, u32[]{:S(2)}, u32[]{:S(2)}) %collective-permute-start.11) | collective-permute-done | bytes 245792 | tf_op jit(solution)/shard_map/ppermute | solution.py:752
  37.1 1.2 %shard_map.106 = (bf16[48,1536]{1,0:T(8,128)(2,1)S(1)}, f32[80,1536]{1,0:T(8,128)S(1)}, f32[80,1536]{1,0:T(8,128)S(1)}) custom-call(f32[96,1536]{1,0:T(8,128)S(1)} %shard_map.105.base_ref, bf16[80,1536]{1,0:T(8,128)(2,1)S(1)} %collective-permute-done.11.refs_0_, f32[1,1536]{1,0:T(1,128)S(1)} %broadcast_in_dim.11.refs_1_.refs_4_, bf16[31,1536]{1,0:T(8,128)(2,1)S(1)} %copy-done.3), custom_call_target="tpu_custom_call" | custom-call | flops 1000000000 | bytes 1000000 | tf_op jit(solution)/shard_map/pallas_call | solution.py:89
  38.4 0.0 collective-permute-done.10.refs_0_
  38.4 1.3 %shard_map.107 = bf16[64,1536]{1,0:T(8,128)(2,1)} custom-call(f32[96,1536]{1,0:T(8,128)S(1)} %shard_map.105.base_ref, bf16[16,1536]{1,0:T(8,128)(2,1)S(1)} %collective-permute-done.10.refs_0_, bf16[48,1536]{1,0:T(8,128)(2,1)S(1)} %get-tuple-element.68.refs_1_, f32[80,1536]{1,0:T(8,128)S(1)} %get-tuple-element.69.refs_2_, ...), custom_call_target="tpu_custom_call" | custom-call | flops 3000000000 | bytes 1000000 | tf_op jit(solution)/shard_map/pallas_call | solution.py:89
  (12 shorter events, 0.1 us)
Async XLA Ops:
  0.0 8.8 %copy-start.1 = (bf16[3,1536,384]{2,1,0:T(8,128)(2,1)S(1)}, bf16[3,1536,384]{2,1,0:T(8,128)(2,1)}, u32[]{:S(2)}) copy-start(bf16[3,1536,384]{2,1,0:T(8,128)(2,1)} %w_att.1) | copy-start | bytes 10616836
  0.0 8.8 %copy-start.2 = (bf16[512,1536]{1,0:T(8,128)(2,1)S(1)}, bf16[512,1536]{1,0:T(8,128)(2,1)}, u32[]{:S(2)}) copy-start(bf16[512,1536]{1,0:T(8,128)(2,1)} %w_sub.1) | copy-start | bytes 4718596
  3.1 9.5 %copy-start = (bf16[384,1536]{1,0:T(8,128)(2,1)S(1)}, bf16[384,1536]{1,0:T(8,128)(2,1)}, u32[]{:S(2)}) copy-start(bf16[384,1536]{1,0:T(8,128)(2,1)} %w_own.1) | copy-start | bytes 3538948
  3.1 9.5 %collective-permute-start.1 = (bf16[1,72,512]{2,1,0:T(8,128)(2,1)}, bf16[1,72,512]{2,1,0:T(8,128)(2,1)S(1)}, u32[]{:S(2)}, u32[]{:S(2)}) collective-permute-start(bf16[1,72,512]{2,1,0:T(8,128)(2,1)} %shard_map.91.stack_ref), channel_id=1, source_target_pairs={{0,12},{4,8},{8,4},{12,0},{1,13},{5,9},{9,5},{13,1},{2,14},{6,10},... | collective-permute-start | bytes 221192 | tf_op jit(solution)/shard_map/ppermute | solution.py:752
  8.2 5.3 %collective-permute-start.2 = (bf16[1,72,512]{2,1,0:T(8,128)(2,1)}, bf16[1,72,512]{2,1,0:T(8,128)(2,1)S(1)}, u32[]{:S(2)}, u32[]{:S(2)}) collective-permute-start(bf16[1,72,512]{2,1,0:T(8,128)(2,1)} %shard_map.91.stack_ref), channel_id=1, source_target_pairs={{0,4},{4,0},{8,12},{12,8},{1,5},{5,1},{9,13},{13,9},{2,6},{6,2},{1... | collective-permute-start | bytes 221192 | tf_op jit(solution)/shard_map/ppermute | solution.py:752
  8.2 6.0 %collective-permute-start.3 = (bf16[1,72,512]{2,1,0:T(8,128)(2,1)}, bf16[1,72,512]{2,1,0:T(8,128)(2,1)S(1)}, u32[]{:S(2)}, u32[]{:S(2)}) collective-permute-start(bf16[1,72,512]{2,1,0:T(8,128)(2,1)} %shard_map.91.stack_ref), channel_id=1, source_target_pairs={{0,8},{4,12},{8,0},{12,4},{1,9},{5,13},{9,1},{13,5},{2,10},{6,14},... | collective-permute-start | bytes 221192 | tf_op jit(solution)/shard_map/ppermute | solution.py:752
  8.8 0.9 %copy-start.4 = (bf16[1,72,512]{2,1,0:T(8,128)(2,1)S(1)}, bf16[1,72,512]{2,1,0:T(8,128)(2,1)}, u32[]{:S(2)}) copy-start(bf16[1,72,512]{2,1,0:T(8,128)(2,1)} %shard_map.91.stack_ref) | copy-start | bytes 221188
  10.9 5.0 %collective-permute-start = (bf16[1,72,512]{2,1,0:T(8,128)(2,1)S(1)}, bf16[1,72,512]{2,1,0:T(8,128)(2,1)S(1)}, u32[]{:S(2)}, u32[]{:S(2)}) collective-permute-start(bf16[1,72,512]{2,1,0:T(8,128)(2,1)S(1)} %get-tuple-element.38.refs_0_), channel_id=1, source_target_pairs={{0,2},{1,3},{2,0},{3,1},{4,6},{5,7},{6,4},{7,5},{8,10},{9,11},{10,... | collective-permute-start | bytes 221192 | tf_op jit(solution)/shard_map/ppermute | solution.py:752
  12.6 15.5 %collective-permute-start.8 = (bf16[384,1536]{1,0:T(8,128)(2,1)S(1)}, bf16[384,1536]{1,0:T(8,128)(2,1)S(1)}, u32[]{:S(2)}, u32[]{:S(2)}) collective-permute-start(bf16[384,1536]{1,0:T(8,128)(2,1)S(1)} %copy-done), channel_id=1, source_target_pairs={{0,1},{1,0},{2,3},{3,2},{4,5},{5,4},{6,7},{7,6},{8,9},{9,8},{10,11... | collective-permute-start | bytes 3538952 | tf_op jit(solution)/shard_map/ppermute | solution.py:752
  14.2 6.3 %collective-permute-start.5 = (bf16[3,72,512]{2,1,0:T(8,128)(2,1)S(1)}, bf16[3,72,512]{2,1,0:T(8,128)(2,1)S(1)}, u32[]{:S(2)}, u32[]{:S(2)}) collective-permute-start(bf16[3,72,512]{2,1,0:T(8,128)(2,1)S(1)} %shard_map.93.refs_2_), channel_id=1, source_target_pairs={{0,2},{1,3},{2,0},{3,1},{4,6},{5,7},{6,4},{7,5},{8,10},{9,11},{10,... | collective-permute-start | bytes 663560 | tf_op jit(solution)/shard_map/ppermute | solution.py:752
  15.9 2.2 %collective-permute-start.4 = (bf16[5,72,512]{2,1,0:T(8,128)(2,1)S(1)}, bf16[5,72,512]{2,1,0:T(8,128)(2,1)S(1)}, u32[]{:S(2)}, u32[]{:S(2)}) collective-permute-start(bf16[5,72,512]{2,1,0:T(8,128)(2,1)S(1)} %shard_map.94.stack_ref.refs_0_), channel_id=1, source_target_pairs={{0,1},{1,0},{2,3},{3,2},{4,5},{5,4},{6,7},{7,6},{8,9},{9,8},{10,11... | collective-permute-start | bytes 1105928 | tf_op jit(solution)/shard_map/ppermute | solution.py:752
  20.6 1.6 %copy-start.5 = (s32[256]{0:T(256)S(1)}, s32[256]{0:T(256)}, u32[]{:S(2)}) copy-start(s32[256]{0:T(256)} %param.10) | copy-start | bytes 3076
  20.6 1.6 %copy-start.6 = (s32[256]{0:T(256)S(1)}, s32[256]{0:T(256)}, u32[]{:S(2)}) copy-start(s32[256]{0:T(256)} %param.11) | copy-start | bytes 3076
  20.6 1.6 %copy-start.7 = (bf16[512,1152]{1,0:T(8,128)(2,1)S(1)}, bf16[512,1152]{1,0:T(8,128)(2,1)}, u32[]{:S(2)}) copy-start(bf16[512,1152]{1,0:T(8,128)(2,1)} %constant.2.clone.table.refs_4_) | copy-start | bytes 3538948
  20.6 1.6 %collective-permute-start.6 = (bf16[3,72,512]{2,1,0:T(8,128)(2,1)S(1)}, bf16[3,72,512]{2,1,0:T(8,128)(2,1)S(1)}, u32[]{:S(2)}, u32[]{:S(2)}) collective-permute-start(bf16[3,72,512]{2,1,0:T(8,128)(2,1)S(1)} %shard_map.97.refs_2_.stack_ref), channel_id=1, source_target_pairs={{0,1},{1,0},{2,3},{3,2},{4,5},{5,4},{6,7},{7,6},{8,9},{9,8},{10,11... | collective-permute-start | bytes 663560 | tf_op jit(solution)/shard_map/ppermute | solution.py:752
  26.7 1.3 %collective-permute-start.7 = (bf16[96,384]{1,0:T(8,128)(2,1)S(1)}, bf16[96,384]{1,0:T(8,128)(2,1)S(1)}, u32[]{:S(2)}, u32[]{:S(2)}) collective-permute-start(bf16[96,384]{1,0:T(8,128)(2,1)S(1)} %get-tuple-element.58), channel_id=1, source_target_pairs={{0,1},{1,0},{2,3},{3,2},{4,5},{5,4},{6,7},{7,6},{8,9},{9,8},{10,11... | collective-permute-start | bytes 221192 | tf_op jit(solution)/shard_map/ppermute | solution.py:752
  28.4 8.7 %collective-permute-start.11 = (bf16[80,1536]{1,0:T(8,128)(2,1)S(1)}, bf16[80,1536]{1,0:T(8,128)(2,1)S(1)}, u32[]{:S(2)}, u32[]{:S(2)}) collective-permute-start(bf16[80,1536]{1,0:T(8,128)(2,1)S(1)} %get-tuple-element.59._), channel_id=1, source_target_pairs={{0,2},{1,3},{2,0},{3,1},{4,6},{5,7},{6,4},{7,5},{8,10},{9,11},{10,... | collective-permute-start | bytes 737288 | tf_op jit(solution)/shard_map/ppermute | solution.py:752
  30.0 2.0 %copy-start.8 = (f32[1536]{0:T(1024)S(1)}, f32[1536]{0:T(1024)}, u32[]{:S(2)}) copy-start(f32[1536]{0:T(1024)} %param.15) | copy-start | bytes 18436
  31.9 1.3 %collective-permute-start.9 = (bf16[96,384]{1,0:T(8,128)(2,1)S(1)}, bf16[96,384]{1,0:T(8,128)(2,1)S(1)}, u32[]{:S(2)}, u32[]{:S(2)}) collective-permute-start(bf16[96,384]{1,0:T(8,128)(2,1)S(1)} %get-tuple-element.66), channel_id=1, source_target_pairs={{0,1},{1,0},{2,3},{3,2},{4,5},{5,4},{6,7},{7,6},{8,9},{9,8},{10,11... | collective-permute-start | bytes 221192 | tf_op jit(solution)/shard_map/ppermute | solution.py:752
  32.0 6.4 %collective-permute-start.10 = (bf16[16,1536]{1,0:T(8,128)(2,1)S(1)}, bf16[16,1536]{1,0:T(8,128)(2,1)S(1)}, u32[]{:S(2)}, u32[]{:S(2)}) collective-permute-start(bf16[16,1536]{1,0:T(8,128)(2,1)S(1)} %get-tuple-element.67), channel_id=1, source_target_pairs={{0,2},{1,3},{2,0},{3,1},{4,6},{5,7},{6,4},{7,5},{8,10},{9,11},{10,... | collective-permute-start | bytes 147464 | tf_op jit(solution)/shard_map/ppermute | solution.py:752
  33.2 3.9 %copy-start.3 = (bf16[31,1536]{1,0:T(8,128)(2,1)S(1)}, bf16[31,1536]{1,0:T(8,128)(2,1)}, u32[]{:S(2)}) copy-start(bf16[31,1536]{1,0:T(8,128)(2,1)} %refs_5_.1) | copy-start | bytes 285700

commit v8 on v7

--- a/solution.py
+++ b/solution.py
@@ -42,8 +42,7 @@
     kept = bin_index <= NFFT // 2
     cosine = np.where(kept, np.cos(angle), 0.0) * window[:, None]
     sine = np.where(kept, -np.sin(angle), 0.0) * window[:, None]
-    table = np.concatenate([cosine, sine], axis=1).astype(np.float32)
-    return np.pad(table, ((0, WIDE - NFFT), (0, 0)))
+    return np.concatenate([cosine, sine], axis=1).astype(np.float32)
 
 
 def mel_bank():
@@ -58,8 +57,9 @@
 
 def front_tables():
     high, low = split_high_low(fourier_table())
-    bank = np.concatenate(split_high_low(mel_bank()), axis=0)
-    return np.concatenate([high, low, bank], axis=1)
+    bank = np.concatenate(split_high_low(mel_bank()), axis=1)
+    bank = np.pad(bank, ((0, 0), (0, high.shape[1] - bank.shape[1])))
+    return np.concatenate([high, low, bank], axis=0)
 
 
 def dot32(left, right):
@@ -130,43 +130,41 @@
     )
 
 
-def padded_row(row):
-    return jnp.concatenate([row, jnp.zeros((1, SUB * NMEL - row.shape[1]), row.dtype)], axis=1)
+def stack_of(ref, block, begin, end):
+    half = (ref.shape[1] - EXTRA) // 2
+    return jnp.concatenate([ref[block, begin:end, :], ref[block, half + begin : half + end, :]], axis=1)
 
 
 def log_mel(windows, tables, copies=()):
-    wide, bank = 2 * BINS, slice(4 * BINS, 4 * BINS + NMEL)
-
-    def fetched(number, rows, columns):
+    lanes = lax.broadcasted_iota(jnp.int32, windows.shape, 1)
+    windows = jnp.where(lanes < NFFT, windows, 0.0)
+
+    def fetched(number, begin):
         def load():
             if copies:
                 copies[number].wait()
-            return tables[rows, columns]
+            return tables[begin : begin + WIDE, :]
 
         return load
 
-    every = slice(None)
-    spectrum = dot_split(
-        windows, fetched(0, every, slice(0, wide)), fetched(1, every, slice(wide, 2 * wide))
-    )
+    spectrum = dot_split(windows, fetched(0, 0), fetched(1, NFFT))
     power = jnp.square(spectrum[:, :BINS]) + jnp.square(spectrum[:, BINS:])
-    bank_high = fetched(2, slice(0, BINS), bank)
-    return jnp.log(dot_split(power, bank_high, lambda: tables[BINS:, bank]) + 1e-06)
+    bank = [tables[2 * NFFT :, part * NMEL : (part + 1) * NMEL] for part in range(2)]
+    return jnp.log(dot_split(power, lambda: bank[0], lambda: bank[1]) + 1e-06)
 
 
 def log_mel_rows(starts, ends, samples, tables, frames_local):
     rows = frames_local * FRAME_ROWS
     frames_shard = starts.shape[1]
 
-    wide = 2 * BINS
-    spans = (slice(0, wide), slice(wide, 2 * wide), slice(2 * wide, tables.shape[1]))
+    spans = (pl.ds(0, WIDE), pl.ds(WIDE, tables.shape[0] - WIDE))
 
     def kernel(start, end, wave, table, out, held, start_ref, end_ref, tables_ref, sems):
         pairs = (
             (wave, held.at[pl.ds(0, rows)]),
             (start, start_ref),
             (end, end_ref),
-        ) + tuple((table.at[:, span], tables_ref.at[:, span]) for span in spans)
+        ) + tuple((table.at[span], tables_ref.at[span]) for span in spans)
         copies = [
             pltpu.make_async_copy(source, target, sems.at[slot])
             for slot, (source, target) in enumerate(pairs)
@@ -182,33 +180,38 @@
             line, lane = divmod(sub * HOP, LANES)
             taken = jnp.concatenate(lines[line : line + WIDE // LANES], axis=1)
             windows.append(pltpu.roll(taken, WIDE - lane, axis=1) if lane else taken)
-        extras = []
+        pieces = []
         for taken in (range(rows - TAIL_LINES, rows), range(HEAD_LINES)):
             line = jnp.concatenate([held[row : row + 1, :] for row in taken], axis=1)
             high = line.astype(jnp.bfloat16).astype(jnp.float32)
-            extras += [padded_row(high), padded_row(line - high)]
+            pieces += [high, line - high]
         for ref in (start_ref, end_ref):
             edge = jnp.concatenate([ref[:, :HALO], ref[:, frames_shard - HALO :]], axis=1)
             high = edge // DIGIT
             low = edge - high * DIGIT
-            extras += [padded_row(digit.astype(jnp.float32)) for digit in (high, low)]
-        out[0, frames_local:, :] = jnp.concatenate(extras, axis=0).astype(jnp.bfloat16)
+            pieces += [digit.astype(jnp.float32) for digit in (high, low)]
+        filled = sum(piece.shape[1] for piece in pieces)
+        pieces.append(jnp.zeros((1, EXTRA * 2 * NMEL - filled), jnp.float32))
+        flat = jnp.concatenate(pieces, axis=1)
+        extras = [flat[:, row * 2 * NMEL : (row + 1) * 2 * NMEL] for row in range(EXTRA)]
+        out[0, 2 * frames_local :, :] = jnp.concatenate(extras, axis=0).astype(jnp.bfloat16)
         mel = log_mel(jnp.concatenate(windows, axis=0), tables_ref, copies[3:])
         for sub in range(SUB):
-            out[0, 0:frames_local, sub * NMEL : (sub + 1) * NMEL] = mel[
+            begin, lane = sub // 2 * frames_local, sub % 2 * NMEL
+            out[0, begin : begin + frames_local, lane : lane + NMEL] = mel[
                 sub * frames_local : (sub + 1) * frames_local
             ].astype(jnp.bfloat16)
 
     return call(
         kernel,
-        jax.ShapeDtypeStruct((1, frames_local + EXTRA, SUB * NMEL), jnp.bfloat16),
+        jax.ShapeDtypeStruct((1, 2 * frames_local + EXTRA, 2 * NMEL), jnp.bfloat16),
         (starts, ends, samples, tables),
         scratch=[
             pltpu.VMEM((rows + 8, LANES), jnp.float32),
             pltpu.VMEM(starts.shape, starts.dtype),
             pltpu.VMEM(ends.shape, ends.dtype),
             pltpu.VMEM(tables.shape, tables.dtype),
-            pltpu.SemaphoreType.DMA((6,)),
+            pltpu.SemaphoreType.DMA((5,)),
         ],
         remote=4,
         vmem=54,
@@ -234,13 +237,19 @@
         slot = 0
         for stack_ref, count in zip(stack_refs, counts):
             for block in range(count):
-                kept = stack_ref[block, frames_local:, :].astype(jnp.float32)
+                kept = stack_ref[block, 2 * frames_local :, :].astype(jnp.float32)
+                flat = jnp.concatenate([kept[row : row + 1] for row in range(EXTRA)], axis=1)
                 here = slice(slot, slot + 1)
-                tails[here, :] = (kept[0:1] + kept[1:2])[:, : TAIL_LINES * LANES]
-                heads[here, :] = (kept[2:3] + kept[3:4])[:, : HEAD_LINES * LANES]
+                tail, head = TAIL_LINES * LANES, HEAD_LINES * LANES
+                tails[here, :] = flat[:, :tail] + flat[:, tail : 2 * tail]
+                heads[here, :] = flat[:, 2 * tail : 2 * tail + head] + flat[
+                    :, 2 * tail + head : 2 * (tail + head)
+                ]
+                digits = flat[:, 2 * (tail + head) :]
                 for line in range(2):
-                    edge = kept[4 + 2 * line : 5 + 2 * line] * DIGIT + kept[5 + 2 * line : 6 + 2 * line]
-                    edges[line, here, :] = edge[:, :LANES]
+                    high = digits[:, 4 * line * HALO : (4 * line + 2) * HALO]
+                    low = digits[:, (4 * line + 2) * HALO : (4 * line + 4) * HALO]
+                    edges[line, here, 0 : 2 * HALO] = high * DIGIT + low
                 slot += 1
         numbers = [
             slot_tm(time_index) * parts + (model_index ^ slot_mp) for slot_tm, slot_mp in places
@@ -297,7 +306,7 @@
     lasts = []
     for stack_ref, count in zip(stack_refs, counts):
         for block in range(count):
-            kept = stack_ref[block, frames_local - HALO : frames_local, 0 : 2 * NMEL]
+            kept = stack_ref[block, frames_local - HALO : frames_local, :]
             lasts.append(kept.astype(jnp.float32)[HALO - 1 : HALO])
     if len(lasts) < rows:
         lasts.append(jnp.zeros((rows - len(lasts), 2 * NMEL), jnp.float32))
@@ -350,8 +359,8 @@
         slot = 0
         for ref, blocks in zip(every_refs, counts):
             for block in range(blocks):
-                heads[slot] = ref[block, 0:HALO, :]
-                tails[slot] = ref[block, frames_local - HALO : frames_local, :]
+                heads[slot] = stack_of(ref, block, 0, HALO)
+                tails[slot] = stack_of(ref, block, frames_local - HALO, frames_local)
                 slot += 1
         time_index, parts = lax.axis_index("tm"), lax.axis_size("mp")
         left = slot_of(places, time_index - 1, parts - 1)
@@ -362,7 +371,7 @@
         return [lasts[...].astype(jnp.bfloat16), tail, heads[right]]
 
     def kernel(stack_ref, w_sub, w_att, sums, *refs):
-        stack_rows = [stack_ref[block, 0:frames_local, :] for block in range(count)]
+        stack_rows = [stack_of(stack_ref, block, 0, frames_local) for block in range(count)]
         if boundary:
             every_refs, refs = refs[: len(every)], refs[len(every) :]
             fixed_ref, *refs = refs
@@ -395,7 +404,7 @@
 
     shapes = [shape(query_rows)] * bool(query_rows) + [shape(extra_rows)] * bool(extra_rows)
     shapes += ([shape(rows)] + [shape(extra_rows)] * bool(extra_rows)) * 2
-    depth = stack.shape[2]
+    depth = weights[0].shape[0]
     return call(
         kernel,
         shapes,
@@ -610,7 +619,7 @@
         begin = 0
         for stack_ref, count in zip(stack_refs, counts):
             for block in range(count):
-                held[begin : begin + frames_local, :] = stack_ref[block, 0:frames_local, :]
+                held[begin : begin + frames_local, :] = stack_of(stack_ref, block, 0, frames_local)
                 begin += frames_local
         rows = last_rows(stack_refs, counts, frames_local, fixed_ref[...], fixed.shape[0])
         patch(held, rows, range(slots), frames_local)

time: 39.8 us -> 39.5 us (level)
  transfers between devices with their start and end apart: 12 -> 12, of which waited for: 6 -> 6; matrix products, arithmetic and copies ran while one was open for 0% -> 0% of each run, Pallas kernels for 39% -> 40%
where the time goes in v8:
time: 39.5 us; the launch traced here: 39.3 us
  Pallas kernels  20.2 us (51%)
  starting transfers between devices  12 us (30%)
  waiting for transfers between devices  5.97 us (15%)
  local copies, waits for them, and re-layouts  0.96 us (2%)
    pallas_call x17, Pallas kernels, call(): pl.pallas_call(kernel, out_shape=out_shape, in_specs=specs, out_specs=jax...  20.2 us
    ppermute x12, starting transfers between devices, exchange(): lax.ppermute(block, axis, [(i, i ^ bit) for i in range(lax.axis_size(axis...  12 us
    ppermute x12, waiting for transfers between devices, exchange(): lax.ppermute(block, axis, [(i, i ^ bit) for i in range(lax.axis_size(axis...  5.97 us
    unnamed x18, local copies, waits for them, and re-layouts  0.95 us
  transfers between devices with their start and end apart: 12, of which 6 were waited for; matrix products, arithmetic and copies ran while one was open for 0% of the time, Pallas kernels for 40%

profile of v8, /device:TPU:0, one launch (start us, length us, event | category | flops | bytes accessed | tf_op | source)
XLA Modules:
  0.0 39.3 jit_solution(1698134842765801241)
XLA Ops:
  0.0 3.0 %shard_map.91.stack_ref = bf16[1,136,256]{2,1,0:T(8,128)(2,1)} custom-call(s32[1,256]{1,0:T(1,128)} %bitcast.3, s32[1,256]{1,0:T(1,128)} %bitcast.5, f32[320,128]{1,0:T(8,128)} %bitcast.7, bf16[1056,512]{1,0:T(8,128)(2,1)} %constant.2.clone.table.refs_4_), custom_call_target="tpu_custom_call" | custom-call | flops 2000000000 | bytes 1000000 | tf_op jit(solution)/shard_map/pallas_call | solution.py:89
  3.0 0.0 copy-start
  3.0 5.1 %collective-permute-start.1 = (bf16[1,136,256]{2,1,0:T(8,128)(2,1)}, bf16[1,136,256]{2,1,0:T(8,128)(2,1)S(1)}, u32[]{:S(2)}, u32[]{:S(2)}) collective-permute-start(bf16[1,136,256]{2,1,0:T(8,128)(2,1)} %shard_map.91.stack_ref), channel_id=1, source_target_pairs={{0,12},{4,8},{8,4},{12,0},{1,13},{5,9},{9,5},{13,1},{2,14},{6,10},... | collective-permute-start | bytes 208904 | tf_op jit(solution)/shard_map/ppermute | solution.py:761
  8.1 0.0 collective-permute-start.2
  8.1 0.6 %collective-permute-start.3 = (bf16[1,136,256]{2,1,0:T(8,128)(2,1)}, bf16[1,136,256]{2,1,0:T(8,128)(2,1)S(1)}, u32[]{:S(2)}, u32[]{:S(2)}) collective-permute-start(bf16[1,136,256]{2,1,0:T(8,128)(2,1)} %shard_map.91.stack_ref), channel_id=1, source_target_pairs={{0,8},{4,12},{8,0},{12,4},{1,9},{5,13},{9,1},{13,5},{2,10},{6,14},... | collective-permute-start | bytes 208904 | tf_op jit(solution)/shard_map/ppermute | solution.py:761
  8.8 0.0 copy-done.1
  8.8 0.9 %copy-done.4 = bf16[1,136,256]{2,1,0:T(8,128)(2,1)S(1)} copy-done((bf16[1,136,256]{2,1,0:T(8,128)(2,1)S(1)}, bf16[1,136,256]{2,1,0:T(8,128)(2,1)}, u32[]{:S(2)}) %copy-start.4) | copy-done | bytes 69656
  9.7 1.2 %shard_map.92 = (bf16[512,1536]{1,0:T(8,128)(2,1)S(1)}, bf16[3,1536,384]{2,1,0:T(8,128)(2,1)S(1)}, f32[8,384]{1,0:T(8,128)S(1)}, bf16[1,136,256]{2,1,0:T(8,128)(2,1)S(1)}) custom-call(bf16[1,136,256]{2,1,0:T(8,128)(2,1)S(1)} %copy-done.4, bf16[512,1536]{1,0:T(8,128)(2,1)S(1)} %copy-done.2, bf16[3,1536,384]{2,1,0:T(8,128)(2,1)S(1)} %copy-done.1), custom_call_target="tpu_custom_call" | custom-call | flops 2000000000 | bytes 1000000 | tf_op jit(solution)/shard_map/pallas_call | solution.py:89
  10.8 1.7 %collective-permute-start = (bf16[1,136,256]{2,1,0:T(8,128)(2,1)S(1)}, bf16[1,136,256]{2,1,0:T(8,128)(2,1)S(1)}, u32[]{:S(2)}, u32[]{:S(2)}) collective-permute-start(bf16[1,136,256]{2,1,0:T(8,128)(2,1)S(1)} %get-tuple-element.38.refs_0_), channel_id=1, source_target_pairs={{0,2},{1,3},{2,0},{3,1},{4,6},{5,7},{6,4},{7,5},{8,10},{9,11},{10,... | collective-permute-start | bytes 208904 | tf_op jit(solution)/shard_map/ppermute | solution.py:761
  12.5 0.0 collective-permute-start.8
  12.5 0.0 collective-permute-done.1.refs_0_
  12.6 0.6 %collective-permute-done.2.refs_1_ = bf16[1,136,256]{2,1,0:T(8,128)(2,1)S(1)} collective-permute-done((bf16[1,136,256]{2,1,0:T(8,128)(2,1)}, bf16[1,136,256]{2,1,0:T(8,128)(2,1)S(1)}, u32[]{:S(2)}, u32[]{:S(2)}) %collective-permute-start.2) | collective-permute-done | bytes 69664 | tf_op jit(solution)/shard_map/ppermute | solution.py:761
  13.2 0.9 %collective-permute-done.3.refs_2_ = bf16[1,136,256]{2,1,0:T(8,128)(2,1)S(1)} collective-permute-done((bf16[1,136,256]{2,1,0:T(8,128)(2,1)}, bf16[1,136,256]{2,1,0:T(8,128)(2,1)S(1)}, u32[]{:S(2)}, u32[]{:S(2)}) %collective-permute-start.3) | collective-permute-done | bytes 69664 | tf_op jit(solution)/shard_map/ppermute | solution.py:761
  14.1 1.6 %collective-permute-start.5 = (bf16[3,136,256]{2,1,0:T(8,128)(2,1)S(1)}, bf16[3,136,256]{2,1,0:T(8,128)(2,1)S(1)}, u32[]{:S(2)}, u32[]{:S(2)}) collective-permute-start(bf16[3,136,256]{2,1,0:T(8,128)(2,1)S(1)} %shard_map.93.refs_2_), channel_id=1, source_target_pairs={{0,2},{1,3},{2,0},{3,1},{4,6},{5,7},{6,4},{7,5},{8,10},{9,11},{10,... | collective-permute-start | bytes 626696 | tf_op jit(solution)/shard_map/ppermute | solution.py:761
  15.6 0.0 collective-permute-done.refs_1_
  15.7 0.1 collective-permute-start.4
  15.7 2.1 %shard_map.95 = (bf16[128,384]{1,0:T(8,128)(2,1)S(1)}, bf16[320,384]{1,0:T(8,128)(2,1)S(1)}, bf16[320,384]{1,0:T(8,128)(2,1)S(1)}) custom-call(bf16[5,136,256]{2,1,0:T(8,128)(2,1)S(1)} %shard_map.94.stack_ref.refs_0_, bf16[512,1536]{1,0:T(8,128)(2,1)S(1)} %get-tuple-element.40.w_sub.refs_5_, bf16[3,1536,384]{2,1,0:T(8,128)(2,1)S(1)} %get-tuple-element.41.w_att, ...), custom_call_target="tpu_custom_call" | custom-call | flops 4840000000 | bytes 1000000 | tf_op jit(solution)/shard_map/pallas_call | solution.py:89
  17.9 0.0 collective-permute-done.4.stack_ref.refs_1_
  17.9 2.1 %shard_map.96 = (bf16[128,384]{1,0:T(8,128)(2,1)S(1)}, bf16[320,384]{1,0:T(8,128)(2,1)S(1)}, bf16[320,384]{1,0:T(8,128)(2,1)S(1)}) custom-call(bf16[5,136,256]{2,1,0:T(8,128)(2,1)S(1)} %collective-permute-done.4.stack_ref.refs_1_, bf16[512,1536]{1,0:T(8,128)(2,1)S(1)} %get-tuple-element.40.w_sub.refs_5_, bf16[3,1536,384]{2,1,0:T(8,128)(2,1)S(1)} %get-tuple-element.41.w_att, ...), custom_call_target="tpu_custom_call" | custom-call | flops 4840000000 | bytes 1000000 | tf_op jit(solution)/shard_map/pallas_call | solution.py:89
  20.1 0.2 collective-permute-done.5.refs_0_
  20.2 0.0 copy-start.5
  20.3 0.0 copy-start.6
  20.3 0.0 copy-start.7
  20.3 0.4 %collective-permute-start.6 = (bf16[3,136,256]{2,1,0:T(8,128)(2,1)S(1)}, bf16[3,136,256]{2,1,0:T(8,128)(2,1)S(1)}, u32[]{:S(2)}, u32[]{:S(2)}) collective-permute-start(bf16[3,136,256]{2,1,0:T(8,128)(2,1)S(1)} %shard_map.97.refs_2_.stack_ref), channel_id=1, source_target_pairs={{0,1},{1,0},{2,3},{3,2},{4,5},{5,4},{6,7},{7,6},{8,9},{9,8},{10,11... | collective-permute-start | bytes 626696 | tf_op jit(solution)/shard_map/ppermute | solution.py:761
  20.7 1.2 %shard_map.99 = (bf16[192,384]{1,0:T(8,128)(2,1)S(1)}, bf16[192,384]{1,0:T(8,128)(2,1)S(1)}) custom-call(bf16[3,136,256]{2,1,0:T(8,128)(2,1)S(1)} %shard_map.97.refs_2_.stack_ref, bf16[512,1536]{1,0:T(8,128)(2,1)S(1)} %get-tuple-element.40.w_sub.refs_5_, bf16[3,1536,384]{2,1,0:T(8,128)(2,1)S(1)} %get-tuple-element.41.w_att, ...), custom_call_target="tpu_custom_call" | custom-call | flops 3304000000 | bytes 1000000 | tf_op jit(solution)/shard_map/pallas_call | solution.py:89
  21.9 0.0 collective-permute-done.6.refs_3_.stack_ref
  21.9 0.0 copy-done.5
  21.9 0.0 copy-done.6
  21.9 0.0 copy-done.7
  21.9 0.6 %shard_map.98 = (bf16[16,256]{1,0:T(8,128)(2,1)S(1)}, f32[2,288]{1,0:T(2,128)S(1)}) custom-call(s32[1,256]{1,0:T(1,128)S(1)} %bitcast.4, s32[1,256]{1,0:T(1,128)S(1)} %bitcast.6, bf16[5,136,256]{2,1,0:T(8,128)(2,1)S(1)} %shard_map.94.stack_ref.refs_0_, bf16[5,136,256]{2,1,0:T(8,128)(2,1)S(1)} %collective-permute-done.4.stack_ref.refs_1_, ...), custom_call_target="tpu_custom_call" | custom-call | flops 1800000000 | bytes 1000000 | tf_op jit(solution)/shard_map/pallas_call | solution.py:89
  22.6 1.7 %shard_map.100 = (bf16[48,384]{1,0:T(8,128)(2,1)S(1)}, bf16[192,384]{1,0:T(8,128)(2,1)S(1)}, bf16[48,384]{1,0:T(8,128)(2,1)S(1)}, bf16[192,384]{1,0:T(8,128)(2,1)S(1)}, bf16[48,384]{1,0:T(8,128)(2,1)S(1)}) custom-call(bf16[3,136,256]{2,1,0:T(8,128)(2,1)S(1)} %collective-permute-done.6.refs_3_.stack_ref, ...), custom_call_target="tpu_custom_call" | custom-call | flops 3880000000 | bytes 1000000 | tf_op jit(solution)/shard_map/pallas_call | solution.py:89
  24.3 2.2 %shard_map.101 = (bf16[96,384]{1,0:T(8,128)(2,1)S(1)}, bf16[96,384]{1,0:T(8,128)(2,1)S(1)}, bf16[288,384]{1,0:T(8,128)(2,1)S(1)}, bf16[1024,384]{1,0:T(8,128)(2,...) custom-call(f32[2,288]{1,0:T(2,128)S(1)} %get-tuple-element.44.bound_ref, ...), custom_call_target="tpu_custom_call" | custom-call | flops 5000000000 | bytes 1000000 | tf_op jit(solution)/shard_map/pallas_call | solution.py:89
  26.4 0.3 collective-permute-start.7
  26.7 0.3 shard_map.102.refs_0_
  27.1 0.7 %collective-permute-done.7.refs_1_ = bf16[96,384]{1,0:T(8,128)(2,1)S(1)} collective-permute-done((bf16[96,384]{1,0:T(8,128)(2,1)S(1)}, bf16[96,384]{1,0:T(8,128)(2,1)S(1)}, u32[]{:S(2)}, u32[]{:S(2)}) %collective-permute-start.7) | collective-permute-done | bytes 73760 | tf_op jit(solution)/shard_map/ppermute | solution.py:761
  27.8 0.0 collective-permute-done.8.refs_2_.w_near
  27.8 0.3 shard_map.103
  28.1 1.3 %collective-permute-start.11 = (bf16[80,1536]{1,0:T(8,128)(2,1)S(1)}, bf16[80,1536]{1,0:T(8,128)(2,1)S(1)}, u32[]{:S(2)}, u32[]{:S(2)}) collective-permute-start(bf16[80,1536]{1,0:T(8,128)(2,1)S(1)} %get-tuple-element.59._), channel_id=1, source_target_pairs={{0,2},{1,3},{2,0},{3,1},{4,6},{5,7},{6,4},{7,5},{8,10},{9,11},{10,... | collective-permute-start | bytes 737288 | tf_op jit(solution)/shard_map/ppermute | solution.py:761
  29.4 1.9 %shard_map.104 = (bf16[96,384]{1,0:T(8,128)(2,1)S(1)}, bf16[96,384]{1,0:T(8,128)(2,1)S(1)}) custom-call(bf16[80,1536]{1,0:T(8,128)(2,1)S(1)} %get-tuple-element.59._, bf16[288,384]{1,0:T(8,128)(2,1)S(1)} %get-tuple-element.60.q_ref, bf16[1024,384]{1,0:T(8,128)(2,1)S(1)} %get-tuple-element.61.k_ref, bf16[1024,384]{1,0:T(8,128)(2,1)S(1)} %get-tuple-element.62.v_ref, ...), custom_call_target="tpu_custom_call" | custom-call | flops 2000000000 | bytes 1000000 | tf_op jit(solution)/shard_map/pallas_call | solution.py:89
  31.4 0.1 collective-permute-start.9
  31.5 0.0 copy-done.8
  31.5 0.8 %collective-permute-start.10 = (bf16[16,1536]{1,0:T(8,128)(2,1)S(1)}, bf16[16,1536]{1,0:T(8,128)(2,1)S(1)}, u32[]{:S(2)}, u32[]{:S(2)}) collective-permute-start(bf16[16,1536]{1,0:T(8,128)(2,1)S(1)} %get-tuple-element.67), channel_id=1, source_target_pairs={{0,2},{1,3},{2,0},{3,1},{4,6},{5,7},{6,4},{7,5},{8,10},{9,11},{10,... | collective-permute-start | bytes 147464 | tf_op jit(solution)/shard_map/ppermute | solution.py:761
  32.3 0.4 collective-permute-done.9.near
  32.7 0.9 %shard_map.105.base_ref = f32[96,1536]{1,0:T(8,128)S(1)} custom-call(bf16[96,384]{1,0:T(8,128)(2,1)S(1)} %get-tuple-element.65.own, bf16[96,384]{1,0:T(8,128)(2,1)S(1)} %collective-permute-done.9.near, bf16[384,1536]{1,0:T(8,128)(2,1)S(1)} %copy-done, bf16[384,1536]{1,0:T(8,128)(2,1)S(1)} %collective-permute-done.8.refs_2_.w_near, ...), custom_call_target="tpu_custom_call" | custom-call | flops 1200000000 | bytes 1000000 | tf_op jit(solution)/shard_map/pallas_call | solution.py:89
  33.6 3.2 %collective-permute-done.11.refs_0_ = bf16[80,1536]{1,0:T(8,128)(2,1)S(1)} collective-permute-done((bf16[80,1536]{1,0:T(8,128)(2,1)S(1)}, bf16[80,1536]{1,0:T(8,128)(2,1)S(1)}, u32[]{:S(2)}, u32[]{:S(2)}) %collective-permute-start.11) | collective-permute-done | bytes 245792 | tf_op jit(solution)/shard_map/ppermute | solution.py:761
  36.8 1.2 %shard_map.106 = (bf16[48,1536]{1,0:T(8,128)(2,1)S(1)}, f32[80,1536]{1,0:T(8,128)S(1)}, f32[80,1536]{1,0:T(8,128)S(1)}) custom-call(f32[96,1536]{1,0:T(8,128)S(1)} %shard_map.105.base_ref, bf16[80,1536]{1,0:T(8,128)(2,1)S(1)} %collective-permute-done.11.refs_0_, f32[1,1536]{1,0:T(1,128)S(1)} %broadcast_in_dim.11.refs_1_.refs_4_, bf16[31,1536]{1,0:T(8,128)(2,1)S(1)} %copy-done.3), custom_call_target="tpu_custom_call" | custom-call | flops 1000000000 | bytes 1000000 | tf_op jit(solution)/shard_map/pallas_call | solution.py:89
  38.0 0.0 collective-permute-done.10.refs_0_
  38.0 1.3 %shard_map.107 = bf16[64,1536]{1,0:T(8,128)(2,1)} custom-call(f32[96,1536]{1,0:T(8,128)S(1)} %shard_map.105.base_ref, bf16[16,1536]{1,0:T(8,128)(2,1)S(1)} %collective-permute-done.10.refs_0_, bf16[48,1536]{1,0:T(8,128)(2,1)S(1)} %get-tuple-element.68.refs_1_, f32[80,1536]{1,0:T(8,128)S(1)} %get-tuple-element.69.refs_2_, ...), custom_call_target="tpu_custom_call" | custom-call | flops 3000000000 | bytes 1000000 | tf_op jit(solution)/shard_map/pallas_call | solution.py:89
  (12 shorter events, 0.1 us)
Async XLA Ops:
  0.0 8.8 %copy-start.1 = (bf16[3,1536,384]{2,1,0:T(8,128)(2,1)S(1)}, bf16[3,1536,384]{2,1,0:T(8,128)(2,1)}, u32[]{:S(2)}) copy-start(bf16[3,1536,384]{2,1,0:T(8,128)(2,1)} %w_att.1) | copy-start | bytes 10616836
  0.0 8.8 %copy-start.2 = (bf16[512,1536]{1,0:T(8,128)(2,1)S(1)}, bf16[512,1536]{1,0:T(8,128)(2,1)}, u32[]{:S(2)}) copy-start(bf16[512,1536]{1,0:T(8,128)(2,1)} %w_sub.1) | copy-start | bytes 4718596
  3.0 9.6 %copy-start = (bf16[384,1536]{1,0:T(8,128)(2,1)S(1)}, bf16[384,1536]{1,0:T(8,128)(2,1)}, u32[]{:S(2)}) copy-start(bf16[384,1536]{1,0:T(8,128)(2,1)} %w_own.1) | copy-start | bytes 3538948
  3.0 9.5 %collective-permute-start.1 = (bf16[1,136,256]{2,1,0:T(8,128)(2,1)}, bf16[1,136,256]{2,1,0:T(8,128)(2,1)S(1)}, u32[]{:S(2)}, u32[]{:S(2)}) collective-permute-start(bf16[1,136,256]{2,1,0:T(8,128)(2,1)} %shard_map.91.stack_ref), channel_id=1, source_target_pairs={{0,12},{4,8},{8,4},{12,0},{1,13},{5,9},{9,5},{13,1},{2,14},{6,10},... | collective-permute-start | bytes 208904 | tf_op jit(solution)/shard_map/ppermute | solution.py:761
  8.1 5.1 %collective-permute-start.2 = (bf16[1,136,256]{2,1,0:T(8,128)(2,1)}, bf16[1,136,256]{2,1,0:T(8,128)(2,1)S(1)}, u32[]{:S(2)}, u32[]{:S(2)}) collective-permute-start(bf16[1,136,256]{2,1,0:T(8,128)(2,1)} %shard_map.91.stack_ref), channel_id=1, source_target_pairs={{0,4},{4,0},{8,12},{12,8},{1,5},{5,1},{9,13},{13,9},{2,6},{6,2},{1... | collective-permute-start | bytes 208904 | tf_op jit(solution)/shard_map/ppermute | solution.py:761
  8.1 5.9 %collective-permute-start.3 = (bf16[1,136,256]{2,1,0:T(8,128)(2,1)}, bf16[1,136,256]{2,1,0:T(8,128)(2,1)S(1)}, u32[]{:S(2)}, u32[]{:S(2)}) collective-permute-start(bf16[1,136,256]{2,1,0:T(8,128)(2,1)} %shard_map.91.stack_ref), channel_id=1, source_target_pairs={{0,8},{4,12},{8,0},{12,4},{1,9},{5,13},{9,1},{13,5},{2,10},{6,14},... | collective-permute-start | bytes 208904 | tf_op jit(solution)/shard_map/ppermute | solution.py:761
  8.8 0.9 %copy-start.4 = (bf16[1,136,256]{2,1,0:T(8,128)(2,1)S(1)}, bf16[1,136,256]{2,1,0:T(8,128)(2,1)}, u32[]{:S(2)}) copy-start(bf16[1,136,256]{2,1,0:T(8,128)(2,1)} %shard_map.91.stack_ref) | copy-start | bytes 208900
  10.8 4.8 %collective-permute-start = (bf16[1,136,256]{2,1,0:T(8,128)(2,1)S(1)}, bf16[1,136,256]{2,1,0:T(8,128)(2,1)S(1)}, u32[]{:S(2)}, u32[]{:S(2)}) collective-permute-start(bf16[1,136,256]{2,1,0:T(8,128)(2,1)S(1)} %get-tuple-element.38.refs_0_), channel_id=1, source_target_pairs={{0,2},{1,3},{2,0},{3,1},{4,6},{5,7},{6,4},{7,5},{8,10},{9,11},{10,... | collective-permute-start | bytes 208904 | tf_op jit(solution)/shard_map/ppermute | solution.py:761
  12.5 15.2 %collective-permute-start.8 = (bf16[384,1536]{1,0:T(8,128)(2,1)S(1)}, bf16[384,1536]{1,0:T(8,128)(2,1)S(1)}, u32[]{:S(2)}, u32[]{:S(2)}) collective-permute-start(bf16[384,1536]{1,0:T(8,128)(2,1)S(1)} %copy-done), channel_id=1, source_target_pairs={{0,1},{1,0},{2,3},{3,2},{4,5},{5,4},{6,7},{7,6},{8,9},{9,8},{10,11... | collective-permute-start | bytes 3538952 | tf_op jit(solution)/shard_map/ppermute | solution.py:761
  14.1 6.2 %collective-permute-start.5 = (bf16[3,136,256]{2,1,0:T(8,128)(2,1)S(1)}, bf16[3,136,256]{2,1,0:T(8,128)(2,1)S(1)}, u32[]{:S(2)}, u32[]{:S(2)}) collective-permute-start(bf16[3,136,256]{2,1,0:T(8,128)(2,1)S(1)} %shard_map.93.refs_2_), channel_id=1, source_target_pairs={{0,2},{1,3},{2,0},{3,1},{4,6},{5,7},{6,4},{7,5},{8,10},{9,11},{10,... | collective-permute-start | bytes 626696 | tf_op jit(solution)/shard_map/ppermute | solution.py:761
  15.7 2.2 %collective-permute-start.4 = (bf16[5,136,256]{2,1,0:T(8,128)(2,1)S(1)}, bf16[5,136,256]{2,1,0:T(8,128)(2,1)S(1)}, u32[]{:S(2)}, u32[]{:S(2)}) collective-permute-start(bf16[5,136,256]{2,1,0:T(8,128)(2,1)S(1)} %shard_map.94.stack_ref.refs_0_), channel_id=1, source_target_pairs={{0,1},{1,0},{2,3},{3,2},{4,5},{5,4},{6,7},{7,6},{8,9},{9,8},{10,11... | collective-permute-start | bytes 1044488 | tf_op jit(solution)/shard_map/ppermute | solution.py:761
  20.2 1.7 %copy-start.5 = (s32[256]{0:T(256)S(1)}, s32[256]{0:T(256)}, u32[]{:S(2)}) copy-start(s32[256]{0:T(256)} %param.10) | copy-start | bytes 3076
  20.3 1.7 %copy-start.6 = (s32[256]{0:T(256)S(1)}, s32[256]{0:T(256)}, u32[]{:S(2)}) copy-start(s32[256]{0:T(256)} %param.11) | copy-start | bytes 3076
  20.3 1.7 %copy-start.7 = (bf16[1056,512]{1,0:T(8,128)(2,1)S(1)}, bf16[1056,512]{1,0:T(8,128)(2,1)}, u32[]{:S(2)}) copy-start(bf16[1056,512]{1,0:T(8,128)(2,1)} %constant.2.clone.table.refs_4_) | copy-start | bytes 3244036
  20.3 1.6 %collective-permute-start.6 = (bf16[3,136,256]{2,1,0:T(8,128)(2,1)S(1)}, bf16[3,136,256]{2,1,0:T(8,128)(2,1)S(1)}, u32[]{:S(2)}, u32[]{:S(2)}) collective-permute-start(bf16[3,136,256]{2,1,0:T(8,128)(2,1)S(1)} %shard_map.97.refs_2_.stack_ref), channel_id=1, source_target_pairs={{0,1},{1,0},{2,3},{3,2},{4,5},{5,4},{6,7},{7,6},{8,9},{9,8},{10,11... | collective-permute-start | bytes 626696 | tf_op jit(solution)/shard_map/ppermute | solution.py:761
  26.4 1.3 %collective-permute-start.7 = (bf16[96,384]{1,0:T(8,128)(2,1)S(1)}, bf16[96,384]{1,0:T(8,128)(2,1)S(1)}, u32[]{:S(2)}, u32[]{:S(2)}) collective-permute-start(bf16[96,384]{1,0:T(8,128)(2,1)S(1)} %get-tuple-element.58), channel_id=1, source_target_pairs={{0,1},{1,0},{2,3},{3,2},{4,5},{5,4},{6,7},{7,6},{8,9},{9,8},{10,11... | collective-permute-start | bytes 221192 | tf_op jit(solution)/shard_map/ppermute | solution.py:761
  28.1 8.7 %collective-permute-start.11 = (bf16[80,1536]{1,0:T(8,128)(2,1)S(1)}, bf16[80,1536]{1,0:T(8,128)(2,1)S(1)}, u32[]{:S(2)}, u32[]{:S(2)}) collective-permute-start(bf16[80,1536]{1,0:T(8,128)(2,1)S(1)} %get-tuple-element.59._), channel_id=1, source_target_pairs={{0,2},{1,3},{2,0},{3,1},{4,6},{5,7},{6,4},{7,5},{8,10},{9,11},{10,... | collective-permute-start | bytes 737288 | tf_op jit(solution)/shard_map/ppermute | solution.py:761
  29.4 2.0 %copy-start.8 = (f32[1536]{0:T(1024)S(1)}, f32[1536]{0:T(1024)}, u32[]{:S(2)}) copy-start(f32[1536]{0:T(1024)} %param.15) | copy-start | bytes 18436
  31.4 1.3 %collective-permute-start.9 = (bf16[96,384]{1,0:T(8,128)(2,1)S(1)}, bf16[96,384]{1,0:T(8,128)(2,1)S(1)}, u32[]{:S(2)}, u32[]{:S(2)}) collective-permute-start(bf16[96,384]{1,0:T(8,128)(2,1)S(1)} %get-tuple-element.66), channel_id=1, source_target_pairs={{0,1},{1,0},{2,3},{3,2},{4,5},{5,4},{6,7},{7,6},{8,9},{9,8},{10,11... | collective-permute-start | bytes 221192 | tf_op jit(solution)/shard_map/ppermute | solution.py:761
  31.5 6.6 %collective-permute-start.10 = (bf16[16,1536]{1,0:T(8,128)(2,1)S(1)}, bf16[16,1536]{1,0:T(8,128)(2,1)S(1)}, u32[]{:S(2)}, u32[]{:S(2)}) collective-permute-start(bf16[16,1536]{1,0:T(8,128)(2,1)S(1)} %get-tuple-element.67), channel_id=1, source_target_pairs={{0,2},{1,3},{2,0},{3,1},{4,6},{5,7},{6,4},{7,5},{8,10},{9,11},{10,... | collective-permute-start | bytes 147464 | tf_op jit(solution)/shard_map/ppermute | solution.py:761
  32.7 4.1 %copy-start.3 = (bf16[31,1536]{1,0:T(8,128)(2,1)S(1)}, bf16[31,1536]{1,0:T(8,128)(2,1)}, u32[]{:S(2)}) copy-start(bf16[31,1536]{1,0:T(8,128)(2,1)} %refs_5_.1) | copy-start | bytes 285700

commit v9 on v8

--- a/solution.py
+++ b/solution.py
@@ -793,7 +793,7 @@
     reach = min((SEG_MAX + HALO - 2) // frames_shard + 1, shards_total - 1)
     whole = reach == shards_total - 1 and shards_total & (shards_total - 1) == 0
     if whole:
-        order = [shards_total - 1, *range(1, shards_total - 1)]
+        order = dict.fromkeys([shards_total // 2, shards_total - 1, *range(1, shards_total)])
         moves = [lambda tm, bit=bit: tm ^ bit for bit in order]
         column = [exchange(stacked, "tm", bit) for bit in order]
     else:
@@ -840,7 +840,7 @@
     arrived = [exchange(window, "mp", 1) for window in windows[1::2]]
     w_rows = (w_output, w_near)
     shares = far_branch_own(windows[0::2], w_output)
-    shares = far_branch(shares, arrived, w_near, frames_local + HALO)
+    shares = far_branch(shares, arrived, w_near, frames_local)
     mine, other = attend_near(places, shares[0], *shared, frames_local)
     shares = [exchange(share, "mp", far[number // 2]) for number, share in enumerate(shares)]
     base = near_branch(

time: 39.5 us -> 38.9 us (0.985)
  waiting for transfers between devices: 5.97 us -> 5.36 us
    ppermute x12, waiting for transfers between devices: 5.97 us -> 5.36 us  [exchange(): lax.ppermute(block, axis, [(i, i ^ bit) for i in range(lax.axis_size(axis...]
  transfers between devices with their start and end apart: 12 -> 12, of which waited for: 6 -> 7; matrix products, arithmetic and copies ran while one was open for 0% -> 0% of each run, Pallas kernels for 40% -> 40%
where the time goes in v9:
time: 38.9 us; the launch traced here: 38.7 us
  Pallas kernels  20.2 us (52%)
  starting transfers between devices  12 us (31%)
  waiting for transfers between devices  5.36 us (14%)
  local copies, waits for them, and re-layouts  0.96 us (2%)
    pallas_call x17, Pallas kernels, call(): pl.pallas_call(kernel, out_shape=out_shape, in_specs=specs, out_specs=jax...  20.2 us
    ppermute x12, starting transfers between devices, exchange(): lax.ppermute(block, axis, [(i, i ^ bit) for i in range(lax.axis_size(axis...  12 us
    ppermute x12, waiting for transfers between devices, exchange(): lax.ppermute(block, axis, [(i, i ^ bit) for i in range(lax.axis_size(axis...  5.36 us
    unnamed x18, local copies, waits for them, and re-layouts  0.95 us
  transfers between devices with their start and end apart: 12, of which 7 were waited for; matrix products, arithmetic and copies ran while one was open for 0% of the time, Pallas kernels for 40%

profile of v9, /device:TPU:0, one launch (start us, length us, event | category | flops | bytes accessed | tf_op | source)
XLA Modules:
  0.0 38.7 jit_solution(9314843028411094493)
XLA Ops:
  0.0 3.0 %shard_map.91.stack_ref = bf16[1,136,256]{2,1,0:T(8,128)(2,1)} custom-call(s32[1,256]{1,0:T(1,128)} %bitcast.3, s32[1,256]{1,0:T(1,128)} %bitcast.5, f32[320,128]{1,0:T(8,128)} %bitcast.7, bf16[1056,512]{1,0:T(8,128)(2,1)} %constant.2.clone.table.refs_4_), custom_call_target="tpu_custom_call" | custom-call | flops 2000000000 | bytes 1000000 | tf_op jit(solution)/shard_map/pallas_call | solution.py:89
  3.0 0.0 copy-start
  3.0 4.1 %collective-permute-start.1 = (bf16[1,136,256]{2,1,0:T(8,128)(2,1)}, bf16[1,136,256]{2,1,0:T(8,128)(2,1)S(1)}, u32[]{:S(2)}, u32[]{:S(2)}) collective-permute-start(bf16[1,136,256]{2,1,0:T(8,128)(2,1)} %shard_map.91.stack_ref), channel_id=1, source_target_pairs={{0,8},{4,12},{8,0},{12,4},{1,9},{5,13},{9,1},{13,5},{2,10},{6,14},... | collective-permute-start | bytes 208904 | tf_op jit(solution)/shard_map/ppermute | solution.py:761
  7.1 1.3 %collective-permute-start.2 = (bf16[1,136,256]{2,1,0:T(8,128)(2,1)}, bf16[1,136,256]{2,1,0:T(8,128)(2,1)S(1)}, u32[]{:S(2)}, u32[]{:S(2)}) collective-permute-start(bf16[1,136,256]{2,1,0:T(8,128)(2,1)} %shard_map.91.stack_ref), channel_id=1, source_target_pairs={{0,12},{4,8},{8,4},{12,0},{1,13},{5,9},{9,5},{13,1},{2,14},{6,10},... | collective-permute-start | bytes 208904 | tf_op jit(solution)/shard_map/ppermute | solution.py:761
  8.5 0.2 collective-permute-start.3
  8.7 0.0 copy-done.1
  8.7 0.0 copy-done.2
  8.7 0.9 %copy-done.4 = bf16[1,136,256]{2,1,0:T(8,128)(2,1)S(1)} copy-done((bf16[1,136,256]{2,1,0:T(8,128)(2,1)S(1)}, bf16[1,136,256]{2,1,0:T(8,128)(2,1)}, u32[]{:S(2)}) %copy-start.4) | copy-done | bytes 69656
  9.6 1.2 %shard_map.92 = (bf16[512,1536]{1,0:T(8,128)(2,1)S(1)}, bf16[3,1536,384]{2,1,0:T(8,128)(2,1)S(1)}, f32[8,384]{1,0:T(8,128)S(1)}, bf16[1,136,256]{2,1,0:T(8,128)(2,1)S(1)}) custom-call(bf16[1,136,256]{2,1,0:T(8,128)(2,1)S(1)} %copy-done.4, bf16[512,1536]{1,0:T(8,128)(2,1)S(1)} %copy-done.2, bf16[3,1536,384]{2,1,0:T(8,128)(2,1)S(1)} %copy-done.1), custom_call_target="tpu_custom_call" | custom-call | flops 2000000000 | bytes 1000000 | tf_op jit(solution)/shard_map/pallas_call | solution.py:89
  10.8 1.6 %collective-permute-start = (bf16[1,136,256]{2,1,0:T(8,128)(2,1)S(1)}, bf16[1,136,256]{2,1,0:T(8,128)(2,1)S(1)}, u32[]{:S(2)}, u32[]{:S(2)}) collective-permute-start(bf16[1,136,256]{2,1,0:T(8,128)(2,1)S(1)} %get-tuple-element.38.refs_0_), channel_id=1, source_target_pairs={{0,2},{1,3},{2,0},{3,1},{4,6},{5,7},{6,4},{7,5},{8,10},{9,11},{10,... | collective-permute-start | bytes 208904 | tf_op jit(solution)/shard_map/ppermute | solution.py:761
  12.3 0.0 copy-done
  12.3 0.0 collective-permute-start.8
  12.3 0.0 collective-permute-done.1.refs_0_
  12.3 1.3 %collective-permute-done.2.refs_1_ = bf16[1,136,256]{2,1,0:T(8,128)(2,1)S(1)} collective-permute-done((bf16[1,136,256]{2,1,0:T(8,128)(2,1)}, bf16[1,136,256]{2,1,0:T(8,128)(2,1)S(1)}, u32[]{:S(2)}, u32[]{:S(2)}) %collective-permute-start.2) | collective-permute-done | bytes 69664 | tf_op jit(solution)/shard_map/ppermute | solution.py:761
  13.7 0.1 collective-permute-done.3.refs_2_
  13.7 1.7 %collective-permute-start.5 = (bf16[3,136,256]{2,1,0:T(8,128)(2,1)S(1)}, bf16[3,136,256]{2,1,0:T(8,128)(2,1)S(1)}, u32[]{:S(2)}, u32[]{:S(2)}) collective-permute-start(bf16[3,136,256]{2,1,0:T(8,128)(2,1)S(1)} %shard_map.93.refs_2_), channel_id=1, source_target_pairs={{0,2},{1,3},{2,0},{3,1},{4,6},{5,7},{6,4},{7,5},{8,10},{9,11},{10,... | collective-permute-start | bytes 626696 | tf_op jit(solution)/shard_map/ppermute | solution.py:761
  15.5 0.0 collective-permute-done.refs_1_
  15.5 0.1 collective-permute-start.4
  15.6 2.1 %shard_map.95 = (bf16[128,384]{1,0:T(8,128)(2,1)S(1)}, bf16[320,384]{1,0:T(8,128)(2,1)S(1)}, bf16[320,384]{1,0:T(8,128)(2,1)S(1)}) custom-call(bf16[5,136,256]{2,1,0:T(8,128)(2,1)S(1)} %shard_map.94.stack_ref.refs_0_, bf16[512,1536]{1,0:T(8,128)(2,1)S(1)} %get-tuple-element.40.w_sub.refs_5_, bf16[3,1536,384]{2,1,0:T(8,128)(2,1)S(1)} %get-tuple-element.41.w_att, ...), custom_call_target="tpu_custom_call" | custom-call | flops 4840000000 | bytes 1000000 | tf_op jit(solution)/shard_map/pallas_call | solution.py:89
  17.7 0.0 collective-permute-done.4.stack_ref.refs_1_
  17.7 2.1 %shard_map.96 = (bf16[128,384]{1,0:T(8,128)(2,1)S(1)}, bf16[320,384]{1,0:T(8,128)(2,1)S(1)}, bf16[320,384]{1,0:T(8,128)(2,1)S(1)}) custom-call(bf16[5,136,256]{2,1,0:T(8,128)(2,1)S(1)} %collective-permute-done.4.stack_ref.refs_1_, bf16[512,1536]{1,0:T(8,128)(2,1)S(1)} %get-tuple-element.40.w_sub.refs_5_, bf16[3,1536,384]{2,1,0:T(8,128)(2,1)S(1)} %get-tuple-element.41.w_att, ...), custom_call_target="tpu_custom_call" | custom-call | flops 4840000000 | bytes 1000000 | tf_op jit(solution)/shard_map/pallas_call | solution.py:89
  19.9 0.1 collective-permute-done.5.refs_0_
  20.0 0.0 copy-start.5
  20.0 0.0 copy-start.6
  20.0 0.0 copy-start.7
  20.1 0.5 %collective-permute-start.6 = (bf16[3,136,256]{2,1,0:T(8,128)(2,1)S(1)}, bf16[3,136,256]{2,1,0:T(8,128)(2,1)S(1)}, u32[]{:S(2)}, u32[]{:S(2)}) collective-permute-start(bf16[3,136,256]{2,1,0:T(8,128)(2,1)S(1)} %shard_map.97.refs_2_.stack_ref), channel_id=1, source_target_pairs={{0,1},{1,0},{2,3},{3,2},{4,5},{5,4},{6,7},{7,6},{8,9},{9,8},{10,11... | collective-permute-start | bytes 626696 | tf_op jit(solution)/shard_map/ppermute | solution.py:761
  20.5 1.2 %shard_map.99 = (bf16[192,384]{1,0:T(8,128)(2,1)S(1)}, bf16[192,384]{1,0:T(8,128)(2,1)S(1)}) custom-call(bf16[3,136,256]{2,1,0:T(8,128)(2,1)S(1)} %shard_map.97.refs_2_.stack_ref, bf16[512,1536]{1,0:T(8,128)(2,1)S(1)} %get-tuple-element.40.w_sub.refs_5_, bf16[3,1536,384]{2,1,0:T(8,128)(2,1)S(1)} %get-tuple-element.41.w_att, ...), custom_call_target="tpu_custom_call" | custom-call | flops 3304000000 | bytes 1000000 | tf_op jit(solution)/shard_map/pallas_call | solution.py:89
  21.7 0.0 collective-permute-done.6.refs_3_.stack_ref
  21.8 0.0 copy-done.5
  21.8 0.0 copy-done.6
  21.8 0.6 %shard_map.98 = (bf16[16,256]{1,0:T(8,128)(2,1)S(1)}, f32[2,288]{1,0:T(2,128)S(1)}) custom-call(s32[1,256]{1,0:T(1,128)S(1)} %bitcast.4, s32[1,256]{1,0:T(1,128)S(1)} %bitcast.6, bf16[5,136,256]{2,1,0:T(8,128)(2,1)S(1)} %shard_map.94.stack_ref.refs_0_, bf16[5,136,256]{2,1,0:T(8,128)(2,1)S(1)} %collective-permute-done.4.stack_ref.refs_1_, ...), custom_call_target="tpu_custom_call" | custom-call | flops 1800000000 | bytes 1000000 | tf_op jit(solution)/shard_map/pallas_call | solution.py:89
  22.4 1.7 %shard_map.100 = (bf16[48,384]{1,0:T(8,128)(2,1)S(1)}, bf16[192,384]{1,0:T(8,128)(2,1)S(1)}, bf16[48,384]{1,0:T(8,128)(2,1)S(1)}, bf16[192,384]{1,0:T(8,128)(2,1)S(1)}, bf16[48,384]{1,0:T(8,128)(2,1)S(1)}) custom-call(bf16[3,136,256]{2,1,0:T(8,128)(2,1)S(1)} %collective-permute-done.6.refs_3_.stack_ref, ...), custom_call_target="tpu_custom_call" | custom-call | flops 3880000000 | bytes 1000000 | tf_op jit(solution)/shard_map/pallas_call | solution.py:89
  24.1 2.2 %shard_map.101 = (bf16[96,384]{1,0:T(8,128)(2,1)S(1)}, bf16[96,384]{1,0:T(8,128)(2,1)S(1)}, bf16[288,384]{1,0:T(8,128)(2,1)S(1)}, bf16[1024,384]{1,0:T(8,128)(2,...) custom-call(f32[2,288]{1,0:T(2,128)S(1)} %get-tuple-element.44.bound_ref, ...), custom_call_target="tpu_custom_call" | custom-call | flops 5000000000 | bytes 1000000 | tf_op jit(solution)/shard_map/pallas_call | solution.py:89
  26.3 0.3 collective-permute-start.7
  26.6 0.3 shard_map.102.refs_0_
  26.9 0.7 %collective-permute-done.7.refs_1_ = bf16[96,384]{1,0:T(8,128)(2,1)S(1)} collective-permute-done((bf16[96,384]{1,0:T(8,128)(2,1)S(1)}, bf16[96,384]{1,0:T(8,128)(2,1)S(1)}, u32[]{:S(2)}, u32[]{:S(2)}) %collective-permute-start.7) | collective-permute-done | bytes 73760 | tf_op jit(solution)/shard_map/ppermute | solution.py:761
  27.6 0.0 collective-permute-done.8.refs_2_.w_near
  27.6 0.3 shard_map.103
  28.0 1.2 %collective-permute-start.11 = (bf16[64,1536]{1,0:T(8,128)(2,1)S(1)}, bf16[64,1536]{1,0:T(8,128)(2,1)S(1)}, u32[]{:S(2)}, u32[]{:S(2)}) collective-permute-start(bf16[64,1536]{1,0:T(8,128)(2,1)S(1)} %get-tuple-element.59._), channel_id=1, source_target_pairs={{0,2},{1,3},{2,0},{3,1},{4,6},{5,7},{6,4},{7,5},{8,10},{9,11},{10,... | collective-permute-start | bytes 589832 | tf_op jit(solution)/shard_map/ppermute | solution.py:761
  29.2 1.9 %shard_map.104 = (bf16[96,384]{1,0:T(8,128)(2,1)S(1)}, bf16[96,384]{1,0:T(8,128)(2,1)S(1)}) custom-call(bf16[64,1536]{1,0:T(8,128)(2,1)S(1)} %get-tuple-element.59._, bf16[288,384]{1,0:T(8,128)(2,1)S(1)} %get-tuple-element.60.q_ref, bf16[1024,384]{1,0:T(8,128)(2,1)S(1)} %get-tuple-element.61.k_ref, bf16[1024,384]{1,0:T(8,128)(2,1)S(1)} %get-tuple-element.62.v_ref, ...), custom_call_target="tpu_custom_call" | custom-call | flops 2000000000 | bytes 1000000 | tf_op jit(solution)/shard_map/pallas_call | solution.py:89
  31.1 0.1 collective-permute-start.9
  31.2 0.9 %collective-permute-start.10 = (bf16[32,1536]{1,0:T(8,128)(2,1)S(1)}, bf16[32,1536]{1,0:T(8,128)(2,1)S(1)}, u32[]{:S(2)}, u32[]{:S(2)}) collective-permute-start(bf16[32,1536]{1,0:T(8,128)(2,1)S(1)} %get-tuple-element.67), channel_id=1, source_target_pairs={{0,2},{1,3},{2,0},{3,1},{4,6},{5,7},{6,4},{7,5},{8,10},{9,11},{10,... | collective-permute-start | bytes 294920 | tf_op jit(solution)/shard_map/ppermute | solution.py:761
  32.2 0.3 collective-permute-done.9.near
  32.5 0.9 %shard_map.105.base_ref = f32[96,1536]{1,0:T(8,128)S(1)} custom-call(bf16[96,384]{1,0:T(8,128)(2,1)S(1)} %get-tuple-element.65.own, bf16[96,384]{1,0:T(8,128)(2,1)S(1)} %collective-permute-done.9.near, bf16[384,1536]{1,0:T(8,128)(2,1)S(1)} %copy-done, bf16[384,1536]{1,0:T(8,128)(2,1)S(1)} %collective-permute-done.8.refs_2_.w_near, ...), custom_call_target="tpu_custom_call" | custom-call | flops 1200000000 | bytes 1000000 | tf_op jit(solution)/shard_map/pallas_call | solution.py:89
  33.4 2.3 %collective-permute-done.11.refs_0_ = bf16[64,1536]{1,0:T(8,128)(2,1)S(1)} collective-permute-done((bf16[64,1536]{1,0:T(8,128)(2,1)S(1)}, bf16[64,1536]{1,0:T(8,128)(2,1)S(1)}, u32[]{:S(2)}, u32[]{:S(2)}) %collective-permute-start.11) | collective-permute-done | bytes 196640 | tf_op jit(solution)/shard_map/ppermute | solution.py:761
  35.7 0.9 %shard_map.106 = (bf16[32,1536]{1,0:T(8,128)(2,1)S(1)}, f32[64,1536]{1,0:T(8,128)S(1)}, f32[64,1536]{1,0:T(8,128)S(1)}) custom-call(f32[96,1536]{1,0:T(8,128)S(1)} %shard_map.105.base_ref, bf16[64,1536]{1,0:T(8,128)(2,1)S(1)} %collective-permute-done.11.refs_0_, f32[1,1536]{1,0:T(1,128)S(1)} %broadcast_in_dim.11.refs_1_.refs_4_, bf16[31,1536]{1,0:T(8,128)(2,1)S(1)} %copy-done.3), custom_call_target="tpu_custom_call" | custom-call | flops 1000000000 | bytes 1000000 | tf_op jit(solution)/shard_map/pallas_call | solution.py:89
  36.6 0.5 %collective-permute-done.10.refs_0_ = bf16[32,1536]{1,0:T(8,128)(2,1)S(1)} collective-permute-done((bf16[32,1536]{1,0:T(8,128)(2,1)S(1)}, bf16[32,1536]{1,0:T(8,128)(2,1)S(1)}, u32[]{:S(2)}, u32[]{:S(2)}) %collective-permute-start.10) | collective-permute-done | bytes 98336 | tf_op jit(solution)/shard_map/ppermute | solution.py:761
  37.2 1.6 %shard_map.107 = bf16[64,1536]{1,0:T(8,128)(2,1)} custom-call(f32[96,1536]{1,0:T(8,128)S(1)} %shard_map.105.base_ref, bf16[32,1536]{1,0:T(8,128)(2,1)S(1)} %collective-permute-done.10.refs_0_, bf16[32,1536]{1,0:T(8,128)(2,1)S(1)} %get-tuple-element.68.refs_1_, f32[64,1536]{1,0:T(8,128)S(1)} %get-tuple-element.69.refs_2_, ...), custom_call_target="tpu_custom_call" | custom-call | flops 3000000000 | bytes 1000000 | tf_op jit(solution)/shard_map/pallas_call | solution.py:89
  (12 shorter events, 0.1 us)
Async XLA Ops:
  0.0 8.7 %copy-start.1 = (bf16[3,1536,384]{2,1,0:T(8,128)(2,1)S(1)}, bf16[3,1536,384]{2,1,0:T(8,128)(2,1)}, u32[]{:S(2)}) copy-start(bf16[3,1536,384]{2,1,0:T(8,128)(2,1)} %w_att.1) | copy-start | bytes 10616836
  0.0 8.7 %copy-start.2 = (bf16[512,1536]{1,0:T(8,128)(2,1)S(1)}, bf16[512,1536]{1,0:T(8,128)(2,1)}, u32[]{:S(2)}) copy-start(bf16[512,1536]{1,0:T(8,128)(2,1)} %w_sub.1) | copy-start | bytes 4718596
  3.0 9.3 %copy-start = (bf16[384,1536]{1,0:T(8,128)(2,1)S(1)}, bf16[384,1536]{1,0:T(8,128)(2,1)}, u32[]{:S(2)}) copy-start(bf16[384,1536]{1,0:T(8,128)(2,1)} %w_own.1) | copy-start | bytes 3538948
  3.0 9.3 %collective-permute-start.1 = (bf16[1,136,256]{2,1,0:T(8,128)(2,1)}, bf16[1,136,256]{2,1,0:T(8,128)(2,1)S(1)}, u32[]{:S(2)}, u32[]{:S(2)}) collective-permute-start(bf16[1,136,256]{2,1,0:T(8,128)(2,1)} %shard_map.91.stack_ref), channel_id=1, source_target_pairs={{0,8},{4,12},{8,0},{12,4},{1,9},{5,13},{9,1},{13,5},{2,10},{6,14},... | collective-permute-start | bytes 208904 | tf_op jit(solution)/shard_map/ppermute | solution.py:761
  7.1 6.6 %collective-permute-start.2 = (bf16[1,136,256]{2,1,0:T(8,128)(2,1)}, bf16[1,136,256]{2,1,0:T(8,128)(2,1)S(1)}, u32[]{:S(2)}, u32[]{:S(2)}) collective-permute-start(bf16[1,136,256]{2,1,0:T(8,128)(2,1)} %shard_map.91.stack_ref), channel_id=1, source_target_pairs={{0,12},{4,8},{8,4},{12,0},{1,13},{5,9},{9,5},{13,1},{2,14},{6,10},... | collective-permute-start | bytes 208904 | tf_op jit(solution)/shard_map/ppermute | solution.py:761
  8.5 5.3 %collective-permute-start.3 = (bf16[1,136,256]{2,1,0:T(8,128)(2,1)}, bf16[1,136,256]{2,1,0:T(8,128)(2,1)S(1)}, u32[]{:S(2)}, u32[]{:S(2)}) collective-permute-start(bf16[1,136,256]{2,1,0:T(8,128)(2,1)} %shard_map.91.stack_ref), channel_id=1, source_target_pairs={{0,4},{4,0},{8,12},{12,8},{1,5},{5,1},{9,13},{13,9},{2,6},{6,2},{1... | collective-permute-start | bytes 208904 | tf_op jit(solution)/shard_map/ppermute | solution.py:761
  8.7 0.9 %copy-start.4 = (bf16[1,136,256]{2,1,0:T(8,128)(2,1)S(1)}, bf16[1,136,256]{2,1,0:T(8,128)(2,1)}, u32[]{:S(2)}) copy-start(bf16[1,136,256]{2,1,0:T(8,128)(2,1)} %shard_map.91.stack_ref) | copy-start | bytes 208900
  10.8 4.7 %collective-permute-start = (bf16[1,136,256]{2,1,0:T(8,128)(2,1)S(1)}, bf16[1,136,256]{2,1,0:T(8,128)(2,1)S(1)}, u32[]{:S(2)}, u32[]{:S(2)}) collective-permute-start(bf16[1,136,256]{2,1,0:T(8,128)(2,1)S(1)} %get-tuple-element.38.refs_0_), channel_id=1, source_target_pairs={{0,2},{1,3},{2,0},{3,1},{4,6},{5,7},{6,4},{7,5},{8,10},{9,11},{10,... | collective-permute-start | bytes 208904 | tf_op jit(solution)/shard_map/ppermute | solution.py:761
  12.3 15.3 %collective-permute-start.8 = (bf16[384,1536]{1,0:T(8,128)(2,1)S(1)}, bf16[384,1536]{1,0:T(8,128)(2,1)S(1)}, u32[]{:S(2)}, u32[]{:S(2)}) collective-permute-start(bf16[384,1536]{1,0:T(8,128)(2,1)S(1)} %copy-done), channel_id=1, source_target_pairs={{0,1},{1,0},{2,3},{3,2},{4,5},{5,4},{6,7},{7,6},{8,9},{9,8},{10,11... | collective-permute-start | bytes 3538952 | tf_op jit(solution)/shard_map/ppermute | solution.py:761
  13.7 6.3 %collective-permute-start.5 = (bf16[3,136,256]{2,1,0:T(8,128)(2,1)S(1)}, bf16[3,136,256]{2,1,0:T(8,128)(2,1)S(1)}, u32[]{:S(2)}, u32[]{:S(2)}) collective-permute-start(bf16[3,136,256]{2,1,0:T(8,128)(2,1)S(1)} %shard_map.93.refs_2_), channel_id=1, source_target_pairs={{0,2},{1,3},{2,0},{3,1},{4,6},{5,7},{6,4},{7,5},{8,10},{9,11},{10,... | collective-permute-start | bytes 626696 | tf_op jit(solution)/shard_map/ppermute | solution.py:761
  15.5 2.2 %collective-permute-start.4 = (bf16[5,136,256]{2,1,0:T(8,128)(2,1)S(1)}, bf16[5,136,256]{2,1,0:T(8,128)(2,1)S(1)}, u32[]{:S(2)}, u32[]{:S(2)}) collective-permute-start(bf16[5,136,256]{2,1,0:T(8,128)(2,1)S(1)} %shard_map.94.stack_ref.refs_0_), channel_id=1, source_target_pairs={{0,1},{1,0},{2,3},{3,2},{4,5},{5,4},{6,7},{7,6},{8,9},{9,8},{10,11... | collective-permute-start | bytes 1044488 | tf_op jit(solution)/shard_map/ppermute | solution.py:761
  20.0 1.7 %copy-start.5 = (s32[256]{0:T(256)S(1)}, s32[256]{0:T(256)}, u32[]{:S(2)}) copy-start(s32[256]{0:T(256)} %param.10) | copy-start | bytes 3076
  20.0 1.7 %copy-start.6 = (s32[256]{0:T(256)S(1)}, s32[256]{0:T(256)}, u32[]{:S(2)}) copy-start(s32[256]{0:T(256)} %param.11) | copy-start | bytes 3076
  20.0 1.7 %copy-start.7 = (bf16[1056,512]{1,0:T(8,128)(2,1)S(1)}, bf16[1056,512]{1,0:T(8,128)(2,1)}, u32[]{:S(2)}) copy-start(bf16[1056,512]{1,0:T(8,128)(2,1)} %constant.2.clone.table.refs_4_) | copy-start | bytes 3244036
  20.1 1.7 %collective-permute-start.6 = (bf16[3,136,256]{2,1,0:T(8,128)(2,1)S(1)}, bf16[3,136,256]{2,1,0:T(8,128)(2,1)S(1)}, u32[]{:S(2)}, u32[]{:S(2)}) collective-permute-start(bf16[3,136,256]{2,1,0:T(8,128)(2,1)S(1)} %shard_map.97.refs_2_.stack_ref), channel_id=1, source_target_pairs={{0,1},{1,0},{2,3},{3,2},{4,5},{5,4},{6,7},{7,6},{8,9},{9,8},{10,11... | collective-permute-start | bytes 626696 | tf_op jit(solution)/shard_map/ppermute | solution.py:761
  26.3 1.3 %collective-permute-start.7 = (bf16[96,384]{1,0:T(8,128)(2,1)S(1)}, bf16[96,384]{1,0:T(8,128)(2,1)S(1)}, u32[]{:S(2)}, u32[]{:S(2)}) collective-permute-start(bf16[96,384]{1,0:T(8,128)(2,1)S(1)} %get-tuple-element.58), channel_id=1, source_target_pairs={{0,1},{1,0},{2,3},{3,2},{4,5},{5,4},{6,7},{7,6},{8,9},{9,8},{10,11... | collective-permute-start | bytes 221192 | tf_op jit(solution)/shard_map/ppermute | solution.py:761
  28.0 7.7 %collective-permute-start.11 = (bf16[64,1536]{1,0:T(8,128)(2,1)S(1)}, bf16[64,1536]{1,0:T(8,128)(2,1)S(1)}, u32[]{:S(2)}, u32[]{:S(2)}) collective-permute-start(bf16[64,1536]{1,0:T(8,128)(2,1)S(1)} %get-tuple-element.59._), channel_id=1, source_target_pairs={{0,2},{1,3},{2,0},{3,1},{4,6},{5,7},{6,4},{7,5},{8,10},{9,11},{10,... | collective-permute-start | bytes 589832 | tf_op jit(solution)/shard_map/ppermute | solution.py:761
  29.2 2.0 %copy-start.8 = (f32[1536]{0:T(1024)S(1)}, f32[1536]{0:T(1024)}, u32[]{:S(2)}) copy-start(f32[1536]{0:T(1024)} %param.15) | copy-start | bytes 18436
  31.1 1.3 %collective-permute-start.9 = (bf16[96,384]{1,0:T(8,128)(2,1)S(1)}, bf16[96,384]{1,0:T(8,128)(2,1)S(1)}, u32[]{:S(2)}, u32[]{:S(2)}) collective-permute-start(bf16[96,384]{1,0:T(8,128)(2,1)S(1)} %get-tuple-element.66), channel_id=1, source_target_pairs={{0,1},{1,0},{2,3},{3,2},{4,5},{5,4},{6,7},{7,6},{8,9},{9,8},{10,11... | collective-permute-start | bytes 221192 | tf_op jit(solution)/shard_map/ppermute | solution.py:761
  31.2 5.9 %collective-permute-start.10 = (bf16[32,1536]{1,0:T(8,128)(2,1)S(1)}, bf16[32,1536]{1,0:T(8,128)(2,1)S(1)}, u32[]{:S(2)}, u32[]{:S(2)}) collective-permute-start(bf16[32,1536]{1,0:T(8,128)(2,1)S(1)} %get-tuple-element.67), channel_id=1, source_target_pairs={{0,2},{1,3},{2,0},{3,1},{4,6},{5,7},{6,4},{7,5},{8,10},{9,11},{10,... | collective-permute-start | bytes 294920 | tf_op jit(solution)/shard_map/ppermute | solution.py:761
  32.5 3.2 %copy-start.3 = (bf16[31,1536]{1,0:T(8,128)(2,1)S(1)}, bf16[31,1536]{1,0:T(8,128)(2,1)}, u32[]{:S(2)}) copy-start(bf16[31,1536]{1,0:T(8,128)(2,1)} %refs_5_.1) | copy-start | bytes 285700

commit v10 on v9

--- a/solution.py
+++ b/solution.py
@@ -447,7 +447,7 @@
         ref[...] = jnp.transpose(jnp.broadcast_to(row, (LANES, row.shape[1])))
 
 
-def attend_rows(places, begin, q_rows, k_all, v_all, first, last, frames_local, result, bias):
+def attend_rows(places, begin, q_rows, k_all, v_all, first, last, frames_local, result, most):
     count, width = result.shape
     rows = k_all.shape[0]
     time_index, model_index = lax.axis_index("tm"), lax.axis_index("mp")
@@ -463,7 +463,7 @@
                 base += (model_index ^ slot_mp) * frames_local - slot * frames_local + lane
                 at = jnp.where(lanes >= slot * frames_local - lane, lanes + base, at)
         at = at.astype(jnp.float32)
-        bias[:, lane : lane + LANES] = jnp.where((at >= lows) & (at < highs), 0.0, -1e30)
+        most[:, lane : lane + LANES] = jnp.where((at >= lows) & (at < highs), jnp.inf, -1e30)
     for lane in range(0, width, LANES):
         span = min(LANES, width - lane)
         q_pair = q_rows[pl.ds(begin, count), lane : lane + span]
@@ -479,7 +479,7 @@
         scores = lax.dot_general(
             stacked, k_pair, (((1,), (1,)), ((), ())), preferred_element_type=jnp.float32
         )
-        scores = scores + jnp.concatenate([bias[...]] * heads, axis=0)
+        scores = jnp.minimum(scores, jnp.concatenate([most[...]] * heads, axis=0))
         weights = jnp.exp(scores - jnp.max(scores, axis=1, keepdims=True))
         total = jnp.sum(weights, axis=1, keepdims=True)
         ratio = dot32(weights.astype(jnp.bfloat16), v_pair) / total
@@ -512,7 +512,7 @@
             refs = refs[size:]
         extra_refs, refs = refs[:3], refs[3:]
         windows, refs = refs[: 2 * len(far)], refs[2 * len(far) :]
-        q_rows, k_all, v_all, first, last, q_all, result, bias = refs
+        q_rows, k_all, v_all, first, last, q_all, result, most = refs
         gather_rows(
             places,
             query_slots,
@@ -526,7 +526,7 @@
         for number, bit in enumerate(far):
             begin = pl.multiple_of((model_index ^ bit) // 2 * (2 * frames_local), HALO)
             attend_rows(
-                places, begin, q_rows, k_all, v_all, first, last, frames_local, result, bias
+                places, begin, q_rows, k_all, v_all, first, last, frames_local, result, most
             )
             split_pair(
                 model_index, result, windows[2 * number], windows[2 * number + 1], frames_local
@@ -556,11 +556,11 @@
     window = frames_local + 2 * HALO
     pair = 2 * frames_local + 2 * HALO
 
-    def kernel(_, q_ref, k_ref, v_ref, first_ref, last_ref, mine, other, result, bias):
+    def kernel(_, q_ref, k_ref, v_ref, first_ref, last_ref, mine, other, result, most):
         model_index = lax.axis_index("mp")
         begin = pl.multiple_of(model_index // 2 * (2 * frames_local), HALO)
         attend_rows(
-            places, begin, q_ref, k_ref, v_ref, first_ref, last_ref, frames_local, result, bias
+            places, begin, q_ref, k_ref, v_ref, first_ref, last_ref, frames_local, result, most
         )
         split_pair(model_index, result, mine, other, frames_local)
 

time: 38.9 us -> 38.9 us (level)
  no operation moved by 1% of the time
where the time goes in v10:
time: 38.9 us; the launch traced here: 38.7 us
  Pallas kernels  20.2 us (52%)
  starting transfers between devices  12 us (31%)
  waiting for transfers between devices  5.33 us (14%)
  local copies, waits for them, and re-layouts  0.96 us (2%)
    pallas_call x17, Pallas kernels, call(): pl.pallas_call(kernel, out_shape=out_shape, in_specs=specs, out_specs=jax...  20.2 us
    ppermute x12, starting transfers between devices, exchange(): lax.ppermute(block, axis, [(i, i ^ bit) for i in range(lax.axis_size(axis...  12 us
    ppermute x12, waiting for transfers between devices, exchange(): lax.ppermute(block, axis, [(i, i ^ bit) for i in range(lax.axis_size(axis...  5.33 us
    unnamed x18, local copies, waits for them, and re-layouts  0.95 us
  transfers between devices with their start and end apart: 12, of which 7 were waited for; matrix products, arithmetic and copies ran while one was open for 0% of the time, Pallas kernels for 40%

profile of v10, /device:TPU:0, one launch (start us, length us, event | category | flops | bytes accessed | tf_op | source)
XLA Modules:
  0.0 38.7 jit_solution(8581291875520396515)
XLA Ops:
  0.0 3.0 %shard_map.91.stack_ref = bf16[1,136,256]{2,1,0:T(8,128)(2,1)} custom-call(s32[1,256]{1,0:T(1,128)} %bitcast.3, s32[1,256]{1,0:T(1,128)} %bitcast.5, f32[320,128]{1,0:T(8,128)} %bitcast.7, bf16[1056,512]{1,0:T(8,128)(2,1)} %constant.2.clone.table.refs_4_), custom_call_target="tpu_custom_call" | custom-call | flops 2000000000 | bytes 1000000 | tf_op jit(solution)/shard_map/pallas_call | solution.py:89
  3.0 0.0 copy-start
  3.0 4.1 %collective-permute-start.1 = (bf16[1,136,256]{2,1,0:T(8,128)(2,1)}, bf16[1,136,256]{2,1,0:T(8,128)(2,1)S(1)}, u32[]{:S(2)}, u32[]{:S(2)}) collective-permute-start(bf16[1,136,256]{2,1,0:T(8,128)(2,1)} %shard_map.91.stack_ref), channel_id=1, source_target_pairs={{0,8},{4,12},{8,0},{12,4},{1,9},{5,13},{9,1},{13,5},{2,10},{6,14},... | collective-permute-start | bytes 208904 | tf_op jit(solution)/shard_map/ppermute | solution.py:761
  7.1 1.3 %collective-permute-start.2 = (bf16[1,136,256]{2,1,0:T(8,128)(2,1)}, bf16[1,136,256]{2,1,0:T(8,128)(2,1)S(1)}, u32[]{:S(2)}, u32[]{:S(2)}) collective-permute-start(bf16[1,136,256]{2,1,0:T(8,128)(2,1)} %shard_map.91.stack_ref), channel_id=1, source_target_pairs={{0,12},{4,8},{8,4},{12,0},{1,13},{5,9},{9,5},{13,1},{2,14},{6,10},... | collective-permute-start | bytes 208904 | tf_op jit(solution)/shard_map/ppermute | solution.py:761
  8.5 0.2 collective-permute-start.3
  8.7 0.0 copy-done.1
  8.7 0.0 copy-done.2
  8.7 0.9 %copy-done.4 = bf16[1,136,256]{2,1,0:T(8,128)(2,1)S(1)} copy-done((bf16[1,136,256]{2,1,0:T(8,128)(2,1)S(1)}, bf16[1,136,256]{2,1,0:T(8,128)(2,1)}, u32[]{:S(2)}) %copy-start.4) | copy-done | bytes 69656
  9.6 1.2 %shard_map.92 = (bf16[512,1536]{1,0:T(8,128)(2,1)S(1)}, bf16[3,1536,384]{2,1,0:T(8,128)(2,1)S(1)}, f32[8,384]{1,0:T(8,128)S(1)}, bf16[1,136,256]{2,1,0:T(8,128)(2,1)S(1)}) custom-call(bf16[1,136,256]{2,1,0:T(8,128)(2,1)S(1)} %copy-done.4, bf16[512,1536]{1,0:T(8,128)(2,1)S(1)} %copy-done.2, bf16[3,1536,384]{2,1,0:T(8,128)(2,1)S(1)} %copy-done.1), custom_call_target="tpu_custom_call" | custom-call | flops 2000000000 | bytes 1000000 | tf_op jit(solution)/shard_map/pallas_call | solution.py:89
  10.8 1.6 %collective-permute-start = (bf16[1,136,256]{2,1,0:T(8,128)(2,1)S(1)}, bf16[1,136,256]{2,1,0:T(8,128)(2,1)S(1)}, u32[]{:S(2)}, u32[]{:S(2)}) collective-permute-start(bf16[1,136,256]{2,1,0:T(8,128)(2,1)S(1)} %get-tuple-element.38.refs_0_), channel_id=1, source_target_pairs={{0,2},{1,3},{2,0},{3,1},{4,6},{5,7},{6,4},{7,5},{8,10},{9,11},{10,... | collective-permute-start | bytes 208904 | tf_op jit(solution)/shard_map/ppermute | solution.py:761
  12.3 0.0 copy-done
  12.3 0.0 collective-permute-start.8
  12.3 0.0 collective-permute-done.1.refs_0_
  12.3 1.3 %collective-permute-done.2.refs_1_ = bf16[1,136,256]{2,1,0:T(8,128)(2,1)S(1)} collective-permute-done((bf16[1,136,256]{2,1,0:T(8,128)(2,1)}, bf16[1,136,256]{2,1,0:T(8,128)(2,1)S(1)}, u32[]{:S(2)}, u32[]{:S(2)}) %collective-permute-start.2) | collective-permute-done | bytes 69664 | tf_op jit(solution)/shard_map/ppermute | solution.py:761
  13.7 0.1 collective-permute-done.3.refs_2_
  13.7 1.7 %collective-permute-start.5 = (bf16[3,136,256]{2,1,0:T(8,128)(2,1)S(1)}, bf16[3,136,256]{2,1,0:T(8,128)(2,1)S(1)}, u32[]{:S(2)}, u32[]{:S(2)}) collective-permute-start(bf16[3,136,256]{2,1,0:T(8,128)(2,1)S(1)} %shard_map.93.refs_2_), channel_id=1, source_target_pairs={{0,2},{1,3},{2,0},{3,1},{4,6},{5,7},{6,4},{7,5},{8,10},{9,11},{10,... | collective-permute-start | bytes 626696 | tf_op jit(solution)/shard_map/ppermute | solution.py:761
  15.5 0.0 collective-permute-done.refs_1_
  15.5 0.1 collective-permute-start.4
  15.6 2.1 %shard_map.95 = (bf16[128,384]{1,0:T(8,128)(2,1)S(1)}, bf16[320,384]{1,0:T(8,128)(2,1)S(1)}, bf16[320,384]{1,0:T(8,128)(2,1)S(1)}) custom-call(bf16[5,136,256]{2,1,0:T(8,128)(2,1)S(1)} %shard_map.94.stack_ref.refs_0_, bf16[512,1536]{1,0:T(8,128)(2,1)S(1)} %get-tuple-element.40.w_sub.refs_5_, bf16[3,1536,384]{2,1,0:T(8,128)(2,1)S(1)} %get-tuple-element.41.w_att, ...), custom_call_target="tpu_custom_call" | custom-call | flops 4840000000 | bytes 1000000 | tf_op jit(solution)/shard_map/pallas_call | solution.py:89
  17.7 0.0 collective-permute-done.4.stack_ref.refs_1_
  17.7 2.1 %shard_map.96 = (bf16[128,384]{1,0:T(8,128)(2,1)S(1)}, bf16[320,384]{1,0:T(8,128)(2,1)S(1)}, bf16[320,384]{1,0:T(8,128)(2,1)S(1)}) custom-call(bf16[5,136,256]{2,1,0:T(8,128)(2,1)S(1)} %collective-permute-done.4.stack_ref.refs_1_, bf16[512,1536]{1,0:T(8,128)(2,1)S(1)} %get-tuple-element.40.w_sub.refs_5_, bf16[3,1536,384]{2,1,0:T(8,128)(2,1)S(1)} %get-tuple-element.41.w_att, ...), custom_call_target="tpu_custom_call" | custom-call | flops 4840000000 | bytes 1000000 | tf_op jit(solution)/shard_map/pallas_call | solution.py:89
  19.9 0.1 collective-permute-done.5.refs_0_
  20.0 0.0 copy-start.5
  20.0 0.0 copy-start.6
  20.0 0.0 copy-start.7
  20.1 0.5 %collective-permute-start.6 = (bf16[3,136,256]{2,1,0:T(8,128)(2,1)S(1)}, bf16[3,136,256]{2,1,0:T(8,128)(2,1)S(1)}, u32[]{:S(2)}, u32[]{:S(2)}) collective-permute-start(bf16[3,136,256]{2,1,0:T(8,128)(2,1)S(1)} %shard_map.97.refs_2_.stack_ref), channel_id=1, source_target_pairs={{0,1},{1,0},{2,3},{3,2},{4,5},{5,4},{6,7},{7,6},{8,9},{9,8},{10,11... | collective-permute-start | bytes 626696 | tf_op jit(solution)/shard_map/ppermute | solution.py:761
  20.5 1.2 %shard_map.99 = (bf16[192,384]{1,0:T(8,128)(2,1)S(1)}, bf16[192,384]{1,0:T(8,128)(2,1)S(1)}) custom-call(bf16[3,136,256]{2,1,0:T(8,128)(2,1)S(1)} %shard_map.97.refs_2_.stack_ref, bf16[512,1536]{1,0:T(8,128)(2,1)S(1)} %get-tuple-element.40.w_sub.refs_5_, bf16[3,1536,384]{2,1,0:T(8,128)(2,1)S(1)} %get-tuple-element.41.w_att, ...), custom_call_target="tpu_custom_call" | custom-call | flops 3304000000 | bytes 1000000 | tf_op jit(solution)/shard_map/pallas_call | solution.py:89
  21.7 0.0 collective-permute-done.6.refs_3_.stack_ref
  21.8 0.0 copy-done.5
  21.8 0.0 copy-done.6
  21.8 0.6 %shard_map.98 = (bf16[16,256]{1,0:T(8,128)(2,1)S(1)}, f32[2,288]{1,0:T(2,128)S(1)}) custom-call(s32[1,256]{1,0:T(1,128)S(1)} %bitcast.4, s32[1,256]{1,0:T(1,128)S(1)} %bitcast.6, bf16[5,136,256]{2,1,0:T(8,128)(2,1)S(1)} %shard_map.94.stack_ref.refs_0_, bf16[5,136,256]{2,1,0:T(8,128)(2,1)S(1)} %collective-permute-done.4.stack_ref.refs_1_, ...), custom_call_target="tpu_custom_call" | custom-call | flops 1800000000 | bytes 1000000 | tf_op jit(solution)/shard_map/pallas_call | solution.py:89
  22.4 1.7 %shard_map.100 = (bf16[48,384]{1,0:T(8,128)(2,1)S(1)}, bf16[192,384]{1,0:T(8,128)(2,1)S(1)}, bf16[48,384]{1,0:T(8,128)(2,1)S(1)}, bf16[192,384]{1,0:T(8,128)(2,1)S(1)}, bf16[48,384]{1,0:T(8,128)(2,1)S(1)}) custom-call(bf16[3,136,256]{2,1,0:T(8,128)(2,1)S(1)} %collective-permute-done.6.refs_3_.stack_ref, ...), custom_call_target="tpu_custom_call" | custom-call | flops 3880000000 | bytes 1000000 | tf_op jit(solution)/shard_map/pallas_call | solution.py:89
  24.1 2.2 %shard_map.101 = (bf16[96,384]{1,0:T(8,128)(2,1)S(1)}, bf16[96,384]{1,0:T(8,128)(2,1)S(1)}, bf16[288,384]{1,0:T(8,128)(2,1)S(1)}, bf16[1024,384]{1,0:T(8,128)(2,...) custom-call(f32[2,288]{1,0:T(2,128)S(1)} %get-tuple-element.44.bound_ref, ...), custom_call_target="tpu_custom_call" | custom-call | flops 5000000000 | bytes 1000000 | tf_op jit(solution)/shard_map/pallas_call | solution.py:89
  26.3 0.3 collective-permute-start.7
  26.6 0.3 shard_map.102.refs_0_
  26.9 0.7 %collective-permute-done.7.refs_1_ = bf16[96,384]{1,0:T(8,128)(2,1)S(1)} collective-permute-done((bf16[96,384]{1,0:T(8,128)(2,1)S(1)}, bf16[96,384]{1,0:T(8,128)(2,1)S(1)}, u32[]{:S(2)}, u32[]{:S(2)}) %collective-permute-start.7) | collective-permute-done | bytes 73760 | tf_op jit(solution)/shard_map/ppermute | solution.py:761
  27.6 0.0 collective-permute-done.8.refs_2_.w_near
  27.6 0.4 shard_map.103
  28.0 1.2 %collective-permute-start.11 = (bf16[64,1536]{1,0:T(8,128)(2,1)S(1)}, bf16[64,1536]{1,0:T(8,128)(2,1)S(1)}, u32[]{:S(2)}, u32[]{:S(2)}) collective-permute-start(bf16[64,1536]{1,0:T(8,128)(2,1)S(1)} %get-tuple-element.59._), channel_id=1, source_target_pairs={{0,2},{1,3},{2,0},{3,1},{4,6},{5,7},{6,4},{7,5},{8,10},{9,11},{10,... | collective-permute-start | bytes 589832 | tf_op jit(solution)/shard_map/ppermute | solution.py:761
  29.2 2.0 %shard_map.104 = (bf16[96,384]{1,0:T(8,128)(2,1)S(1)}, bf16[96,384]{1,0:T(8,128)(2,1)S(1)}) custom-call(bf16[64,1536]{1,0:T(8,128)(2,1)S(1)} %get-tuple-element.59._, bf16[288,384]{1,0:T(8,128)(2,1)S(1)} %get-tuple-element.60.q_ref, bf16[1024,384]{1,0:T(8,128)(2,1)S(1)} %get-tuple-element.61.k_ref, bf16[1024,384]{1,0:T(8,128)(2,1)S(1)} %get-tuple-element.62.v_ref, ...), custom_call_target="tpu_custom_call" | custom-call | flops 2000000000 | bytes 1000000 | tf_op jit(solution)/shard_map/pallas_call | solution.py:89
  31.2 0.1 collective-permute-start.9
  31.3 0.9 %collective-permute-start.10 = (bf16[32,1536]{1,0:T(8,128)(2,1)S(1)}, bf16[32,1536]{1,0:T(8,128)(2,1)S(1)}, u32[]{:S(2)}, u32[]{:S(2)}) collective-permute-start(bf16[32,1536]{1,0:T(8,128)(2,1)S(1)} %get-tuple-element.67), channel_id=1, source_target_pairs={{0,2},{1,3},{2,0},{3,1},{4,6},{5,7},{6,4},{7,5},{8,10},{9,11},{10,... | collective-permute-start | bytes 294920 | tf_op jit(solution)/shard_map/ppermute | solution.py:761
  32.2 0.3 collective-permute-done.9.near
  32.5 0.9 %shard_map.105.base_ref = f32[96,1536]{1,0:T(8,128)S(1)} custom-call(bf16[96,384]{1,0:T(8,128)(2,1)S(1)} %get-tuple-element.65.own, bf16[96,384]{1,0:T(8,128)(2,1)S(1)} %collective-permute-done.9.near, bf16[384,1536]{1,0:T(8,128)(2,1)S(1)} %copy-done, bf16[384,1536]{1,0:T(8,128)(2,1)S(1)} %collective-permute-done.8.refs_2_.w_near, ...), custom_call_target="tpu_custom_call" | custom-call | flops 1200000000 | bytes 1000000 | tf_op jit(solution)/shard_map/pallas_call | solution.py:89
  33.4 2.3 %collective-permute-done.11.refs_0_ = bf16[64,1536]{1,0:T(8,128)(2,1)S(1)} collective-permute-done((bf16[64,1536]{1,0:T(8,128)(2,1)S(1)}, bf16[64,1536]{1,0:T(8,128)(2,1)S(1)}, u32[]{:S(2)}, u32[]{:S(2)}) %collective-permute-start.11) | collective-permute-done | bytes 196640 | tf_op jit(solution)/shard_map/ppermute | solution.py:761
  35.6 0.9 %shard_map.106 = (bf16[32,1536]{1,0:T(8,128)(2,1)S(1)}, f32[64,1536]{1,0:T(8,128)S(1)}, f32[64,1536]{1,0:T(8,128)S(1)}) custom-call(f32[96,1536]{1,0:T(8,128)S(1)} %shard_map.105.base_ref, bf16[64,1536]{1,0:T(8,128)(2,1)S(1)} %collective-permute-done.11.refs_0_, f32[1,1536]{1,0:T(1,128)S(1)} %broadcast_in_dim.11.refs_1_.refs_4_, bf16[31,1536]{1,0:T(8,128)(2,1)S(1)} %copy-done.3), custom_call_target="tpu_custom_call" | custom-call | flops 1000000000 | bytes 1000000 | tf_op jit(solution)/shard_map/pallas_call | solution.py:89
  36.6 0.6 %collective-permute-done.10.refs_0_ = bf16[32,1536]{1,0:T(8,128)(2,1)S(1)} collective-permute-done((bf16[32,1536]{1,0:T(8,128)(2,1)S(1)}, bf16[32,1536]{1,0:T(8,128)(2,1)S(1)}, u32[]{:S(2)}, u32[]{:S(2)}) %collective-permute-start.10) | collective-permute-done | bytes 98336 | tf_op jit(solution)/shard_map/ppermute | solution.py:761
  37.2 1.6 %shard_map.107 = bf16[64,1536]{1,0:T(8,128)(2,1)} custom-call(f32[96,1536]{1,0:T(8,128)S(1)} %shard_map.105.base_ref, bf16[32,1536]{1,0:T(8,128)(2,1)S(1)} %collective-permute-done.10.refs_0_, bf16[32,1536]{1,0:T(8,128)(2,1)S(1)} %get-tuple-element.68.refs_1_, f32[64,1536]{1,0:T(8,128)S(1)} %get-tuple-element.69.refs_2_, ...), custom_call_target="tpu_custom_call" | custom-call | flops 3000000000 | bytes 1000000 | tf_op jit(solution)/shard_map/pallas_call | solution.py:89
  (12 shorter events, 0.1 us)
Async XLA Ops:
  0.0 8.7 %copy-start.1 = (bf16[3,1536,384]{2,1,0:T(8,128)(2,1)S(1)}, bf16[3,1536,384]{2,1,0:T(8,128)(2,1)}, u32[]{:S(2)}) copy-start(bf16[3,1536,384]{2,1,0:T(8,128)(2,1)} %w_att.1) | copy-start | bytes 10616836
  0.0 8.7 %copy-start.2 = (bf16[512,1536]{1,0:T(8,128)(2,1)S(1)}, bf16[512,1536]{1,0:T(8,128)(2,1)}, u32[]{:S(2)}) copy-start(bf16[512,1536]{1,0:T(8,128)(2,1)} %w_sub.1) | copy-start | bytes 4718596
  3.0 9.3 %copy-start = (bf16[384,1536]{1,0:T(8,128)(2,1)S(1)}, bf16[384,1536]{1,0:T(8,128)(2,1)}, u32[]{:S(2)}) copy-start(bf16[384,1536]{1,0:T(8,128)(2,1)} %w_own.1) | copy-start | bytes 3538948
  3.0 9.3 %collective-permute-start.1 = (bf16[1,136,256]{2,1,0:T(8,128)(2,1)}, bf16[1,136,256]{2,1,0:T(8,128)(2,1)S(1)}, u32[]{:S(2)}, u32[]{:S(2)}) collective-permute-start(bf16[1,136,256]{2,1,0:T(8,128)(2,1)} %shard_map.91.stack_ref), channel_id=1, source_target_pairs={{0,8},{4,12},{8,0},{12,4},{1,9},{5,13},{9,1},{13,5},{2,10},{6,14},... | collective-permute-start | bytes 208904 | tf_op jit(solution)/shard_map/ppermute | solution.py:761
  7.1 6.6 %collective-permute-start.2 = (bf16[1,136,256]{2,1,0:T(8,128)(2,1)}, bf16[1,136,256]{2,1,0:T(8,128)(2,1)S(1)}, u32[]{:S(2)}, u32[]{:S(2)}) collective-permute-start(bf16[1,136,256]{2,1,0:T(8,128)(2,1)} %shard_map.91.stack_ref), channel_id=1, source_target_pairs={{0,12},{4,8},{8,4},{12,0},{1,13},{5,9},{9,5},{13,1},{2,14},{6,10},... | collective-permute-start | bytes 208904 | tf_op jit(solution)/shard_map/ppermute | solution.py:761
  8.5 5.3 %collective-permute-start.3 = (bf16[1,136,256]{2,1,0:T(8,128)(2,1)}, bf16[1,136,256]{2,1,0:T(8,128)(2,1)S(1)}, u32[]{:S(2)}, u32[]{:S(2)}) collective-permute-start(bf16[1,136,256]{2,1,0:T(8,128)(2,1)} %shard_map.91.stack_ref), channel_id=1, source_target_pairs={{0,4},{4,0},{8,12},{12,8},{1,5},{5,1},{9,13},{13,9},{2,6},{6,2},{1... | collective-permute-start | bytes 208904 | tf_op jit(solution)/shard_map/ppermute | solution.py:761
  8.7 0.9 %copy-start.4 = (bf16[1,136,256]{2,1,0:T(8,128)(2,1)S(1)}, bf16[1,136,256]{2,1,0:T(8,128)(2,1)}, u32[]{:S(2)}) copy-start(bf16[1,136,256]{2,1,0:T(8,128)(2,1)} %shard_map.91.stack_ref) | copy-start | bytes 208900
  10.8 4.7 %collective-permute-start = (bf16[1,136,256]{2,1,0:T(8,128)(2,1)S(1)}, bf16[1,136,256]{2,1,0:T(8,128)(2,1)S(1)}, u32[]{:S(2)}, u32[]{:S(2)}) collective-permute-start(bf16[1,136,256]{2,1,0:T(8,128)(2,1)S(1)} %get-tuple-element.38.refs_0_), channel_id=1, source_target_pairs={{0,2},{1,3},{2,0},{3,1},{4,6},{5,7},{6,4},{7,5},{8,10},{9,11},{10,... | collective-permute-start | bytes 208904 | tf_op jit(solution)/shard_map/ppermute | solution.py:761
  12.3 15.3 %collective-permute-start.8 = (bf16[384,1536]{1,0:T(8,128)(2,1)S(1)}, bf16[384,1536]{1,0:T(8,128)(2,1)S(1)}, u32[]{:S(2)}, u32[]{:S(2)}) collective-permute-start(bf16[384,1536]{1,0:T(8,128)(2,1)S(1)} %copy-done), channel_id=1, source_target_pairs={{0,1},{1,0},{2,3},{3,2},{4,5},{5,4},{6,7},{7,6},{8,9},{9,8},{10,11... | collective-permute-start | bytes 3538952 | tf_op jit(solution)/shard_map/ppermute | solution.py:761
  13.7 6.3 %collective-permute-start.5 = (bf16[3,136,256]{2,1,0:T(8,128)(2,1)S(1)}, bf16[3,136,256]{2,1,0:T(8,128)(2,1)S(1)}, u32[]{:S(2)}, u32[]{:S(2)}) collective-permute-start(bf16[3,136,256]{2,1,0:T(8,128)(2,1)S(1)} %shard_map.93.refs_2_), channel_id=1, source_target_pairs={{0,2},{1,3},{2,0},{3,1},{4,6},{5,7},{6,4},{7,5},{8,10},{9,11},{10,... | collective-permute-start | bytes 626696 | tf_op jit(solution)/shard_map/ppermute | solution.py:761
  15.5 2.2 %collective-permute-start.4 = (bf16[5,136,256]{2,1,0:T(8,128)(2,1)S(1)}, bf16[5,136,256]{2,1,0:T(8,128)(2,1)S(1)}, u32[]{:S(2)}, u32[]{:S(2)}) collective-permute-start(bf16[5,136,256]{2,1,0:T(8,128)(2,1)S(1)} %shard_map.94.stack_ref.refs_0_), channel_id=1, source_target_pairs={{0,1},{1,0},{2,3},{3,2},{4,5},{5,4},{6,7},{7,6},{8,9},{9,8},{10,11... | collective-permute-start | bytes 1044488 | tf_op jit(solution)/shard_map/ppermute | solution.py:761
  20.0 1.7 %copy-start.5 = (s32[256]{0:T(256)S(1)}, s32[256]{0:T(256)}, u32[]{:S(2)}) copy-start(s32[256]{0:T(256)} %param.10) | copy-start | bytes 3076
  20.0 1.7 %copy-start.6 = (s32[256]{0:T(256)S(1)}, s32[256]{0:T(256)}, u32[]{:S(2)}) copy-start(s32[256]{0:T(256)} %param.11) | copy-start | bytes 3076
  20.0 1.7 %copy-start.7 = (bf16[1056,512]{1,0:T(8,128)(2,1)S(1)}, bf16[1056,512]{1,0:T(8,128)(2,1)}, u32[]{:S(2)}) copy-start(bf16[1056,512]{1,0:T(8,128)(2,1)} %constant.2.clone.table.refs_4_) | copy-start | bytes 3244036
  20.1 1.7 %collective-permute-start.6 = (bf16[3,136,256]{2,1,0:T(8,128)(2,1)S(1)}, bf16[3,136,256]{2,1,0:T(8,128)(2,1)S(1)}, u32[]{:S(2)}, u32[]{:S(2)}) collective-permute-start(bf16[3,136,256]{2,1,0:T(8,128)(2,1)S(1)} %shard_map.97.refs_2_.stack_ref), channel_id=1, source_target_pairs={{0,1},{1,0},{2,3},{3,2},{4,5},{5,4},{6,7},{7,6},{8,9},{9,8},{10,11... | collective-permute-start | bytes 626696 | tf_op jit(solution)/shard_map/ppermute | solution.py:761
  26.3 1.3 %collective-permute-start.7 = (bf16[96,384]{1,0:T(8,128)(2,1)S(1)}, bf16[96,384]{1,0:T(8,128)(2,1)S(1)}, u32[]{:S(2)}, u32[]{:S(2)}) collective-permute-start(bf16[96,384]{1,0:T(8,128)(2,1)S(1)} %get-tuple-element.58), channel_id=1, source_target_pairs={{0,1},{1,0},{2,3},{3,2},{4,5},{5,4},{6,7},{7,6},{8,9},{9,8},{10,11... | collective-permute-start | bytes 221192 | tf_op jit(solution)/shard_map/ppermute | solution.py:761
  28.0 7.7 %collective-permute-start.11 = (bf16[64,1536]{1,0:T(8,128)(2,1)S(1)}, bf16[64,1536]{1,0:T(8,128)(2,1)S(1)}, u32[]{:S(2)}, u32[]{:S(2)}) collective-permute-start(bf16[64,1536]{1,0:T(8,128)(2,1)S(1)} %get-tuple-element.59._), channel_id=1, source_target_pairs={{0,2},{1,3},{2,0},{3,1},{4,6},{5,7},{6,4},{7,5},{8,10},{9,11},{10,... | collective-permute-start | bytes 589832 | tf_op jit(solution)/shard_map/ppermute | solution.py:761
  29.2 2.1 %copy-start.8 = (f32[1536]{0:T(1024)S(1)}, f32[1536]{0:T(1024)}, u32[]{:S(2)}) copy-start(f32[1536]{0:T(1024)} %param.15) | copy-start | bytes 18436
  31.2 1.3 %collective-permute-start.9 = (bf16[96,384]{1,0:T(8,128)(2,1)S(1)}, bf16[96,384]{1,0:T(8,128)(2,1)S(1)}, u32[]{:S(2)}, u32[]{:S(2)}) collective-permute-start(bf16[96,384]{1,0:T(8,128)(2,1)S(1)} %get-tuple-element.66), channel_id=1, source_target_pairs={{0,1},{1,0},{2,3},{3,2},{4,5},{5,4},{6,7},{7,6},{8,9},{9,8},{10,11... | collective-permute-start | bytes 221192 | tf_op jit(solution)/shard_map/ppermute | solution.py:761
  31.3 5.9 %collective-permute-start.10 = (bf16[32,1536]{1,0:T(8,128)(2,1)S(1)}, bf16[32,1536]{1,0:T(8,128)(2,1)S(1)}, u32[]{:S(2)}, u32[]{:S(2)}) collective-permute-start(bf16[32,1536]{1,0:T(8,128)(2,1)S(1)} %get-tuple-element.67), channel_id=1, source_target_pairs={{0,2},{1,3},{2,0},{3,1},{4,6},{5,7},{6,4},{7,5},{8,10},{9,11},{10,... | collective-permute-start | bytes 294920 | tf_op jit(solution)/shard_map/ppermute | solution.py:761
  32.5 3.1 %copy-start.3 = (bf16[31,1536]{1,0:T(8,128)(2,1)S(1)}, bf16[31,1536]{1,0:T(8,128)(2,1)}, u32[]{:S(2)}) copy-start(bf16[31,1536]{1,0:T(8,128)(2,1)} %refs_5_.1) | copy-start | bytes 285700

commit v11 on v10

--- a/solution.py
+++ b/solution.py
@@ -481,8 +481,10 @@
         )
         scores = jnp.minimum(scores, jnp.concatenate([most[...]] * heads, axis=0))
         weights = jnp.exp(scores - jnp.max(scores, axis=1, keepdims=True))
-        total = jnp.sum(weights, axis=1, keepdims=True)
-        ratio = dot32(weights.astype(jnp.bfloat16), v_pair) / total
+        summed = dot32(
+            weights.astype(jnp.bfloat16), jnp.concatenate([v_pair, jnp.ones_like(v_pair)], axis=1)
+        )
+        ratio = summed[:, :span] / summed[:, span:]
         merged = ratio[0:count]
         for head in range(1, heads):
             merged = jnp.where(head_of == head, ratio[head * count : (head + 1) * count], merged)

time: 38.9 us -> 38.7 us (level)
  transfers between devices with their start and end apart: 12 -> 12, of which waited for: 7 -> 7; matrix products, arithmetic and copies ran while one was open for 0% -> 0% of each run, Pallas kernels for 40% -> 39%
where the time goes in v11:
time: 38.7 us; the launch traced here: 38.6 us
  Pallas kernels  19.9 us (51%)
  starting transfers between devices  12 us (31%)
  waiting for transfers between devices  5.45 us (14%)
  local copies, waits for them, and re-layouts  0.96 us (2%)
    pallas_call x17, Pallas kernels, call(): pl.pallas_call(kernel, out_shape=out_shape, in_specs=specs, out_specs=jax...  19.9 us
    ppermute x12, starting transfers between devices, exchange(): lax.ppermute(block, axis, [(i, i ^ bit) for i in range(lax.axis_size(axis...  12 us
    ppermute x12, waiting for transfers between devices, exchange(): lax.ppermute(block, axis, [(i, i ^ bit) for i in range(lax.axis_size(axis...  5.45 us
    unnamed x18, local copies, waits for them, and re-layouts  0.95 us
  transfers between devices with their start and end apart: 12, of which 7 were waited for; matrix products, arithmetic and copies ran while one was open for 0% of the time, Pallas kernels for 39%

profile of v11, /device:TPU:0, one launch (start us, length us, event | category | flops | bytes accessed | tf_op | source)
XLA Modules:
  0.0 38.6 jit_solution(16603390594312829593)
XLA Ops:
  0.0 3.0 %shard_map.91.stack_ref = bf16[1,136,256]{2,1,0:T(8,128)(2,1)} custom-call(s32[1,256]{1,0:T(1,128)} %bitcast.3, s32[1,256]{1,0:T(1,128)} %bitcast.5, f32[320,128]{1,0:T(8,128)} %bitcast.7, bf16[1056,512]{1,0:T(8,128)(2,1)} %constant.2.clone.table.refs_4_), custom_call_target="tpu_custom_call" | custom-call | flops 2000000000 | bytes 1000000 | tf_op jit(solution)/shard_map/pallas_call | solution.py:89
  3.0 0.0 copy-start
  3.0 4.1 %collective-permute-start.1 = (bf16[1,136,256]{2,1,0:T(8,128)(2,1)}, bf16[1,136,256]{2,1,0:T(8,128)(2,1)S(1)}, u32[]{:S(2)}, u32[]{:S(2)}) collective-permute-start(bf16[1,136,256]{2,1,0:T(8,128)(2,1)} %shard_map.91.stack_ref), channel_id=1, source_target_pairs={{0,8},{4,12},{8,0},{12,4},{1,9},{5,13},{9,1},{13,5},{2,10},{6,14},... | collective-permute-start | bytes 208904 | tf_op jit(solution)/shard_map/ppermute | solution.py:763
  7.1 1.3 %collective-permute-start.2 = (bf16[1,136,256]{2,1,0:T(8,128)(2,1)}, bf16[1,136,256]{2,1,0:T(8,128)(2,1)S(1)}, u32[]{:S(2)}, u32[]{:S(2)}) collective-permute-start(bf16[1,136,256]{2,1,0:T(8,128)(2,1)} %shard_map.91.stack_ref), channel_id=1, source_target_pairs={{0,12},{4,8},{8,4},{12,0},{1,13},{5,9},{9,5},{13,1},{2,14},{6,10},... | collective-permute-start | bytes 208904 | tf_op jit(solution)/shard_map/ppermute | solution.py:763
  8.5 0.2 collective-permute-start.3
  8.7 0.9 %copy-done.4 = bf16[1,136,256]{2,1,0:T(8,128)(2,1)S(1)} copy-done((bf16[1,136,256]{2,1,0:T(8,128)(2,1)S(1)}, bf16[1,136,256]{2,1,0:T(8,128)(2,1)}, u32[]{:S(2)}) %copy-start.4) | copy-done | bytes 69656
  9.6 1.2 %shard_map.92 = (bf16[512,1536]{1,0:T(8,128)(2,1)S(1)}, bf16[3,1536,384]{2,1,0:T(8,128)(2,1)S(1)}, f32[8,384]{1,0:T(8,128)S(1)}, bf16[1,136,256]{2,1,0:T(8,128)(2,1)S(1)}) custom-call(bf16[1,136,256]{2,1,0:T(8,128)(2,1)S(1)} %copy-done.4, bf16[512,1536]{1,0:T(8,128)(2,1)S(1)} %copy-done.2, bf16[3,1536,384]{2,1,0:T(8,128)(2,1)S(1)} %copy-done.1), custom_call_target="tpu_custom_call" | custom-call | flops 2000000000 | bytes 1000000 | tf_op jit(solution)/shard_map/pallas_call | solution.py:89
  10.8 1.6 %collective-permute-start = (bf16[1,136,256]{2,1,0:T(8,128)(2,1)S(1)}, bf16[1,136,256]{2,1,0:T(8,128)(2,1)S(1)}, u32[]{:S(2)}, u32[]{:S(2)}) collective-permute-start(bf16[1,136,256]{2,1,0:T(8,128)(2,1)S(1)} %get-tuple-element.38.refs_0_), channel_id=1, source_target_pairs={{0,2},{1,3},{2,0},{3,1},{4,6},{5,7},{6,4},{7,5},{8,10},{9,11},{10,... | collective-permute-start | bytes 208904 | tf_op jit(solution)/shard_map/ppermute | solution.py:763
  12.3 0.0 collective-permute-start.8
  12.3 0.0 collective-permute-done.1.refs_0_
  12.3 1.3 %collective-permute-done.2.refs_1_ = bf16[1,136,256]{2,1,0:T(8,128)(2,1)S(1)} collective-permute-done((bf16[1,136,256]{2,1,0:T(8,128)(2,1)}, bf16[1,136,256]{2,1,0:T(8,128)(2,1)S(1)}, u32[]{:S(2)}, u32[]{:S(2)}) %collective-permute-start.2) | collective-permute-done | bytes 69664 | tf_op jit(solution)/shard_map/ppermute | solution.py:763
  13.7 0.1 collective-permute-done.3.refs_2_
  13.7 1.7 %collective-permute-start.5 = (bf16[3,136,256]{2,1,0:T(8,128)(2,1)S(1)}, bf16[3,136,256]{2,1,0:T(8,128)(2,1)S(1)}, u32[]{:S(2)}, u32[]{:S(2)}) collective-permute-start(bf16[3,136,256]{2,1,0:T(8,128)(2,1)S(1)} %shard_map.93.refs_2_), channel_id=1, source_target_pairs={{0,2},{1,3},{2,0},{3,1},{4,6},{5,7},{6,4},{7,5},{8,10},{9,11},{10,... | collective-permute-start | bytes 626696 | tf_op jit(solution)/shard_map/ppermute | solution.py:763
  15.5 0.0 collective-permute-done.refs_1_
  15.5 0.1 collective-permute-start.4
  15.6 2.1 %shard_map.95 = (bf16[128,384]{1,0:T(8,128)(2,1)S(1)}, bf16[320,384]{1,0:T(8,128)(2,1)S(1)}, bf16[320,384]{1,0:T(8,128)(2,1)S(1)}) custom-call(bf16[5,136,256]{2,1,0:T(8,128)(2,1)S(1)} %shard_map.94.stack_ref.refs_0_, bf16[512,1536]{1,0:T(8,128)(2,1)S(1)} %get-tuple-element.40.w_sub.refs_5_, bf16[3,1536,384]{2,1,0:T(8,128)(2,1)S(1)} %get-tuple-element.41.w_att, ...), custom_call_target="tpu_custom_call" | custom-call | flops 4840000000 | bytes 1000000 | tf_op jit(solution)/shard_map/pallas_call | solution.py:89
  17.7 0.0 collective-permute-done.4.stack_ref.refs_1_
  17.7 2.1 %shard_map.96 = (bf16[128,384]{1,0:T(8,128)(2,1)S(1)}, bf16[320,384]{1,0:T(8,128)(2,1)S(1)}, bf16[320,384]{1,0:T(8,128)(2,1)S(1)}) custom-call(bf16[5,136,256]{2,1,0:T(8,128)(2,1)S(1)} %collective-permute-done.4.stack_ref.refs_1_, bf16[512,1536]{1,0:T(8,128)(2,1)S(1)} %get-tuple-element.40.w_sub.refs_5_, bf16[3,1536,384]{2,1,0:T(8,128)(2,1)S(1)} %get-tuple-element.41.w_att, ...), custom_call_target="tpu_custom_call" | custom-call | flops 4840000000 | bytes 1000000 | tf_op jit(solution)/shard_map/pallas_call | solution.py:89
  19.9 0.1 collective-permute-done.5.refs_0_
  20.0 0.0 copy-start.5
  20.0 0.0 copy-start.6
  20.0 0.0 copy-start.7
  20.1 0.5 %collective-permute-start.6 = (bf16[3,136,256]{2,1,0:T(8,128)(2,1)S(1)}, bf16[3,136,256]{2,1,0:T(8,128)(2,1)S(1)}, u32[]{:S(2)}, u32[]{:S(2)}) collective-permute-start(bf16[3,136,256]{2,1,0:T(8,128)(2,1)S(1)} %shard_map.97.refs_2_.stack_ref), channel_id=1, source_target_pairs={{0,1},{1,0},{2,3},{3,2},{4,5},{5,4},{6,7},{7,6},{8,9},{9,8},{10,11... | collective-permute-start | bytes 626696 | tf_op jit(solution)/shard_map/ppermute | solution.py:763
  20.5 1.2 %shard_map.99 = (bf16[192,384]{1,0:T(8,128)(2,1)S(1)}, bf16[192,384]{1,0:T(8,128)(2,1)S(1)}) custom-call(bf16[3,136,256]{2,1,0:T(8,128)(2,1)S(1)} %shard_map.97.refs_2_.stack_ref, bf16[512,1536]{1,0:T(8,128)(2,1)S(1)} %get-tuple-element.40.w_sub.refs_5_, bf16[3,1536,384]{2,1,0:T(8,128)(2,1)S(1)} %get-tuple-element.41.w_att, ...), custom_call_target="tpu_custom_call" | custom-call | flops 3304000000 | bytes 1000000 | tf_op jit(solution)/shard_map/pallas_call | solution.py:89
  21.7 0.0 collective-permute-done.6.refs_3_.stack_ref
  21.8 0.0 copy-done.5
  21.8 0.0 copy-done.6
  21.8 0.0 copy-done.7
  21.8 0.6 %shard_map.98 = (bf16[16,256]{1,0:T(8,128)(2,1)S(1)}, f32[2,288]{1,0:T(2,128)S(1)}) custom-call(s32[1,256]{1,0:T(1,128)S(1)} %bitcast.4, s32[1,256]{1,0:T(1,128)S(1)} %bitcast.6, bf16[5,136,256]{2,1,0:T(8,128)(2,1)S(1)} %shard_map.94.stack_ref.refs_0_, bf16[5,136,256]{2,1,0:T(8,128)(2,1)S(1)} %collective-permute-done.4.stack_ref.refs_1_, ...), custom_call_target="tpu_custom_call" | custom-call | flops 1800000000 | bytes 1000000 | tf_op jit(solution)/shard_map/pallas_call | solution.py:89
  22.4 1.7 %shard_map.100 = (bf16[48,384]{1,0:T(8,128)(2,1)S(1)}, bf16[192,384]{1,0:T(8,128)(2,1)S(1)}, bf16[48,384]{1,0:T(8,128)(2,1)S(1)}, bf16[192,384]{1,0:T(8,128)(2,1)S(1)}, bf16[48,384]{1,0:T(8,128)(2,1)S(1)}) custom-call(bf16[3,136,256]{2,1,0:T(8,128)(2,1)S(1)} %collective-permute-done.6.refs_3_.stack_ref, ...), custom_call_target="tpu_custom_call" | custom-call | flops 3880000000 | bytes 1000000 | tf_op jit(solution)/shard_map/pallas_call | solution.py:89
  24.1 2.0 %shard_map.101 = (bf16[96,384]{1,0:T(8,128)(2,1)S(1)}, bf16[96,384]{1,0:T(8,128)(2,1)S(1)}, bf16[288,384]{1,0:T(8,128)(2,1)S(1)}, bf16[1024,384]{1,0:T(8,128)(2,...) custom-call(f32[2,288]{1,0:T(2,128)S(1)} %get-tuple-element.44.bound_ref, ...), custom_call_target="tpu_custom_call" | custom-call | flops 5000000000 | bytes 1000000 | tf_op jit(solution)/shard_map/pallas_call | solution.py:89
  26.1 0.3 collective-permute-start.7
  26.4 0.3 shard_map.102.refs_0_
  26.8 0.7 %collective-permute-done.7.refs_1_ = bf16[96,384]{1,0:T(8,128)(2,1)S(1)} collective-permute-done((bf16[96,384]{1,0:T(8,128)(2,1)S(1)}, bf16[96,384]{1,0:T(8,128)(2,1)S(1)}, u32[]{:S(2)}, u32[]{:S(2)}) %collective-permute-start.7) | collective-permute-done | bytes 73760 | tf_op jit(solution)/shard_map/ppermute | solution.py:763
  27.5 0.0 collective-permute-done.8.refs_2_.w_near
  27.5 0.3 shard_map.103
  27.8 1.2 %collective-permute-start.11 = (bf16[64,1536]{1,0:T(8,128)(2,1)S(1)}, bf16[64,1536]{1,0:T(8,128)(2,1)S(1)}, u32[]{:S(2)}, u32[]{:S(2)}) collective-permute-start(bf16[64,1536]{1,0:T(8,128)(2,1)S(1)} %get-tuple-element.59._), channel_id=1, source_target_pairs={{0,2},{1,3},{2,0},{3,1},{4,6},{5,7},{6,4},{7,5},{8,10},{9,11},{10,... | collective-permute-start | bytes 589832 | tf_op jit(solution)/shard_map/ppermute | solution.py:763
  29.0 1.9 %shard_map.104 = (bf16[96,384]{1,0:T(8,128)(2,1)S(1)}, bf16[96,384]{1,0:T(8,128)(2,1)S(1)}) custom-call(bf16[64,1536]{1,0:T(8,128)(2,1)S(1)} %get-tuple-element.59._, bf16[288,384]{1,0:T(8,128)(2,1)S(1)} %get-tuple-element.60.q_ref, bf16[1024,384]{1,0:T(8,128)(2,1)S(1)} %get-tuple-element.61.k_ref, bf16[1024,384]{1,0:T(8,128)(2,1)S(1)} %get-tuple-element.62.v_ref, ...), custom_call_target="tpu_custom_call" | custom-call | flops 2000000000 | bytes 1000000 | tf_op jit(solution)/shard_map/pallas_call | solution.py:89
  30.9 0.1 collective-permute-start.9
  31.0 0.0 copy-done.8
  31.0 0.9 %collective-permute-start.10 = (bf16[32,1536]{1,0:T(8,128)(2,1)S(1)}, bf16[32,1536]{1,0:T(8,128)(2,1)S(1)}, u32[]{:S(2)}, u32[]{:S(2)}) collective-permute-start(bf16[32,1536]{1,0:T(8,128)(2,1)S(1)} %get-tuple-element.67), channel_id=1, source_target_pairs={{0,2},{1,3},{2,0},{3,1},{4,6},{5,7},{6,4},{7,5},{8,10},{9,11},{10,... | collective-permute-start | bytes 294920 | tf_op jit(solution)/shard_map/ppermute | solution.py:763
  31.9 0.3 collective-permute-done.9.near
  32.2 0.9 %shard_map.105.base_ref = f32[96,1536]{1,0:T(8,128)S(1)} custom-call(bf16[96,384]{1,0:T(8,128)(2,1)S(1)} %get-tuple-element.65.own, bf16[96,384]{1,0:T(8,128)(2,1)S(1)} %collective-permute-done.9.near, bf16[384,1536]{1,0:T(8,128)(2,1)S(1)} %copy-done, bf16[384,1536]{1,0:T(8,128)(2,1)S(1)} %collective-permute-done.8.refs_2_.w_near, ...), custom_call_target="tpu_custom_call" | custom-call | flops 1200000000 | bytes 1000000 | tf_op jit(solution)/shard_map/pallas_call | solution.py:89
  33.1 2.5 %collective-permute-done.11.refs_0_ = bf16[64,1536]{1,0:T(8,128)(2,1)S(1)} collective-permute-done((bf16[64,1536]{1,0:T(8,128)(2,1)S(1)}, bf16[64,1536]{1,0:T(8,128)(2,1)S(1)}, u32[]{:S(2)}, u32[]{:S(2)}) %collective-permute-start.11) | collective-permute-done | bytes 196640 | tf_op jit(solution)/shard_map/ppermute | solution.py:763
  35.6 0.0 copy-done.3
  35.6 0.9 %shard_map.106 = (bf16[32,1536]{1,0:T(8,128)(2,1)S(1)}, f32[64,1536]{1,0:T(8,128)S(1)}, f32[64,1536]{1,0:T(8,128)S(1)}) custom-call(f32[96,1536]{1,0:T(8,128)S(1)} %shard_map.105.base_ref, bf16[64,1536]{1,0:T(8,128)(2,1)S(1)} %collective-permute-done.11.refs_0_, f32[1,1536]{1,0:T(1,128)S(1)} %broadcast_in_dim.11.refs_1_.refs_4_, bf16[31,1536]{1,0:T(8,128)(2,1)S(1)} %copy-done.3), custom_call_target="tpu_custom_call" | custom-call | flops 1000000000 | bytes 1000000 | tf_op jit(solution)/shard_map/pallas_call | solution.py:89
  36.6 0.4 %collective-permute-done.10.refs_0_ = bf16[32,1536]{1,0:T(8,128)(2,1)S(1)} collective-permute-done((bf16[32,1536]{1,0:T(8,128)(2,1)S(1)}, bf16[32,1536]{1,0:T(8,128)(2,1)S(1)}, u32[]{:S(2)}, u32[]{:S(2)}) %collective-permute-start.10) | collective-permute-done | bytes 98336 | tf_op jit(solution)/shard_map/ppermute | solution.py:763
  37.0 1.6 %shard_map.107 = bf16[64,1536]{1,0:T(8,128)(2,1)} custom-call(f32[96,1536]{1,0:T(8,128)S(1)} %shard_map.105.base_ref, bf16[32,1536]{1,0:T(8,128)(2,1)S(1)} %collective-permute-done.10.refs_0_, bf16[32,1536]{1,0:T(8,128)(2,1)S(1)} %get-tuple-element.68.refs_1_, f32[64,1536]{1,0:T(8,128)S(1)} %get-tuple-element.69.refs_2_, ...), custom_call_target="tpu_custom_call" | custom-call | flops 3000000000 | bytes 1000000 | tf_op jit(solution)/shard_map/pallas_call | solution.py:89
  (12 shorter events, 0.1 us)
Async XLA Ops:
  0.0 8.7 %copy-start.1 = (bf16[3,1536,384]{2,1,0:T(8,128)(2,1)S(1)}, bf16[3,1536,384]{2,1,0:T(8,128)(2,1)}, u32[]{:S(2)}) copy-start(bf16[3,1536,384]{2,1,0:T(8,128)(2,1)} %w_att.1) | copy-start | bytes 10616836
  0.0 8.7 %copy-start.2 = (bf16[512,1536]{1,0:T(8,128)(2,1)S(1)}, bf16[512,1536]{1,0:T(8,128)(2,1)}, u32[]{:S(2)}) copy-start(bf16[512,1536]{1,0:T(8,128)(2,1)} %w_sub.1) | copy-start | bytes 4718596
  3.0 9.3 %copy-start = (bf16[384,1536]{1,0:T(8,128)(2,1)S(1)}, bf16[384,1536]{1,0:T(8,128)(2,1)}, u32[]{:S(2)}) copy-start(bf16[384,1536]{1,0:T(8,128)(2,1)} %w_own.1) | copy-start | bytes 3538948
  3.0 9.3 %collective-permute-start.1 = (bf16[1,136,256]{2,1,0:T(8,128)(2,1)}, bf16[1,136,256]{2,1,0:T(8,128)(2,1)S(1)}, u32[]{:S(2)}, u32[]{:S(2)}) collective-permute-start(bf16[1,136,256]{2,1,0:T(8,128)(2,1)} %shard_map.91.stack_ref), channel_id=1, source_target_pairs={{0,8},{4,12},{8,0},{12,4},{1,9},{5,13},{9,1},{13,5},{2,10},{6,14},... | collective-permute-start | bytes 208904 | tf_op jit(solution)/shard_map/ppermute | solution.py:763
  7.1 6.6 %collective-permute-start.2 = (bf16[1,136,256]{2,1,0:T(8,128)(2,1)}, bf16[1,136,256]{2,1,0:T(8,128)(2,1)S(1)}, u32[]{:S(2)}, u32[]{:S(2)}) collective-permute-start(bf16[1,136,256]{2,1,0:T(8,128)(2,1)} %shard_map.91.stack_ref), channel_id=1, source_target_pairs={{0,12},{4,8},{8,4},{12,0},{1,13},{5,9},{9,5},{13,1},{2,14},{6,10},... | collective-permute-start | bytes 208904 | tf_op jit(solution)/shard_map/ppermute | solution.py:763
  8.5 5.3 %collective-permute-start.3 = (bf16[1,136,256]{2,1,0:T(8,128)(2,1)}, bf16[1,136,256]{2,1,0:T(8,128)(2,1)S(1)}, u32[]{:S(2)}, u32[]{:S(2)}) collective-permute-start(bf16[1,136,256]{2,1,0:T(8,128)(2,1)} %shard_map.91.stack_ref), channel_id=1, source_target_pairs={{0,4},{4,0},{8,12},{12,8},{1,5},{5,1},{9,13},{13,9},{2,6},{6,2},{1... | collective-permute-start | bytes 208904 | tf_op jit(solution)/shard_map/ppermute | solution.py:763
  8.7 0.9 %copy-start.4 = (bf16[1,136,256]{2,1,0:T(8,128)(2,1)S(1)}, bf16[1,136,256]{2,1,0:T(8,128)(2,1)}, u32[]{:S(2)}) copy-start(bf16[1,136,256]{2,1,0:T(8,128)(2,1)} %shard_map.91.stack_ref) | copy-start | bytes 208900
  10.8 4.7 %collective-permute-start = (bf16[1,136,256]{2,1,0:T(8,128)(2,1)S(1)}, bf16[1,136,256]{2,1,0:T(8,128)(2,1)S(1)}, u32[]{:S(2)}, u32[]{:S(2)}) collective-permute-start(bf16[1,136,256]{2,1,0:T(8,128)(2,1)S(1)} %get-tuple-element.38.refs_0_), channel_id=1, source_target_pairs={{0,2},{1,3},{2,0},{3,1},{4,6},{5,7},{6,4},{7,5},{8,10},{9,11},{10,... | collective-permute-start | bytes 208904 | tf_op jit(solution)/shard_map/ppermute | solution.py:763
  12.3 15.1 %collective-permute-start.8 = (bf16[384,1536]{1,0:T(8,128)(2,1)S(1)}, bf16[384,1536]{1,0:T(8,128)(2,1)S(1)}, u32[]{:S(2)}, u32[]{:S(2)}) collective-permute-start(bf16[384,1536]{1,0:T(8,128)(2,1)S(1)} %copy-done), channel_id=1, source_target_pairs={{0,1},{1,0},{2,3},{3,2},{4,5},{5,4},{6,7},{7,6},{8,9},{9,8},{10,11... | collective-permute-start | bytes 3538952 | tf_op jit(solution)/shard_map/ppermute | solution.py:763
  13.7 6.3 %collective-permute-start.5 = (bf16[3,136,256]{2,1,0:T(8,128)(2,1)S(1)}, bf16[3,136,256]{2,1,0:T(8,128)(2,1)S(1)}, u32[]{:S(2)}, u32[]{:S(2)}) collective-permute-start(bf16[3,136,256]{2,1,0:T(8,128)(2,1)S(1)} %shard_map.93.refs_2_), channel_id=1, source_target_pairs={{0,2},{1,3},{2,0},{3,1},{4,6},{5,7},{6,4},{7,5},{8,10},{9,11},{10,... | collective-permute-start | bytes 626696 | tf_op jit(solution)/shard_map/ppermute | solution.py:763
  15.5 2.2 %collective-permute-start.4 = (bf16[5,136,256]{2,1,0:T(8,128)(2,1)S(1)}, bf16[5,136,256]{2,1,0:T(8,128)(2,1)S(1)}, u32[]{:S(2)}, u32[]{:S(2)}) collective-permute-start(bf16[5,136,256]{2,1,0:T(8,128)(2,1)S(1)} %shard_map.94.stack_ref.refs_0_), channel_id=1, source_target_pairs={{0,1},{1,0},{2,3},{3,2},{4,5},{5,4},{6,7},{7,6},{8,9},{9,8},{10,11... | collective-permute-start | bytes 1044488 | tf_op jit(solution)/shard_map/ppermute | solution.py:763
  20.0 1.7 %copy-start.5 = (s32[256]{0:T(256)S(1)}, s32[256]{0:T(256)}, u32[]{:S(2)}) copy-start(s32[256]{0:T(256)} %param.10) | copy-start | bytes 3076
  20.0 1.7 %copy-start.6 = (s32[256]{0:T(256)S(1)}, s32[256]{0:T(256)}, u32[]{:S(2)}) copy-start(s32[256]{0:T(256)} %param.11) | copy-start | bytes 3076
  20.0 1.7 %copy-start.7 = (bf16[1056,512]{1,0:T(8,128)(2,1)S(1)}, bf16[1056,512]{1,0:T(8,128)(2,1)}, u32[]{:S(2)}) copy-start(bf16[1056,512]{1,0:T(8,128)(2,1)} %constant.2.clone.table.refs_4_) | copy-start | bytes 3244036
  20.1 1.7 %collective-permute-start.6 = (bf16[3,136,256]{2,1,0:T(8,128)(2,1)S(1)}, bf16[3,136,256]{2,1,0:T(8,128)(2,1)S(1)}, u32[]{:S(2)}, u32[]{:S(2)}) collective-permute-start(bf16[3,136,256]{2,1,0:T(8,128)(2,1)S(1)} %shard_map.97.refs_2_.stack_ref), channel_id=1, source_target_pairs={{0,1},{1,0},{2,3},{3,2},{4,5},{5,4},{6,7},{7,6},{8,9},{9,8},{10,11... | collective-permute-start | bytes 626696 | tf_op jit(solution)/shard_map/ppermute | solution.py:763
  26.1 1.3 %collective-permute-start.7 = (bf16[96,384]{1,0:T(8,128)(2,1)S(1)}, bf16[96,384]{1,0:T(8,128)(2,1)S(1)}, u32[]{:S(2)}, u32[]{:S(2)}) collective-permute-start(bf16[96,384]{1,0:T(8,128)(2,1)S(1)} %get-tuple-element.58), channel_id=1, source_target_pairs={{0,1},{1,0},{2,3},{3,2},{4,5},{5,4},{6,7},{7,6},{8,9},{9,8},{10,11... | collective-permute-start | bytes 221192 | tf_op jit(solution)/shard_map/ppermute | solution.py:763
  27.8 7.8 %collective-permute-start.11 = (bf16[64,1536]{1,0:T(8,128)(2,1)S(1)}, bf16[64,1536]{1,0:T(8,128)(2,1)S(1)}, u32[]{:S(2)}, u32[]{:S(2)}) collective-permute-start(bf16[64,1536]{1,0:T(8,128)(2,1)S(1)} %get-tuple-element.59._), channel_id=1, source_target_pairs={{0,2},{1,3},{2,0},{3,1},{4,6},{5,7},{6,4},{7,5},{8,10},{9,11},{10,... | collective-permute-start | bytes 589832 | tf_op jit(solution)/shard_map/ppermute | solution.py:763
  29.0 1.9 %copy-start.8 = (f32[1536]{0:T(1024)S(1)}, f32[1536]{0:T(1024)}, u32[]{:S(2)}) copy-start(f32[1536]{0:T(1024)} %param.15) | copy-start | bytes 18436
  30.9 1.3 %collective-permute-start.9 = (bf16[96,384]{1,0:T(8,128)(2,1)S(1)}, bf16[96,384]{1,0:T(8,128)(2,1)S(1)}, u32[]{:S(2)}, u32[]{:S(2)}) collective-permute-start(bf16[96,384]{1,0:T(8,128)(2,1)S(1)} %get-tuple-element.66), channel_id=1, source_target_pairs={{0,1},{1,0},{2,3},{3,2},{4,5},{5,4},{6,7},{7,6},{8,9},{9,8},{10,11... | collective-permute-start | bytes 221192 | tf_op jit(solution)/shard_map/ppermute | solution.py:763
  31.0 6.0 %collective-permute-start.10 = (bf16[32,1536]{1,0:T(8,128)(2,1)S(1)}, bf16[32,1536]{1,0:T(8,128)(2,1)S(1)}, u32[]{:S(2)}, u32[]{:S(2)}) collective-permute-start(bf16[32,1536]{1,0:T(8,128)(2,1)S(1)} %get-tuple-element.67), channel_id=1, source_target_pairs={{0,2},{1,3},{2,0},{3,1},{4,6},{5,7},{6,4},{7,5},{8,10},{9,11},{10,... | collective-permute-start | bytes 294920 | tf_op jit(solution)/shard_map/ppermute | solution.py:763
  32.2 3.4 %copy-start.3 = (bf16[31,1536]{1,0:T(8,128)(2,1)S(1)}, bf16[31,1536]{1,0:T(8,128)(2,1)}, u32[]{:S(2)}) copy-start(bf16[31,1536]{1,0:T(8,128)(2,1)} %refs_5_.1) | copy-start | bytes 285700
